TPU v7x, 256 devices: a whole 4x4x8 slice. The times are simulated.
256 devices in a mesh: row: 8 (over z), col: 32 (over y, x, core).
Axes of the slice: x: 4, y: 4, z: 8, core: 2. Of those that a mesh axis runs over, the one named last changes fastest.
Arguments:
- features: bfloat16 [32, 2048, 256], P('col', 'row'), may hold values from -6 to 6
- weight: bfloat16 [256, 256], replicated, may hold values from -0.375 to 0.375
- cotangent: bfloat16 [65536, 256], P(('row', 'col')), may hold values from -6 to 6
- blk_vals: bfloat16 [8, 32, 192, 128, 128], P('row', 'col'), may hold values from -0.0546875 to 0.0546875
- blk_rows: int32 [8, 32, 192], P('row', 'col'), may hold values from 0 to 63
- blk_cols: int32 [8, 32, 192], P('row', 'col'), may hold values from 0 to 15
- blk_count: int32 [8, 32], P('row', 'col'), may hold values from 24 to 192, as said below
Outputs:
- activated: bfloat16 [65536, 256], P(('row', 'col'))
- grad_weight: float32 [256, 256], replicated
- grad_features: bfloat16 [32, 2048, 256], P('col', 'row')
Inputs may be any that keep to these rules, and one draw needn't show every extreme that they name: Only the first blk_count slots of a panel pair are used; a pair whose row and column node ranges intersect uses all 192, every other pair at most 96.
All inputs are finite; a program needn't handle non-finite values.
Results may differ from a plain program's by a relative error of at most 0.0059.
Values may be sent and summed in bfloat16 or wider, within the bound.
No kernel may reach another device: no remote copies, remote signals or barrier semaphores. Data moves between devices by JAX's collectives and lax.ppermute only.
A program may use at most 128 MiB of HBM per device.

v0:
```python
import jax
import jax.numpy as jnp
from jax import lax
from jax.sharding import PartitionSpec as P


def block_terms(values, index, source, live_count, transpose):
    total_slots = values.shape[0]
    group = 64
    width = source.shape[-1]
    side = values.shape[-1]
    if transpose:
        form = "bji,bjf->bif"
    else:
        form = "bij,bjf->bif"

    def one_group(group_index, buffer):
        first = group_index * group
        block_vals = lax.dynamic_slice_in_dim(values, first, group, 0)
        block_ids = lax.dynamic_slice_in_dim(index, first, group, 0)
        picked = jnp.take(source, block_ids, axis=0)
        product = jnp.einsum(form, block_vals, picked, preferred_element_type=jnp.float32)
        alive = first + jnp.arange(group, dtype=jnp.int32) < live_count
        product = jnp.where(alive[:, None, None], product, 0.0)
        return lax.dynamic_update_slice_in_dim(buffer, product, first, 0)

    buffer = jnp.zeros((total_slots, side, width), jnp.float32)
    groups = total_slots // group
    return lax.fori_loop(0, groups, one_group, buffer)


def per_device(features, weight, cotangent, blk_vals, blk_rows, blk_cols, blk_count):
    rows_here = cotangent.shape[0]
    width = cotangent.shape[1]
    side = blk_vals.shape[-1]
    row_blocks = rows_here * lax.axis_size("col") // side
    col_blocks = rows_here * lax.axis_size("row") // side
    values = blk_vals[0, 0]
    row_ids = blk_rows[0, 0]
    col_ids = blk_cols[0, 0]
    live_count = blk_count[0, 0]
    panel = lax.all_gather(features, "row", axis=1, tiled=True)
    source = panel.reshape(col_blocks, side, width)
    products = block_terms(values, col_ids, source, live_count, False)
    partial_rows = jax.ops.segment_sum(products, row_ids, num_segments=row_blocks)
    own_rows = lax.psum_scatter(
        partial_rows.reshape(row_blocks * side, width), "col", scatter_dimension=0, tiled=True
    )
    aggregated = own_rows.astype(jnp.bfloat16)
    pre = jnp.dot(aggregated, weight, preferred_element_type=jnp.float32)
    sigma = jax.nn.sigmoid(pre)
    activated = (pre * sigma).astype(jnp.bfloat16)
    grad_pre = (cotangent.astype(jnp.float32) * sigma * (1.0 + pre * (1.0 - sigma))).astype(
        jnp.bfloat16
    )
    local_weight = lax.dot_general(
        aggregated, grad_pre, (((0,), (0,)), ((), ())), preferred_element_type=jnp.float32
    )
    grad_weight = lax.psum(local_weight, ("row", "col"))
    grad_agg = lax.dot_general(
        grad_pre, weight, (((1,), (1,)), ((), ())), preferred_element_type=jnp.float32
    ).astype(jnp.bfloat16)
    grad_rows = lax.all_gather(grad_agg, "col", axis=0, tiled=True)
    grad_source = grad_rows.reshape(row_blocks, side, width)
    back_products = block_terms(values, row_ids, grad_source, live_count, True)
    partial_cols = jax.ops.segment_sum(back_products, col_ids, num_segments=col_blocks)
    own_cols = lax.psum_scatter(
        partial_cols.reshape(col_blocks * side, width), "row", scatter_dimension=0, tiled=True
    )
    grad_features = own_cols.astype(jnp.bfloat16).reshape(1, rows_here, width)
    return (activated, grad_weight, grad_features)


def solution(mesh):
    return jax.shard_map(
        per_device,
        mesh=mesh,
        in_specs=(
            P("col", "row", None),
            P(),
            P(("row", "col"), None),
            P("row", "col", None, None, None),
            P("row", "col", None),
            P("row", "col", None),
            P("row", "col"),
        ),
        out_specs=(P(("row", "col"), None), P(), P("col", "row", None)),
        check_vma=False,
    )
```

profile of v0, /device:TPU:1, one launch (start us, length us, event | category | flops | bytes accessed | tf_op | source)
XLA Modules:
  0.0 704.2 jit_solution(3789345493444295329)
XLA Ops:
  7.2 0.0 all-gather.3.cloned.1.call-start
  7.2 0.7 all-gather.3.cloned.1.call-update
  7.9 0.0 reduce-scatter.3.cloned.1.call-start
  8.0 39.3 %all-gather.3.cloned.1.call-done = bf16[1,2048,256]{2,1,0:T(8,128)(2,1)} async-done(((bf16[1,256,256]{2,1,0:T(8,128)(2,1)}), bf16[1,2048,256]{2,1,0:T(8,128)(2,1)}) %all-gather.3.cloned.1.call-update) | async-done | bytes 1048592 | tf_op jit(solution)/shard_map/all_gather | solution.py:42
  47.3 11.5 %broadcast.44.clone = f32[192,128,256]{2,1,0:T(8,128)} broadcast(f32[]{:T(128)} %constant.126.clone.1), dimensions={} | broadcast | bytes 25165828 | tf_op jit(solution)/shard_map/broadcast.3
  58.8 32.7 %while.26 = (s32[]{:T(128)}, f32[192,128,256]{2,1,0:T(8,128)}, s32[]{:T(128)}, bf16[192,128,128]{2,1,0:T(8,128)(2,1)}, s32[192]{0:T(256)S(1)}, /*index=5*/bf16[1...) while((s32[]{:T(128)}, f32[192,128,256]{2,1,0:T(8,128)}, s32[]{:T(128)}, ...), condition=%wide.region_1.0_spmd, body=%wide.region_0.1_spmd.sunk | while | flops 541066752 | bytes 23075232 | solution.py:29
  58.8 0.7 compare_and_fusion.4
  59.5 2.8 gather_fusion
  62.3 7.4 %select_dynamic-update-slice_fusion.4 = f32[192,128,256]{2,1,0:T(8,128)} fusion(f32[192,128,256]{2,1,0:T(8,128)} %get-tuple-element.358, s32[]{:T(128)S(6)} %select_n.88, pred[64]{0:T(512)(128)(4,1)S(1)} %get-tuple-element.335, bf16[64,128,256]{2,1,0:T(8,128)(2,1)} %gather_fusion, pred[64]{0:T(512)(128)(4,1)S(1)} %get-tuple-element.337, ...), kind=kOutput, calls=%fused_computation.4.clone.1 | convolution fusion | flops 541065216 | bytes 14681216 | tf_op jit(solution)/shard_map/while/body/eval_jaxpr/bij,bjf->bif/dot_general | solution.py:22
  69.7 0.7 compare_and_fusion.4
  70.4 2.8 gather_fusion
  73.2 7.4 %select_dynamic-update-slice_fusion.4 = f32[192,128,256]{2,1,0:T(8,128)} fusion(f32[192,128,256]{2,1,0:T(8,128)} %get-tuple-element.358, s32[]{:T(128)S(6)} %select_n.88, pred[64]{0:T(512)(128)(4,1)S(1)} %get-tuple-element.335, bf16[64,128,256]{2,1,0:T(8,128)(2,1)} %gather_fusion, pred[64]{0:T(512)(128)(4,1)S(1)} %get-tuple-element.337, ...), kind=kOutput, calls=%fused_computation.4.clone.1 | convolution fusion | flops 541065216 | bytes 14681216 | tf_op jit(solution)/shard_map/while/body/eval_jaxpr/bij,bjf->bif/dot_general | solution.py:22
  80.6 0.7 compare_and_fusion.4
  81.3 2.8 gather_fusion
  84.1 7.4 %select_dynamic-update-slice_fusion.4 = f32[192,128,256]{2,1,0:T(8,128)} fusion(f32[192,128,256]{2,1,0:T(8,128)} %get-tuple-element.358, s32[]{:T(128)S(6)} %select_n.88, pred[64]{0:T(512)(128)(4,1)S(1)} %get-tuple-element.335, bf16[64,128,256]{2,1,0:T(8,128)(2,1)} %gather_fusion, pred[64]{0:T(512)(128)(4,1)S(1)} %get-tuple-element.337, ...), kind=kOutput, calls=%fused_computation.4.clone.1 | convolution fusion | flops 541065216 | bytes 14681216 | tf_op jit(solution)/shard_map/while/body/eval_jaxpr/bij,bjf->bif/dot_general | solution.py:22
  91.5 4.3 broadcast_in_dim.108
  95.7 56.0 %scatter_fusion = f32[64,128,256]{2,1,0:T(8,128)} fusion(f32[64,128,256]{2,1,0:T(8,128)} %broadcast_in_dim.108, s32[192]{0:T(256)S(1)} %bitcast.22, f32[192,128,256]{2,1,0:T(8,128)} %get-tuple-element.221), kind=kCustom, calls=%fused_computation.2 | custom fusion | flops 6291456 | bytes 75498240 | tf_op jit(solution)/shard_map/scatter-add | solution.py:45
  151.8 0.0 reduce-scatter.3.cloned.1.call-update
  151.8 0.0 all-gather.5.cloned.1.call-start
  151.8 103.8 %reduce-scatter.3.cloned.1.call-done = f32[256,256]{1,0:T(8,128)} async-done(((f32[8192,256]{1,0:T(8,128)}), f32[256,256]{1,0:T(8,128)}) %reduce-scatter.3.cloned.1.call-update) | async-done | bytes 262160 | tf_op jit(solution)/shard_map/reduce_scatter | solution.py:46
  255.6 1.9 multiply_convert_fusion
  257.5 0.9 convolution_convert_fusion
  258.3 0.0 all-gather.5.cloned.1.call-update
  258.4 0.0 reduce-scatter.5.cloned.1.call-start
  258.4 8.5 %copy.10 = bf16[1,1,192,128,128]{3,4,2,1,0:T(8,128)(2,1)} copy(bf16[1,1,192,128,128]{4,3,2,1,0:T(8,128)(2,1)} %bitcast.20) | data formatting | bytes 12582912 | tf_op args[3]
  266.9 44.7 %all-gather.5.cloned.1.call-done = bf16[8192,256]{1,0:T(8,128)(2,1)} async-done(((bf16[256,256]{1,0:T(8,128)(2,1)}), bf16[8192,256]{1,0:T(8,128)(2,1)}) %all-gather.5.cloned.1.call-update) | async-done | bytes 4194320 | tf_op jit(solution)/shard_map/all_gather | solution.py:63
  311.7 11.5 %broadcast.44 = f32[192,128,256]{2,1,0:T(8,128)} broadcast(f32[]{:T(128)} %constant.126.clone.1), dimensions={} | broadcast | bytes 25165828 | tf_op jit(solution)/shard_map/broadcast.3
  323.2 39.2 %while.27 = (s32[]{:T(128)}, f32[192,128,256]{2,1,0:T(8,128)}, s32[]{:T(128)}, bf16[192,128,128]{1,2,0:T(8,128)(2,1)}, s32[192]{0:T(256)S(1)}, /*index=5*/bf16[6...) while((s32[]{:T(128)}, f32[192,128,256]{2,1,0:T(8,128)}, s32[]{:T(128)}, ...), condition=%wide.region_6.7_spmd, body=%wide.region_5.6_spmd.sunk | while | flops 541066752 | bytes 23075232 | solution.py:29
  323.2 0.7 compare_and_fusion.5
  323.9 5.0 gather_fusion.1
  328.9 7.4 %select_dynamic-update-slice_fusion.5 = f32[192,128,256]{2,1,0:T(8,128)} fusion(f32[192,128,256]{2,1,0:T(8,128)} %get-tuple-element.388, s32[]{:T(128)S(6)} %select_n.91, pred[64]{0:T(512)(128)(4,1)S(1)} %get-tuple-element.344, bf16[64,128,256]{2,1,0:T(8,128)(2,1)} %gather_fusion.1, pred[64]{0:T(512)(128)(4,1)S(1)} %get-tuple-element.346, ...), kind=kOutput, calls=%fused_computation.16.clone.1 | convolution fusion | flops 541065216 | bytes 14681216 | tf_op jit(solution)/shard_map/while/body/eval_jaxpr/bji,bjf->bif/dot_general | solution.py:22
  336.2 0.7 compare_and_fusion.5
  337.0 5.0 gather_fusion.1
  341.9 7.4 %select_dynamic-update-slice_fusion.5 = f32[192,128,256]{2,1,0:T(8,128)} fusion(f32[192,128,256]{2,1,0:T(8,128)} %get-tuple-element.388, s32[]{:T(128)S(6)} %select_n.91, pred[64]{0:T(512)(128)(4,1)S(1)} %get-tuple-element.344, bf16[64,128,256]{2,1,0:T(8,128)(2,1)} %gather_fusion.1, pred[64]{0:T(512)(128)(4,1)S(1)} %get-tuple-element.346, ...), kind=kOutput, calls=%fused_computation.16.clone.1 | convolution fusion | flops 541065216 | bytes 14681216 | tf_op jit(solution)/shard_map/while/body/eval_jaxpr/bji,bjf->bif/dot_general | solution.py:22
  349.3 0.7 compare_and_fusion.5
  350.1 5.0 gather_fusion.1
  355.0 7.4 %select_dynamic-update-slice_fusion.5 = f32[192,128,256]{2,1,0:T(8,128)} fusion(f32[192,128,256]{2,1,0:T(8,128)} %get-tuple-element.388, s32[]{:T(128)S(6)} %select_n.91, pred[64]{0:T(512)(128)(4,1)S(1)} %get-tuple-element.344, bf16[64,128,256]{2,1,0:T(8,128)(2,1)} %gather_fusion.1, pred[64]{0:T(512)(128)(4,1)S(1)} %get-tuple-element.346, ...), kind=kOutput, calls=%fused_computation.16.clone.1 | convolution fusion | flops 541065216 | bytes 14681216 | tf_op jit(solution)/shard_map/while/body/eval_jaxpr/bji,bjf->bif/dot_general | solution.py:22
  362.4 0.2 broadcast_in_dim.109
  362.6 36.1 %scatter_fusion.1 = f32[16,128,256]{2,1,0:T(8,128)S(1)} fusion(f32[16,128,256]{2,1,0:T(8,128)S(1)} %broadcast_in_dim.109, s32[192]{0:T(256)S(1)} %get-tuple-element.431, f32[192,128,256]{2,1,0:T(8,128)} %get-tuple-element.222), kind=kCustom, calls=%fused_computation.3 | custom fusion | flops 6291456 | bytes 75498240 | tf_op jit(solution)/shard_map/scatter-add | solution.py:66
  398.8 1.3 copy-done.3
  400.1 0.0 reduce-scatter.5.cloned.1.call-update
  400.1 0.0 all-reduce.2.cloned.1.call-start
  400.2 0.9 fusion.18
  401.1 0.0 all-reduce.2.cloned.1.call-update
  401.1 36.2 %reduce-scatter.5.cloned.1.call-done = f32[256,256]{1,0:T(8,128)} async-done(((f32[2048,256]{1,0:T(8,128)}), f32[256,256]{1,0:T(8,128)}) %reduce-scatter.5.cloned.1.call-update) | async-done | bytes 262160 | tf_op jit(solution)/shard_map/reduce_scatter | solution.py:67
  437.3 1.6 convert_bitcast_fusion
  438.9 257.0 %all-reduce.2.cloned.1.call-done = f32[256,256]{1,0:T(8,128)} async-done(((f32[256,256]{1,0:T(8,128)}), f32[256,256]{1,0:T(8,128)}) %all-reduce.2.cloned.1.call-update) | async-done | bytes 262160 | tf_op jit(solution)/shard_map/psum | solution.py:59
  696.0 1.7 copy.30
  (21 shorter events, 0.1 us)
Async XLA Ops:
  7.2 248.4 %copy-start = (bf16[256,256]{1,0:T(8,128)(2,1)S(1)}, bf16[256,256]{1,0:T(8,128)(2,1)}, u32[]{:S(2)}) copy-start(bf16[256,256]{1,0:T(8,128)(2,1)} %param.12) | copy-start | bytes 393220
  7.2 40.1 %all-gather.3.cloned.1.call-start = ((), (), s32[]{:S(2)}) async-start(), calls=%async_computation.2 | async-start | bytes 1179648 | tf_op jit(solution)/shard_map/all_gather | solution.py:42
  7.9 247.7 %reduce-scatter.3.cloned.1.call-start = ((), (), s32[]{:S(2)}) async-start(), calls=%async_computation.3 | async-start | bytes 8650752 | tf_op jit(solution)/shard_map/reduce_scatter | solution.py:46
  47.3 11.5 %copy-start.2 = (bf16[1,2048,256]{2,1,0:T(8,128)(2,1)S(1)}, bf16[1,2048,256]{2,1,0:T(8,128)(2,1)}, u32[]{:S(2)}) copy-start(bf16[1,2048,256]{2,1,0:T(8,128)(2,1)} %all-gather.3.cloned.1.call-done) | copy-start | bytes 3145732
  47.3 11.5 %copy-start.6 = (s32[1,1,192]{2,1,0:T(1,128)S(1)}, s32[1,1,192]{2,1,0:T(1,128)}, u32[]{:S(2)}) copy-start(s32[1,1,192]{2,1,0:T(1,128)} %param.16) | copy-start | bytes 2308
  91.5 4.3 copy-start.5
  151.7 103.8 %copy-start.7 = (bf16[256,256]{1,0:T(8,128)(2,1)S(1)}, bf16[256,256]{1,0:T(8,128)(2,1)}, u32[]{:S(2)}) copy-start(bf16[256,256]{1,0:T(8,128)(2,1)} %param.13) | copy-start | bytes 393220
  151.8 159.9 %all-gather.5.cloned.1.call-start = ((), (), s32[]{:S(2)}) async-start(), calls=%async_computation.5 | async-start | bytes 4325376 | tf_op jit(solution)/shard_map/all_gather | solution.py:63
  258.4 178.9 %reduce-scatter.5.cloned.1.call-start = ((), (), s32[]{:S(2)}) async-start(), calls=%async_computation.6 | async-start | bytes 2359296 | tf_op jit(solution)/shard_map/reduce_scatter | solution.py:67
  362.6 37.6 %copy-start.4 = (f32[256,256]{1,0:T(8,128)S(1)}, f32[256,256]{1,0:T(8,128)}, u32[]{:S(2)}) copy-start(f32[256,256]{1,0:T(8,128)} %reduce-scatter.3.cloned.1.call-done) | copy-start | bytes 786436
  362.6 335.0 %copy-start.1 = (bf16[256,256]{1,0:T(8,128)(2,1)S(1)}, bf16[256,256]{1,0:T(8,128)(2,1)}, u32[]{:S(2)}) copy-start(bf16[256,256]{1,0:T(8,128)(2,1)} %param.12) | copy-start | bytes 393220
  398.8 1.3 copy-start.3
  400.1 295.8 %all-reduce.2.cloned.1.call-start = ((), (), s32[]{:S(2)}) async-start(), calls=%async_computation.4 | async-start | bytes 524288 | tf_op jit(solution)/shard_map/psum | solution.py:59
Sparse Core Ops, SparseCore 0:
  9.8 37.4 all-gather.2
  151.9 103.6 reduce-scatter.2
  259.0 52.5 all-gather.4
  400.2 37.0 reduce-scatter.4
  444.1 251.8 all-reduce.1
where the time goes:
time: 706 us; the launch traced here: 704 us
  waiting for transfers between devices  482 us (68%)
  other arithmetic  98.2 us (14%)
  local copies, waits for them, and re-layouts  62.2 us (9%)
  matrix products  48 us (7%)
  between operations  13.8 us (2%)
    psum x1, waiting for transfers between devices, per_device(): grad_weight = lax.psum(local_weight, ('row', 'col'))  257 us
    reduce_scatter x1, waiting for transfers between devices, per_device(): lax.psum_scatter(partial_rows.reshape(row_blocks * side, width), 'col', s...  104 us
    scatter-add x1, other arithmetic, per_device(): jax.ops.segment_sum(products, row_ids, num_segments=row_blocks)  56 us
    all_gather x1, waiting for transfers between devices, per_device(): grad_rows = lax.all_gather(grad_agg, 'col', axis=0, tiled=True)  44.7 us
    dot_general x6, matrix products, one_group(): jnp.einsum(form, block_vals, picked, preferred_element_type=jnp.float32)  44.3 us
    all_gather x1, waiting for transfers between devices, per_device(): panel = lax.all_gather(features, 'row', axis=1, tiled=True)  39.3 us
    reduce_scatter x1, waiting for transfers between devices, per_device(): lax.psum_scatter(partial_cols.reshape(col_blocks * side, width), 'row', s...  36.2 us
    scatter-add x1, other arithmetic, per_device(): jax.ops.segment_sum(back_products, col_ids, num_segments=col_blocks)  36.1 us
  transfers between devices with their start and end apart: 5, of which 5 were waited for; matrix products, arithmetic and copies ran while one was open for 2% of the time, Pallas kernels for 0%

commit v1 on v0

v1 whole, which is shorter than its diff:
```python
import functools

import jax
import jax.numpy as jnp
from jax import lax
from jax.experimental import pallas as pl
from jax.experimental.pallas import tpu as pltpu
from jax.sharding import PartitionSpec as P

BF16 = jnp.bfloat16
F32 = jnp.float32
UNROLL = 4
MIB = 1 << 20


def start_chunks(live, vals_hbm, vals, sems, chunk):
    for piece in range(vals.shape[0] // chunk):

        @pl.when(piece * chunk < live)
        def _():
            part = pl.ds(piece * chunk, chunk)
            pltpu.make_async_copy(vals_hbm.at[part], vals.at[part], sems.at[piece]).start()


def each_live_slot(live, vals_hbm, vals, sems, chunk, one_slot):
    def one_chunk(piece, unused):
        part = pl.ds(piece * chunk, chunk)
        pltpu.make_async_copy(vals_hbm.at[part], vals.at[part], sems.at[piece]).wait()

        def one_group(group, unused):
            for lane in range(UNROLL):
                slot = piece * chunk + group * UNROLL + lane
                one_slot(slot, slot < live)
            return unused

        groups = (jnp.minimum(chunk, live - piece * chunk) + UNROLL - 1) // UNROLL
        return lax.fori_loop(0, groups, one_group, unused)

    lax.fori_loop(0, (live + chunk - 1) // chunk, one_chunk, 0)


def forward_kernel(chunk, place, rows, cols, count, vals_hbm, *refs):
    n_row = len(refs) - 7
    pieces = refs[:n_row]
    send, keep, vals, panel, total, val_sems, piece_sems = refs[n_row:]
    core, row, live = place[0], place[1], count[0]
    blocks_here = pieces[0].shape[0]
    copies = []
    for step, piece in enumerate(pieces):
        owner = lax.rem(row + n_row - step, n_row)
        copies.append(
            pltpu.make_async_copy(
                piece, panel.at[pl.ds(owner * blocks_here, blocks_here)], piece_sems.at[step]
            )
        )
        copies[-1].start()
    start_chunks(live, vals_hbm, vals, val_sems, chunk)
    spare = total.shape[0] - 1

    def clear(block, unused):
        total[block] = jnp.zeros(total.shape[1:], F32)
        return unused

    lax.fori_loop(0, spare, clear, 0)
    for copy in copies:
        copy.wait()

    def one_slot(slot, alive):
        target = jnp.where(alive, rows[slot], spare)
        total[target] += jnp.dot(vals[slot], panel[cols[slot]], preferred_element_type=F32)

    each_live_slot(live, vals_hbm, vals, val_sems, chunk, one_slot)
    side, width = total.shape[1:]

    def split(chip, unused):
        first = 2 * blocks_here * chip
        other = total[pl.ds(first + blocks_here * (1 - core), blocks_here)]
        mine = total[pl.ds(first + blocks_here * core, blocks_here)]
        send[chip] = other.reshape(blocks_here * side, width).astype(BF16)
        keep[chip] = mine.reshape(blocks_here * side, width)
        return unused

    lax.fori_loop(0, send.shape[0], split, 0)


def backward_kernel(chunk, place, rows, cols, count, vals_hbm, same, other, out, vals, grads, total, val_sems, grad_sems):
    core, live = place[0], count[0]
    half = grads.shape[0] // 2
    copies = [
        pltpu.make_async_copy(same, grads.at[pl.ds(core * half, half)], grad_sems.at[0]),
        pltpu.make_async_copy(other, grads.at[pl.ds((1 - core) * half, half)], grad_sems.at[1]),
    ]
    for copy in copies:
        copy.start()
    start_chunks(live, vals_hbm, vals, val_sems, chunk)
    spare = total.shape[0] - 1
    for block in range(spare):
        total[block] = jnp.zeros(total.shape[1:], F32)
    for copy in copies:
        copy.wait()

    def one_slot(slot, alive):
        target = jnp.where(alive, cols[slot], spare)
        block = rows[slot]
        source = ((block >> 1) & 1) * half + (block >> 2) * 2 + (block & 1)
        total[target] += lax.dot_general(
            vals[slot], grads[source], (((0,), (0,)), ((), ())), preferred_element_type=F32
        )

    each_live_slot(live, vals_hbm, vals, val_sems, chunk, one_slot)
    for block in range(spare):
        out[block] = total[block].astype(BF16)


def dense_kernel(parts, weight, cotangent, activated, grad_agg, local_weight):
    total = parts[0].astype(F32)
    for chip in range(1, parts.shape[0]):
        total += parts[chip].astype(F32)
    aggregated = total.astype(BF16)
    pre = jnp.dot(aggregated, weight[...], preferred_element_type=F32)
    sigma = jax.nn.sigmoid(pre)
    activated[...] = (pre * sigma).astype(BF16)
    grad_pre = (cotangent[...].astype(F32) * sigma * (1.0 + pre * (1.0 - sigma))).astype(BF16)
    local_weight[...] = lax.dot_general(
        aggregated, grad_pre, (((0,), (0,)), ((), ())), preferred_element_type=F32
    )
    grad = lax.dot_general(
        grad_pre, weight[...], (((1,), (1,)), ((), ())), preferred_element_type=F32
    ).astype(BF16)
    for chip in range(grad_agg.shape[0]):
        grad_agg[chip] = grad


def per_device(features, weight, cotangent, blk_vals, blk_rows, blk_cols, blk_count):
    n_row, n_col = lax.axis_size("row"), lax.axis_size("col")
    nodes, width = cotangent.shape
    slots, side = blk_vals.shape[2], blk_vals.shape[3]
    here = nodes // side
    chips = n_col // 2
    chunk = slots // 8
    values = blk_vals[0, 0]
    place = jnp.stack([lax.axis_index("col") % 2, lax.axis_index("row")]).astype(jnp.int32)
    scalars = (place, blk_rows[0, 0], blk_cols[0, 0], blk_count[0])
    smem = pl.BlockSpec(memory_space=pltpu.SMEM)
    vmem = pl.BlockSpec(memory_space=pltpu.VMEM)
    hbm = pl.BlockSpec(memory_space=pl.ANY)
    swap = [(i, i ^ 1) for i in range(n_col)]
    same_core = [list(range(core, n_col, 2)) for core in range(2)]
    work = 2 * slots * side * side * width

    own = features.reshape(here, side, width)
    steps = [0] + sorted(range(1, n_row), key=lambda k: -min(k, n_row - k))
    moved = {0: own}
    for k in steps[1:]:
        moved[k] = lax.ppermute(own, "row", [(i, (i + k) % n_row) for i in range(n_row)])
    pieces = [moved[k] for k in range(n_row)]

    send, keep = pl.pallas_call(
        functools.partial(forward_kernel, chunk),
        out_shape=(
            jax.ShapeDtypeStruct((chips, nodes, width), BF16),
            jax.ShapeDtypeStruct((chips, nodes, width), F32),
        ),
        in_specs=[smem] * 4 + [hbm] * (1 + n_row),
        out_specs=(vmem, vmem),
        scratch_shapes=[
            pltpu.VMEM((slots, side, side), BF16),
            pltpu.VMEM((here * n_row, side, width), BF16),
            pltpu.VMEM((here * n_col + 1, side, width), F32),
            pltpu.SemaphoreType.DMA((slots // chunk,)),
            pltpu.SemaphoreType.DMA((n_row,)),
        ],
        compiler_params=pltpu.CompilerParams(vmem_limit_bytes=40 * MIB),
        cost_estimate=pl.CostEstimate(flops=work, bytes_accessed=14 * MIB, transcendentals=0),
    )(*scalars, values, *pieces)

    arrived = lax.ppermute(send, "col", swap)
    shares = (keep + arrived.astype(F32)).astype(BF16)
    parts = lax.all_to_all(shares, "col", 0, 0, tiled=True, axis_index_groups=same_core)

    activated, grad_agg, local_weight = pl.pallas_call(
        dense_kernel,
        out_shape=(
            jax.ShapeDtypeStruct((nodes, width), BF16),
            jax.ShapeDtypeStruct((chips, nodes, width), BF16),
            jax.ShapeDtypeStruct((width, width), F32),
        ),
        in_specs=[vmem] * 3,
        out_specs=(vmem,) * 3,
        compiler_params=pltpu.CompilerParams(vmem_limit_bytes=24 * MIB),
        cost_estimate=pl.CostEstimate(
            flops=6 * nodes * width * width, bytes_accessed=5 * MIB, transcendentals=nodes * width
        ),
    )(parts, weight, cotangent)

    same = lax.all_to_all(grad_agg, "col", 0, 0, tiled=True, axis_index_groups=same_core)
    other = lax.ppermute(same, "col", swap)

    strip = width // n_col
    terms = lax.all_to_all(local_weight.reshape(n_col, strip, width), "col", 0, 0, tiled=True)
    panel_sum = jnp.sum(terms, axis=0)
    copies = jnp.broadcast_to(panel_sum[None], (n_row, strip, width))
    strips = lax.all_to_all(copies, "row", 0, 0, tiled=True)
    strip_sum = jnp.sum(strips, axis=0)
    copies = jnp.broadcast_to(strip_sum[None], (n_col, strip, width))
    grad_weight = lax.all_to_all(copies, "col", 0, 0, tiled=True).reshape(width, width)

    blocks = chips * here
    partial_cols = pl.pallas_call(
        functools.partial(backward_kernel, chunk),
        out_shape=jax.ShapeDtypeStruct((here * n_row, side, width), BF16),
        in_specs=[smem] * 4 + [hbm] * 3,
        out_specs=vmem,
        scratch_shapes=[
            pltpu.VMEM((slots, side, side), BF16),
            pltpu.VMEM((2 * blocks, side, width), BF16),
            pltpu.VMEM((here * n_row + 1, side, width), F32),
            pltpu.SemaphoreType.DMA((slots // chunk,)),
            pltpu.SemaphoreType.DMA((2,)),
        ],
        compiler_params=pltpu.CompilerParams(vmem_limit_bytes=40 * MIB),
        cost_estimate=pl.CostEstimate(flops=work, bytes_accessed=11 * MIB, transcendentals=0),
    )(*scalars, values, same.reshape(blocks, side, width), other.reshape(blocks, side, width))

    own_cols = lax.all_to_all(
        partial_cols.reshape(n_row, nodes, width), "row", 0, 0, tiled=True
    )
    grad_features = jnp.sum(own_cols.astype(F32), axis=0).astype(BF16).reshape(1, nodes, width)
    return (activated, grad_weight, grad_features)


def solution(mesh):
    return jax.shard_map(
        per_device,
        mesh=mesh,
        in_specs=(
            P("col", "row", None),
            P(),
            P(("row", "col"), None),
            P("row", "col", None, None, None),
            P("row", "col", None),
            P("row", "col", None),
            P("row", "col"),
        ),
        out_specs=(P(("row", "col"), None), P(), P("col", "row", None)),
        check_vma=False,
    )
```

time: 706 us -> 212 us (0.30)
  waiting for transfers between devices: 482 us -> 54.5 us
  other arithmetic: 98.2 us -> 1.56 us
  blocking collectives: 0 us -> 85.8 us
  local copies, waits for them, and re-layouts: 62.2 us -> 9.27 us
  matrix products: 48 us -> 0 us
  Pallas kernels: 0 us -> 32.2 us
  starting transfers between devices: 0.2 us -> 26.5 us
  between operations: 13.8 us -> 1.42 us
    psum x1 -> x0, waiting for transfers between devices: 257 us -> none  [per_device(): grad_weight = lax.psum(local_weight, ('row', 'col'))]
    reduce_scatter x2 -> x0, waiting for transfers between devices: 140 us -> none  [the longest x1 104 us: per_device(): lax.psum_scatter(partial_rows.reshape(row_blocks * side, width), 'col', s...]
    scatter-add x2 -> x0, other arithmetic: 92.2 us -> none  [the longest x1 56 us: per_device(): jax.ops.segment_sum(products, row_ids, num_segments=row_blocks)]
    all_to_all x0 -> x4, blocking collectives: none -> 85.8 us  [the longest x1 30.7 us: per_device(): lax.all_to_all(shares, 'col', 0, 0, tiled=True, axis_index_groups=same_core)]
    all_gather x2 -> x0, waiting for transfers between devices: 84 us -> none  [the longest x1 44.7 us: per_device(): grad_rows = lax.all_gather(grad_agg, 'col', axis=0, tiled=True)]
    dot_general x9 -> x0, matrix products: 48 us -> none  [the longest x6 44.3 us: one_group(): jnp.einsum(form, block_vals, picked, preferred_element_type=jnp.float32)]
    pallas_call x0 -> x3, Pallas kernels: none -> 32.2 us  [the longest x1 16.3 us: per_device(): pl.pallas_call(functools.partial(backward_kernel, chunk), out_shape=jax.S...]
    all_to_all x0 -> x2, waiting for transfers between devices: none -> 29.2 us  [the longest x1 29.2 us: per_device(): lax.all_to_all(partial_cols.reshape(n_row, nodes, width), 'row', 0, 0, ti...]
  transfers between devices with their start and end apart: 5 -> 11, of which waited for: 5 -> 8; matrix products, arithmetic and copies ran while one was open for 2% -> 0% of each run, Pallas kernels for 0% -> 8%
where the time goes in v1:
time: 212 us; the launch traced here: 211 us
  blocking collectives  85.8 us (40%)
  waiting for transfers between devices  54.5 us (26%)
  Pallas kernels  32.2 us (15%)
  starting transfers between devices  26.5 us (12%)
  local copies, waits for them, and re-layouts  9.27 us (4%)
    all_to_all x1, blocking collectives, per_device(): lax.all_to_all(shares, 'col', 0, 0, tiled=True, axis_index_groups=same_core)  30.7 us
    all_to_all x1, blocking collectives, per_device(): lax.all_to_all(grad_agg, 'col', 0, 0, tiled=True, axis_index_groups=same_...  30.1 us
    all_to_all x1, waiting for transfers between devices, per_device(): lax.all_to_all(partial_cols.reshape(n_row, nodes, width), 'row', 0, 0, ti...  29.2 us
    ppermute x7, waiting for transfers between devices, per_device(): lax.ppermute(own, 'row', [(i, (i + k) % n_row) for i in range(n_row)])  21.5 us
    pallas_call x1, Pallas kernels, per_device(): pl.pallas_call(functools.partial(backward_kernel, chunk), out_shape=jax.S...  16.3 us
    pallas_call x1, Pallas kernels, per_device(): pl.pallas_call(functools.partial(forward_kernel, chunk), out_shape=(jax.S...  14.8 us
    ppermute x7, starting transfers between devices, per_device(): lax.ppermute(own, 'row', [(i, (i + k) % n_row) for i in range(n_row)])  14.8 us
    all_to_all x1, blocking collectives, per_device(): strips = lax.all_to_all(copies, 'row', 0, 0, tiled=True)  13 us
  transfers between devices with their start and end apart: 11, of which 8 were waited for; matrix products, arithmetic and copies ran while one was open for 0% of the time, Pallas kernels for 8%

profile of v1, /device:TPU:1, one launch (start us, length us, event | category | flops | bytes accessed | tf_op | source)
XLA Modules:
  0.0 211.3 jit_solution(1425243041982411110)
XLA Ops:
  0.6 6.5 %collective-permute-start.6 = (bf16[2,128,256]{2,1,0:T(8,128)(2,1)}, bf16[2,128,256]{2,1,0:T(8,128)(2,1)S(1)}, u32[]{:S(2)}, u32[]{:S(2)}) collective-permute-start(bf16[2,128,256]{2,1,0:T(8,128)(2,1)} %bitcast.19), channel_id=1, source_target_pairs={{0,224},{32,0},{64,32},{96,64},{128,96},{160,128},{192,160},{224,1... | collective-permute-start | bytes 393224 | tf_op jit(solution)/shard_map/ppermute | solution.py:155
  7.1 1.2 collective-permute-start.5
  8.3 0.4 collective-permute-start.4
  8.7 4.5 %collective-permute-start.3 = (bf16[2,128,256]{2,1,0:T(8,128)(2,1)}, bf16[2,128,256]{2,1,0:T(8,128)(2,1)S(1)}, u32[]{:S(2)}, u32[]{:S(2)}) collective-permute-start(bf16[2,128,256]{2,1,0:T(8,128)(2,1)} %bitcast.22), channel_id=1, source_target_pairs={{0,128},{32,160},{64,192},{96,224},{128,0},{160,32},{192,64},{224,... | collective-permute-start | bytes 393224 | tf_op jit(solution)/shard_map/ppermute | solution.py:155
  13.2 0.0 collective-permute-start.2
  13.2 0.0 collective-permute-done.6.refs_7_
  13.2 2.2 %collective-permute-start.1 = (bf16[2,128,256]{2,1,0:T(8,128)(2,1)}, bf16[2,128,256]{2,1,0:T(8,128)(2,1)S(1)}, u32[]{:S(2)}, u32[]{:S(2)}) collective-permute-start(bf16[2,128,256]{2,1,0:T(8,128)(2,1)} %bitcast.24), channel_id=1, source_target_pairs={{0,64},{32,96},{64,128},{96,160},{128,192},{160,224},{192,0},{224,... | collective-permute-start | bytes 393224 | tf_op jit(solution)/shard_map/ppermute | solution.py:155
  15.4 1.7 collective-permute-done.5.refs_6_
  17.1 0.0 collective-permute-start
  17.8 0.1 pad_add_fusion.place
  17.8 2.3 %collective-permute-done.4.refs_5_ = bf16[2,128,256]{2,1,0:T(8,128)(2,1)S(1)} collective-permute-done((bf16[2,128,256]{2,1,0:T(8,128)(2,1)}, bf16[2,128,256]{2,1,0:T(8,128)(2,1)S(1)}, u32[]{:S(2)}, u32[]{:S(2)}) %collective-permute-start.4) | collective-permute-done | bytes 131104 | tf_op jit(solution)/shard_map/ppermute | solution.py:155
  20.1 2.4 %collective-permute-done.3.refs_4_ = bf16[2,128,256]{2,1,0:T(8,128)(2,1)S(1)} collective-permute-done((bf16[2,128,256]{2,1,0:T(8,128)(2,1)}, bf16[2,128,256]{2,1,0:T(8,128)(2,1)S(1)}, u32[]{:S(2)}, u32[]{:S(2)}) %collective-permute-start.3) | collective-permute-done | bytes 131104 | tf_op jit(solution)/shard_map/ppermute | solution.py:155
  22.5 1.5 collective-permute-done.2.refs_3_
  24.0 8.1 %collective-permute-done.1.refs_2_ = bf16[2,128,256]{2,1,0:T(8,128)(2,1)S(1)} collective-permute-done((bf16[2,128,256]{2,1,0:T(8,128)(2,1)}, bf16[2,128,256]{2,1,0:T(8,128)(2,1)S(1)}, u32[]{:S(2)}, u32[]{:S(2)}) %collective-permute-start.1) | collective-permute-done | bytes 131104 | tf_op jit(solution)/shard_map/ppermute | solution.py:155
  32.1 5.5 %collective-permute-done.refs_1_ = bf16[2,128,256]{2,1,0:T(8,128)(2,1)S(1)} collective-permute-done((bf16[2,128,256]{2,1,0:T(8,128)(2,1)}, bf16[2,128,256]{2,1,0:T(8,128)(2,1)S(1)}, u32[]{:S(2)}, u32[]{:S(2)}) %collective-permute-start) | collective-permute-done | bytes 131104 | tf_op jit(solution)/shard_map/ppermute | solution.py:155
  37.6 0.0 copy-start
  37.6 2.8 %copy-done = bf16[1,1,192,128,128]{4,3,2,1,0:T(8,128)(2,1)S(1)} copy-done((bf16[1,1,192,128,128]{4,3,2,1,0:T(8,128)(2,1)S(1)}, bf16[1,1,192,128,128]{4,3,2,1,0:T(8,128)(2,1)}, u32[]{:S(2)}) %copy-start) | copy-done | bytes 6291480
  40.4 0.0 copy-start.2
  40.4 0.9 copy-done.2
  41.3 0.7 copy-done.5
  42.0 0.7 copy-done.7
  42.7 14.8 %shard_map.94 = (bf16[16,256,256]{2,1,0:T(8,128)(2,1)S(1)}, f32[16,256,256]{2,1,0:T(8,128)S(1)}) custom-call(s32[2]{0:T(128)S(1)} %pad_add_fusion.place, s32[192]{0:T(256)S(1)} %bitcast.27, s32[192]{0:T(256)S(1)} %bitcast.29, s32[1]{0:T(128)} %bitcast.13.count, bf16[192,128,128]{2,1,0:T(8,128)(2,1)S(1)} %bitcast.15, bf16[2,128,256]{2,1,0:T(8,128)(2,1)S(1)} %bitcast.26, ...), custom_call_target="tpu_custom_call" | custom-call | flops 1610612736 | bytes 14680064 | tf_op jit(solution)/shard_map/pallas_call | solution.py:158
  57.5 0.8 collective-permute-start.7
  58.3 3.8 %collective-permute-done.7 = bf16[16,256,256]{2,1,0:T(8,128)(2,1)S(1)} collective-permute-done((bf16[16,256,256]{2,1,0:T(8,128)(2,1)S(1)}, bf16[16,256,256]{2,1,0:T(8,128)(2,1)S(1)}, u32[]{:S(2)}, u32[]{:S(2)}) %collective-permute-start.7) | collective-permute-done | bytes 2097184 | tf_op jit(solution)/shard_map/ppermute | solution.py:177
  62.1 0.6 add_convert_fusion
  62.7 0.0 copy-start.3
  62.7 0.0 copy-start.4
  62.7 30.7 %all_to_all.30.parts = bf16[16,256,256]{2,1,0:T(8,128)(2,1)S(1)} all-to-all(bf16[16,256,256]{2,1,0:T(8,128)(2,1)S(1)} %add_convert_fusion), channel_id=1, replica_groups={{0,2,4,6,8,10,12,14,16,18,20,22,24,26,28,30},{1,3,5,7,9,11,13,15,17,19,..., dimensions={0} | all-to-all | bytes 4194304 | tf_op jit(solution)/shard_map/all_to_all | solution.py:179
  93.4 0.0 copy-done.3
  93.4 0.0 copy-done.4
  93.4 1.1 shard_map.95
  94.5 30.1 %all_to_all.31 = bf16[16,256,256]{2,1,0:T(8,128)(2,1)S(1)} all-to-all(bf16[16,256,256]{2,1,0:T(8,128)(2,1)S(1)} %get-tuple-element.12), channel_id=1, replica_groups={{0,2,4,6,8,10,12,14,16,18,20,22,24,26,28,30},{1,3,5,7,9,11,13,15,17,19,..., dimensions={0} | all-to-all | bytes 4194304 | tf_op jit(solution)/shard_map/all_to_all | solution.py:196
  124.6 2.3 %collective-permute-start.8 = (bf16[16,256,256]{2,1,0:T(8,128)(2,1)S(1)}, bf16[16,256,256]{2,1,0:T(8,128)(2,1)}, u32[]{:S(2)}, u32[]{:S(2)}) collective-permute-start(bf16[16,256,256]{2,1,0:T(8,128)(2,1)S(1)} %all_to_all.31), channel_id=1, source_target_pairs={{0,1},{1,0},{2,3},{3,2},{4,5},{5,4},{6,7},{7,6},{8,9},{9,8},{10,11... | collective-permute-start | bytes 6291464 | tf_op jit(solution)/shard_map/ppermute | solution.py:197
  126.8 12.0 %all_to_all.32 = f32[32,8,256]{2,1,0:T(8,128)S(1)} all-to-all(f32[32,8,256]{2,1,0:T(8,128)S(1)} %bitcast.18), channel_id=1, replica_groups=mesh['row'=8,'col'=32] {'col'}, dimensions={0} | all-to-all | bytes 524288 | tf_op jit(solution)/shard_map/all_to_all | solution.py:200
  138.9 13.0 %all_to_all.33 = f32[8,8,256]{2,1,0:T(8,128)S(1)} all-to-all(f32[8,8,256]{2,1,0:T(8,128)S(1)} %broadcast_in_dim.4), channel_id=1, replica_groups=mesh['row'=8,'col'=32] {'row'}, dimensions={0} | all-to-all | bytes 131072 | tf_op jit(solution)/shard_map/all_to_all | solution.py:203
  151.9 0.7 broadcast_in_dim.5
  152.6 5.2 %all-to-all-start.3 = ((f32[32,8,256]{2,1,0:T(8,128)}), f32[32,8,256]{2,1,0:T(8,128)S(1)}, u32[]{:S(2)}, u32[]{:S(2)}) async-start(f32[32,8,256]{2,1,0:T(8,128)} %broadcast_in_dim.5), calls=%async_computation.3 | async-start | bytes 524288 | tf_op jit(solution)/shard_map/all_to_all | solution.py:206
  157.8 0.0 collective-permute-done.8
  157.9 0.0 copy-done.6
  157.9 0.0 copy-done.8
  157.9 0.0 copy-start.1
  157.9 2.8 %copy-done.1 = bf16[1,1,192,128,128]{4,3,2,1,0:T(8,128)(2,1)S(1)} copy-done((bf16[1,1,192,128,128]{4,3,2,1,0:T(8,128)(2,1)S(1)}, bf16[1,1,192,128,128]{4,3,2,1,0:T(8,128)(2,1)}, u32[]{:S(2)}) %copy-start.1) | copy-done | bytes 6291480
  160.7 16.3 %shard_map.96 = bf16[16,128,256]{2,1,0:T(8,128)(2,1)} custom-call(s32[2]{0:T(128)S(1)} %pad_add_fusion.place, s32[192]{0:T(256)S(1)} %bitcast.28, s32[192]{0:T(256)S(1)} %bitcast.30, s32[1]{0:T(128)} %bitcast.14.count, bf16[192,128,128]{2,1,0:T(8,128)(2,1)S(1)} %bitcast.16, bf16[32,128,256]{2,1,0:T(8,128)(2,1)S(1)} %bitcast.17, ...), custom_call_target="tpu_custom_call" | custom-call | flops 1610612736 | bytes 11534336 | tf_op jit(solution)/shard_map/pallas_call | solution.py:209
  177.0 0.0 all-to-all-done.3
  177.0 3.6 %all-to-all-start.5 = ((bf16[8,256,256]{2,1,0:T(8,128)(2,1)}), bf16[8,256,256]{2,1,0:T(8,128)(2,1)S(1)}, u32[]{:S(2)}, u32[]{:S(2)}) async-start(bf16[8,256,256]{2,1,0:T(8,128)(2,1)} %bitcast.11), calls=%async_computation.5 | async-start | bytes 2097152 | tf_op jit(solution)/shard_map/all_to_all | solution.py:225
  180.5 29.2 %all-to-all-done.5 = bf16[8,256,256]{2,1,0:T(8,128)(2,1)S(1)} async-done(((bf16[8,256,256]{2,1,0:T(8,128)(2,1)}), bf16[8,256,256]{2,1,0:T(8,128)(2,1)S(1)}, u32[]{:S(2)}, u32[]{:S(2)}) %all-to-all-start.5) | async-done | bytes 1048608 | tf_op jit(solution)/shard_map/all_to_all | solution.py:225
  209.8 0.8 reduce_sum.32
  210.6 0.7 copy.12
  (7 shorter events, 0.1 us)
Async XLA Ops:
  0.6 12.6 %collective-permute-start.6 = (bf16[2,128,256]{2,1,0:T(8,128)(2,1)}, bf16[2,128,256]{2,1,0:T(8,128)(2,1)S(1)}, u32[]{:S(2)}, u32[]{:S(2)}) collective-permute-start(bf16[2,128,256]{2,1,0:T(8,128)(2,1)} %bitcast.19), channel_id=1, source_target_pairs={{0,224},{32,0},{64,32},{96,64},{128,96},{160,128},{192,160},{224,1... | collective-permute-start | bytes 393224 | tf_op jit(solution)/shard_map/ppermute | solution.py:155
  7.1 10.0 %collective-permute-start.5 = (bf16[2,128,256]{2,1,0:T(8,128)(2,1)}, bf16[2,128,256]{2,1,0:T(8,128)(2,1)S(1)}, u32[]{:S(2)}, u32[]{:S(2)}) collective-permute-start(bf16[2,128,256]{2,1,0:T(8,128)(2,1)} %bitcast.20), channel_id=1, source_target_pairs={{0,192},{32,224},{64,0},{96,32},{128,64},{160,96},{192,128},{224,1... | collective-permute-start | bytes 393224 | tf_op jit(solution)/shard_map/ppermute | solution.py:155
  8.3 11.8 %collective-permute-start.4 = (bf16[2,128,256]{2,1,0:T(8,128)(2,1)}, bf16[2,128,256]{2,1,0:T(8,128)(2,1)S(1)}, u32[]{:S(2)}, u32[]{:S(2)}) collective-permute-start(bf16[2,128,256]{2,1,0:T(8,128)(2,1)} %bitcast.21), channel_id=1, source_target_pairs={{0,160},{32,192},{64,224},{96,0},{128,32},{160,64},{192,96},{224,1... | collective-permute-start | bytes 393224 | tf_op jit(solution)/shard_map/ppermute | solution.py:155
  8.7 13.8 %collective-permute-start.3 = (bf16[2,128,256]{2,1,0:T(8,128)(2,1)}, bf16[2,128,256]{2,1,0:T(8,128)(2,1)S(1)}, u32[]{:S(2)}, u32[]{:S(2)}) collective-permute-start(bf16[2,128,256]{2,1,0:T(8,128)(2,1)} %bitcast.22), channel_id=1, source_target_pairs={{0,128},{32,160},{64,192},{96,224},{128,0},{160,32},{192,64},{224,... | collective-permute-start | bytes 393224 | tf_op jit(solution)/shard_map/ppermute | solution.py:155
  13.2 10.8 %collective-permute-start.2 = (bf16[2,128,256]{2,1,0:T(8,128)(2,1)}, bf16[2,128,256]{2,1,0:T(8,128)(2,1)S(1)}, u32[]{:S(2)}, u32[]{:S(2)}) collective-permute-start(bf16[2,128,256]{2,1,0:T(8,128)(2,1)} %bitcast.23), channel_id=1, source_target_pairs={{0,96},{32,128},{64,160},{96,192},{128,224},{160,0},{192,32},{224,... | collective-permute-start | bytes 393224 | tf_op jit(solution)/shard_map/ppermute | solution.py:155
  13.2 18.9 %collective-permute-start.1 = (bf16[2,128,256]{2,1,0:T(8,128)(2,1)}, bf16[2,128,256]{2,1,0:T(8,128)(2,1)S(1)}, u32[]{:S(2)}, u32[]{:S(2)}) collective-permute-start(bf16[2,128,256]{2,1,0:T(8,128)(2,1)} %bitcast.24), channel_id=1, source_target_pairs={{0,64},{32,96},{64,128},{96,160},{128,192},{160,224},{192,0},{224,... | collective-permute-start | bytes 393224 | tf_op jit(solution)/shard_map/ppermute | solution.py:155
  17.1 20.5 %collective-permute-start = (bf16[2,128,256]{2,1,0:T(8,128)(2,1)}, bf16[2,128,256]{2,1,0:T(8,128)(2,1)S(1)}, u32[]{:S(2)}, u32[]{:S(2)}) collective-permute-start(bf16[2,128,256]{2,1,0:T(8,128)(2,1)} %bitcast.25), channel_id=1, source_target_pairs={{0,32},{32,64},{64,96},{96,128},{128,160},{160,192},{192,224},{224... | collective-permute-start | bytes 393224 | tf_op jit(solution)/shard_map/ppermute | solution.py:155
  37.6 2.8 %copy-start = (bf16[1,1,192,128,128]{4,3,2,1,0:T(8,128)(2,1)S(1)}, bf16[1,1,192,128,128]{4,3,2,1,0:T(8,128)(2,1)}, u32[]{:S(2)}) copy-start(bf16[1,1,192,128,128]{4,3,2,1,0:T(8,128)(2,1)} %param.10) | copy-start | bytes 18874372
  40.4 0.9 copy-start.2
  41.3 0.7 copy-start.5
  42.0 0.7 copy-start.7
  57.5 4.6 %collective-permute-start.7 = (bf16[16,256,256]{2,1,0:T(8,128)(2,1)S(1)}, bf16[16,256,256]{2,1,0:T(8,128)(2,1)S(1)}, u32[]{:S(2)}, u32[]{:S(2)}) collective-permute-start(bf16[16,256,256]{2,1,0:T(8,128)(2,1)S(1)} %get-tuple-element.9), channel_id=1, source_target_pairs={{0,1},{1,0},{2,3},{3,2},{4,5},{5,4},{6,7},{7,6},{8,9},{9,8},{10,11... | collective-permute-start | bytes 6291464 | tf_op jit(solution)/shard_map/ppermute | solution.py:177
  62.7 30.7 %copy-start.3 = (bf16[256,256]{1,0:T(8,128)(2,1)S(1)}, bf16[256,256]{1,0:T(8,128)(2,1)}, u32[]{:S(2)}) copy-start(bf16[256,256]{1,0:T(8,128)(2,1)} %weight.1) | copy-start | bytes 393220
  62.7 30.7 %copy-start.4 = (bf16[256,256]{1,0:T(8,128)(2,1)S(1)}, bf16[256,256]{1,0:T(8,128)(2,1)}, u32[]{:S(2)}) copy-start(bf16[256,256]{1,0:T(8,128)(2,1)} %cotangent.1) | copy-start | bytes 393220
  94.5 63.4 %copy-start.6 = (s32[1,1,192]{2,1,0:T(1,128)S(1)}, s32[1,1,192]{2,1,0:T(1,128)}, u32[]{:S(2)}) copy-start(s32[1,1,192]{2,1,0:T(1,128)} %param.11) | copy-start | bytes 2308
  94.5 63.4 %copy-start.8 = (s32[1,1,192]{2,1,0:T(1,128)S(1)}, s32[1,1,192]{2,1,0:T(1,128)}, u32[]{:S(2)}) copy-start(s32[1,1,192]{2,1,0:T(1,128)} %param.12) | copy-start | bytes 2308
  124.6 33.3 %collective-permute-start.8 = (bf16[16,256,256]{2,1,0:T(8,128)(2,1)S(1)}, bf16[16,256,256]{2,1,0:T(8,128)(2,1)}, u32[]{:S(2)}, u32[]{:S(2)}) collective-permute-start(bf16[16,256,256]{2,1,0:T(8,128)(2,1)S(1)} %all_to_all.31), channel_id=1, source_target_pairs={{0,1},{1,0},{2,3},{3,2},{4,5},{5,4},{6,7},{7,6},{8,9},{9,8},{10,11... | collective-permute-start | bytes 6291464 | tf_op jit(solution)/shard_map/ppermute | solution.py:197
  152.6 24.3 %all-to-all-start.3 = ((f32[32,8,256]{2,1,0:T(8,128)}), f32[32,8,256]{2,1,0:T(8,128)S(1)}, u32[]{:S(2)}, u32[]{:S(2)}) async-start(f32[32,8,256]{2,1,0:T(8,128)} %broadcast_in_dim.5), calls=%async_computation.3 | async-start | bytes 524288 | tf_op jit(solution)/shard_map/all_to_all | solution.py:206
  157.9 2.8 %copy-start.1 = (bf16[1,1,192,128,128]{4,3,2,1,0:T(8,128)(2,1)S(1)}, bf16[1,1,192,128,128]{4,3,2,1,0:T(8,128)(2,1)}, u32[]{:S(2)}) copy-start(bf16[1,1,192,128,128]{4,3,2,1,0:T(8,128)(2,1)} %param.10) | copy-start | bytes 18874372
  177.0 32.8 %all-to-all-start.5 = ((bf16[8,256,256]{2,1,0:T(8,128)(2,1)}), bf16[8,256,256]{2,1,0:T(8,128)(2,1)S(1)}, u32[]{:S(2)}, u32[]{:S(2)}) async-start(bf16[8,256,256]{2,1,0:T(8,128)(2,1)} %bitcast.11), calls=%async_computation.5 | async-start | bytes 2097152 | tf_op jit(solution)/shard_map/all_to_all | solution.py:225

commit v2 on v1

--- a/solution.py
+++ b/solution.py
@@ -9,7 +9,7 @@
 
 BF16 = jnp.bfloat16
 F32 = jnp.float32
-UNROLL = 4
+UNROLL = 16
 MIB = 1 << 20
 
 
@@ -85,10 +85,10 @@
 
 def backward_kernel(chunk, place, rows, cols, count, vals_hbm, same, other, out, vals, grads, total, val_sems, grad_sems):
     core, live = place[0], count[0]
-    half = grads.shape[0] // 2
+    side = total.shape[1]
     copies = [
-        pltpu.make_async_copy(same, grads.at[pl.ds(core * half, half)], grad_sems.at[0]),
-        pltpu.make_async_copy(other, grads.at[pl.ds((1 - core) * half, half)], grad_sems.at[1]),
+        pltpu.make_async_copy(same, grads.at[core], grad_sems.at[0]),
+        pltpu.make_async_copy(other, grads.at[1 - core], grad_sems.at[1]),
     ]
     for copy in copies:
         copy.start()
@@ -102,9 +102,10 @@
     def one_slot(slot, alive):
         target = jnp.where(alive, cols[slot], spare)
         block = rows[slot]
-        source = ((block >> 1) & 1) * half + (block >> 2) * 2 + (block & 1)
+        first = pl.multiple_of((block & 1) * side, side)
+        picked = grads[(block >> 1) & 1, block >> 2, pl.ds(first, side)]
         total[target] += lax.dot_general(
-            vals[slot], grads[source], (((0,), (0,)), ((), ())), preferred_element_type=F32
+            vals[slot], picked, (((0,), (0,)), ((), ())), preferred_element_type=F32
         )
 
     each_live_slot(live, vals_hbm, vals, val_sems, chunk, one_slot)
@@ -112,7 +113,7 @@
         out[block] = total[block].astype(BF16)
 
 
-def dense_kernel(parts, weight, cotangent, activated, grad_agg, local_weight):
+def dense_kernel(parts, weight, cotangent, activated, grad_agg):
     total = parts[0].astype(F32)
     for chip in range(1, parts.shape[0]):
         total += parts[chip].astype(F32)
@@ -121,14 +122,17 @@
     sigma = jax.nn.sigmoid(pre)
     activated[...] = (pre * sigma).astype(BF16)
     grad_pre = (cotangent[...].astype(F32) * sigma * (1.0 + pre * (1.0 - sigma))).astype(BF16)
-    local_weight[...] = lax.dot_general(
+    local_weight = lax.dot_general(
         aggregated, grad_pre, (((0,), (0,)), ((), ())), preferred_element_type=F32
-    )
+    ).astype(BF16)
     grad = lax.dot_general(
         grad_pre, weight[...], (((1,), (1,)), ((), ())), preferred_element_type=F32
     ).astype(BF16)
+    nodes = grad.shape[0]
+    strip = grad_agg.shape[1] - nodes
     for chip in range(grad_agg.shape[0]):
-        grad_agg[chip] = grad
+        grad_agg[chip, :nodes] = grad
+        grad_agg[chip, nodes:] = local_weight[chip * strip : (chip + 1) * strip]
 
 
 def per_device(features, weight, cotangent, blk_vals, blk_rows, blk_cols, blk_count):
@@ -137,13 +141,14 @@
     slots, side = blk_vals.shape[2], blk_vals.shape[3]
     here = nodes // side
     chips = n_col // 2
-    chunk = slots // 8
-    values = blk_vals[0, 0]
+    chunk = slots // 6
+    values = pltpu.with_memory_space_constraint(blk_vals[0, 0], pltpu.HBM)
     place = jnp.stack([lax.axis_index("col") % 2, lax.axis_index("row")]).astype(jnp.int32)
     scalars = (place, blk_rows[0, 0], blk_cols[0, 0], blk_count[0])
     smem = pl.BlockSpec(memory_space=pltpu.SMEM)
     vmem = pl.BlockSpec(memory_space=pltpu.VMEM)
-    hbm = pl.BlockSpec(memory_space=pl.ANY)
+    near = pl.BlockSpec(memory_space=pl.ANY)
+    hbm = pl.BlockSpec(memory_space=pltpu.HBM)
     swap = [(i, i ^ 1) for i in range(n_col)]
     same_core = [list(range(core, n_col, 2)) for core in range(2)]
     work = 2 * slots * side * side * width
@@ -161,7 +166,7 @@
             jax.ShapeDtypeStruct((chips, nodes, width), BF16),
             jax.ShapeDtypeStruct((chips, nodes, width), F32),
         ),
-        in_specs=[smem] * 4 + [hbm] * (1 + n_row),
+        in_specs=[smem] * 4 + [hbm] + [near] * n_row,
         out_specs=(vmem, vmem),
         scratch_shapes=[
             pltpu.VMEM((slots, side, side), BF16),
@@ -178,15 +183,15 @@
     shares = (keep + arrived.astype(F32)).astype(BF16)
     parts = lax.all_to_all(shares, "col", 0, 0, tiled=True, axis_index_groups=same_core)
 
-    activated, grad_agg, local_weight = pl.pallas_call(
+    strip = width // chips
+    activated, grad_agg = pl.pallas_call(
         dense_kernel,
         out_shape=(
             jax.ShapeDtypeStruct((nodes, width), BF16),
-            jax.ShapeDtypeStruct((chips, nodes, width), BF16),
-            jax.ShapeDtypeStruct((width, width), F32),
+            jax.ShapeDtypeStruct((chips, nodes + strip, width), BF16),
         ),
         in_specs=[vmem] * 3,
-        out_specs=(vmem,) * 3,
+        out_specs=(vmem,) * 2,
         compiler_params=pltpu.CompilerParams(vmem_limit_bytes=24 * MIB),
         cost_estimate=pl.CostEstimate(
             flops=6 * nodes * width * width, bytes_accessed=5 * MIB, transcendentals=nodes * width
@@ -196,31 +201,26 @@
     same = lax.all_to_all(grad_agg, "col", 0, 0, tiled=True, axis_index_groups=same_core)
     other = lax.ppermute(same, "col", swap)
 
-    strip = width // n_col
-    terms = lax.all_to_all(local_weight.reshape(n_col, strip, width), "col", 0, 0, tiled=True)
-    panel_sum = jnp.sum(terms, axis=0)
-    copies = jnp.broadcast_to(panel_sum[None], (n_row, strip, width))
-    strips = lax.all_to_all(copies, "row", 0, 0, tiled=True)
-    strip_sum = jnp.sum(strips, axis=0)
-    copies = jnp.broadcast_to(strip_sum[None], (n_col, strip, width))
-    grad_weight = lax.all_to_all(copies, "col", 0, 0, tiled=True).reshape(width, width)
-
-    blocks = chips * here
+    terms = jnp.sum(same[:, nodes:].astype(F32), axis=0) + jnp.sum(other[:, nodes:].astype(F32), axis=0)
+    half_strip = lax.dynamic_slice_in_dim(terms, place[0] * (strip // 2), strip // 2, 0)
+    strips = lax.all_gather(half_strip, ("row", "col"), axis=0, tiled=True)
+    grad_weight = jnp.sum(strips.reshape(n_row, width, width), axis=0)
+
     partial_cols = pl.pallas_call(
         functools.partial(backward_kernel, chunk),
         out_shape=jax.ShapeDtypeStruct((here * n_row, side, width), BF16),
-        in_specs=[smem] * 4 + [hbm] * 3,
+        in_specs=[smem] * 4 + [hbm] + [near] * 2,
         out_specs=vmem,
         scratch_shapes=[
             pltpu.VMEM((slots, side, side), BF16),
-            pltpu.VMEM((2 * blocks, side, width), BF16),
+            pltpu.VMEM((2, chips, nodes + strip, width), BF16),
             pltpu.VMEM((here * n_row + 1, side, width), F32),
             pltpu.SemaphoreType.DMA((slots // chunk,)),
             pltpu.SemaphoreType.DMA((2,)),
         ],
         compiler_params=pltpu.CompilerParams(vmem_limit_bytes=40 * MIB),
         cost_estimate=pl.CostEstimate(flops=work, bytes_accessed=11 * MIB, transcendentals=0),
-    )(*scalars, values, same.reshape(blocks, side, width), other.reshape(blocks, side, width))
+    )(*scalars, values, same, other)
 
     own_cols = lax.all_to_all(
         partial_cols.reshape(n_row, nodes, width), "row", 0, 0, tiled=True

time: 212 us -> 248 us (1.17)
  waiting for transfers between devices: 54.5 us -> 91.7 us
  between operations: 1.42 us -> 14.8 us
  Pallas kernels: 32.2 us -> 20.4 us
  blocking collectives: 85.8 us -> 94.6 us
  starting transfers between devices: 26.5 us -> 18.1 us
  local copies, waits for them, and re-layouts: 9.27 us -> 2.28 us
  other arithmetic: 1.56 us -> 5.54 us
    all_gather x0 -> x1, waiting for transfers between devices: none -> 62.3 us  [per_device(): strips = lax.all_gather(half_strip, ('row', 'col'), axis=0, tiled=True)]
    all_to_all x2 -> x0, waiting for transfers between devices: 29.2 us -> none  [the longest x1 29.2 us: per_device(): lax.all_to_all(partial_cols.reshape(n_row, nodes, width), 'row', 0, 0, ti...]
    all_to_all x2 -> x0, starting transfers between devices: 8.76 us -> none  [the longest x1 5.19 us: per_device(): lax.all_to_all(copies, 'col', 0, 0, tiled=True).reshape(width, width)]
    all_to_all x2 -> x1, blocking collectives: 25 us -> 31.7 us  [per_device(): lax.all_to_all(partial_cols.reshape(n_row, nodes, width), 'row', 0, 0, ti...]
    unnamed x19 -> x14, local copies, waits for them, and re-layouts: 8.55 us -> 2.28 us
    pallas_call x1, Pallas kernels: 16.3 us -> 10.2 us  [per_device(): pl.pallas_call(functools.partial(backward_kernel, chunk), out_shape=jax.S...]
    pallas_call x1, Pallas kernels: 14.8 us -> 9.18 us  [per_device(): pl.pallas_call(functools.partial(forward_kernel, chunk), out_shape=(jax.S...]
    ppermute x1, waiting for transfers between devices: 0.01 us -> 4.08 us  [per_device(): other = lax.ppermute(same, 'col', swap)]
  transfers between devices with their start and end apart: 11 -> 10, of which waited for: 8 -> 9; matrix products, arithmetic and copies ran while one was open for 0% -> 0% of each run, Pallas kernels for 8% -> 4%
where the time goes in v2:
time: 248 us; the launch traced here: 247 us
  blocking collectives  94.6 us (38%)
  waiting for transfers between devices  91.7 us (37%)
  Pallas kernels  20.4 us (8%)
  starting transfers between devices  18.1 us (7%)
  between operations  14.8 us (6%)
  other arithmetic  5.54 us (2%)
    all_gather x1, waiting for transfers between devices, per_device(): strips = lax.all_gather(half_strip, ('row', 'col'), axis=0, tiled=True)  62.3 us
    all_to_all x1, blocking collectives, per_device(): lax.all_to_all(partial_cols.reshape(n_row, nodes, width), 'row', 0, 0, ti...  31.7 us
    all_to_all x1, blocking collectives, per_device(): lax.all_to_all(grad_agg, 'col', 0, 0, tiled=True, axis_index_groups=same_...  31.7 us
    all_to_all x1, blocking collectives, per_device(): lax.all_to_all(shares, 'col', 0, 0, tiled=True, axis_index_groups=same_core)  31.2 us
    ppermute x7, waiting for transfers between devices, per_device(): lax.ppermute(own, 'row', [(i, (i + k) % n_row) for i in range(n_row)])  21.5 us
    ppermute x7, starting transfers between devices, per_device(): lax.ppermute(own, 'row', [(i, (i + k) % n_row) for i in range(n_row)])  14.8 us
    pallas_call x1, Pallas kernels, per_device(): pl.pallas_call(functools.partial(backward_kernel, chunk), out_shape=jax.S...  10.2 us
    pallas_call x1, Pallas kernels, per_device(): pl.pallas_call(functools.partial(forward_kernel, chunk), out_shape=(jax.S...  9.18 us
  transfers between devices with their start and end apart: 10, of which 9 were waited for; matrix products, arithmetic and copies ran while one was open for 0% of the time, Pallas kernels for 4%

profile of v2, /device:TPU:1, one launch (start us, length us, event | category | flops | bytes accessed | tf_op | source)
XLA Modules:
  0.0 247.4 jit_solution(7055750074758368263)
XLA Ops:
  7.2 0.0 all-gather.2.cloned.1.call-start
  7.2 6.5 %collective-permute-start.6 = (bf16[2,128,256]{2,1,0:T(8,128)(2,1)}, bf16[2,128,256]{2,1,0:T(8,128)(2,1)S(1)}, u32[]{:S(2)}, u32[]{:S(2)}) collective-permute-start(bf16[2,128,256]{2,1,0:T(8,128)(2,1)} %bitcast.13), channel_id=1, source_target_pairs={{0,224},{32,0},{64,32},{96,64},{128,96},{160,128},{192,160},{224,1... | collective-permute-start | bytes 393224 | tf_op jit(solution)/shard_map/ppermute | solution.py:160
  13.7 1.2 collective-permute-start.5
  14.9 0.4 collective-permute-start.4
  15.3 4.5 %collective-permute-start.3 = (bf16[2,128,256]{2,1,0:T(8,128)(2,1)}, bf16[2,128,256]{2,1,0:T(8,128)(2,1)S(1)}, u32[]{:S(2)}, u32[]{:S(2)}) collective-permute-start(bf16[2,128,256]{2,1,0:T(8,128)(2,1)} %bitcast.16), channel_id=1, source_target_pairs={{0,128},{32,160},{64,192},{96,224},{128,0},{160,32},{192,64},{224,... | collective-permute-start | bytes 393224 | tf_op jit(solution)/shard_map/ppermute | solution.py:160
  19.8 0.0 collective-permute-start.2
  19.8 0.0 collective-permute-done.6.refs_7_
  19.8 2.2 collective-permute-start.1
  22.0 1.7 collective-permute-done.5.refs_6_
  23.7 0.0 collective-permute-start
  24.4 0.1 pad_add_fusion.place
  24.4 2.3 collective-permute-done.4.refs_5_
  26.7 2.4 collective-permute-done.3.refs_4_
  29.1 1.5 collective-permute-done.2.refs_3_
  30.6 8.1 %collective-permute-done.1.refs_2_ = bf16[2,128,256]{2,1,0:T(8,128)(2,1)S(1)} collective-permute-done((bf16[2,128,256]{2,1,0:T(8,128)(2,1)}, bf16[2,128,256]{2,1,0:T(8,128)(2,1)S(1)}, u32[]{:S(2)}, u32[]{:S(2)}) %collective-permute-start.1) | collective-permute-done | bytes 131104 | tf_op jit(solution)/shard_map/ppermute | solution.py:160
  38.7 5.5 %collective-permute-done.refs_1_ = bf16[2,128,256]{2,1,0:T(8,128)(2,1)S(1)} collective-permute-done((bf16[2,128,256]{2,1,0:T(8,128)(2,1)}, bf16[2,128,256]{2,1,0:T(8,128)(2,1)S(1)}, u32[]{:S(2)}, u32[]{:S(2)}) %collective-permute-start) | collective-permute-done | bytes 131104 | tf_op jit(solution)/shard_map/ppermute | solution.py:160
  44.2 0.0 copy-start
  44.2 0.9 copy-done
  45.1 0.0 copy-start.3
  45.1 0.7 copy-done.3
  45.8 0.0 copy-start.5
  45.8 0.7 copy-done.5
  46.5 9.2 %shard_map.94 = (bf16[16,256,256]{2,1,0:T(8,128)(2,1)S(1)}, f32[16,256,256]{2,1,0:T(8,128)S(1)}) custom-call(s32[2]{0:T(128)S(1)} %pad_add_fusion.place, s32[192]{0:T(256)S(1)} %bitcast.21, s32[192]{0:T(256)S(1)} %bitcast.23, s32[1]{0:T(128)} %bitcast.10.count, bf16[192,128,128]{2,1,0:T(8,128)(2,1)} %bitcast.25, bf16[2,128,256]{2,1,0:T(8,128)(2,1)S(1)} %bitcast.20, ...), custom_call_target="tpu_custom_call" | custom-call | flops 1610612736 | bytes 14680064 | tf_op jit(solution)/shard_map/pallas_call | solution.py:163
  55.7 0.8 collective-permute-start.7
  56.4 3.8 %collective-permute-done.7 = bf16[16,256,256]{2,1,0:T(8,128)(2,1)S(1)} collective-permute-done((bf16[16,256,256]{2,1,0:T(8,128)(2,1)S(1)}, bf16[16,256,256]{2,1,0:T(8,128)(2,1)S(1)}, u32[]{:S(2)}, u32[]{:S(2)}) %collective-permute-start.7) | collective-permute-done | bytes 2097184 | tf_op jit(solution)/shard_map/ppermute | solution.py:182
  60.2 0.6 add_convert_fusion
  60.8 0.0 copy-start.1
  60.9 0.0 copy-start.2
  60.9 31.2 %all_to_all.15.parts = bf16[16,256,256]{2,1,0:T(8,128)(2,1)S(1)} all-to-all(bf16[16,256,256]{2,1,0:T(8,128)(2,1)S(1)} %add_convert_fusion), channel_id=1, replica_groups={{0,2,4,6,8,10,12,14,16,18,20,22,24,26,28,30},{1,3,5,7,9,11,13,15,17,19,..., dimensions={0} | all-to-all | bytes 4194304 | tf_op jit(solution)/shard_map/all_to_all | solution.py:184
  92.0 0.0 copy-done.1
  92.0 0.0 copy-done.2
  92.0 1.1 shard_map.95
  93.1 0.0 copy-start.4
  93.1 0.0 copy-start.6
  93.1 31.7 %all_to_all.16.same = bf16[16,272,256]{2,1,0:T(8,128)(2,1)S(1)} all-to-all(bf16[16,272,256]{2,1,0:T(8,128)(2,1)S(1)} %get-tuple-element.10), channel_id=1, replica_groups={{0,2,4,6,8,10,12,14,16,18,20,22,24,26,28,30},{1,3,5,7,9,11,13,15,17,19,..., dimensions={0} | all-to-all | bytes 4456448 | tf_op jit(solution)/shard_map/all_to_all | solution.py:201
  124.8 2.5 %collective-permute-start.8 = (bf16[16,272,256]{2,1,0:T(8,128)(2,1)S(1)}, bf16[16,272,256]{2,1,0:T(8,128)(2,1)}, u32[]{:S(2)}, u32[]{:S(2)}) collective-permute-start(bf16[16,272,256]{2,1,0:T(8,128)(2,1)S(1)} %all_to_all.16.same), channel_id=1, source_target_pairs={{0,1},{1,0},{2,3},{3,2},{4,5},{5,4},{6,7},{7,6},{8,9},{9,8},{10,11... | collective-permute-start | bytes 6684680 | tf_op jit(solution)/shard_map/ppermute | solution.py:202
  127.4 4.1 %collective-permute-done.8.other = bf16[16,272,256]{2,1,0:T(8,128)(2,1)} collective-permute-done((bf16[16,272,256]{2,1,0:T(8,128)(2,1)S(1)}, bf16[16,272,256]{2,1,0:T(8,128)(2,1)}, u32[]{:S(2)}, u32[]{:S(2)}) %collective-permute-start.8) | collective-permute-done | bytes 2228256 | tf_op jit(solution)/shard_map/ppermute | solution.py:202
  131.5 0.9 convert_reduce_fusion
  132.4 0.6 dynamic-slice_add_fusion
  133.0 0.0 all-gather.2.cloned.1.call-update
  133.0 0.0 copy-done.4
  133.0 0.0 copy-done.6
  133.1 10.2 %shard_map.96 = bf16[16,128,256]{2,1,0:T(8,128)(2,1)S(1)} custom-call(s32[2]{0:T(128)S(1)} %pad_add_fusion.place, s32[192]{0:T(256)S(1)} %bitcast.22, s32[192]{0:T(256)S(1)} %bitcast.24, s32[1]{0:T(128)} %bitcast.11.count, bf16[192,128,128]{2,1,0:T(8,128)(2,1)} %bitcast.26, bf16[16,272,256]{2,1,0:T(8,128)(2,1)S(1)} %all_to_all.16.same, ...), custom_call_target="tpu_custom_call" | custom-call | flops 1610612736 | bytes 11534336 | tf_op jit(solution)/shard_map/pallas_call | solution.py:209
  143.3 31.7 %all_to_all.17 = bf16[8,256,256]{2,1,0:T(8,128)(2,1)S(1)} all-to-all(bf16[8,256,256]{2,1,0:T(8,128)(2,1)S(1)} %bitcast.12), channel_id=1, replica_groups=mesh['row'=8,'col'=32] {'row'}, dimensions={0} | all-to-all | bytes 2097152 | tf_op jit(solution)/shard_map/all_to_all | solution.py:225
  175.0 0.8 reduce_sum.42
  175.8 62.3 %all-gather.2.cloned.1.call-done = f32[2048,256]{1,0:T(8,128)} async-done(((f32[8,256]{1,0:T(8,128)}), f32[2048,256]{1,0:T(8,128)}) %all-gather.2.cloned.1.call-update) | async-done | bytes 2097168 | tf_op jit(solution)/shard_map/all_gather | solution.py:206
  238.1 2.5 reduce_sum.41
  (1 shorter events, 0.0 us)
Async XLA Ops:
  7.2 231.0 %all-gather.2.cloned.1.call-start = ((), (), s32[]{:S(2)}) async-start(), calls=%async_computation.3 | async-start | bytes 2105344 | tf_op jit(solution)/shard_map/all_gather | solution.py:206
  7.2 12.6 %collective-permute-start.6 = (bf16[2,128,256]{2,1,0:T(8,128)(2,1)}, bf16[2,128,256]{2,1,0:T(8,128)(2,1)S(1)}, u32[]{:S(2)}, u32[]{:S(2)}) collective-permute-start(bf16[2,128,256]{2,1,0:T(8,128)(2,1)} %bitcast.13), channel_id=1, source_target_pairs={{0,224},{32,0},{64,32},{96,64},{128,96},{160,128},{192,160},{224,1... | collective-permute-start | bytes 393224 | tf_op jit(solution)/shard_map/ppermute | solution.py:160
  13.7 10.0 %collective-permute-start.5 = (bf16[2,128,256]{2,1,0:T(8,128)(2,1)}, bf16[2,128,256]{2,1,0:T(8,128)(2,1)S(1)}, u32[]{:S(2)}, u32[]{:S(2)}) collective-permute-start(bf16[2,128,256]{2,1,0:T(8,128)(2,1)} %bitcast.14), channel_id=1, source_target_pairs={{0,192},{32,224},{64,0},{96,32},{128,64},{160,96},{192,128},{224,1... | collective-permute-start | bytes 393224 | tf_op jit(solution)/shard_map/ppermute | solution.py:160
  14.9 11.8 %collective-permute-start.4 = (bf16[2,128,256]{2,1,0:T(8,128)(2,1)}, bf16[2,128,256]{2,1,0:T(8,128)(2,1)S(1)}, u32[]{:S(2)}, u32[]{:S(2)}) collective-permute-start(bf16[2,128,256]{2,1,0:T(8,128)(2,1)} %bitcast.15), channel_id=1, source_target_pairs={{0,160},{32,192},{64,224},{96,0},{128,32},{160,64},{192,96},{224,1... | collective-permute-start | bytes 393224 | tf_op jit(solution)/shard_map/ppermute | solution.py:160
  15.3 13.8 %collective-permute-start.3 = (bf16[2,128,256]{2,1,0:T(8,128)(2,1)}, bf16[2,128,256]{2,1,0:T(8,128)(2,1)S(1)}, u32[]{:S(2)}, u32[]{:S(2)}) collective-permute-start(bf16[2,128,256]{2,1,0:T(8,128)(2,1)} %bitcast.16), channel_id=1, source_target_pairs={{0,128},{32,160},{64,192},{96,224},{128,0},{160,32},{192,64},{224,... | collective-permute-start | bytes 393224 | tf_op jit(solution)/shard_map/ppermute | solution.py:160
  19.8 10.8 %collective-permute-start.2 = (bf16[2,128,256]{2,1,0:T(8,128)(2,1)}, bf16[2,128,256]{2,1,0:T(8,128)(2,1)S(1)}, u32[]{:S(2)}, u32[]{:S(2)}) collective-permute-start(bf16[2,128,256]{2,1,0:T(8,128)(2,1)} %bitcast.17), channel_id=1, source_target_pairs={{0,96},{32,128},{64,160},{96,192},{128,224},{160,0},{192,32},{224,... | collective-permute-start | bytes 393224 | tf_op jit(solution)/shard_map/ppermute | solution.py:160
  19.8 18.9 %collective-permute-start.1 = (bf16[2,128,256]{2,1,0:T(8,128)(2,1)}, bf16[2,128,256]{2,1,0:T(8,128)(2,1)S(1)}, u32[]{:S(2)}, u32[]{:S(2)}) collective-permute-start(bf16[2,128,256]{2,1,0:T(8,128)(2,1)} %bitcast.18), channel_id=1, source_target_pairs={{0,64},{32,96},{64,128},{96,160},{128,192},{160,224},{192,0},{224,... | collective-permute-start | bytes 393224 | tf_op jit(solution)/shard_map/ppermute | solution.py:160
  23.7 20.5 %collective-permute-start = (bf16[2,128,256]{2,1,0:T(8,128)(2,1)}, bf16[2,128,256]{2,1,0:T(8,128)(2,1)S(1)}, u32[]{:S(2)}, u32[]{:S(2)}) collective-permute-start(bf16[2,128,256]{2,1,0:T(8,128)(2,1)} %bitcast.19), channel_id=1, source_target_pairs={{0,32},{32,64},{64,96},{96,128},{128,160},{160,192},{192,224},{224... | collective-permute-start | bytes 393224 | tf_op jit(solution)/shard_map/ppermute | solution.py:160
  44.2 0.9 copy-start
  45.1 0.7 copy-start.3
  45.8 0.7 copy-start.5
  55.7 4.5 %collective-permute-start.7 = (bf16[16,256,256]{2,1,0:T(8,128)(2,1)S(1)}, bf16[16,256,256]{2,1,0:T(8,128)(2,1)S(1)}, u32[]{:S(2)}, u32[]{:S(2)}) collective-permute-start(bf16[16,256,256]{2,1,0:T(8,128)(2,1)S(1)} %get-tuple-element.8), channel_id=1, source_target_pairs={{0,1},{1,0},{2,3},{3,2},{4,5},{5,4},{6,7},{7,6},{8,9},{9,8},{10,11... | collective-permute-start | bytes 6291464 | tf_op jit(solution)/shard_map/ppermute | solution.py:182
  60.8 31.2 %copy-start.1 = (bf16[256,256]{1,0:T(8,128)(2,1)S(1)}, bf16[256,256]{1,0:T(8,128)(2,1)}, u32[]{:S(2)}) copy-start(bf16[256,256]{1,0:T(8,128)(2,1)} %weight.1) | copy-start | bytes 393220
  60.9 31.2 %copy-start.2 = (bf16[256,256]{1,0:T(8,128)(2,1)S(1)}, bf16[256,256]{1,0:T(8,128)(2,1)}, u32[]{:S(2)}) copy-start(bf16[256,256]{1,0:T(8,128)(2,1)} %cotangent.1) | copy-start | bytes 393220
  93.1 39.9 %copy-start.4 = (s32[1,1,192]{2,1,0:T(1,128)S(1)}, s32[1,1,192]{2,1,0:T(1,128)}, u32[]{:S(2)}) copy-start(s32[1,1,192]{2,1,0:T(1,128)} %param.11) | copy-start | bytes 2308
  93.1 40.0 %copy-start.6 = (s32[1,1,192]{2,1,0:T(1,128)S(1)}, s32[1,1,192]{2,1,0:T(1,128)}, u32[]{:S(2)}) copy-start(s32[1,1,192]{2,1,0:T(1,128)} %param.12) | copy-start | bytes 2308
  124.8 6.6 %collective-permute-start.8 = (bf16[16,272,256]{2,1,0:T(8,128)(2,1)S(1)}, bf16[16,272,256]{2,1,0:T(8,128)(2,1)}, u32[]{:S(2)}, u32[]{:S(2)}) collective-permute-start(bf16[16,272,256]{2,1,0:T(8,128)(2,1)S(1)} %all_to_all.16.same), channel_id=1, source_target_pairs={{0,1},{1,0},{2,3},{3,2},{4,5},{5,4},{6,7},{7,6},{8,9},{9,8},{10,11... | collective-permute-start | bytes 6684680 | tf_op jit(solution)/shard_map/ppermute | solution.py:202
Sparse Core Ops, SparseCore 0:
  133.2 104.9 all-gather.1

commit v3 on v2

--- a/solution.py
+++ b/solution.py
@@ -9,7 +9,7 @@
 
 BF16 = jnp.bfloat16
 F32 = jnp.float32
-UNROLL = 16
+UNROLL = 32
 MIB = 1 << 20
 
 
@@ -39,18 +39,18 @@
     lax.fori_loop(0, (live + chunk - 1) // chunk, one_chunk, 0)
 
 
-def forward_kernel(chunk, place, rows, cols, count, vals_hbm, *refs):
+def forward_kernel(chunk, steps, place, rows, cols, count, vals_hbm, *refs):
     n_row = len(refs) - 7
     pieces = refs[:n_row]
     send, keep, vals, panel, total, val_sems, piece_sems = refs[n_row:]
     core, row, live = place[0], place[1], count[0]
     blocks_here = pieces[0].shape[0]
     copies = []
-    for step, piece in enumerate(pieces):
+    for at, (step, piece) in enumerate(zip(steps, pieces)):
         owner = lax.rem(row + n_row - step, n_row)
         copies.append(
             pltpu.make_async_copy(
-                piece, panel.at[pl.ds(owner * blocks_here, blocks_here)], piece_sems.at[step]
+                piece, panel.at[pl.ds(owner * blocks_here, blocks_here)], piece_sems.at[at]
             )
         )
         copies[-1].start()
@@ -83,8 +83,11 @@
     lax.fori_loop(0, send.shape[0], split, 0)
 
 
-def backward_kernel(chunk, place, rows, cols, count, vals_hbm, same, other, out, vals, grads, total, val_sems, grad_sems):
-    core, live = place[0], count[0]
+def backward_kernel(chunk, steps, place, rows, cols, count, vals_hbm, same, other, *refs):
+    n_row = len(steps)
+    outs = refs[:n_row]
+    vals, grads, total, val_sems, grad_sems = refs[n_row:]
+    core, row, live = place[0], place[1], count[0]
     side = total.shape[1]
     copies = [
         pltpu.make_async_copy(same, grads.at[core], grad_sems.at[0]),
@@ -109,8 +112,11 @@
         )
 
     each_live_slot(live, vals_hbm, vals, val_sems, chunk, one_slot)
-    for block in range(spare):
-        out[block] = total[block].astype(BF16)
+    blocks_here = spare // n_row
+    for step, out in zip(steps, outs):
+        owner = lax.rem(row + step, n_row)
+        mine = total[pl.ds(owner * blocks_here, blocks_here)]
+        out[...] = mine.reshape(out.shape).astype(BF16)
 
 
 def dense_kernel(parts, weight, cotangent, activated, grad_agg):
@@ -135,6 +141,10 @@
         grad_agg[chip, nodes:] = local_weight[chip * strip : (chip + 1) * strip]
 
 
+def turn(size, step):
+    return [(i, (i + step) % size) for i in range(size)]
+
+
 def per_device(features, weight, cotangent, blk_vals, blk_rows, blk_cols, blk_count):
     n_row, n_col = lax.axis_size("row"), lax.axis_size("col")
     nodes, width = cotangent.shape
@@ -154,14 +164,11 @@
     work = 2 * slots * side * side * width
 
     own = features.reshape(here, side, width)
-    steps = [0] + sorted(range(1, n_row), key=lambda k: -min(k, n_row - k))
-    moved = {0: own}
-    for k in steps[1:]:
-        moved[k] = lax.ppermute(own, "row", [(i, (i + k) % n_row) for i in range(n_row)])
-    pieces = [moved[k] for k in range(n_row)]
+    steps = [0] + sorted(range(1, n_row), key=lambda k: (-min(k, n_row - k), k))
+    pieces = [own] + [lax.ppermute(own, "row", turn(n_row, k)) for k in steps[1:]]
 
     send, keep = pl.pallas_call(
-        functools.partial(forward_kernel, chunk),
+        functools.partial(forward_kernel, chunk, steps),
         out_shape=(
             jax.ShapeDtypeStruct((chips, nodes, width), BF16),
             jax.ShapeDtypeStruct((chips, nodes, width), F32),
@@ -202,15 +209,18 @@
     other = lax.ppermute(same, "col", swap)
 
     terms = jnp.sum(same[:, nodes:].astype(F32), axis=0) + jnp.sum(other[:, nodes:].astype(F32), axis=0)
-    half_strip = lax.dynamic_slice_in_dim(terms, place[0] * (strip // 2), strip // 2, 0)
-    strips = lax.all_gather(half_strip, ("row", "col"), axis=0, tiled=True)
-    grad_weight = jnp.sum(strips.reshape(n_row, width, width), axis=0)
-
-    partial_cols = pl.pallas_call(
-        functools.partial(backward_kernel, chunk),
-        out_shape=jax.ShapeDtypeStruct((here * n_row, side, width), BF16),
+    rows_core = strip // 2
+    half_strip = lax.dynamic_slice_in_dim(terms, place[0] * rows_core, rows_core, 0)
+    copies = jnp.broadcast_to(half_strip[None], (n_row, rows_core, width))
+    strips = lax.all_to_all(copies, "row", 0, 0, tiled=True)
+    copies = jnp.broadcast_to(jnp.sum(strips, axis=0)[None], (n_col, rows_core, width))
+    grad_weight = lax.all_to_all(copies, "col", 0, 0, tiled=True).reshape(width, width)
+
+    shares = pl.pallas_call(
+        functools.partial(backward_kernel, chunk, steps),
+        out_shape=(jax.ShapeDtypeStruct((nodes, width), BF16),) * n_row,
         in_specs=[smem] * 4 + [hbm] + [near] * 2,
-        out_specs=vmem,
+        out_specs=(vmem,) * n_row,
         scratch_shapes=[
             pltpu.VMEM((slots, side, side), BF16),
             pltpu.VMEM((2, chips, nodes + strip, width), BF16),
@@ -222,10 +232,10 @@
         cost_estimate=pl.CostEstimate(flops=work, bytes_accessed=11 * MIB, transcendentals=0),
     )(*scalars, values, same, other)
 
-    own_cols = lax.all_to_all(
-        partial_cols.reshape(n_row, nodes, width), "row", 0, 0, tiled=True
-    )
-    grad_features = jnp.sum(own_cols.astype(F32), axis=0).astype(BF16).reshape(1, nodes, width)
+    total = shares[0].astype(F32)
+    for step, share in zip(steps[1:], shares[1:]):
+        total += lax.ppermute(share, "row", turn(n_row, step)).astype(F32)
+    grad_features = total.astype(BF16).reshape(1, nodes, width)
     return (activated, grad_weight, grad_features)
 
 

time: 248 us -> 177 us (0.71)
  waiting for transfers between devices: 91.7 us -> 34.1 us
  starting transfers between devices: 18.1 us -> 39.9 us
  blocking collectives: 94.6 us -> 76.7 us
  between operations: 14.8 us -> 1.43 us
  other arithmetic: 5.54 us -> 2.48 us
    all_gather x1 -> x0, waiting for transfers between devices: 62.3 us -> none  [per_device(): strips = lax.all_gather(half_strip, ('row', 'col'), axis=0, tiled=True)]
    all_to_all x1, blocking collectives: 31.7 us -> 12.9 us  [per_device(): strips = lax.all_to_all(copies, 'row', 0, 0, tiled=True)]
    ppermute x7 -> x14, starting transfers between devices: 14.8 us -> 27.7 us  [the longest x7 15.7 us: per_device(): lax.ppermute(own, 'row', turn(n_row, k))]
    all_to_all x0 -> x1, waiting for transfers between devices: none -> 8.04 us  [per_device(): lax.all_to_all(copies, 'col', 0, 0, tiled=True).reshape(width, width)]
    all_to_all x0 -> x1, starting transfers between devices: none -> 7.64 us  [per_device(): lax.all_to_all(copies, 'col', 0, 0, tiled=True).reshape(width, width)]
    ppermute x7 -> x14, waiting for transfers between devices: 21.5 us -> 18.1 us  [the longest x7 12.8 us: per_device(): lax.ppermute(own, 'row', turn(n_row, k))]
    reduce_sum x2 -> x1, other arithmetic: 3.27 us -> 0.01 us  [per_device(): jnp.sum(strips, axis=0)[None]]
  transfers between devices with their start and end apart: 10 -> 17, of which waited for: 9 -> 7; matrix products, arithmetic and copies ran while one was open for 0% -> 1% of each run, Pallas kernels for 4% -> 0%
where the time goes in v3:
time: 177 us
  blocking collectives  76.7 us (43%)
  starting transfers between devices  39.9 us (23%)
  waiting for transfers between devices  34.1 us (19%)
  Pallas kernels  18.4 us (10%)
  local copies, waits for them, and re-layouts  3.71 us (2%)
  other arithmetic  2.48 us (1%)
    all_to_all x1, blocking collectives, per_device(): lax.all_to_all(shares, 'col', 0, 0, tiled=True, axis_index_groups=same_core)  32.1 us
    all_to_all x1, blocking collectives, per_device(): lax.all_to_all(grad_agg, 'col', 0, 0, tiled=True, axis_index_groups=same_...  31.7 us
    ppermute x7, starting transfers between devices, per_device(): lax.ppermute(own, 'row', turn(n_row, k))  15.7 us
    all_to_all x1, blocking collectives, per_device(): strips = lax.all_to_all(copies, 'row', 0, 0, tiled=True)  12.9 us
    ppermute x7, waiting for transfers between devices, per_device(): lax.ppermute(own, 'row', turn(n_row, k))  12.8 us
    ppermute x7, starting transfers between devices, per_device(): total += lax.ppermute(share, 'row', turn(n_row, step)).astype(F32)  11.9 us
    pallas_call x1, Pallas kernels, per_device(): pl.pallas_call(functools.partial(backward_kernel, chunk, steps), out_shap...  9.07 us
    pallas_call x1, Pallas kernels, per_device(): pl.pallas_call(functools.partial(forward_kernel, chunk, steps), out_shape...  8.23 us
  transfers between devices with their start and end apart: 17, of which 7 were waited for; matrix products, arithmetic and copies ran while one was open for 1% of the time, Pallas kernels for 0%

profile of v3, /device:TPU:1, one launch (start us, length us, event | category | flops | bytes accessed | tf_op | source)
XLA Modules:
  0.0 176.6 jit_solution(8422422762953239520)
XLA Ops:
  0.6 6.5 %collective-permute-start.6 = (bf16[2,128,256]{2,1,0:T(8,128)(2,1)}, bf16[2,128,256]{2,1,0:T(8,128)(2,1)S(1)}, u32[]{:S(2)}, u32[]{:S(2)}) collective-permute-start(bf16[2,128,256]{2,1,0:T(8,128)(2,1)} %bitcast.12), channel_id=1, source_target_pairs={{0,224},{32,0},{64,32},{96,64},{128,96},{160,128},{192,160},{224,1... | collective-permute-start | bytes 393224 | tf_op jit(solution)/shard_map/ppermute | solution.py:168
  7.1 1.9 %collective-permute-start.4 = (bf16[2,128,256]{2,1,0:T(8,128)(2,1)}, bf16[2,128,256]{2,1,0:T(8,128)(2,1)S(1)}, u32[]{:S(2)}, u32[]{:S(2)}) collective-permute-start(bf16[2,128,256]{2,1,0:T(8,128)(2,1)} %bitcast.14), channel_id=1, source_target_pairs={{0,192},{32,224},{64,0},{96,32},{128,64},{160,96},{192,128},{224,1... | collective-permute-start | bytes 393224 | tf_op jit(solution)/shard_map/ppermute | solution.py:168
  9.0 0.5 collective-permute-start.3
  9.5 2.4 %collective-permute-start.2 = (bf16[2,128,256]{2,1,0:T(8,128)(2,1)}, bf16[2,128,256]{2,1,0:T(8,128)(2,1)S(1)}, u32[]{:S(2)}, u32[]{:S(2)}) collective-permute-start(bf16[2,128,256]{2,1,0:T(8,128)(2,1)} %bitcast.16), channel_id=1, source_target_pairs={{0,160},{32,192},{64,224},{96,0},{128,32},{160,64},{192,96},{224,1... | collective-permute-start | bytes 393224 | tf_op jit(solution)/shard_map/ppermute | solution.py:168
  11.9 0.0 collective-permute-done.6.refs_7_
  11.9 0.9 collective-permute-start.1
  12.7 0.0 collective-permute-done.5.refs_6_
  12.8 3.6 %collective-permute-start = (bf16[2,128,256]{2,1,0:T(8,128)(2,1)}, bf16[2,128,256]{2,1,0:T(8,128)(2,1)S(1)}, u32[]{:S(2)}, u32[]{:S(2)}) collective-permute-start(bf16[2,128,256]{2,1,0:T(8,128)(2,1)} %bitcast.18), channel_id=1, source_target_pairs={{0,128},{32,160},{64,192},{96,224},{128,0},{160,32},{192,64},{224,... | collective-permute-start | bytes 393224 | tf_op jit(solution)/shard_map/ppermute | solution.py:168
  17.0 0.1 pad_add_fusion.place
  17.1 0.6 collective-permute-done.4.refs_5_
  17.7 0.0 collective-permute-done.3.refs_4_
  17.7 0.0 collective-permute-done.2.refs_3_
  17.7 11.8 %collective-permute-done.1.refs_2_ = bf16[2,128,256]{2,1,0:T(8,128)(2,1)S(1)} collective-permute-done((bf16[2,128,256]{2,1,0:T(8,128)(2,1)}, bf16[2,128,256]{2,1,0:T(8,128)(2,1)S(1)}, u32[]{:S(2)}, u32[]{:S(2)}) %collective-permute-start.1) | collective-permute-done | bytes 131104 | tf_op jit(solution)/shard_map/ppermute | solution.py:168
  29.5 0.4 collective-permute-done.refs_1_
  29.9 0.9 copy-done
  30.8 0.7 copy-done.3
  31.5 0.7 copy-done.5
  32.2 8.2 %shard_map.94 = (bf16[16,256,256]{2,1,0:T(8,128)(2,1)S(1)}, f32[16,256,256]{2,1,0:T(8,128)S(1)}) custom-call(s32[2]{0:T(128)S(1)} %pad_add_fusion.place, s32[192]{0:T(256)S(1)} %bitcast.20, s32[192]{0:T(256)S(1)} %bitcast.22, s32[1]{0:T(128)} %bitcast.10.count, bf16[192,128,128]{2,1,0:T(8,128)(2,1)} %bitcast.24, bf16[2,128,256]{2,1,0:T(8,128)(2,1)S(1)} %bitcast.19, ...), custom_call_target="tpu_custom_call" | custom-call | flops 1610612736 | bytes 14680064 | tf_op jit(solution)/shard_map/pallas_call | solution.py:170
  40.4 2.1 %collective-permute-start.7 = (bf16[16,256,256]{2,1,0:T(8,128)(2,1)S(1)}, bf16[16,256,256]{2,1,0:T(8,128)(2,1)S(1)}, u32[]{:S(2)}, u32[]{:S(2)}) collective-permute-start(bf16[16,256,256]{2,1,0:T(8,128)(2,1)S(1)} %get-tuple-element.16), channel_id=1, source_target_pairs={{0,1},{1,0},{2,3},{3,2},{4,5},{5,4},{6,7},{7,6},{8,9},{9,8},{10,11... | collective-permute-start | bytes 6291464 | tf_op jit(solution)/shard_map/ppermute | solution.py:189
  42.5 3.8 %collective-permute-done.7 = bf16[16,256,256]{2,1,0:T(8,128)(2,1)S(1)} collective-permute-done((bf16[16,256,256]{2,1,0:T(8,128)(2,1)S(1)}, bf16[16,256,256]{2,1,0:T(8,128)(2,1)S(1)}, u32[]{:S(2)}, u32[]{:S(2)}) %collective-permute-start.7) | collective-permute-done | bytes 2097184 | tf_op jit(solution)/shard_map/ppermute | solution.py:189
  46.3 0.6 add_convert_fusion
  46.9 0.0 copy-start.1
  46.9 0.0 copy-start.2
  46.9 32.1 %all_to_all.20.parts = bf16[16,256,256]{2,1,0:T(8,128)(2,1)S(1)} all-to-all(bf16[16,256,256]{2,1,0:T(8,128)(2,1)S(1)} %add_convert_fusion), channel_id=1, replica_groups={{0,2,4,6,8,10,12,14,16,18,20,22,24,26,28,30},{1,3,5,7,9,11,13,15,17,19,..., dimensions={0} | all-to-all | bytes 4194304 | tf_op jit(solution)/shard_map/all_to_all | solution.py:191
  79.0 1.1 shard_map.95
  80.1 31.7 %all_to_all.21.same = bf16[16,272,256]{2,1,0:T(8,128)(2,1)S(1)} all-to-all(bf16[16,272,256]{2,1,0:T(8,128)(2,1)S(1)} %get-tuple-element.18), channel_id=1, replica_groups={{0,2,4,6,8,10,12,14,16,18,20,22,24,26,28,30},{1,3,5,7,9,11,13,15,17,19,..., dimensions={0} | all-to-all | bytes 4456448 | tf_op jit(solution)/shard_map/all_to_all | solution.py:208
  111.8 2.5 %collective-permute-start.8 = (bf16[16,272,256]{2,1,0:T(8,128)(2,1)S(1)}, bf16[16,272,256]{2,1,0:T(8,128)(2,1)}, u32[]{:S(2)}, u32[]{:S(2)}) collective-permute-start(bf16[16,272,256]{2,1,0:T(8,128)(2,1)S(1)} %all_to_all.21.same), channel_id=1, source_target_pairs={{0,1},{1,0},{2,3},{3,2},{4,5},{5,4},{6,7},{7,6},{8,9},{9,8},{10,11... | collective-permute-start | bytes 6684680 | tf_op jit(solution)/shard_map/ppermute | solution.py:209
  114.3 4.1 %collective-permute-done.8.other = bf16[16,272,256]{2,1,0:T(8,128)(2,1)} collective-permute-done((bf16[16,272,256]{2,1,0:T(8,128)(2,1)S(1)}, bf16[16,272,256]{2,1,0:T(8,128)(2,1)}, u32[]{:S(2)}, u32[]{:S(2)}) %collective-permute-start.8) | collective-permute-done | bytes 2228256 | tf_op jit(solution)/shard_map/ppermute | solution.py:209
  118.5 9.1 %shard_map.96 = (bf16[256,256]{1,0:T(8,128)(2,1)S(1)}, bf16[256,256]{1,0:T(8,128)(2,1)S(1)}, bf16[256,256]{1,0:T(8,128)(2,1)S(1)}, bf16[256,256]{1,0:T(8,128)(2,...) custom-call(s32[2]{0:T(128)S(1)} %pad_add_fusion.place, ...), custom_call_target="tpu_custom_call" | custom-call | flops 1610612736 | bytes 11534336 | tf_op jit(solution)/shard_map/pallas_call | solution.py:219
  127.5 0.1 collective-permute-start.9
  127.6 0.1 collective-permute-start.10
  127.8 4.5 %collective-permute-start.11 = (bf16[256,256]{1,0:T(8,128)(2,1)S(1)}, bf16[256,256]{1,0:T(8,128)(2,1)S(1)}, u32[]{:S(2)}, u32[]{:S(2)}) collective-permute-start(bf16[256,256]{1,0:T(8,128)(2,1)S(1)} %get-tuple-element.22), channel_id=1, source_target_pairs={{0,160},{32,192},{64,224},{96,0},{128,32},{160,64},{192,96},{224,1... | collective-permute-start | bytes 393224 | tf_op jit(solution)/shard_map/ppermute | solution.py:237
  132.3 4.1 %collective-permute-start.12 = (bf16[256,256]{1,0:T(8,128)(2,1)S(1)}, bf16[256,256]{1,0:T(8,128)(2,1)S(1)}, u32[]{:S(2)}, u32[]{:S(2)}) collective-permute-start(bf16[256,256]{1,0:T(8,128)(2,1)S(1)} %get-tuple-element.23), channel_id=1, source_target_pairs={{0,64},{32,96},{64,128},{96,160},{128,192},{160,224},{192,0},{224,... | collective-permute-start | bytes 393224 | tf_op jit(solution)/shard_map/ppermute | solution.py:237
  136.4 0.4 collective-permute-start.13
  136.8 0.9 convert_reduce_fusion
  137.7 0.0 collective-permute-done.9
  137.7 2.8 %collective-permute-start.14 = (bf16[256,256]{1,0:T(8,128)(2,1)S(1)}, bf16[256,256]{1,0:T(8,128)(2,1)S(1)}, u32[]{:S(2)}, u32[]{:S(2)}) collective-permute-start(bf16[256,256]{1,0:T(8,128)(2,1)S(1)} %get-tuple-element.25), channel_id=1, source_target_pairs={{0,32},{32,64},{64,96},{96,128},{128,160},{160,192},{192,224},{224... | collective-permute-start | bytes 393224 | tf_op jit(solution)/shard_map/ppermute | solution.py:237
  140.5 5.3 %collective-permute-done.10 = bf16[256,256]{1,0:T(8,128)(2,1)S(1)} collective-permute-done((bf16[256,256]{1,0:T(8,128)(2,1)S(1)}, bf16[256,256]{1,0:T(8,128)(2,1)S(1)}, u32[]{:S(2)}, u32[]{:S(2)}) %collective-permute-start.10) | collective-permute-done | bytes 131104 | tf_op jit(solution)/shard_map/ppermute | solution.py:237
  145.8 0.0 collective-permute-start.15
  145.8 12.9 %all_to_all.22 = f32[8,8,256]{2,1,0:T(8,128)S(1)} all-to-all(f32[8,8,256]{2,1,0:T(8,128)S(1)} %broadcast_in_dim.4), channel_id=1, replica_groups=mesh['row'=8,'col'=32] {'row'}, dimensions={0} | all-to-all | bytes 131072 | tf_op jit(solution)/shard_map/all_to_all | solution.py:215
  158.7 0.7 broadcast_in_dim.5
  159.4 7.6 %all-to-all-start.3 = ((f32[32,8,256]{2,1,0:T(8,128)}), f32[32,8,256]{2,1,0:T(8,128)S(1)}, u32[]{:S(2)}, u32[]{:S(2)}) async-start(f32[32,8,256]{2,1,0:T(8,128)} %broadcast_in_dim.5), calls=%async_computation.3 | async-start | bytes 524288 | tf_op jit(solution)/shard_map/all_to_all | solution.py:217
  167.0 0.0 collective-permute-done.11
  167.1 0.0 collective-permute-done.13
  167.1 0.0 collective-permute-done.14
  167.1 0.8 fusion
  167.9 8.0 %all-to-all-done.3 = f32[32,8,256]{2,1,0:T(8,128)S(1)} async-done(((f32[32,8,256]{2,1,0:T(8,128)}), f32[32,8,256]{2,1,0:T(8,128)S(1)}, u32[]{:S(2)}, u32[]{:S(2)}) %all-to-all-start.3) | async-done | bytes 262176 | tf_op jit(solution)/shard_map/all_to_all | solution.py:217
  175.9 0.7 copy.12
  (16 shorter events, 0.1 us)
Async XLA Ops:
  0.6 11.2 %collective-permute-start.6 = (bf16[2,128,256]{2,1,0:T(8,128)(2,1)}, bf16[2,128,256]{2,1,0:T(8,128)(2,1)S(1)}, u32[]{:S(2)}, u32[]{:S(2)}) collective-permute-start(bf16[2,128,256]{2,1,0:T(8,128)(2,1)} %bitcast.12), channel_id=1, source_target_pairs={{0,224},{32,0},{64,32},{96,64},{128,96},{160,128},{192,160},{224,1... | collective-permute-start | bytes 393224 | tf_op jit(solution)/shard_map/ppermute | solution.py:168
  7.1 5.6 %collective-permute-start.5 = (bf16[2,128,256]{2,1,0:T(8,128)(2,1)}, bf16[2,128,256]{2,1,0:T(8,128)(2,1)S(1)}, u32[]{:S(2)}, u32[]{:S(2)}) collective-permute-start(bf16[2,128,256]{2,1,0:T(8,128)(2,1)} %bitcast.13), channel_id=1, source_target_pairs={{0,32},{32,64},{64,96},{96,128},{128,160},{160,192},{192,224},{224... | collective-permute-start | bytes 393224 | tf_op jit(solution)/shard_map/ppermute | solution.py:168
  7.1 10.6 %collective-permute-start.4 = (bf16[2,128,256]{2,1,0:T(8,128)(2,1)}, bf16[2,128,256]{2,1,0:T(8,128)(2,1)S(1)}, u32[]{:S(2)}, u32[]{:S(2)}) collective-permute-start(bf16[2,128,256]{2,1,0:T(8,128)(2,1)} %bitcast.14), channel_id=1, source_target_pairs={{0,192},{32,224},{64,0},{96,32},{128,64},{160,96},{192,128},{224,1... | collective-permute-start | bytes 393224 | tf_op jit(solution)/shard_map/ppermute | solution.py:168
  9.0 8.7 %collective-permute-start.3 = (bf16[2,128,256]{2,1,0:T(8,128)(2,1)}, bf16[2,128,256]{2,1,0:T(8,128)(2,1)S(1)}, u32[]{:S(2)}, u32[]{:S(2)}) collective-permute-start(bf16[2,128,256]{2,1,0:T(8,128)(2,1)} %bitcast.15), channel_id=1, source_target_pairs={{0,64},{32,96},{64,128},{96,160},{128,192},{160,224},{192,0},{224,... | collective-permute-start | bytes 393224 | tf_op jit(solution)/shard_map/ppermute | solution.py:168
  9.5 8.2 %collective-permute-start.2 = (bf16[2,128,256]{2,1,0:T(8,128)(2,1)}, bf16[2,128,256]{2,1,0:T(8,128)(2,1)S(1)}, u32[]{:S(2)}, u32[]{:S(2)}) collective-permute-start(bf16[2,128,256]{2,1,0:T(8,128)(2,1)} %bitcast.16), channel_id=1, source_target_pairs={{0,160},{32,192},{64,224},{96,0},{128,32},{160,64},{192,96},{224,1... | collective-permute-start | bytes 393224 | tf_op jit(solution)/shard_map/ppermute | solution.py:168
  11.9 17.6 %collective-permute-start.1 = (bf16[2,128,256]{2,1,0:T(8,128)(2,1)}, bf16[2,128,256]{2,1,0:T(8,128)(2,1)S(1)}, u32[]{:S(2)}, u32[]{:S(2)}) collective-permute-start(bf16[2,128,256]{2,1,0:T(8,128)(2,1)} %bitcast.17), channel_id=1, source_target_pairs={{0,96},{32,128},{64,160},{96,192},{128,224},{160,0},{192,32},{224,... | collective-permute-start | bytes 393224 | tf_op jit(solution)/shard_map/ppermute | solution.py:168
  12.8 17.1 %collective-permute-start = (bf16[2,128,256]{2,1,0:T(8,128)(2,1)}, bf16[2,128,256]{2,1,0:T(8,128)(2,1)S(1)}, u32[]{:S(2)}, u32[]{:S(2)}) collective-permute-start(bf16[2,128,256]{2,1,0:T(8,128)(2,1)} %bitcast.18), channel_id=1, source_target_pairs={{0,128},{32,160},{64,192},{96,224},{128,0},{160,32},{192,64},{224,... | collective-permute-start | bytes 393224 | tf_op jit(solution)/shard_map/ppermute | solution.py:168
  29.9 0.9 copy-start
  30.8 0.7 copy-start.3
  31.5 0.7 copy-start.5
  40.4 5.9 %collective-permute-start.7 = (bf16[16,256,256]{2,1,0:T(8,128)(2,1)S(1)}, bf16[16,256,256]{2,1,0:T(8,128)(2,1)S(1)}, u32[]{:S(2)}, u32[]{:S(2)}) collective-permute-start(bf16[16,256,256]{2,1,0:T(8,128)(2,1)S(1)} %get-tuple-element.16), channel_id=1, source_target_pairs={{0,1},{1,0},{2,3},{3,2},{4,5},{5,4},{6,7},{7,6},{8,9},{9,8},{10,11... | collective-permute-start | bytes 6291464 | tf_op jit(solution)/shard_map/ppermute | solution.py:189
  46.9 32.1 %copy-start.1 = (bf16[256,256]{1,0:T(8,128)(2,1)S(1)}, bf16[256,256]{1,0:T(8,128)(2,1)}, u32[]{:S(2)}) copy-start(bf16[256,256]{1,0:T(8,128)(2,1)} %weight.1) | copy-start | bytes 393220
  46.9 32.1 %copy-start.2 = (bf16[256,256]{1,0:T(8,128)(2,1)S(1)}, bf16[256,256]{1,0:T(8,128)(2,1)}, u32[]{:S(2)}) copy-start(bf16[256,256]{1,0:T(8,128)(2,1)} %cotangent.1) | copy-start | bytes 393220
  80.1 38.4 %copy-start.4 = (s32[1,1,192]{2,1,0:T(1,128)S(1)}, s32[1,1,192]{2,1,0:T(1,128)}, u32[]{:S(2)}) copy-start(s32[1,1,192]{2,1,0:T(1,128)} %param.11) | copy-start | bytes 2308
  80.1 38.4 %copy-start.6 = (s32[1,1,192]{2,1,0:T(1,128)S(1)}, s32[1,1,192]{2,1,0:T(1,128)}, u32[]{:S(2)}) copy-start(s32[1,1,192]{2,1,0:T(1,128)} %param.12) | copy-start | bytes 2308
  111.8 6.6 %collective-permute-start.8 = (bf16[16,272,256]{2,1,0:T(8,128)(2,1)S(1)}, bf16[16,272,256]{2,1,0:T(8,128)(2,1)}, u32[]{:S(2)}, u32[]{:S(2)}) collective-permute-start(bf16[16,272,256]{2,1,0:T(8,128)(2,1)S(1)} %all_to_all.21.same), channel_id=1, source_target_pairs={{0,1},{1,0},{2,3},{3,2},{4,5},{5,4},{6,7},{7,6},{8,9},{9,8},{10,11... | collective-permute-start | bytes 6684680 | tf_op jit(solution)/shard_map/ppermute | solution.py:209
  127.5 10.2 %collective-permute-start.9 = (bf16[256,256]{1,0:T(8,128)(2,1)S(1)}, bf16[256,256]{1,0:T(8,128)(2,1)S(1)}, u32[]{:S(2)}, u32[]{:S(2)}) collective-permute-start(bf16[256,256]{1,0:T(8,128)(2,1)S(1)} %get-tuple-element.20), channel_id=1, source_target_pairs={{0,128},{32,160},{64,192},{96,224},{128,0},{160,32},{192,64},{224,... | collective-permute-start | bytes 393224 | tf_op jit(solution)/shard_map/ppermute | solution.py:237
  127.6 18.1 %collective-permute-start.10 = (bf16[256,256]{1,0:T(8,128)(2,1)S(1)}, bf16[256,256]{1,0:T(8,128)(2,1)S(1)}, u32[]{:S(2)}, u32[]{:S(2)}) collective-permute-start(bf16[256,256]{1,0:T(8,128)(2,1)S(1)} %get-tuple-element.21), channel_id=1, source_target_pairs={{0,96},{32,128},{64,160},{96,192},{128,224},{160,0},{192,32},{224,... | collective-permute-start | bytes 393224 | tf_op jit(solution)/shard_map/ppermute | solution.py:237
  127.8 39.3 %collective-permute-start.11 = (bf16[256,256]{1,0:T(8,128)(2,1)S(1)}, bf16[256,256]{1,0:T(8,128)(2,1)S(1)}, u32[]{:S(2)}, u32[]{:S(2)}) collective-permute-start(bf16[256,256]{1,0:T(8,128)(2,1)S(1)} %get-tuple-element.22), channel_id=1, source_target_pairs={{0,160},{32,192},{64,224},{96,0},{128,32},{160,64},{192,96},{224,1... | collective-permute-start | bytes 393224 | tf_op jit(solution)/shard_map/ppermute | solution.py:237
  132.3 34.8 %collective-permute-start.12 = (bf16[256,256]{1,0:T(8,128)(2,1)S(1)}, bf16[256,256]{1,0:T(8,128)(2,1)S(1)}, u32[]{:S(2)}, u32[]{:S(2)}) collective-permute-start(bf16[256,256]{1,0:T(8,128)(2,1)S(1)} %get-tuple-element.23), channel_id=1, source_target_pairs={{0,64},{32,96},{64,128},{96,160},{128,192},{160,224},{192,0},{224,... | collective-permute-start | bytes 393224 | tf_op jit(solution)/shard_map/ppermute | solution.py:237
  136.4 30.7 %collective-permute-start.13 = (bf16[256,256]{1,0:T(8,128)(2,1)S(1)}, bf16[256,256]{1,0:T(8,128)(2,1)S(1)}, u32[]{:S(2)}, u32[]{:S(2)}) collective-permute-start(bf16[256,256]{1,0:T(8,128)(2,1)S(1)} %get-tuple-element.24), channel_id=1, source_target_pairs={{0,192},{32,224},{64,0},{96,32},{128,64},{160,96},{192,128},{224,1... | collective-permute-start | bytes 393224 | tf_op jit(solution)/shard_map/ppermute | solution.py:237
  137.7 29.4 %collective-permute-start.14 = (bf16[256,256]{1,0:T(8,128)(2,1)S(1)}, bf16[256,256]{1,0:T(8,128)(2,1)S(1)}, u32[]{:S(2)}, u32[]{:S(2)}) collective-permute-start(bf16[256,256]{1,0:T(8,128)(2,1)S(1)} %get-tuple-element.25), channel_id=1, source_target_pairs={{0,32},{32,64},{64,96},{96,128},{128,160},{160,192},{192,224},{224... | collective-permute-start | bytes 393224 | tf_op jit(solution)/shard_map/ppermute | solution.py:237
  145.8 21.3 %collective-permute-start.15 = (bf16[256,256]{1,0:T(8,128)(2,1)S(1)}, bf16[256,256]{1,0:T(8,128)(2,1)S(1)}, u32[]{:S(2)}, u32[]{:S(2)}) collective-permute-start(bf16[256,256]{1,0:T(8,128)(2,1)S(1)} %get-tuple-element.26), channel_id=1, source_target_pairs={{0,224},{32,0},{64,32},{96,64},{128,96},{160,128},{192,160},{224,1... | collective-permute-start | bytes 393224 | tf_op jit(solution)/shard_map/ppermute | solution.py:237
  159.4 16.5 %all-to-all-start.3 = ((f32[32,8,256]{2,1,0:T(8,128)}), f32[32,8,256]{2,1,0:T(8,128)S(1)}, u32[]{:S(2)}, u32[]{:S(2)}) async-start(f32[32,8,256]{2,1,0:T(8,128)} %broadcast_in_dim.5), calls=%async_computation.3 | async-start | bytes 524288 | tf_op jit(solution)/shard_map/all_to_all | solution.py:217

commit v4 on v3

--- a/solution.py
+++ b/solution.py
@@ -214,7 +214,6 @@
     copies = jnp.broadcast_to(half_strip[None], (n_row, rows_core, width))
     strips = lax.all_to_all(copies, "row", 0, 0, tiled=True)
     copies = jnp.broadcast_to(jnp.sum(strips, axis=0)[None], (n_col, rows_core, width))
-    grad_weight = lax.all_to_all(copies, "col", 0, 0, tiled=True).reshape(width, width)
 
     shares = pl.pallas_call(
         functools.partial(backward_kernel, chunk, steps),
@@ -232,6 +231,8 @@
         cost_estimate=pl.CostEstimate(flops=work, bytes_accessed=11 * MIB, transcendentals=0),
     )(*scalars, values, same, other)
 
+    shares, copies = lax.optimization_barrier((shares, copies))
+    grad_weight = lax.all_to_all(copies, "col", 0, 0, tiled=True).reshape(width, width)
     total = shares[0].astype(F32)
     for step, share in zip(steps[1:], shares[1:]):
         total += lax.ppermute(share, "row", turn(n_row, step)).astype(F32)

time: 177 us -> 176 us (level)
  blocking collectives: 76.7 us -> 63.8 us
  starting transfers between devices: 39.9 us -> 45.5 us
  waiting for transfers between devices: 34.1 us -> 39.5 us
    all_to_all x1 -> x0, blocking collectives: 12.9 us -> none  [per_device(): strips = lax.all_to_all(copies, 'row', 0, 0, tiled=True)]
    all_to_all x0 -> x1, starting transfers between devices: none -> 7.91 us  [per_device(): strips = lax.all_to_all(copies, 'row', 0, 0, tiled=True)]
    ppermute x7, waiting for transfers between devices: 5.31 us -> 10.8 us  [per_device(): total += lax.ppermute(share, 'row', turn(n_row, step)).astype(F32)]
    ppermute x7, starting transfers between devices: 11.9 us -> 9.24 us  [per_device(): total += lax.ppermute(share, 'row', turn(n_row, step)).astype(F32)]
  transfers between devices with their start and end apart: 17 -> 18, of which waited for: 7 -> 8; matrix products, arithmetic and copies ran while one was open for 1% -> 1% of each run, Pallas kernels for 0% -> 5%
where the time goes in v4:
time: 176 us
  blocking collectives  63.8 us (36%)
  starting transfers between devices  45.5 us (26%)
  waiting for transfers between devices  39.5 us (22%)
  Pallas kernels  18.4 us (10%)
  local copies, waits for them, and re-layouts  4.34 us (2%)
  other arithmetic  2.48 us (1%)
    all_to_all x1, blocking collectives, per_device(): lax.all_to_all(shares, 'col', 0, 0, tiled=True, axis_index_groups=same_core)  32.1 us
    all_to_all x1, blocking collectives, per_device(): lax.all_to_all(grad_agg, 'col', 0, 0, tiled=True, axis_index_groups=same_...  31.7 us
    ppermute x7, starting transfers between devices, per_device(): lax.ppermute(own, 'row', turn(n_row, k))  15.7 us
    ppermute x7, waiting for transfers between devices, per_device(): lax.ppermute(own, 'row', turn(n_row, k))  12.8 us
    ppermute x7, waiting for transfers between devices, per_device(): total += lax.ppermute(share, 'row', turn(n_row, step)).astype(F32)  10.8 us
    ppermute x7, starting transfers between devices, per_device(): total += lax.ppermute(share, 'row', turn(n_row, step)).astype(F32)  9.24 us
    pallas_call x1, Pallas kernels, per_device(): pl.pallas_call(functools.partial(backward_kernel, chunk, steps), out_shap...  9.12 us
    pallas_call x1, Pallas kernels, per_device(): pl.pallas_call(functools.partial(forward_kernel, chunk, steps), out_shape...  8.23 us
  transfers between devices with their start and end apart: 18, of which 8 were waited for; matrix products, arithmetic and copies ran while one was open for 1% of the time, Pallas kernels for 5%

profile of v4, /device:TPU:1, one launch (start us, length us, event | category | flops | bytes accessed | tf_op | source)
XLA Modules:
  0.0 175.5 jit_solution(9919700904321341228)
XLA Ops:
  0.6 6.5 %collective-permute-start.6 = (bf16[2,128,256]{2,1,0:T(8,128)(2,1)}, bf16[2,128,256]{2,1,0:T(8,128)(2,1)S(1)}, u32[]{:S(2)}, u32[]{:S(2)}) collective-permute-start(bf16[2,128,256]{2,1,0:T(8,128)(2,1)} %bitcast.12), channel_id=1, source_target_pairs={{0,224},{32,0},{64,32},{96,64},{128,96},{160,128},{192,160},{224,1... | collective-permute-start | bytes 393224 | tf_op jit(solution)/shard_map/ppermute | solution.py:168
  7.1 1.9 %collective-permute-start.4 = (bf16[2,128,256]{2,1,0:T(8,128)(2,1)}, bf16[2,128,256]{2,1,0:T(8,128)(2,1)S(1)}, u32[]{:S(2)}, u32[]{:S(2)}) collective-permute-start(bf16[2,128,256]{2,1,0:T(8,128)(2,1)} %bitcast.14), channel_id=1, source_target_pairs={{0,192},{32,224},{64,0},{96,32},{128,64},{160,96},{192,128},{224,1... | collective-permute-start | bytes 393224 | tf_op jit(solution)/shard_map/ppermute | solution.py:168
  9.0 0.5 collective-permute-start.3
  9.5 2.4 %collective-permute-start.2 = (bf16[2,128,256]{2,1,0:T(8,128)(2,1)}, bf16[2,128,256]{2,1,0:T(8,128)(2,1)S(1)}, u32[]{:S(2)}, u32[]{:S(2)}) collective-permute-start(bf16[2,128,256]{2,1,0:T(8,128)(2,1)} %bitcast.16), channel_id=1, source_target_pairs={{0,160},{32,192},{64,224},{96,0},{128,32},{160,64},{192,96},{224,1... | collective-permute-start | bytes 393224 | tf_op jit(solution)/shard_map/ppermute | solution.py:168
  11.9 0.0 collective-permute-done.6.refs_7_
  11.9 0.9 collective-permute-start.1
  12.7 0.0 collective-permute-done.5.refs_6_
  12.8 3.6 %collective-permute-start = (bf16[2,128,256]{2,1,0:T(8,128)(2,1)}, bf16[2,128,256]{2,1,0:T(8,128)(2,1)S(1)}, u32[]{:S(2)}, u32[]{:S(2)}) collective-permute-start(bf16[2,128,256]{2,1,0:T(8,128)(2,1)} %bitcast.18), channel_id=1, source_target_pairs={{0,128},{32,160},{64,192},{96,224},{128,0},{160,32},{192,64},{224,... | collective-permute-start | bytes 393224 | tf_op jit(solution)/shard_map/ppermute | solution.py:168
  17.0 0.1 pad_add_fusion.place
  17.1 0.6 collective-permute-done.4.refs_5_
  17.7 0.0 collective-permute-done.3.refs_4_
  17.7 0.0 collective-permute-done.2.refs_3_
  17.7 11.8 %collective-permute-done.1.refs_2_ = bf16[2,128,256]{2,1,0:T(8,128)(2,1)S(1)} collective-permute-done((bf16[2,128,256]{2,1,0:T(8,128)(2,1)}, bf16[2,128,256]{2,1,0:T(8,128)(2,1)S(1)}, u32[]{:S(2)}, u32[]{:S(2)}) %collective-permute-start.1) | collective-permute-done | bytes 131104 | tf_op jit(solution)/shard_map/ppermute | solution.py:168
  29.5 0.4 collective-permute-done.refs_1_
  29.9 0.9 copy-done
  30.8 0.7 copy-done.3
  31.5 0.7 copy-done.5
  32.2 8.2 %shard_map.94 = (bf16[16,256,256]{2,1,0:T(8,128)(2,1)S(1)}, f32[16,256,256]{2,1,0:T(8,128)S(1)}) custom-call(s32[2]{0:T(128)S(1)} %pad_add_fusion.place, s32[192]{0:T(256)S(1)} %bitcast.20, s32[192]{0:T(256)S(1)} %bitcast.22, s32[1]{0:T(128)} %bitcast.10.count, bf16[192,128,128]{2,1,0:T(8,128)(2,1)} %bitcast.24, bf16[2,128,256]{2,1,0:T(8,128)(2,1)S(1)} %bitcast.19, ...), custom_call_target="tpu_custom_call" | custom-call | flops 1610612736 | bytes 14680064 | tf_op jit(solution)/shard_map/pallas_call | solution.py:170
  40.4 2.1 %collective-permute-start.7 = (bf16[16,256,256]{2,1,0:T(8,128)(2,1)S(1)}, bf16[16,256,256]{2,1,0:T(8,128)(2,1)S(1)}, u32[]{:S(2)}, u32[]{:S(2)}) collective-permute-start(bf16[16,256,256]{2,1,0:T(8,128)(2,1)S(1)} %get-tuple-element.25), channel_id=1, source_target_pairs={{0,1},{1,0},{2,3},{3,2},{4,5},{5,4},{6,7},{7,6},{8,9},{9,8},{10,11... | collective-permute-start | bytes 6291464 | tf_op jit(solution)/shard_map/ppermute | solution.py:189
  42.5 3.8 %collective-permute-done.7 = bf16[16,256,256]{2,1,0:T(8,128)(2,1)S(1)} collective-permute-done((bf16[16,256,256]{2,1,0:T(8,128)(2,1)S(1)}, bf16[16,256,256]{2,1,0:T(8,128)(2,1)S(1)}, u32[]{:S(2)}, u32[]{:S(2)}) %collective-permute-start.7) | collective-permute-done | bytes 2097184 | tf_op jit(solution)/shard_map/ppermute | solution.py:189
  46.3 0.6 add_convert_fusion
  46.9 0.0 copy-start.1
  46.9 0.0 copy-start.2
  46.9 32.1 %all_to_all.20.parts = bf16[16,256,256]{2,1,0:T(8,128)(2,1)S(1)} all-to-all(bf16[16,256,256]{2,1,0:T(8,128)(2,1)S(1)} %add_convert_fusion), channel_id=1, replica_groups={{0,2,4,6,8,10,12,14,16,18,20,22,24,26,28,30},{1,3,5,7,9,11,13,15,17,19,..., dimensions={0} | all-to-all | bytes 4194304 | tf_op jit(solution)/shard_map/all_to_all | solution.py:191
  79.0 1.1 shard_map.95
  80.1 31.7 %all_to_all.21.same = bf16[16,272,256]{2,1,0:T(8,128)(2,1)S(1)} all-to-all(bf16[16,272,256]{2,1,0:T(8,128)(2,1)S(1)} %get-tuple-element.27), channel_id=1, replica_groups={{0,2,4,6,8,10,12,14,16,18,20,22,24,26,28,30},{1,3,5,7,9,11,13,15,17,19,..., dimensions={0} | all-to-all | bytes 4456448 | tf_op jit(solution)/shard_map/all_to_all | solution.py:208
  111.8 2.5 %collective-permute-start.8 = (bf16[16,272,256]{2,1,0:T(8,128)(2,1)S(1)}, bf16[16,272,256]{2,1,0:T(8,128)(2,1)}, u32[]{:S(2)}, u32[]{:S(2)}) collective-permute-start(bf16[16,272,256]{2,1,0:T(8,128)(2,1)S(1)} %all_to_all.21.same), channel_id=1, source_target_pairs={{0,1},{1,0},{2,3},{3,2},{4,5},{5,4},{6,7},{7,6},{8,9},{9,8},{10,11... | collective-permute-start | bytes 6684680 | tf_op jit(solution)/shard_map/ppermute | solution.py:209
  114.4 4.1 %collective-permute-done.8.other = bf16[16,272,256]{2,1,0:T(8,128)(2,1)} collective-permute-done((bf16[16,272,256]{2,1,0:T(8,128)(2,1)S(1)}, bf16[16,272,256]{2,1,0:T(8,128)(2,1)}, u32[]{:S(2)}, u32[]{:S(2)}) %collective-permute-start.8) | collective-permute-done | bytes 2228256 | tf_op jit(solution)/shard_map/ppermute | solution.py:209
  118.5 0.9 convert_reduce_fusion
  119.4 0.6 broadcast_in_dim.4
  120.0 7.9 %all-to-all-start.2 = ((f32[8,8,256]{2,1,0:T(8,128)}), f32[8,8,256]{2,1,0:T(8,128)S(1)}, u32[]{:S(2)}, u32[]{:S(2)}) async-start(f32[8,8,256]{2,1,0:T(8,128)} %broadcast_in_dim.4), calls=%async_computation.2 | async-start | bytes 131072 | tf_op jit(solution)/shard_map/all_to_all | solution.py:215
  128.0 9.1 %shard_map.96 = (bf16[256,256]{1,0:T(8,128)(2,1)S(1)}, bf16[256,256]{1,0:T(8,128)(2,1)S(1)}, bf16[256,256]{1,0:T(8,128)(2,1)S(1)}, bf16[256,256]{1,0:T(8,128)(2,...) custom-call(s32[2]{0:T(128)S(1)} %pad_add_fusion.place, ...), custom_call_target="tpu_custom_call" | custom-call | flops 1610612736 | bytes 11534336 | tf_op jit(solution)/shard_map/pallas_call | solution.py:218
  137.1 0.7 broadcast_in_dim.5
  137.8 1.2 collective-permute-start.9
  139.0 1.4 collective-permute-start.10
  140.4 3.1 %collective-permute-start.11 = (bf16[256,256]{1,0:T(8,128)(2,1)S(1)}, bf16[256,256]{1,0:T(8,128)(2,1)S(1)}, u32[]{:S(2)}, u32[]{:S(2)}) collective-permute-start(bf16[256,256]{1,0:T(8,128)(2,1)S(1)} %get-tuple-element.40), channel_id=1, source_target_pairs={{0,160},{32,192},{64,224},{96,0},{128,32},{160,64},{192,96},{224,1... | collective-permute-start | bytes 393224 | tf_op jit(solution)/shard_map/ppermute | solution.py:238
  143.5 1.4 collective-permute-start.12
  144.9 2.2 %collective-permute-start.13 = (bf16[256,256]{1,0:T(8,128)(2,1)S(1)}, bf16[256,256]{1,0:T(8,128)(2,1)S(1)}, u32[]{:S(2)}, u32[]{:S(2)}) collective-permute-start(bf16[256,256]{1,0:T(8,128)(2,1)S(1)} %get-tuple-element.42), channel_id=1, source_target_pairs={{0,192},{32,224},{64,0},{96,32},{128,64},{160,96},{192,128},{224,1... | collective-permute-start | bytes 393224 | tf_op jit(solution)/shard_map/ppermute | solution.py:238
  147.1 3.6 %collective-permute-done.9 = bf16[256,256]{1,0:T(8,128)(2,1)S(1)} collective-permute-done((bf16[256,256]{1,0:T(8,128)(2,1)S(1)}, bf16[256,256]{1,0:T(8,128)(2,1)S(1)}, u32[]{:S(2)}, u32[]{:S(2)}) %collective-permute-start.9) | collective-permute-done | bytes 131104 | tf_op jit(solution)/shard_map/ppermute | solution.py:238
  150.7 0.0 collective-permute-start.14
  150.7 7.2 %collective-permute-done.10 = bf16[256,256]{1,0:T(8,128)(2,1)S(1)} collective-permute-done((bf16[256,256]{1,0:T(8,128)(2,1)S(1)}, bf16[256,256]{1,0:T(8,128)(2,1)S(1)}, u32[]{:S(2)}, u32[]{:S(2)}) %collective-permute-start.10) | collective-permute-done | bytes 131104 | tf_op jit(solution)/shard_map/ppermute | solution.py:238
  157.9 0.0 collective-permute-start.15
  157.9 8.0 %all-to-all-start.3 = ((f32[32,8,256]{2,1,0:T(8,128)}), f32[32,8,256]{2,1,0:T(8,128)S(1)}, u32[]{:S(2)}, u32[]{:S(2)}) async-start(f32[32,8,256]{2,1,0:T(8,128)} %broadcast_in_dim.5), calls=%async_computation.3 | async-start | bytes 524288 | tf_op jit(solution)/shard_map/all_to_all | solution.py:235
  165.9 0.0 collective-permute-done.12
  165.9 0.0 collective-permute-done.13
  165.9 0.8 fusion
  166.7 8.1 %all-to-all-done.3 = f32[32,8,256]{2,1,0:T(8,128)S(1)} async-done(((f32[32,8,256]{2,1,0:T(8,128)}), f32[32,8,256]{2,1,0:T(8,128)S(1)}, u32[]{:S(2)}, u32[]{:S(2)}) %all-to-all-start.3) | async-done | bytes 262176 | tf_op jit(solution)/shard_map/all_to_all | solution.py:235
  174.8 0.7 copy.12
  (17 shorter events, 0.1 us)
Async XLA Ops:
  0.6 11.2 %collective-permute-start.6 = (bf16[2,128,256]{2,1,0:T(8,128)(2,1)}, bf16[2,128,256]{2,1,0:T(8,128)(2,1)S(1)}, u32[]{:S(2)}, u32[]{:S(2)}) collective-permute-start(bf16[2,128,256]{2,1,0:T(8,128)(2,1)} %bitcast.12), channel_id=1, source_target_pairs={{0,224},{32,0},{64,32},{96,64},{128,96},{160,128},{192,160},{224,1... | collective-permute-start | bytes 393224 | tf_op jit(solution)/shard_map/ppermute | solution.py:168
  7.1 5.6 %collective-permute-start.5 = (bf16[2,128,256]{2,1,0:T(8,128)(2,1)}, bf16[2,128,256]{2,1,0:T(8,128)(2,1)S(1)}, u32[]{:S(2)}, u32[]{:S(2)}) collective-permute-start(bf16[2,128,256]{2,1,0:T(8,128)(2,1)} %bitcast.13), channel_id=1, source_target_pairs={{0,32},{32,64},{64,96},{96,128},{128,160},{160,192},{192,224},{224... | collective-permute-start | bytes 393224 | tf_op jit(solution)/shard_map/ppermute | solution.py:168
  7.1 10.6 %collective-permute-start.4 = (bf16[2,128,256]{2,1,0:T(8,128)(2,1)}, bf16[2,128,256]{2,1,0:T(8,128)(2,1)S(1)}, u32[]{:S(2)}, u32[]{:S(2)}) collective-permute-start(bf16[2,128,256]{2,1,0:T(8,128)(2,1)} %bitcast.14), channel_id=1, source_target_pairs={{0,192},{32,224},{64,0},{96,32},{128,64},{160,96},{192,128},{224,1... | collective-permute-start | bytes 393224 | tf_op jit(solution)/shard_map/ppermute | solution.py:168
  9.0 8.7 %collective-permute-start.3 = (bf16[2,128,256]{2,1,0:T(8,128)(2,1)}, bf16[2,128,256]{2,1,0:T(8,128)(2,1)S(1)}, u32[]{:S(2)}, u32[]{:S(2)}) collective-permute-start(bf16[2,128,256]{2,1,0:T(8,128)(2,1)} %bitcast.15), channel_id=1, source_target_pairs={{0,64},{32,96},{64,128},{96,160},{128,192},{160,224},{192,0},{224,... | collective-permute-start | bytes 393224 | tf_op jit(solution)/shard_map/ppermute | solution.py:168
  9.5 8.2 %collective-permute-start.2 = (bf16[2,128,256]{2,1,0:T(8,128)(2,1)}, bf16[2,128,256]{2,1,0:T(8,128)(2,1)S(1)}, u32[]{:S(2)}, u32[]{:S(2)}) collective-permute-start(bf16[2,128,256]{2,1,0:T(8,128)(2,1)} %bitcast.16), channel_id=1, source_target_pairs={{0,160},{32,192},{64,224},{96,0},{128,32},{160,64},{192,96},{224,1... | collective-permute-start | bytes 393224 | tf_op jit(solution)/shard_map/ppermute | solution.py:168
  11.9 17.6 %collective-permute-start.1 = (bf16[2,128,256]{2,1,0:T(8,128)(2,1)}, bf16[2,128,256]{2,1,0:T(8,128)(2,1)S(1)}, u32[]{:S(2)}, u32[]{:S(2)}) collective-permute-start(bf16[2,128,256]{2,1,0:T(8,128)(2,1)} %bitcast.17), channel_id=1, source_target_pairs={{0,96},{32,128},{64,160},{96,192},{128,224},{160,0},{192,32},{224,... | collective-permute-start | bytes 393224 | tf_op jit(solution)/shard_map/ppermute | solution.py:168
  12.8 17.1 %collective-permute-start = (bf16[2,128,256]{2,1,0:T(8,128)(2,1)}, bf16[2,128,256]{2,1,0:T(8,128)(2,1)S(1)}, u32[]{:S(2)}, u32[]{:S(2)}) collective-permute-start(bf16[2,128,256]{2,1,0:T(8,128)(2,1)} %bitcast.18), channel_id=1, source_target_pairs={{0,128},{32,160},{64,192},{96,224},{128,0},{160,32},{192,64},{224,... | collective-permute-start | bytes 393224 | tf_op jit(solution)/shard_map/ppermute | solution.py:168
  29.9 0.9 copy-start
  30.8 0.7 copy-start.3
  31.5 0.7 copy-start.5
  40.4 5.9 %collective-permute-start.7 = (bf16[16,256,256]{2,1,0:T(8,128)(2,1)S(1)}, bf16[16,256,256]{2,1,0:T(8,128)(2,1)S(1)}, u32[]{:S(2)}, u32[]{:S(2)}) collective-permute-start(bf16[16,256,256]{2,1,0:T(8,128)(2,1)S(1)} %get-tuple-element.25), channel_id=1, source_target_pairs={{0,1},{1,0},{2,3},{3,2},{4,5},{5,4},{6,7},{7,6},{8,9},{9,8},{10,11... | collective-permute-start | bytes 6291464 | tf_op jit(solution)/shard_map/ppermute | solution.py:189
  46.9 32.1 %copy-start.1 = (bf16[256,256]{1,0:T(8,128)(2,1)S(1)}, bf16[256,256]{1,0:T(8,128)(2,1)}, u32[]{:S(2)}) copy-start(bf16[256,256]{1,0:T(8,128)(2,1)} %weight.1) | copy-start | bytes 393220
  46.9 32.1 %copy-start.2 = (bf16[256,256]{1,0:T(8,128)(2,1)S(1)}, bf16[256,256]{1,0:T(8,128)(2,1)}, u32[]{:S(2)}) copy-start(bf16[256,256]{1,0:T(8,128)(2,1)} %cotangent.1) | copy-start | bytes 393220
  80.1 47.9 %copy-start.4 = (s32[1,1,192]{2,1,0:T(1,128)S(1)}, s32[1,1,192]{2,1,0:T(1,128)}, u32[]{:S(2)}) copy-start(s32[1,1,192]{2,1,0:T(1,128)} %param.11) | copy-start | bytes 2308
  80.1 47.9 %copy-start.6 = (s32[1,1,192]{2,1,0:T(1,128)S(1)}, s32[1,1,192]{2,1,0:T(1,128)}, u32[]{:S(2)}) copy-start(s32[1,1,192]{2,1,0:T(1,128)} %param.12) | copy-start | bytes 2308
  111.8 6.6 %collective-permute-start.8 = (bf16[16,272,256]{2,1,0:T(8,128)(2,1)S(1)}, bf16[16,272,256]{2,1,0:T(8,128)(2,1)}, u32[]{:S(2)}, u32[]{:S(2)}) collective-permute-start(bf16[16,272,256]{2,1,0:T(8,128)(2,1)S(1)} %all_to_all.21.same), channel_id=1, source_target_pairs={{0,1},{1,0},{2,3},{3,2},{4,5},{5,4},{6,7},{7,6},{8,9},{9,8},{10,11... | collective-permute-start | bytes 6684680 | tf_op jit(solution)/shard_map/ppermute | solution.py:209
  120.0 17.1 %all-to-all-start.2 = ((f32[8,8,256]{2,1,0:T(8,128)}), f32[8,8,256]{2,1,0:T(8,128)S(1)}, u32[]{:S(2)}, u32[]{:S(2)}) async-start(f32[8,8,256]{2,1,0:T(8,128)} %broadcast_in_dim.4), calls=%async_computation.2 | async-start | bytes 131072 | tf_op jit(solution)/shard_map/all_to_all | solution.py:215
  137.8 12.8 %collective-permute-start.9 = (bf16[256,256]{1,0:T(8,128)(2,1)S(1)}, bf16[256,256]{1,0:T(8,128)(2,1)S(1)}, u32[]{:S(2)}, u32[]{:S(2)}) collective-permute-start(bf16[256,256]{1,0:T(8,128)(2,1)S(1)} %get-tuple-element.38), channel_id=1, source_target_pairs={{0,128},{32,160},{64,192},{96,224},{128,0},{160,32},{192,64},{224,... | collective-permute-start | bytes 393224 | tf_op jit(solution)/shard_map/ppermute | solution.py:238
  139.0 18.8 %collective-permute-start.10 = (bf16[256,256]{1,0:T(8,128)(2,1)S(1)}, bf16[256,256]{1,0:T(8,128)(2,1)S(1)}, u32[]{:S(2)}, u32[]{:S(2)}) collective-permute-start(bf16[256,256]{1,0:T(8,128)(2,1)S(1)} %get-tuple-element.39), channel_id=1, source_target_pairs={{0,96},{32,128},{64,160},{96,192},{128,224},{160,0},{192,32},{224,... | collective-permute-start | bytes 393224 | tf_op jit(solution)/shard_map/ppermute | solution.py:238
  140.4 25.5 %collective-permute-start.11 = (bf16[256,256]{1,0:T(8,128)(2,1)S(1)}, bf16[256,256]{1,0:T(8,128)(2,1)S(1)}, u32[]{:S(2)}, u32[]{:S(2)}) collective-permute-start(bf16[256,256]{1,0:T(8,128)(2,1)S(1)} %get-tuple-element.40), channel_id=1, source_target_pairs={{0,160},{32,192},{64,224},{96,0},{128,32},{160,64},{192,96},{224,1... | collective-permute-start | bytes 393224 | tf_op jit(solution)/shard_map/ppermute | solution.py:238
  143.5 22.4 %collective-permute-start.12 = (bf16[256,256]{1,0:T(8,128)(2,1)S(1)}, bf16[256,256]{1,0:T(8,128)(2,1)S(1)}, u32[]{:S(2)}, u32[]{:S(2)}) collective-permute-start(bf16[256,256]{1,0:T(8,128)(2,1)S(1)} %get-tuple-element.41), channel_id=1, source_target_pairs={{0,64},{32,96},{64,128},{96,160},{128,192},{160,224},{192,0},{224,... | collective-permute-start | bytes 393224 | tf_op jit(solution)/shard_map/ppermute | solution.py:238
  144.9 21.0 %collective-permute-start.13 = (bf16[256,256]{1,0:T(8,128)(2,1)S(1)}, bf16[256,256]{1,0:T(8,128)(2,1)S(1)}, u32[]{:S(2)}, u32[]{:S(2)}) collective-permute-start(bf16[256,256]{1,0:T(8,128)(2,1)S(1)} %get-tuple-element.42), channel_id=1, source_target_pairs={{0,192},{32,224},{64,0},{96,32},{128,64},{160,96},{192,128},{224,1... | collective-permute-start | bytes 393224 | tf_op jit(solution)/shard_map/ppermute | solution.py:238
  150.7 15.3 %collective-permute-start.14 = (bf16[256,256]{1,0:T(8,128)(2,1)S(1)}, bf16[256,256]{1,0:T(8,128)(2,1)S(1)}, u32[]{:S(2)}, u32[]{:S(2)}) collective-permute-start(bf16[256,256]{1,0:T(8,128)(2,1)S(1)} %get-tuple-element.43), channel_id=1, source_target_pairs={{0,32},{32,64},{64,96},{96,128},{128,160},{160,192},{192,224},{224... | collective-permute-start | bytes 393224 | tf_op jit(solution)/shard_map/ppermute | solution.py:238
  157.9 8.1 %collective-permute-start.15 = (bf16[256,256]{1,0:T(8,128)(2,1)S(1)}, bf16[256,256]{1,0:T(8,128)(2,1)S(1)}, u32[]{:S(2)}, u32[]{:S(2)}) collective-permute-start(bf16[256,256]{1,0:T(8,128)(2,1)S(1)} %get-tuple-element.44), channel_id=1, source_target_pairs={{0,224},{32,0},{64,32},{96,64},{128,96},{160,128},{192,160},{224,1... | collective-permute-start | bytes 393224 | tf_op jit(solution)/shard_map/ppermute | solution.py:238
  157.9 16.9 %all-to-all-start.3 = ((f32[32,8,256]{2,1,0:T(8,128)}), f32[32,8,256]{2,1,0:T(8,128)S(1)}, u32[]{:S(2)}, u32[]{:S(2)}) async-start(f32[32,8,256]{2,1,0:T(8,128)} %broadcast_in_dim.5), calls=%async_computation.3 | async-start | bytes 524288 | tf_op jit(solution)/shard_map/all_to_all | solution.py:235

commit v5 on v3

--- a/solution.py
+++ b/solution.py
@@ -13,6 +13,16 @@
 MIB = 1 << 20
 
 
+def start_lists(sources, targets, sems):
+    copies = [
+        pltpu.make_async_copy(source, target, sems.at[at])
+        for at, (source, target) in enumerate(zip(sources, targets))
+    ]
+    for copy in copies:
+        copy.start()
+    return copies
+
+
 def start_chunks(live, vals_hbm, vals, sems, chunk):
     for piece in range(vals.shape[0] // chunk):
 
@@ -39,13 +49,13 @@
     lax.fori_loop(0, (live + chunk - 1) // chunk, one_chunk, 0)
 
 
-def forward_kernel(chunk, steps, place, rows, cols, count, vals_hbm, *refs):
-    n_row = len(refs) - 7
+def forward_kernel(chunk, steps, place, count, rows_hbm, cols_hbm, vals_hbm, *refs):
+    n_row = len(refs) - 10
     pieces = refs[:n_row]
-    send, keep, vals, panel, total, val_sems, piece_sems = refs[n_row:]
+    send, keep, rows, cols, vals, panel, total, index_sems, val_sems, piece_sems = refs[n_row:]
     core, row, live = place[0], place[1], count[0]
     blocks_here = pieces[0].shape[0]
-    copies = []
+    copies = start_lists((rows_hbm, cols_hbm), (rows, cols), index_sems)
     for at, (step, piece) in enumerate(zip(steps, pieces)):
         owner = lax.rem(row + n_row - step, n_row)
         copies.append(
@@ -83,10 +93,10 @@
     lax.fori_loop(0, send.shape[0], split, 0)
 
 
-def backward_kernel(chunk, steps, place, rows, cols, count, vals_hbm, same, other, *refs):
+def backward_kernel(chunk, steps, place, count, rows_hbm, cols_hbm, vals_hbm, same, other, *refs):
     n_row = len(steps)
     outs = refs[:n_row]
-    vals, grads, total, val_sems, grad_sems = refs[n_row:]
+    rows, cols, vals, grads, total, index_sems, val_sems, grad_sems = refs[n_row:]
     core, row, live = place[0], place[1], count[0]
     side = total.shape[1]
     copies = [
@@ -95,6 +105,7 @@
     ]
     for copy in copies:
         copy.start()
+    copies += start_lists((rows_hbm, cols_hbm), (rows, cols), index_sems)
     start_chunks(live, vals_hbm, vals, val_sems, chunk)
     spare = total.shape[0] - 1
     for block in range(spare):
@@ -113,10 +124,25 @@
 
     each_live_slot(live, vals_hbm, vals, val_sems, chunk, one_slot)
     blocks_here = spare // n_row
+    nodes = blocks_here * side
+    terms = jnp.sum(grads[0, :, nodes:].astype(F32), axis=0) + jnp.sum(
+        grads[1, :, nodes:].astype(F32), axis=0
+    )
+    half = terms.shape[0] // 2
+    terms = jnp.where(core == 0, terms[:half], terms[half:])
+    high = terms.astype(BF16).astype(F32)
+    tail = jnp.concatenate([high, terms - high], axis=0).astype(BF16)
     for step, out in zip(steps, outs):
         owner = lax.rem(row + step, n_row)
         mine = total[pl.ds(owner * blocks_here, blocks_here)]
-        out[...] = mine.reshape(out.shape).astype(BF16)
+        out[:nodes] = mine.reshape(nodes, out.shape[1]).astype(BF16)
+        out[nodes:] = tail
+
+
+def copy_kernel(source, target, sem):
+    copy = pltpu.make_async_copy(source, target, sem)
+    copy.start()
+    copy.wait()
 
 
 def dense_kernel(parts, weight, cotangent, activated, grad_agg):
@@ -152,9 +178,10 @@
     here = nodes // side
     chips = n_col // 2
     chunk = slots // 6
-    values = pltpu.with_memory_space_constraint(blk_vals[0, 0], pltpu.HBM)
     place = jnp.stack([lax.axis_index("col") % 2, lax.axis_index("row")]).astype(jnp.int32)
-    scalars = (place, blk_rows[0, 0], blk_cols[0, 0], blk_count[0])
+    in_hbm = functools.partial(pltpu.with_memory_space_constraint, memory_space=pltpu.HBM)
+    scalars = (place, blk_count[0], in_hbm(blk_rows[0, 0]), in_hbm(blk_cols[0, 0]))
+    values = in_hbm(blk_vals[0, 0])
     smem = pl.BlockSpec(memory_space=pltpu.SMEM)
     vmem = pl.BlockSpec(memory_space=pltpu.VMEM)
     near = pl.BlockSpec(memory_space=pl.ANY)
@@ -163,7 +190,14 @@
     same_core = [list(range(core, n_col, 2)) for core in range(2)]
     work = 2 * slots * side * side * width
 
-    own = features.reshape(here, side, width)
+    own = pl.pallas_call(
+        copy_kernel,
+        out_shape=jax.ShapeDtypeStruct((here, side, width), BF16),
+        in_specs=[hbm],
+        out_specs=vmem,
+        scratch_shapes=[pltpu.SemaphoreType.DMA],
+        compiler_params=pltpu.CompilerParams(vmem_limit_bytes=4 * MIB),
+    )(in_hbm(features.reshape(here, side, width)))
     steps = [0] + sorted(range(1, n_row), key=lambda k: (-min(k, n_row - k), k))
     pieces = [own] + [lax.ppermute(own, "row", turn(n_row, k)) for k in steps[1:]]
 
@@ -173,12 +207,15 @@
             jax.ShapeDtypeStruct((chips, nodes, width), BF16),
             jax.ShapeDtypeStruct((chips, nodes, width), F32),
         ),
-        in_specs=[smem] * 4 + [hbm] + [near] * n_row,
+        in_specs=[smem] * 2 + [hbm] * 3 + [near] * n_row,
         out_specs=(vmem, vmem),
         scratch_shapes=[
+            pltpu.SMEM((slots,), jnp.int32),
+            pltpu.SMEM((slots,), jnp.int32),
             pltpu.VMEM((slots, side, side), BF16),
             pltpu.VMEM((here * n_row, side, width), BF16),
             pltpu.VMEM((here * n_col + 1, side, width), F32),
+            pltpu.SemaphoreType.DMA((2,)),
             pltpu.SemaphoreType.DMA((slots // chunk,)),
             pltpu.SemaphoreType.DMA((n_row,)),
         ],
@@ -208,23 +245,18 @@
     same = lax.all_to_all(grad_agg, "col", 0, 0, tiled=True, axis_index_groups=same_core)
     other = lax.ppermute(same, "col", swap)
 
-    terms = jnp.sum(same[:, nodes:].astype(F32), axis=0) + jnp.sum(other[:, nodes:].astype(F32), axis=0)
-    rows_core = strip // 2
-    half_strip = lax.dynamic_slice_in_dim(terms, place[0] * rows_core, rows_core, 0)
-    copies = jnp.broadcast_to(half_strip[None], (n_row, rows_core, width))
-    strips = lax.all_to_all(copies, "row", 0, 0, tiled=True)
-    copies = jnp.broadcast_to(jnp.sum(strips, axis=0)[None], (n_col, rows_core, width))
-    grad_weight = lax.all_to_all(copies, "col", 0, 0, tiled=True).reshape(width, width)
-
     shares = pl.pallas_call(
         functools.partial(backward_kernel, chunk, steps),
-        out_shape=(jax.ShapeDtypeStruct((nodes, width), BF16),) * n_row,
-        in_specs=[smem] * 4 + [hbm] + [near] * 2,
+        out_shape=(jax.ShapeDtypeStruct((nodes + strip, width), BF16),) * n_row,
+        in_specs=[smem] * 2 + [hbm] * 3 + [near] * 2,
         out_specs=(vmem,) * n_row,
         scratch_shapes=[
+            pltpu.SMEM((slots,), jnp.int32),
+            pltpu.SMEM((slots,), jnp.int32),
             pltpu.VMEM((slots, side, side), BF16),
             pltpu.VMEM((2, chips, nodes + strip, width), BF16),
             pltpu.VMEM((here * n_row + 1, side, width), F32),
+            pltpu.SemaphoreType.DMA((2,)),
             pltpu.SemaphoreType.DMA((slots // chunk,)),
             pltpu.SemaphoreType.DMA((2,)),
         ],
@@ -235,7 +267,10 @@
     total = shares[0].astype(F32)
     for step, share in zip(steps[1:], shares[1:]):
         total += lax.ppermute(share, "row", turn(n_row, step)).astype(F32)
-    grad_features = total.astype(BF16).reshape(1, nodes, width)
+    grad_features = total[:nodes].astype(BF16).reshape(1, nodes, width)
+    high, low = total[nodes : nodes + strip // 2], total[nodes + strip // 2 :]
+    copies = jnp.broadcast_to((high + low)[None], (n_col, strip // 2, width))
+    grad_weight = lax.all_to_all(copies, "col", 0, 0, tiled=True).reshape(width, width)
     return (activated, grad_weight, grad_features)
 
 

time: 177 us -> 169 us (0.955)
  blocking collectives: 76.7 us -> 63.5 us
  waiting for transfers between devices: 34.1 us -> 44.8 us
    all_to_all x1 -> x0, blocking collectives: 12.9 us -> none  [per_device(): strips = lax.all_to_all(copies, 'row', 0, 0, tiled=True)]
    ppermute x7, waiting for transfers between devices: 5.31 us -> 16.1 us  [per_device(): total += lax.ppermute(share, 'row', turn(n_row, step)).astype(F32)]
    all_to_all x1, starting transfers between devices: 7.64 us -> 4.13 us  [per_device(): lax.all_to_all(copies, 'col', 0, 0, tiled=True).reshape(width, width)]
    unnamed x15 -> x5, local copies, waits for them, and re-layouts: 2.98 us -> 0.72 us
  transfers between devices with their start and end apart: 17 -> 17, of which waited for: 7 -> 9; matrix products, arithmetic and copies ran while one was open for 1% -> 0% of each run, Pallas kernels for 0% -> 0%
where the time goes in v5:
time: 169 us
  blocking collectives  63.5 us (38%)
  waiting for transfers between devices  44.8 us (27%)
  starting transfers between devices  38.2 us (23%)
  Pallas kernels  17.6 us (10%)
  local copies, waits for them, and re-layouts  2.11 us (1%)
    all_to_all x1, blocking collectives, per_device(): lax.all_to_all(shares, 'col', 0, 0, tiled=True, axis_index_groups=same_core)  31.9 us
    all_to_all x1, blocking collectives, per_device(): lax.all_to_all(grad_agg, 'col', 0, 0, tiled=True, axis_index_groups=same_...  31.6 us
    ppermute x7, waiting for transfers between devices, per_device(): total += lax.ppermute(share, 'row', turn(n_row, step)).astype(F32)  16.1 us
    ppermute x7, starting transfers between devices, per_device(): lax.ppermute(own, 'row', turn(n_row, k))  15.7 us
    ppermute x7, starting transfers between devices, per_device(): total += lax.ppermute(share, 'row', turn(n_row, step)).astype(F32)  13.7 us
    ppermute x7, waiting for transfers between devices, per_device(): lax.ppermute(own, 'row', turn(n_row, k))  12.7 us
    all_to_all x1, waiting for transfers between devices, per_device(): lax.all_to_all(copies, 'col', 0, 0, tiled=True).reshape(width, width)  8.23 us
    pallas_call x1, Pallas kernels, per_device(): pl.pallas_call(functools.partial(forward_kernel, chunk, steps), out_shape...  8.22 us
  transfers between devices with their start and end apart: 17, of which 9 were waited for; matrix products, arithmetic and copies ran while one was open for 0% of the time, Pallas kernels for 0%

profile of v5, /device:TPU:1, one launch (start us, length us, event | category | flops | bytes accessed | tf_op | source)
XLA Modules:
  0.0 168.5 jit_solution(9022296349984282499)
XLA Ops:
  0.6 0.9 shard_map.94.refs_0_
  1.6 6.5 %collective-permute-start.6 = (bf16[2,128,256]{2,1,0:T(8,128)(2,1)S(1)}, bf16[2,128,256]{2,1,0:T(8,128)(2,1)S(1)}, u32[]{:S(2)}, u32[]{:S(2)}) collective-permute-start(bf16[2,128,256]{2,1,0:T(8,128)(2,1)S(1)} %shard_map.94.refs_0_), channel_id=1, source_target_pairs={{0,224},{32,0},{64,32},{96,64},{128,96},{160,128},{192,160},{224,1... | collective-permute-start | bytes 393224 | tf_op jit(solution)/shard_map/ppermute | solution.py:202
  8.0 0.0 collective-permute-start.5
  8.0 1.9 %collective-permute-start.4 = (bf16[2,128,256]{2,1,0:T(8,128)(2,1)S(1)}, bf16[2,128,256]{2,1,0:T(8,128)(2,1)S(1)}, u32[]{:S(2)}, u32[]{:S(2)}) collective-permute-start(bf16[2,128,256]{2,1,0:T(8,128)(2,1)S(1)} %shard_map.94.refs_0_), channel_id=1, source_target_pairs={{0,192},{32,224},{64,0},{96,32},{128,64},{160,96},{192,128},{224,1... | collective-permute-start | bytes 393224 | tf_op jit(solution)/shard_map/ppermute | solution.py:202
  9.9 0.5 collective-permute-start.3
  10.4 2.4 %collective-permute-start.2 = (bf16[2,128,256]{2,1,0:T(8,128)(2,1)S(1)}, bf16[2,128,256]{2,1,0:T(8,128)(2,1)S(1)}, u32[]{:S(2)}, u32[]{:S(2)}) collective-permute-start(bf16[2,128,256]{2,1,0:T(8,128)(2,1)S(1)} %shard_map.94.refs_0_), channel_id=1, source_target_pairs={{0,160},{32,192},{64,224},{96,0},{128,32},{160,64},{192,96},{224,1... | collective-permute-start | bytes 393224 | tf_op jit(solution)/shard_map/ppermute | solution.py:202
  12.8 0.0 collective-permute-done.6.refs_7_
  12.8 0.9 collective-permute-start.1
  13.7 0.0 collective-permute-done.5.refs_6_
  13.7 3.6 %collective-permute-start = (bf16[2,128,256]{2,1,0:T(8,128)(2,1)S(1)}, bf16[2,128,256]{2,1,0:T(8,128)(2,1)S(1)}, u32[]{:S(2)}, u32[]{:S(2)}) collective-permute-start(bf16[2,128,256]{2,1,0:T(8,128)(2,1)S(1)} %shard_map.94.refs_0_), channel_id=1, source_target_pairs={{0,128},{32,160},{64,192},{96,224},{128,0},{160,32},{192,64},{224,... | collective-permute-start | bytes 393224 | tf_op jit(solution)/shard_map/ppermute | solution.py:202
  17.9 0.1 pad_add_fusion.place
  18.0 0.4 collective-permute-done.4.refs_5_
  18.4 0.0 collective-permute-done.3.refs_4_
  18.4 0.0 collective-permute-done.2.refs_3_
  18.4 11.8 %collective-permute-done.1.refs_2_ = bf16[2,128,256]{2,1,0:T(8,128)(2,1)S(1)} collective-permute-done((bf16[2,128,256]{2,1,0:T(8,128)(2,1)S(1)}, bf16[2,128,256]{2,1,0:T(8,128)(2,1)S(1)}, u32[]{:S(2)}, u32[]{:S(2)}) %collective-permute-start.1) | collective-permute-done | bytes 131104 | tf_op jit(solution)/shard_map/ppermute | solution.py:202
  30.2 0.5 collective-permute-done.refs_1_
  30.7 8.2 %shard_map.95 = (bf16[16,256,256]{2,1,0:T(8,128)(2,1)S(1)}, f32[16,256,256]{2,1,0:T(8,128)S(1)}) custom-call(s32[2]{0:T(128)S(1)} %pad_add_fusion.place, s32[1]{0:T(128)} %bitcast.10.count, s32[192]{0:T(256)} %bitcast.16, s32[192]{0:T(256)} %bitcast.18, bf16[192,128,128]{2,1,0:T(8,128)(2,1)} %bitcast.12, bf16[2,128,256]{2,1,0:T(8,128)(2,1)S(1)} %shard_map.94.refs_0_, ...), custom_call_target="tpu_custom_call" | custom-call | flops 1610612736 | bytes 14680064 | tf_op jit(solution)/shard_map/pallas_call | solution.py:204
  38.9 2.1 %collective-permute-start.7 = (bf16[16,256,256]{2,1,0:T(8,128)(2,1)S(1)}, bf16[16,256,256]{2,1,0:T(8,128)(2,1)S(1)}, u32[]{:S(2)}, u32[]{:S(2)}) collective-permute-start(bf16[16,256,256]{2,1,0:T(8,128)(2,1)S(1)} %get-tuple-element.16), channel_id=1, source_target_pairs={{0,1},{1,0},{2,3},{3,2},{4,5},{5,4},{6,7},{7,6},{8,9},{9,8},{10,11... | collective-permute-start | bytes 6291464 | tf_op jit(solution)/shard_map/ppermute | solution.py:226
  41.0 3.8 %collective-permute-done.7 = bf16[16,256,256]{2,1,0:T(8,128)(2,1)S(1)} collective-permute-done((bf16[16,256,256]{2,1,0:T(8,128)(2,1)S(1)}, bf16[16,256,256]{2,1,0:T(8,128)(2,1)S(1)}, u32[]{:S(2)}, u32[]{:S(2)}) %collective-permute-start.7) | collective-permute-done | bytes 2097184 | tf_op jit(solution)/shard_map/ppermute | solution.py:226
  44.8 0.8 add_convert_fusion
  45.6 0.0 copy-start
  45.6 0.0 copy-start.1
  45.6 31.9 %all_to_all.15.parts = bf16[16,256,256]{2,1,0:T(8,128)(2,1)S(1)} all-to-all(bf16[16,256,256]{2,1,0:T(8,128)(2,1)S(1)} %add_convert_fusion), channel_id=1, replica_groups={{0,2,4,6,8,10,12,14,16,18,20,22,24,26,28,30},{1,3,5,7,9,11,13,15,17,19,..., dimensions={0} | all-to-all | bytes 4194304 | tf_op jit(solution)/shard_map/all_to_all | solution.py:228
  77.5 1.1 shard_map.96
  78.5 31.6 %all_to_all.16.same = bf16[16,272,256]{2,1,0:T(8,128)(2,1)S(1)} all-to-all(bf16[16,272,256]{2,1,0:T(8,128)(2,1)S(1)} %get-tuple-element.18), channel_id=1, replica_groups={{0,2,4,6,8,10,12,14,16,18,20,22,24,26,28,30},{1,3,5,7,9,11,13,15,17,19,..., dimensions={0} | all-to-all | bytes 4456448 | tf_op jit(solution)/shard_map/all_to_all | solution.py:245
  110.1 2.5 %collective-permute-start.8 = (bf16[16,272,256]{2,1,0:T(8,128)(2,1)S(1)}, bf16[16,272,256]{2,1,0:T(8,128)(2,1)S(1)}, u32[]{:S(2)}, u32[]{:S(2)}) collective-permute-start(bf16[16,272,256]{2,1,0:T(8,128)(2,1)S(1)} %all_to_all.16.same), channel_id=1, source_target_pairs={{0,1},{1,0},{2,3},{3,2},{4,5},{5,4},{6,7},{7,6},{8,9},{9,8},{10,11... | collective-permute-start | bytes 6684680 | tf_op jit(solution)/shard_map/ppermute | solution.py:246
  112.7 4.0 %collective-permute-done.8.other = bf16[16,272,256]{2,1,0:T(8,128)(2,1)S(1)} collective-permute-done((bf16[16,272,256]{2,1,0:T(8,128)(2,1)S(1)}, bf16[16,272,256]{2,1,0:T(8,128)(2,1)S(1)}, u32[]{:S(2)}, u32[]{:S(2)}) %collective-permute-start.8) | collective-permute-done | bytes 2228256 | tf_op jit(solution)/shard_map/ppermute | solution.py:246
  116.6 7.4 %shard_map.97 = (bf16[272,256]{1,0:T(8,128)(2,1)S(1)}, bf16[272,256]{1,0:T(8,128)(2,1)S(1)}, bf16[272,256]{1,0:T(8,128)(2,1)S(1)}, bf16[272,256]{1,0:T(8,128)(2,...) custom-call(s32[2]{0:T(128)S(1)} %pad_add_fusion.place, ...), custom_call_target="tpu_custom_call" | custom-call | flops 1610612736 | bytes 11534336 | tf_op jit(solution)/shard_map/pallas_call | solution.py:248
  124.1 0.5 collective-permute-start.9
  124.6 1.2 collective-permute-start.10
  125.8 3.3 %collective-permute-start.11 = (bf16[272,256]{1,0:T(8,128)(2,1)S(1)}, bf16[272,256]{1,0:T(8,128)(2,1)S(1)}, u32[]{:S(2)}, u32[]{:S(2)}) collective-permute-start(bf16[272,256]{1,0:T(8,128)(2,1)S(1)} %get-tuple-element.22), channel_id=1, source_target_pairs={{0,160},{32,192},{64,224},{96,0},{128,32},{160,64},{192,96},{224,1... | collective-permute-start | bytes 417800 | tf_op jit(solution)/shard_map/ppermute | solution.py:269
  129.1 4.4 %collective-permute-start.12 = (bf16[272,256]{1,0:T(8,128)(2,1)S(1)}, bf16[272,256]{1,0:T(8,128)(2,1)S(1)}, u32[]{:S(2)}, u32[]{:S(2)}) collective-permute-start(bf16[272,256]{1,0:T(8,128)(2,1)S(1)} %get-tuple-element.23), channel_id=1, source_target_pairs={{0,64},{32,96},{64,128},{96,160},{128,192},{160,224},{192,0},{224,... | collective-permute-start | bytes 417800 | tf_op jit(solution)/shard_map/ppermute | solution.py:269
  133.5 0.0 collective-permute-start.13
  133.5 0.0 collective-permute-done.9
  133.5 4.2 %collective-permute-start.14 = (bf16[272,256]{1,0:T(8,128)(2,1)S(1)}, bf16[272,256]{1,0:T(8,128)(2,1)S(1)}, u32[]{:S(2)}, u32[]{:S(2)}) collective-permute-start(bf16[272,256]{1,0:T(8,128)(2,1)S(1)} %get-tuple-element.25), channel_id=1, source_target_pairs={{0,32},{32,64},{64,96},{96,128},{128,160},{160,192},{192,224},{224... | collective-permute-start | bytes 417800 | tf_op jit(solution)/shard_map/ppermute | solution.py:269
  137.7 6.4 %collective-permute-done.10 = bf16[272,256]{1,0:T(8,128)(2,1)S(1)} collective-permute-done((bf16[272,256]{1,0:T(8,128)(2,1)S(1)}, bf16[272,256]{1,0:T(8,128)(2,1)S(1)}, u32[]{:S(2)}, u32[]{:S(2)}) %collective-permute-start.10) | collective-permute-done | bytes 139296 | tf_op jit(solution)/shard_map/ppermute | solution.py:269
  144.1 0.0 collective-permute-start.15
  144.1 0.0 collective-permute-done.11
  144.1 4.8 %collective-permute-done.12 = bf16[272,256]{1,0:T(8,128)(2,1)S(1)} collective-permute-done((bf16[272,256]{1,0:T(8,128)(2,1)S(1)}, bf16[272,256]{1,0:T(8,128)(2,1)S(1)}, u32[]{:S(2)}, u32[]{:S(2)}) %collective-permute-start.12) | collective-permute-done | bytes 139296 | tf_op jit(solution)/shard_map/ppermute | solution.py:269
  148.9 0.0 collective-permute-done.13
  148.9 5.0 %collective-permute-done.14 = bf16[272,256]{1,0:T(8,128)(2,1)S(1)} collective-permute-done((bf16[272,256]{1,0:T(8,128)(2,1)S(1)}, bf16[272,256]{1,0:T(8,128)(2,1)S(1)}, u32[]{:S(2)}, u32[]{:S(2)}) %collective-permute-start.14) | collective-permute-done | bytes 139296 | tf_op jit(solution)/shard_map/ppermute | solution.py:269
  153.9 0.0 collective-permute-done.15
  153.9 0.1 convert_add_fusion
  154.1 0.7 broadcast_in_dim.2
  154.8 4.1 %all-to-all-start.2 = ((f32[32,8,256]{2,1,0:T(8,128)}), f32[32,8,256]{2,1,0:T(8,128)S(1)}, u32[]{:S(2)}, u32[]{:S(2)}) async-start(f32[32,8,256]{2,1,0:T(8,128)} %broadcast_in_dim.2), calls=%async_computation.2 | async-start | bytes 524288 | tf_op jit(solution)/shard_map/all_to_all | solution.py:273
  158.9 0.7 fusion
  159.6 8.2 %all-to-all-done.2 = f32[32,8,256]{2,1,0:T(8,128)S(1)} async-done(((f32[32,8,256]{2,1,0:T(8,128)}), f32[32,8,256]{2,1,0:T(8,128)S(1)}, u32[]{:S(2)}, u32[]{:S(2)}) %all-to-all-start.2) | async-done | bytes 262176 | tf_op jit(solution)/shard_map/all_to_all | solution.py:273
  167.8 0.7 copy.12
  (3 shorter events, 0.0 us)
Async XLA Ops:
  1.6 11.2 %collective-permute-start.6 = (bf16[2,128,256]{2,1,0:T(8,128)(2,1)S(1)}, bf16[2,128,256]{2,1,0:T(8,128)(2,1)S(1)}, u32[]{:S(2)}, u32[]{:S(2)}) collective-permute-start(bf16[2,128,256]{2,1,0:T(8,128)(2,1)S(1)} %shard_map.94.refs_0_), channel_id=1, source_target_pairs={{0,224},{32,0},{64,32},{96,64},{128,96},{160,128},{192,160},{224,1... | collective-permute-start | bytes 393224 | tf_op jit(solution)/shard_map/ppermute | solution.py:202
  8.0 5.6 %collective-permute-start.5 = (bf16[2,128,256]{2,1,0:T(8,128)(2,1)S(1)}, bf16[2,128,256]{2,1,0:T(8,128)(2,1)S(1)}, u32[]{:S(2)}, u32[]{:S(2)}) collective-permute-start(bf16[2,128,256]{2,1,0:T(8,128)(2,1)S(1)} %shard_map.94.refs_0_), channel_id=1, source_target_pairs={{0,32},{32,64},{64,96},{96,128},{128,160},{160,192},{192,224},{224... | collective-permute-start | bytes 393224 | tf_op jit(solution)/shard_map/ppermute | solution.py:202
  8.0 10.4 %collective-permute-start.4 = (bf16[2,128,256]{2,1,0:T(8,128)(2,1)S(1)}, bf16[2,128,256]{2,1,0:T(8,128)(2,1)S(1)}, u32[]{:S(2)}, u32[]{:S(2)}) collective-permute-start(bf16[2,128,256]{2,1,0:T(8,128)(2,1)S(1)} %shard_map.94.refs_0_), channel_id=1, source_target_pairs={{0,192},{32,224},{64,0},{96,32},{128,64},{160,96},{192,128},{224,1... | collective-permute-start | bytes 393224 | tf_op jit(solution)/shard_map/ppermute | solution.py:202
  9.9 8.4 %collective-permute-start.3 = (bf16[2,128,256]{2,1,0:T(8,128)(2,1)S(1)}, bf16[2,128,256]{2,1,0:T(8,128)(2,1)S(1)}, u32[]{:S(2)}, u32[]{:S(2)}) collective-permute-start(bf16[2,128,256]{2,1,0:T(8,128)(2,1)S(1)} %shard_map.94.refs_0_), channel_id=1, source_target_pairs={{0,64},{32,96},{64,128},{96,160},{128,192},{160,224},{192,0},{224,... | collective-permute-start | bytes 393224 | tf_op jit(solution)/shard_map/ppermute | solution.py:202
  10.4 8.0 %collective-permute-start.2 = (bf16[2,128,256]{2,1,0:T(8,128)(2,1)S(1)}, bf16[2,128,256]{2,1,0:T(8,128)(2,1)S(1)}, u32[]{:S(2)}, u32[]{:S(2)}) collective-permute-start(bf16[2,128,256]{2,1,0:T(8,128)(2,1)S(1)} %shard_map.94.refs_0_), channel_id=1, source_target_pairs={{0,160},{32,192},{64,224},{96,0},{128,32},{160,64},{192,96},{224,1... | collective-permute-start | bytes 393224 | tf_op jit(solution)/shard_map/ppermute | solution.py:202
  12.8 17.4 %collective-permute-start.1 = (bf16[2,128,256]{2,1,0:T(8,128)(2,1)S(1)}, bf16[2,128,256]{2,1,0:T(8,128)(2,1)S(1)}, u32[]{:S(2)}, u32[]{:S(2)}) collective-permute-start(bf16[2,128,256]{2,1,0:T(8,128)(2,1)S(1)} %shard_map.94.refs_0_), channel_id=1, source_target_pairs={{0,96},{32,128},{64,160},{96,192},{128,224},{160,0},{192,32},{224,... | collective-permute-start | bytes 393224 | tf_op jit(solution)/shard_map/ppermute | solution.py:202
  13.7 17.0 %collective-permute-start = (bf16[2,128,256]{2,1,0:T(8,128)(2,1)S(1)}, bf16[2,128,256]{2,1,0:T(8,128)(2,1)S(1)}, u32[]{:S(2)}, u32[]{:S(2)}) collective-permute-start(bf16[2,128,256]{2,1,0:T(8,128)(2,1)S(1)} %shard_map.94.refs_0_), channel_id=1, source_target_pairs={{0,128},{32,160},{64,192},{96,224},{128,0},{160,32},{192,64},{224,... | collective-permute-start | bytes 393224 | tf_op jit(solution)/shard_map/ppermute | solution.py:202
  38.9 5.9 %collective-permute-start.7 = (bf16[16,256,256]{2,1,0:T(8,128)(2,1)S(1)}, bf16[16,256,256]{2,1,0:T(8,128)(2,1)S(1)}, u32[]{:S(2)}, u32[]{:S(2)}) collective-permute-start(bf16[16,256,256]{2,1,0:T(8,128)(2,1)S(1)} %get-tuple-element.16), channel_id=1, source_target_pairs={{0,1},{1,0},{2,3},{3,2},{4,5},{5,4},{6,7},{7,6},{8,9},{9,8},{10,11... | collective-permute-start | bytes 6291464 | tf_op jit(solution)/shard_map/ppermute | solution.py:226
  45.6 31.9 %copy-start = (bf16[256,256]{1,0:T(8,128)(2,1)S(1)}, bf16[256,256]{1,0:T(8,128)(2,1)}, u32[]{:S(2)}) copy-start(bf16[256,256]{1,0:T(8,128)(2,1)} %weight.1) | copy-start | bytes 393220
  45.6 31.9 %copy-start.1 = (bf16[256,256]{1,0:T(8,128)(2,1)S(1)}, bf16[256,256]{1,0:T(8,128)(2,1)}, u32[]{:S(2)}) copy-start(bf16[256,256]{1,0:T(8,128)(2,1)} %cotangent.1) | copy-start | bytes 393220
  110.1 6.5 %collective-permute-start.8 = (bf16[16,272,256]{2,1,0:T(8,128)(2,1)S(1)}, bf16[16,272,256]{2,1,0:T(8,128)(2,1)S(1)}, u32[]{:S(2)}, u32[]{:S(2)}) collective-permute-start(bf16[16,272,256]{2,1,0:T(8,128)(2,1)S(1)} %all_to_all.16.same), channel_id=1, source_target_pairs={{0,1},{1,0},{2,3},{3,2},{4,5},{5,4},{6,7},{7,6},{8,9},{9,8},{10,11... | collective-permute-start | bytes 6684680 | tf_op jit(solution)/shard_map/ppermute | solution.py:246
  124.1 9.5 %collective-permute-start.9 = (bf16[272,256]{1,0:T(8,128)(2,1)S(1)}, bf16[272,256]{1,0:T(8,128)(2,1)S(1)}, u32[]{:S(2)}, u32[]{:S(2)}) collective-permute-start(bf16[272,256]{1,0:T(8,128)(2,1)S(1)} %get-tuple-element.20), channel_id=1, source_target_pairs={{0,128},{32,160},{64,192},{96,224},{128,0},{160,32},{192,64},{224,... | collective-permute-start | bytes 417800 | tf_op jit(solution)/shard_map/ppermute | solution.py:269
  124.6 19.5 %collective-permute-start.10 = (bf16[272,256]{1,0:T(8,128)(2,1)S(1)}, bf16[272,256]{1,0:T(8,128)(2,1)S(1)}, u32[]{:S(2)}, u32[]{:S(2)}) collective-permute-start(bf16[272,256]{1,0:T(8,128)(2,1)S(1)} %get-tuple-element.21), channel_id=1, source_target_pairs={{0,96},{32,128},{64,160},{96,192},{128,224},{160,0},{192,32},{224,... | collective-permute-start | bytes 417800 | tf_op jit(solution)/shard_map/ppermute | solution.py:269
  125.8 18.4 %collective-permute-start.11 = (bf16[272,256]{1,0:T(8,128)(2,1)S(1)}, bf16[272,256]{1,0:T(8,128)(2,1)S(1)}, u32[]{:S(2)}, u32[]{:S(2)}) collective-permute-start(bf16[272,256]{1,0:T(8,128)(2,1)S(1)} %get-tuple-element.22), channel_id=1, source_target_pairs={{0,160},{32,192},{64,224},{96,0},{128,32},{160,64},{192,96},{224,1... | collective-permute-start | bytes 417800 | tf_op jit(solution)/shard_map/ppermute | solution.py:269
  129.1 19.8 %collective-permute-start.12 = (bf16[272,256]{1,0:T(8,128)(2,1)S(1)}, bf16[272,256]{1,0:T(8,128)(2,1)S(1)}, u32[]{:S(2)}, u32[]{:S(2)}) collective-permute-start(bf16[272,256]{1,0:T(8,128)(2,1)S(1)} %get-tuple-element.23), channel_id=1, source_target_pairs={{0,64},{32,96},{64,128},{96,160},{128,192},{160,224},{192,0},{224,... | collective-permute-start | bytes 417800 | tf_op jit(solution)/shard_map/ppermute | solution.py:269
  133.5 15.4 %collective-permute-start.13 = (bf16[272,256]{1,0:T(8,128)(2,1)S(1)}, bf16[272,256]{1,0:T(8,128)(2,1)S(1)}, u32[]{:S(2)}, u32[]{:S(2)}) collective-permute-start(bf16[272,256]{1,0:T(8,128)(2,1)S(1)} %get-tuple-element.24), channel_id=1, source_target_pairs={{0,192},{32,224},{64,0},{96,32},{128,64},{160,96},{192,128},{224,1... | collective-permute-start | bytes 417800 | tf_op jit(solution)/shard_map/ppermute | solution.py:269
  133.5 20.4 %collective-permute-start.14 = (bf16[272,256]{1,0:T(8,128)(2,1)S(1)}, bf16[272,256]{1,0:T(8,128)(2,1)S(1)}, u32[]{:S(2)}, u32[]{:S(2)}) collective-permute-start(bf16[272,256]{1,0:T(8,128)(2,1)S(1)} %get-tuple-element.25), channel_id=1, source_target_pairs={{0,32},{32,64},{64,96},{96,128},{128,160},{160,192},{192,224},{224... | collective-permute-start | bytes 417800 | tf_op jit(solution)/shard_map/ppermute | solution.py:269
  144.1 9.8 %collective-permute-start.15 = (bf16[272,256]{1,0:T(8,128)(2,1)S(1)}, bf16[272,256]{1,0:T(8,128)(2,1)S(1)}, u32[]{:S(2)}, u32[]{:S(2)}) collective-permute-start(bf16[272,256]{1,0:T(8,128)(2,1)S(1)} %get-tuple-element.26), channel_id=1, source_target_pairs={{0,224},{32,0},{64,32},{96,64},{128,96},{160,128},{192,160},{224,1... | collective-permute-start | bytes 417800 | tf_op jit(solution)/shard_map/ppermute | solution.py:269
  154.8 13.0 %all-to-all-start.2 = ((f32[32,8,256]{2,1,0:T(8,128)}), f32[32,8,256]{2,1,0:T(8,128)S(1)}, u32[]{:S(2)}, u32[]{:S(2)}) async-start(f32[32,8,256]{2,1,0:T(8,128)} %broadcast_in_dim.2), calls=%async_computation.2 | async-start | bytes 524288 | tf_op jit(solution)/shard_map/all_to_all | solution.py:273

commit v6 on v5

--- a/solution.py
+++ b/solution.py
@@ -124,19 +124,10 @@
 
     each_live_slot(live, vals_hbm, vals, val_sems, chunk, one_slot)
     blocks_here = spare // n_row
-    nodes = blocks_here * side
-    terms = jnp.sum(grads[0, :, nodes:].astype(F32), axis=0) + jnp.sum(
-        grads[1, :, nodes:].astype(F32), axis=0
-    )
-    half = terms.shape[0] // 2
-    terms = jnp.where(core == 0, terms[:half], terms[half:])
-    high = terms.astype(BF16).astype(F32)
-    tail = jnp.concatenate([high, terms - high], axis=0).astype(BF16)
     for step, out in zip(steps, outs):
         owner = lax.rem(row + step, n_row)
         mine = total[pl.ds(owner * blocks_here, blocks_here)]
-        out[:nodes] = mine.reshape(nodes, out.shape[1]).astype(BF16)
-        out[nodes:] = tail
+        out[...] = mine.reshape(out.shape).astype(BF16)
 
 
 def copy_kernel(source, target, sem):
@@ -171,6 +162,15 @@
     return [(i, (i + step) % size) for i in range(size)]
 
 
+def add_partners(value, size, distances):
+    for other in [
+        lax.ppermute(value, "row", [(i, i ^ distance) for i in range(size)])
+        for distance in distances
+    ]:
+        value = value + other
+    return value
+
+
 def per_device(features, weight, cotangent, blk_vals, blk_rows, blk_cols, blk_count):
     n_row, n_col = lax.axis_size("row"), lax.axis_size("col")
     nodes, width = cotangent.shape
@@ -198,7 +198,7 @@
         scratch_shapes=[pltpu.SemaphoreType.DMA],
         compiler_params=pltpu.CompilerParams(vmem_limit_bytes=4 * MIB),
     )(in_hbm(features.reshape(here, side, width)))
-    steps = [0] + sorted(range(1, n_row), key=lambda k: (-min(k, n_row - k), k))
+    steps = [0] + sorted(range(1, n_row), key=lambda k: (min(k, n_row - k), k))
     pieces = [own] + [lax.ppermute(own, "row", turn(n_row, k)) for k in steps[1:]]
 
     send, keep = pl.pallas_call(
@@ -244,10 +244,14 @@
 
     same = lax.all_to_all(grad_agg, "col", 0, 0, tiled=True, axis_index_groups=same_core)
     other = lax.ppermute(same, "col", swap)
+    strips = jnp.sum(same[:, nodes:].astype(F32), axis=0)
+    strips = add_partners(strips, n_row, [1])
+    same, other, strips = lax.optimization_barrier((same, other, strips))
+    strips = add_partners(strips, n_row, range(2, n_row, 2))
 
     shares = pl.pallas_call(
         functools.partial(backward_kernel, chunk, steps),
-        out_shape=(jax.ShapeDtypeStruct((nodes + strip, width), BF16),) * n_row,
+        out_shape=(jax.ShapeDtypeStruct((nodes, width), BF16),) * n_row,
         in_specs=[smem] * 2 + [hbm] * 3 + [near] * 2,
         out_specs=(vmem,) * n_row,
         scratch_shapes=[
@@ -264,13 +268,21 @@
         cost_estimate=pl.CostEstimate(flops=work, bytes_accessed=11 * MIB, transcendentals=0),
     )(*scalars, values, same, other)
 
-    total = shares[0].astype(F32)
-    for step, share in zip(steps[1:], shares[1:]):
-        total += lax.ppermute(share, "row", turn(n_row, step)).astype(F32)
-    grad_features = total[:nodes].astype(BF16).reshape(1, nodes, width)
-    high, low = total[nodes : nodes + strip // 2], total[nodes + strip // 2 :]
-    copies = jnp.broadcast_to((high + low)[None], (n_col, strip // 2, width))
-    grad_weight = lax.all_to_all(copies, "col", 0, 0, tiled=True).reshape(width, width)
+    shares, strips = lax.optimization_barrier((shares, strips))
+    order = list(zip(steps, shares))[::-1]
+    far, close, own_share = order[: n_row // 2], order[n_row // 2 : -1], shares[0]
+    moved = [lax.ppermute(share, "row", turn(n_row, step)) for step, share in far]
+    copies = jnp.broadcast_to(strips[None], (n_col, strip, width))
+    every = lax.all_to_all(copies, "col", 0, 0, tiled=True)
+    every, held = lax.optimization_barrier((every, [share for unused, share in close]))
+    moved += [
+        lax.ppermute(share, "row", turn(n_row, step)) for (step, unused), share in zip(close, held)
+    ]
+    total = own_share.astype(F32)
+    for share in moved:
+        total += share.astype(F32)
+    grad_features = total.astype(BF16).reshape(1, nodes, width)
+    grad_weight = jnp.sum(every.reshape(chips, 2, strip, width), axis=1).reshape(width, width)
     return (activated, grad_weight, grad_features)
 
 

time: 169 us -> 167 us (0.988)
  waiting for transfers between devices: 44.8 us -> 27.2 us
  starting transfers between devices: 38.2 us -> 54.1 us
    ppermute x7 -> x11, starting transfers between devices: 13.7 us -> 24.5 us  [the longest x7 18 us: per_device(): lax.ppermute(share, 'row', turn(n_row, step))]
    all_to_all x1, waiting for transfers between devices: 8.23 us -> 1.87 us  [per_device(): every = lax.all_to_all(copies, 'col', 0, 0, tiled=True)]
    ppermute x7 -> x11, waiting for transfers between devices: 16.1 us -> 10.6 us  [the longest x7 8.64 us: per_device(): lax.ppermute(share, 'row', turn(n_row, step))]
    ppermute x7, starting transfers between devices: 15.7 us -> 20.8 us  [per_device(): lax.ppermute(own, 'row', turn(n_row, k))]
    ppermute x7, waiting for transfers between devices: 12.7 us -> 9.74 us  [per_device(): lax.ppermute(own, 'row', turn(n_row, k))]
    ppermute x1, waiting for transfers between devices: 3.97 us -> 1.27 us  [per_device(): other = lax.ppermute(same, 'col', swap)]
  transfers between devices with their start and end apart: 17 -> 21, of which waited for: 9 -> 11; matrix products, arithmetic and copies ran while one was open for 0% -> 1% of each run, Pallas kernels for 0% -> 5%
where the time goes in v6:
time: 167 us
  blocking collectives  62.9 us (38%)
  starting transfers between devices  54.1 us (32%)
  waiting for transfers between devices  27.2 us (16%)
  Pallas kernels  17.8 us (11%)
  other arithmetic  2.42 us (1%)
    all_to_all x1, blocking collectives, per_device(): lax.all_to_all(grad_agg, 'col', 0, 0, tiled=True, axis_index_groups=same_...  31.6 us
    all_to_all x1, blocking collectives, per_device(): lax.all_to_all(shares, 'col', 0, 0, tiled=True, axis_index_groups=same_core)  31.3 us
    ppermute x7, starting transfers between devices, per_device(): lax.ppermute(own, 'row', turn(n_row, k))  20.8 us
    ppermute x7, starting transfers between devices, per_device(): lax.ppermute(share, 'row', turn(n_row, step))  18 us
    ppermute x7, waiting for transfers between devices, per_device(): lax.ppermute(own, 'row', turn(n_row, k))  9.74 us
    ppermute x7, waiting for transfers between devices, per_device(): lax.ppermute(share, 'row', turn(n_row, step))  8.64 us
    pallas_call x1, Pallas kernels, per_device(): pl.pallas_call(functools.partial(forward_kernel, chunk, steps), out_shape...  8.22 us
    pallas_call x1, Pallas kernels, per_device(): pl.pallas_call(functools.partial(backward_kernel, chunk, steps), out_shap...  7.56 us
  transfers between devices with their start and end apart: 21, of which 11 were waited for; matrix products, arithmetic and copies ran while one was open for 1% of the time, Pallas kernels for 5%

profile of v6, /device:TPU:1, one launch (start us, length us, event | category | flops | bytes accessed | tf_op | source)
XLA Modules:
  0.0 166.7 jit_solution(128214958143246345)
XLA Ops:
  0.6 0.9 shard_map.94.refs_0_
  1.6 7.8 %collective-permute-start.6 = (bf16[2,128,256]{2,1,0:T(8,128)(2,1)S(1)}, bf16[2,128,256]{2,1,0:T(8,128)(2,1)S(1)}, u32[]{:S(2)}, u32[]{:S(2)}) collective-permute-start(bf16[2,128,256]{2,1,0:T(8,128)(2,1)S(1)} %shard_map.94.refs_0_), channel_id=1, source_target_pairs={{0,128},{32,160},{64,192},{96,224},{128,0},{160,32},{192,64},{224,... | collective-permute-start | bytes 393224 | tf_op jit(solution)/shard_map/ppermute | solution.py:202
  9.4 0.0 collective-permute-start.5
  9.4 3.3 %collective-permute-start.4 = (bf16[2,128,256]{2,1,0:T(8,128)(2,1)S(1)}, bf16[2,128,256]{2,1,0:T(8,128)(2,1)S(1)}, u32[]{:S(2)}, u32[]{:S(2)}) collective-permute-start(bf16[2,128,256]{2,1,0:T(8,128)(2,1)S(1)} %shard_map.94.refs_0_), channel_id=1, source_target_pairs={{0,96},{32,128},{64,160},{96,192},{128,224},{160,0},{192,32},{224,... | collective-permute-start | bytes 393224 | tf_op jit(solution)/shard_map/ppermute | solution.py:202
  12.6 0.8 collective-permute-start.3
  13.4 1.6 collective-permute-start.2
  15.0 0.0 collective-permute-done.6.refs_7_
  15.1 6.0 %collective-permute-start.1 = (bf16[2,128,256]{2,1,0:T(8,128)(2,1)S(1)}, bf16[2,128,256]{2,1,0:T(8,128)(2,1)S(1)}, u32[]{:S(2)}, u32[]{:S(2)}) collective-permute-start(bf16[2,128,256]{2,1,0:T(8,128)(2,1)S(1)} %shard_map.94.refs_0_), channel_id=1, source_target_pairs={{0,224},{32,0},{64,32},{96,64},{128,96},{160,128},{192,160},{224,1... | collective-permute-start | bytes 393224 | tf_op jit(solution)/shard_map/ppermute | solution.py:202
  21.0 3.8 %collective-permute-done.5.refs_6_ = bf16[2,128,256]{2,1,0:T(8,128)(2,1)S(1)} collective-permute-done((bf16[2,128,256]{2,1,0:T(8,128)(2,1)S(1)}, bf16[2,128,256]{2,1,0:T(8,128)(2,1)S(1)}, u32[]{:S(2)}, u32[]{:S(2)}) %collective-permute-start.5) | collective-permute-done | bytes 131104 | tf_op jit(solution)/shard_map/ppermute | solution.py:202
  24.8 1.3 collective-permute-start
  26.7 0.1 pad_add_fusion.place
  26.8 2.0 %collective-permute-done.4.refs_5_ = bf16[2,128,256]{2,1,0:T(8,128)(2,1)S(1)} collective-permute-done((bf16[2,128,256]{2,1,0:T(8,128)(2,1)S(1)}, bf16[2,128,256]{2,1,0:T(8,128)(2,1)S(1)}, u32[]{:S(2)}, u32[]{:S(2)}) %collective-permute-start.4) | collective-permute-done | bytes 131104 | tf_op jit(solution)/shard_map/ppermute | solution.py:202
  28.8 1.8 %collective-permute-done.3.refs_4_ = bf16[2,128,256]{2,1,0:T(8,128)(2,1)S(1)} collective-permute-done((bf16[2,128,256]{2,1,0:T(8,128)(2,1)S(1)}, bf16[2,128,256]{2,1,0:T(8,128)(2,1)S(1)}, u32[]{:S(2)}, u32[]{:S(2)}) %collective-permute-start.3) | collective-permute-done | bytes 131104 | tf_op jit(solution)/shard_map/ppermute | solution.py:202
  30.6 0.0 collective-permute-done.2.refs_3_
  30.6 2.1 %collective-permute-done.1.refs_2_ = bf16[2,128,256]{2,1,0:T(8,128)(2,1)S(1)} collective-permute-done((bf16[2,128,256]{2,1,0:T(8,128)(2,1)S(1)}, bf16[2,128,256]{2,1,0:T(8,128)(2,1)S(1)}, u32[]{:S(2)}, u32[]{:S(2)}) %collective-permute-start.1) | collective-permute-done | bytes 131104 | tf_op jit(solution)/shard_map/ppermute | solution.py:202
  32.8 8.2 %shard_map.95 = (bf16[16,256,256]{2,1,0:T(8,128)(2,1)S(1)}, f32[16,256,256]{2,1,0:T(8,128)S(1)}) custom-call(s32[2]{0:T(128)S(1)} %pad_add_fusion.place, s32[1]{0:T(128)} %bitcast.12.count, s32[192]{0:T(256)} %bitcast.18, s32[192]{0:T(256)} %bitcast.20, bf16[192,128,128]{2,1,0:T(8,128)(2,1)} %bitcast.14, bf16[2,128,256]{2,1,0:T(8,128)(2,1)S(1)} %shard_map.94.refs_0_, ...), custom_call_target="tpu_custom_call" | custom-call | flops 1610612736 | bytes 14680064 | tf_op jit(solution)/shard_map/pallas_call | solution.py:204
  41.0 1.6 collective-permute-start.7
  42.6 3.8 %collective-permute-done.7 = bf16[16,256,256]{2,1,0:T(8,128)(2,1)S(1)} collective-permute-done((bf16[16,256,256]{2,1,0:T(8,128)(2,1)S(1)}, bf16[16,256,256]{2,1,0:T(8,128)(2,1)S(1)}, u32[]{:S(2)}, u32[]{:S(2)}) %collective-permute-start.7) | collective-permute-done | bytes 2097184 | tf_op jit(solution)/shard_map/ppermute | solution.py:226
  46.4 0.8 add_convert_fusion
  47.2 0.0 copy-start
  47.2 0.0 copy-start.1
  47.2 31.3 %all_to_all.15.parts = bf16[16,256,256]{2,1,0:T(8,128)(2,1)S(1)} all-to-all(bf16[16,256,256]{2,1,0:T(8,128)(2,1)S(1)} %add_convert_fusion), channel_id=1, replica_groups={{0,2,4,6,8,10,12,14,16,18,20,22,24,26,28,30},{1,3,5,7,9,11,13,15,17,19,..., dimensions={0} | all-to-all | bytes 4194304 | tf_op jit(solution)/shard_map/all_to_all | solution.py:228
  78.5 1.1 shard_map.96
  79.6 31.6 %all_to_all.16.same = bf16[16,272,256]{2,1,0:T(8,128)(2,1)S(1)} all-to-all(bf16[16,272,256]{2,1,0:T(8,128)(2,1)S(1)} %get-tuple-element.34), channel_id=1, replica_groups={{0,2,4,6,8,10,12,14,16,18,20,22,24,26,28,30},{1,3,5,7,9,11,13,15,17,19,..., dimensions={0} | all-to-all | bytes 4456448 | tf_op jit(solution)/shard_map/all_to_all | solution.py:245
  111.2 2.5 %collective-permute-start.8 = (bf16[16,272,256]{2,1,0:T(8,128)(2,1)S(1)}, bf16[16,272,256]{2,1,0:T(8,128)(2,1)S(1)}, u32[]{:S(2)}, u32[]{:S(2)}) collective-permute-start(bf16[16,272,256]{2,1,0:T(8,128)(2,1)S(1)} %all_to_all.16.same), channel_id=1, source_target_pairs={{0,1},{1,0},{2,3},{3,2},{4,5},{5,4},{6,7},{7,6},{8,9},{9,8},{10,11... | collective-permute-start | bytes 6684680 | tf_op jit(solution)/shard_map/ppermute | solution.py:246
  113.7 0.8 collective-permute-start.9
  114.5 1.9 %collective-permute-done.9 = f32[16,256]{1,0:T(8,128)S(1)} collective-permute-done((f32[16,256]{1,0:T(8,128)S(1)}, f32[16,256]{1,0:T(8,128)S(1)}, u32[]{:S(2)}, u32[]{:S(2)}) %collective-permute-start.9) | collective-permute-done | bytes 16416 | tf_op jit(solution)/shard_map/ppermute | solution.py:167
  116.4 1.3 collective-permute-done.8.other
  117.7 3.2 %collective-permute-start.12 = (f32[16,256]{1,0:T(8,128)S(1)}, f32[16,256]{1,0:T(8,128)S(1)}, u32[]{:S(2)}, u32[]{:S(2)}) collective-permute-start(f32[16,256]{1,0:T(8,128)S(1)} %add.42), channel_id=1, source_target_pairs={{0,192},{32,224},{64,128},{96,160},{128,64},{160,96},{192,0},{224,... | collective-permute-start | bytes 49160 | tf_op jit(solution)/shard_map/ppermute | solution.py:167
  120.9 1.9 %collective-permute-start.11 = (f32[16,256]{1,0:T(8,128)S(1)}, f32[16,256]{1,0:T(8,128)S(1)}, u32[]{:S(2)}, u32[]{:S(2)}) collective-permute-start(f32[16,256]{1,0:T(8,128)S(1)} %add.42), channel_id=1, source_target_pairs={{0,128},{32,160},{64,192},{96,224},{128,0},{160,32},{192,64},{224,... | collective-permute-start | bytes 49160 | tf_op jit(solution)/shard_map/ppermute | solution.py:167
  122.8 0.6 collective-permute-start.10
  123.4 7.6 %shard_map.97 = (bf16[256,256]{1,0:T(8,128)(2,1)S(1)}, bf16[256,256]{1,0:T(8,128)(2,1)S(1)}, bf16[256,256]{1,0:T(8,128)(2,1)S(1)}, bf16[256,256]{1,0:T(8,128)(2,...) custom-call(s32[2]{0:T(128)S(1)} %pad_add_fusion.place, ...), custom_call_target="tpu_custom_call" | custom-call | flops 1610612736 | bytes 11534336 | tf_op jit(solution)/shard_map/pallas_call | solution.py:252
  130.9 0.0 collective-permute-done.12
  130.9 0.0 collective-permute-done.11
  131.0 0.9 broadcast_in_dim.2
  131.8 4.7 %all-to-all-start.2 = ((f32[32,16,256]{2,1,0:T(8,128)}), f32[32,16,256]{2,1,0:T(8,128)S(1)}, u32[]{:S(2)}, u32[]{:S(2)}) async-start(f32[32,16,256]{2,1,0:T(8,128)} %broadcast_in_dim.2), calls=%async_computation.2 | async-start | bytes 1048576 | tf_op jit(solution)/shard_map/all_to_all | solution.py:276
  136.6 4.0 %collective-permute-start.13 = (bf16[256,256]{1,0:T(8,128)(2,1)S(1)}, bf16[256,256]{1,0:T(8,128)(2,1)S(1)}, u32[]{:S(2)}, u32[]{:S(2)}) collective-permute-start(bf16[256,256]{1,0:T(8,128)(2,1)S(1)} %get-tuple-element.52), channel_id=1, source_target_pairs={{0,128},{32,160},{64,192},{96,224},{128,0},{160,32},{192,64},{224,... | collective-permute-start | bytes 393224 | tf_op jit(solution)/shard_map/ppermute | solution.py:274
  140.6 1.3 collective-permute-start.14
  141.9 2.1 %collective-permute-start.15 = (bf16[256,256]{1,0:T(8,128)(2,1)S(1)}, bf16[256,256]{1,0:T(8,128)(2,1)S(1)}, u32[]{:S(2)}, u32[]{:S(2)}) collective-permute-start(bf16[256,256]{1,0:T(8,128)(2,1)S(1)} %get-tuple-element.54), channel_id=1, source_target_pairs={{0,96},{32,128},{64,160},{96,192},{128,224},{160,0},{192,32},{224,... | collective-permute-start | bytes 393224 | tf_op jit(solution)/shard_map/ppermute | solution.py:274
  144.0 2.4 %collective-permute-start.16 = (bf16[256,256]{1,0:T(8,128)(2,1)S(1)}, bf16[256,256]{1,0:T(8,128)(2,1)S(1)}, u32[]{:S(2)}, u32[]{:S(2)}) collective-permute-start(bf16[256,256]{1,0:T(8,128)(2,1)S(1)} %get-tuple-element.55), channel_id=1, source_target_pairs={{0,192},{32,224},{64,0},{96,32},{128,64},{160,96},{192,128},{224,1... | collective-permute-start | bytes 393224 | tf_op jit(solution)/shard_map/ppermute | solution.py:274
  146.4 1.9 %all-to-all-done.2 = f32[32,16,256]{2,1,0:T(8,128)S(1)} async-done(((f32[32,16,256]{2,1,0:T(8,128)}), f32[32,16,256]{2,1,0:T(8,128)S(1)}, u32[]{:S(2)}, u32[]{:S(2)}) %all-to-all-start.2) | async-done | bytes 524320 | tf_op jit(solution)/shard_map/all_to_all | solution.py:276
  148.3 4.2 %collective-permute-start.18 = (bf16[256,256]{1,0:T(8,128)(2,1)S(1)}, bf16[256,256]{1,0:T(8,128)(2,1)S(1)}, u32[]{:S(2)}, u32[]{:S(2)}) collective-permute-start(bf16[256,256]{1,0:T(8,128)(2,1)S(1)} %get-tuple-element.57), channel_id=1, source_target_pairs={{0,224},{32,0},{64,32},{96,64},{128,96},{160,128},{192,160},{224,1... | collective-permute-start | bytes 393224 | tf_op jit(solution)/shard_map/ppermute | solution.py:279
  152.5 4.3 %collective-permute-done.14 = bf16[256,256]{1,0:T(8,128)(2,1)S(1)} collective-permute-done((bf16[256,256]{1,0:T(8,128)(2,1)S(1)}, bf16[256,256]{1,0:T(8,128)(2,1)S(1)}, u32[]{:S(2)}, u32[]{:S(2)}) %collective-permute-start.14) | collective-permute-done | bytes 131104 | tf_op jit(solution)/shard_map/ppermute | solution.py:274
  156.8 4.0 %collective-permute-start.19 = (bf16[256,256]{1,0:T(8,128)(2,1)S(1)}, bf16[256,256]{1,0:T(8,128)(2,1)S(1)}, u32[]{:S(2)}, u32[]{:S(2)}) collective-permute-start(bf16[256,256]{1,0:T(8,128)(2,1)S(1)} %get-tuple-element.58), channel_id=1, source_target_pairs={{0,32},{32,64},{64,96},{96,128},{128,160},{160,192},{192,224},{224... | collective-permute-start | bytes 393224 | tf_op jit(solution)/shard_map/ppermute | solution.py:279
  160.7 0.7 bitcast_reduce_fusion
  161.5 2.0 %collective-permute-done.16 = bf16[256,256]{1,0:T(8,128)(2,1)S(1)} collective-permute-done((bf16[256,256]{1,0:T(8,128)(2,1)S(1)}, bf16[256,256]{1,0:T(8,128)(2,1)S(1)}, u32[]{:S(2)}, u32[]{:S(2)}) %collective-permute-start.16) | collective-permute-done | bytes 131104 | tf_op jit(solution)/shard_map/ppermute | solution.py:274
  163.5 2.4 %collective-permute-done.18 = bf16[256,256]{1,0:T(8,128)(2,1)S(1)} collective-permute-done((bf16[256,256]{1,0:T(8,128)(2,1)S(1)}, bf16[256,256]{1,0:T(8,128)(2,1)S(1)}, u32[]{:S(2)}, u32[]{:S(2)}) %collective-permute-start.18) | collective-permute-done | bytes 131104 | tf_op jit(solution)/shard_map/ppermute | solution.py:279
  165.9 0.8 fusion
  (12 shorter events, 0.1 us)
Async XLA Ops:
  1.6 13.5 %collective-permute-start.6 = (bf16[2,128,256]{2,1,0:T(8,128)(2,1)S(1)}, bf16[2,128,256]{2,1,0:T(8,128)(2,1)S(1)}, u32[]{:S(2)}, u32[]{:S(2)}) collective-permute-start(bf16[2,128,256]{2,1,0:T(8,128)(2,1)S(1)} %shard_map.94.refs_0_), channel_id=1, source_target_pairs={{0,128},{32,160},{64,192},{96,224},{128,0},{160,32},{192,64},{224,... | collective-permute-start | bytes 393224 | tf_op jit(solution)/shard_map/ppermute | solution.py:202
  9.4 15.4 %collective-permute-start.5 = (bf16[2,128,256]{2,1,0:T(8,128)(2,1)S(1)}, bf16[2,128,256]{2,1,0:T(8,128)(2,1)S(1)}, u32[]{:S(2)}, u32[]{:S(2)}) collective-permute-start(bf16[2,128,256]{2,1,0:T(8,128)(2,1)S(1)} %shard_map.94.refs_0_), channel_id=1, source_target_pairs={{0,160},{32,192},{64,224},{96,0},{128,32},{160,64},{192,96},{224,1... | collective-permute-start | bytes 393224 | tf_op jit(solution)/shard_map/ppermute | solution.py:202
  9.4 19.4 %collective-permute-start.4 = (bf16[2,128,256]{2,1,0:T(8,128)(2,1)S(1)}, bf16[2,128,256]{2,1,0:T(8,128)(2,1)S(1)}, u32[]{:S(2)}, u32[]{:S(2)}) collective-permute-start(bf16[2,128,256]{2,1,0:T(8,128)(2,1)S(1)} %shard_map.94.refs_0_), channel_id=1, source_target_pairs={{0,96},{32,128},{64,160},{96,192},{128,224},{160,0},{192,32},{224,... | collective-permute-start | bytes 393224 | tf_op jit(solution)/shard_map/ppermute | solution.py:202
  12.6 18.0 %collective-permute-start.3 = (bf16[2,128,256]{2,1,0:T(8,128)(2,1)S(1)}, bf16[2,128,256]{2,1,0:T(8,128)(2,1)S(1)}, u32[]{:S(2)}, u32[]{:S(2)}) collective-permute-start(bf16[2,128,256]{2,1,0:T(8,128)(2,1)S(1)} %shard_map.94.refs_0_), channel_id=1, source_target_pairs={{0,192},{32,224},{64,0},{96,32},{128,64},{160,96},{192,128},{224,1... | collective-permute-start | bytes 393224 | tf_op jit(solution)/shard_map/ppermute | solution.py:202
  13.4 17.2 %collective-permute-start.2 = (bf16[2,128,256]{2,1,0:T(8,128)(2,1)S(1)}, bf16[2,128,256]{2,1,0:T(8,128)(2,1)S(1)}, u32[]{:S(2)}, u32[]{:S(2)}) collective-permute-start(bf16[2,128,256]{2,1,0:T(8,128)(2,1)S(1)} %shard_map.94.refs_0_), channel_id=1, source_target_pairs={{0,64},{32,96},{64,128},{96,160},{128,192},{160,224},{192,0},{224,... | collective-permute-start | bytes 393224 | tf_op jit(solution)/shard_map/ppermute | solution.py:202
  15.1 17.7 %collective-permute-start.1 = (bf16[2,128,256]{2,1,0:T(8,128)(2,1)S(1)}, bf16[2,128,256]{2,1,0:T(8,128)(2,1)S(1)}, u32[]{:S(2)}, u32[]{:S(2)}) collective-permute-start(bf16[2,128,256]{2,1,0:T(8,128)(2,1)S(1)} %shard_map.94.refs_0_), channel_id=1, source_target_pairs={{0,224},{32,0},{64,32},{96,64},{128,96},{160,128},{192,160},{224,1... | collective-permute-start | bytes 393224 | tf_op jit(solution)/shard_map/ppermute | solution.py:202
  24.8 8.0 %collective-permute-start = (bf16[2,128,256]{2,1,0:T(8,128)(2,1)S(1)}, bf16[2,128,256]{2,1,0:T(8,128)(2,1)S(1)}, u32[]{:S(2)}, u32[]{:S(2)}) collective-permute-start(bf16[2,128,256]{2,1,0:T(8,128)(2,1)S(1)} %shard_map.94.refs_0_), channel_id=1, source_target_pairs={{0,32},{32,64},{64,96},{96,128},{128,160},{160,192},{192,224},{224... | collective-permute-start | bytes 393224 | tf_op jit(solution)/shard_map/ppermute | solution.py:202
  41.0 5.4 %collective-permute-start.7 = (bf16[16,256,256]{2,1,0:T(8,128)(2,1)S(1)}, bf16[16,256,256]{2,1,0:T(8,128)(2,1)S(1)}, u32[]{:S(2)}, u32[]{:S(2)}) collective-permute-start(bf16[16,256,256]{2,1,0:T(8,128)(2,1)S(1)} %get-tuple-element.32), channel_id=1, source_target_pairs={{0,1},{1,0},{2,3},{3,2},{4,5},{5,4},{6,7},{7,6},{8,9},{9,8},{10,11... | collective-permute-start | bytes 6291464 | tf_op jit(solution)/shard_map/ppermute | solution.py:226
  47.2 31.4 %copy-start = (bf16[256,256]{1,0:T(8,128)(2,1)S(1)}, bf16[256,256]{1,0:T(8,128)(2,1)}, u32[]{:S(2)}) copy-start(bf16[256,256]{1,0:T(8,128)(2,1)} %weight.1) | copy-start | bytes 393220
  47.2 31.4 %copy-start.1 = (bf16[256,256]{1,0:T(8,128)(2,1)S(1)}, bf16[256,256]{1,0:T(8,128)(2,1)}, u32[]{:S(2)}) copy-start(bf16[256,256]{1,0:T(8,128)(2,1)} %cotangent.1) | copy-start | bytes 393220
  111.2 6.5 %collective-permute-start.8 = (bf16[16,272,256]{2,1,0:T(8,128)(2,1)S(1)}, bf16[16,272,256]{2,1,0:T(8,128)(2,1)S(1)}, u32[]{:S(2)}, u32[]{:S(2)}) collective-permute-start(bf16[16,272,256]{2,1,0:T(8,128)(2,1)S(1)} %all_to_all.16.same), channel_id=1, source_target_pairs={{0,1},{1,0},{2,3},{3,2},{4,5},{5,4},{6,7},{7,6},{8,9},{9,8},{10,11... | collective-permute-start | bytes 6684680 | tf_op jit(solution)/shard_map/ppermute | solution.py:246
  113.7 2.7 %collective-permute-start.9 = (f32[16,256]{1,0:T(8,128)S(1)}, f32[16,256]{1,0:T(8,128)S(1)}, u32[]{:S(2)}, u32[]{:S(2)}) collective-permute-start(f32[16,256]{1,0:T(8,128)S(1)} %convert_reduce_fusion), channel_id=1, source_target_pairs={{0,32},{32,0},{64,96},{96,64},{128,160},{160,128},{192,224},{224,1... | collective-permute-start | bytes 49160 | tf_op jit(solution)/shard_map/ppermute | solution.py:167
  117.7 13.2 %collective-permute-start.12 = (f32[16,256]{1,0:T(8,128)S(1)}, f32[16,256]{1,0:T(8,128)S(1)}, u32[]{:S(2)}, u32[]{:S(2)}) collective-permute-start(f32[16,256]{1,0:T(8,128)S(1)} %add.42), channel_id=1, source_target_pairs={{0,192},{32,224},{64,128},{96,160},{128,64},{160,96},{192,0},{224,... | collective-permute-start | bytes 49160 | tf_op jit(solution)/shard_map/ppermute | solution.py:167
  120.9 10.1 %collective-permute-start.11 = (f32[16,256]{1,0:T(8,128)S(1)}, f32[16,256]{1,0:T(8,128)S(1)}, u32[]{:S(2)}, u32[]{:S(2)}) collective-permute-start(f32[16,256]{1,0:T(8,128)S(1)} %add.42), channel_id=1, source_target_pairs={{0,128},{32,160},{64,192},{96,224},{128,0},{160,32},{192,64},{224,... | collective-permute-start | bytes 49160 | tf_op jit(solution)/shard_map/ppermute | solution.py:167
  122.8 8.2 %collective-permute-start.10 = (f32[16,256]{1,0:T(8,128)S(1)}, f32[16,256]{1,0:T(8,128)S(1)}, u32[]{:S(2)}, u32[]{:S(2)}) collective-permute-start(f32[16,256]{1,0:T(8,128)S(1)} %add.42), channel_id=1, source_target_pairs={{0,64},{32,96},{64,0},{96,32},{128,192},{160,224},{192,128},{224,1... | collective-permute-start | bytes 49160 | tf_op jit(solution)/shard_map/ppermute | solution.py:167
  131.8 16.4 %all-to-all-start.2 = ((f32[32,16,256]{2,1,0:T(8,128)}), f32[32,16,256]{2,1,0:T(8,128)S(1)}, u32[]{:S(2)}, u32[]{:S(2)}) async-start(f32[32,16,256]{2,1,0:T(8,128)} %broadcast_in_dim.2), calls=%async_computation.2 | async-start | bytes 1048576 | tf_op jit(solution)/shard_map/all_to_all | solution.py:276
  136.6 11.7 %collective-permute-start.13 = (bf16[256,256]{1,0:T(8,128)(2,1)S(1)}, bf16[256,256]{1,0:T(8,128)(2,1)S(1)}, u32[]{:S(2)}, u32[]{:S(2)}) collective-permute-start(bf16[256,256]{1,0:T(8,128)(2,1)S(1)} %get-tuple-element.52), channel_id=1, source_target_pairs={{0,128},{32,160},{64,192},{96,224},{128,0},{160,32},{192,64},{224,... | collective-permute-start | bytes 393224 | tf_op jit(solution)/shard_map/ppermute | solution.py:274
  140.6 16.2 %collective-permute-start.14 = (bf16[256,256]{1,0:T(8,128)(2,1)S(1)}, bf16[256,256]{1,0:T(8,128)(2,1)S(1)}, u32[]{:S(2)}, u32[]{:S(2)}) collective-permute-start(bf16[256,256]{1,0:T(8,128)(2,1)S(1)} %get-tuple-element.53), channel_id=1, source_target_pairs={{0,160},{32,192},{64,224},{96,0},{128,32},{160,64},{192,96},{224,1... | collective-permute-start | bytes 393224 | tf_op jit(solution)/shard_map/ppermute | solution.py:274
  141.9 19.6 %collective-permute-start.15 = (bf16[256,256]{1,0:T(8,128)(2,1)S(1)}, bf16[256,256]{1,0:T(8,128)(2,1)S(1)}, u32[]{:S(2)}, u32[]{:S(2)}) collective-permute-start(bf16[256,256]{1,0:T(8,128)(2,1)S(1)} %get-tuple-element.54), channel_id=1, source_target_pairs={{0,96},{32,128},{64,160},{96,192},{128,224},{160,0},{192,32},{224,... | collective-permute-start | bytes 393224 | tf_op jit(solution)/shard_map/ppermute | solution.py:274
  144.0 19.5 %collective-permute-start.16 = (bf16[256,256]{1,0:T(8,128)(2,1)S(1)}, bf16[256,256]{1,0:T(8,128)(2,1)S(1)}, u32[]{:S(2)}, u32[]{:S(2)}) collective-permute-start(bf16[256,256]{1,0:T(8,128)(2,1)S(1)} %get-tuple-element.55), channel_id=1, source_target_pairs={{0,192},{32,224},{64,0},{96,32},{128,64},{160,96},{192,128},{224,1... | collective-permute-start | bytes 393224 | tf_op jit(solution)/shard_map/ppermute | solution.py:274
  148.3 15.2 %collective-permute-start.17 = (bf16[256,256]{1,0:T(8,128)(2,1)S(1)}, bf16[256,256]{1,0:T(8,128)(2,1)S(1)}, u32[]{:S(2)}, u32[]{:S(2)}) collective-permute-start(bf16[256,256]{1,0:T(8,128)(2,1)S(1)} %get-tuple-element.56), channel_id=1, source_target_pairs={{0,64},{32,96},{64,128},{96,160},{128,192},{160,224},{192,0},{224,... | collective-permute-start | bytes 393224 | tf_op jit(solution)/shard_map/ppermute | solution.py:279
  148.3 17.6 %collective-permute-start.18 = (bf16[256,256]{1,0:T(8,128)(2,1)S(1)}, bf16[256,256]{1,0:T(8,128)(2,1)S(1)}, u32[]{:S(2)}, u32[]{:S(2)}) collective-permute-start(bf16[256,256]{1,0:T(8,128)(2,1)S(1)} %get-tuple-element.57), channel_id=1, source_target_pairs={{0,224},{32,0},{64,32},{96,64},{128,96},{160,128},{192,160},{224,1... | collective-permute-start | bytes 393224 | tf_op jit(solution)/shard_map/ppermute | solution.py:279
  156.8 9.1 %collective-permute-start.19 = (bf16[256,256]{1,0:T(8,128)(2,1)S(1)}, bf16[256,256]{1,0:T(8,128)(2,1)S(1)}, u32[]{:S(2)}, u32[]{:S(2)}) collective-permute-start(bf16[256,256]{1,0:T(8,128)(2,1)S(1)} %get-tuple-element.58), channel_id=1, source_target_pairs={{0,32},{32,64},{64,96},{96,128},{128,160},{160,192},{192,224},{224... | collective-permute-start | bytes 393224 | tf_op jit(solution)/shard_map/ppermute | solution.py:279

commit v7 on v5

--- a/solution.py
+++ b/solution.py
@@ -93,7 +93,7 @@
     lax.fori_loop(0, send.shape[0], split, 0)
 
 
-def backward_kernel(chunk, steps, place, count, rows_hbm, cols_hbm, vals_hbm, same, other, *refs):
+def backward_kernel(chunk, steps, place, count, rows_hbm, cols_hbm, vals_hbm, same, other, strip, *refs):
     n_row = len(steps)
     outs = refs[:n_row]
     rows, cols, vals, grads, total, index_sems, val_sems, grad_sems = refs[n_row:]
@@ -125,13 +125,8 @@
     each_live_slot(live, vals_hbm, vals, val_sems, chunk, one_slot)
     blocks_here = spare // n_row
     nodes = blocks_here * side
-    terms = jnp.sum(grads[0, :, nodes:].astype(F32), axis=0) + jnp.sum(
-        grads[1, :, nodes:].astype(F32), axis=0
-    )
-    half = terms.shape[0] // 2
-    terms = jnp.where(core == 0, terms[:half], terms[half:])
-    high = terms.astype(BF16).astype(F32)
-    tail = jnp.concatenate([high, terms - high], axis=0).astype(BF16)
+    high = strip[...].astype(BF16)
+    tail = jnp.concatenate([high, (strip[...] - high.astype(F32)).astype(BF16)], axis=0)
     for step, out in zip(steps, outs):
         owner = lax.rem(row + step, n_row)
         mine = total[pl.ds(owner * blocks_here, blocks_here)]
@@ -145,7 +140,8 @@
     copy.wait()
 
 
-def dense_kernel(parts, weight, cotangent, activated, grad_agg):
+def dense_kernel(n_row, place, parts, weight, cotangent, activated, grad_agg, *refs):
+    strips, local_weight = refs[:n_row], refs[n_row]
     total = parts[0].astype(F32)
     for chip in range(1, parts.shape[0]):
         total += parts[chip].astype(F32)
@@ -154,21 +150,48 @@
     sigma = jax.nn.sigmoid(pre)
     activated[...] = (pre * sigma).astype(BF16)
     grad_pre = (cotangent[...].astype(F32) * sigma * (1.0 + pre * (1.0 - sigma))).astype(BF16)
-    local_weight = lax.dot_general(
-        aggregated, grad_pre, (((0,), (0,)), ((), ())), preferred_element_type=F32
-    ).astype(BF16)
     grad = lax.dot_general(
         grad_pre, weight[...], (((1,), (1,)), ((), ())), preferred_element_type=F32
     ).astype(BF16)
-    nodes = grad.shape[0]
-    strip = grad_agg.shape[1] - nodes
     for chip in range(grad_agg.shape[0]):
-        grad_agg[chip, :nodes] = grad
-        grad_agg[chip, nodes:] = local_weight[chip * strip : (chip + 1) * strip]
+        grad_agg[chip] = grad
+    local_weight[...] = lax.dot_general(
+        aggregated, grad_pre, (((0,), (0,)), ((), ())), preferred_element_type=F32
+    )
+    rows_strip = strips[0].shape[0]
+    for step, strip in enumerate(strips):
+        owner = lax.rem(place[1] + step, n_row)
+        first = pl.multiple_of(owner * rows_strip, rows_strip)
+        strip[...] = local_weight[pl.ds(first, rows_strip)]
+
+
+def last_kernel(steps, place, *refs):
+    n_row = len(steps)
+    shares, (grad_features, grad_weight) = refs[:n_row], refs[n_row:]
+    nodes = grad_features.shape[0]
+    rows_strip = grad_weight.shape[0] // n_row
+    total = shares[0][:nodes].astype(F32)
+    for share in shares[1:]:
+        total += share[:nodes].astype(F32)
+    grad_features[...] = total.astype(BF16)
+    for step, share in zip(steps, shares):
+        owner = lax.rem(place[1] + n_row - step, n_row)
+        first = pl.multiple_of(owner * rows_strip, rows_strip)
+        high, low = share[nodes : nodes + rows_strip], share[nodes + rows_strip :]
+        grad_weight[pl.ds(first, rows_strip)] = high.astype(F32) + low.astype(F32)
 
 
 def turn(size, step):
     return [(i, (i + step) % size) for i in range(size)]
+
+
+def add_partners(value, axis, size, distances):
+    for other in [
+        lax.ppermute(value, axis, [(i, i ^ distance) for i in range(size)])
+        for distance in distances
+    ]:
+        value = value + other
+    return value
 
 
 def per_device(features, weight, cotangent, blk_vals, blk_rows, blk_cols, blk_count):
@@ -198,7 +221,7 @@
         scratch_shapes=[pltpu.SemaphoreType.DMA],
         compiler_params=pltpu.CompilerParams(vmem_limit_bytes=4 * MIB),
     )(in_hbm(features.reshape(here, side, width)))
-    steps = [0] + sorted(range(1, n_row), key=lambda k: (-min(k, n_row - k), k))
+    steps = [0] + sorted(range(1, n_row), key=lambda k: (min(k, n_row - k), k))
     pieces = [own] + [lax.ppermute(own, "row", turn(n_row, k)) for k in steps[1:]]
 
     send, keep = pl.pallas_call(
@@ -227,34 +250,44 @@
     shares = (keep + arrived.astype(F32)).astype(BF16)
     parts = lax.all_to_all(shares, "col", 0, 0, tiled=True, axis_index_groups=same_core)
 
-    strip = width // chips
-    activated, grad_agg = pl.pallas_call(
-        dense_kernel,
+    rows_strip = width // n_row
+    activated, grad_agg, *strips = pl.pallas_call(
+        functools.partial(dense_kernel, n_row),
         out_shape=(
             jax.ShapeDtypeStruct((nodes, width), BF16),
-            jax.ShapeDtypeStruct((chips, nodes + strip, width), BF16),
-        ),
-        in_specs=[vmem] * 3,
-        out_specs=(vmem,) * 2,
+            jax.ShapeDtypeStruct((chips, nodes, width), BF16),
+        )
+        + (jax.ShapeDtypeStruct((rows_strip, width), F32),) * n_row,
+        in_specs=[smem] + [vmem] * 3,
+        out_specs=(vmem,) * (2 + n_row),
+        scratch_shapes=[pltpu.VMEM((width, width), F32)],
         compiler_params=pltpu.CompilerParams(vmem_limit_bytes=24 * MIB),
         cost_estimate=pl.CostEstimate(
             flops=6 * nodes * width * width, bytes_accessed=5 * MIB, transcendentals=nodes * width
         ),
-    )(parts, weight, cotangent)
+    )(place, parts, weight, cotangent)
 
     same = lax.all_to_all(grad_agg, "col", 0, 0, tiled=True, axis_index_groups=same_core)
+    moved = [lax.ppermute(strips[k], "row", turn(n_row, k)) for k in steps[:0:-1]]
+    strip = strips[0]
+    for other_strip in moved:
+        strip = strip + other_strip
+    strip = add_partners(strip, "col", n_col, [1])
+    strip = add_partners(strip, "col", n_col, [2, 4, 6])
+    strip = add_partners(strip, "col", n_col, [8, 16, 24])
+    same, strip = lax.optimization_barrier((same, strip))
     other = lax.ppermute(same, "col", swap)
 
     shares = pl.pallas_call(
         functools.partial(backward_kernel, chunk, steps),
-        out_shape=(jax.ShapeDtypeStruct((nodes + strip, width), BF16),) * n_row,
-        in_specs=[smem] * 2 + [hbm] * 3 + [near] * 2,
+        out_shape=(jax.ShapeDtypeStruct((nodes + 2 * rows_strip, width), BF16),) * n_row,
+        in_specs=[smem] * 2 + [hbm] * 3 + [near] * 2 + [vmem],
         out_specs=(vmem,) * n_row,
         scratch_shapes=[
             pltpu.SMEM((slots,), jnp.int32),
             pltpu.SMEM((slots,), jnp.int32),
             pltpu.VMEM((slots, side, side), BF16),
-            pltpu.VMEM((2, chips, nodes + strip, width), BF16),
+            pltpu.VMEM((2, chips, nodes, width), BF16),
             pltpu.VMEM((here * n_row + 1, side, width), F32),
             pltpu.SemaphoreType.DMA((2,)),
             pltpu.SemaphoreType.DMA((slots // chunk,)),
@@ -262,15 +295,22 @@
         ],
         compiler_params=pltpu.CompilerParams(vmem_limit_bytes=40 * MIB),
         cost_estimate=pl.CostEstimate(flops=work, bytes_accessed=11 * MIB, transcendentals=0),
-    )(*scalars, values, same, other)
-
-    total = shares[0].astype(F32)
-    for step, share in zip(steps[1:], shares[1:]):
-        total += lax.ppermute(share, "row", turn(n_row, step)).astype(F32)
-    grad_features = total[:nodes].astype(BF16).reshape(1, nodes, width)
-    high, low = total[nodes : nodes + strip // 2], total[nodes + strip // 2 :]
-    copies = jnp.broadcast_to((high + low)[None], (n_col, strip // 2, width))
-    grad_weight = lax.all_to_all(copies, "col", 0, 0, tiled=True).reshape(width, width)
+    )(*scalars, values, same, other, strip)
+
+    shares = [shares[0]] + [
+        lax.ppermute(share, "row", turn(n_row, step)) for step, share in zip(steps[1:], shares[1:])
+    ]
+    grad_features, grad_weight = pl.pallas_call(
+        functools.partial(last_kernel, steps),
+        out_shape=(
+            jax.ShapeDtypeStruct((nodes, width), BF16),
+            jax.ShapeDtypeStruct((width, width), F32),
+        ),
+        in_specs=[smem] + [vmem] * n_row,
+        out_specs=(vmem, vmem),
+        compiler_params=pltpu.CompilerParams(vmem_limit_bytes=16 * MIB),
+    )(place, *shares)
+    grad_features = grad_features.reshape(1, nodes, width)
     return (activated, grad_weight, grad_features)
 
 

time: 169 us -> 171 us (1.012); the launches traced: 169 us -> 168 us
  blocking collectives: 63.5 us -> 31.8 us
  starting transfers between devices: 38.2 us -> 65.2 us
  waiting for transfers between devices: 44.8 us -> 48.4 us
    all_to_all x1 -> x0, blocking collectives: 31.6 us -> none  [per_device(): lax.all_to_all(grad_agg, 'col', 0, 0, tiled=True, axis_index_groups=same_...]
    ppermute x7 -> x21, starting transfers between devices: 13.7 us -> 36.1 us  [the longest x7 13 us: per_device(): lax.ppermute(strips[k], 'row', turn(n_row, k))]
    ppermute x7 -> x21, waiting for transfers between devices: 16.1 us -> 31.1 us  [the longest x7 18.5 us: per_device(): lax.ppermute(share, 'row', turn(n_row, step))]
    all_to_all x1, waiting for transfers between devices: 8.23 us -> 0.01 us  [per_device(): lax.all_to_all(grad_agg, 'col', 0, 0, tiled=True, axis_index_groups=same_...]
    ppermute x7, starting transfers between devices: 15.7 us -> 20.8 us  [per_device(): lax.ppermute(own, 'row', turn(n_row, k))]
    ppermute x7, waiting for transfers between devices: 12.7 us -> 9.74 us  [per_device(): lax.ppermute(own, 'row', turn(n_row, k))]
    pallas_call x1 -> x2, Pallas kernels: 1.07 us -> 3.26 us  [the longest x1 1.82 us: per_device(): pl.pallas_call(functools.partial(dense_kernel, n_row), out_shape=(jax.Sha...]
  transfers between devices with their start and end apart: 17 -> 31, of which waited for: 9 -> 18; matrix products, arithmetic and copies ran while one was open for 0% -> 0% of each run, Pallas kernels for 0% -> 0%
where the time goes in v7:
time: 171 us; the launch traced here: 168 us
  starting transfers between devices  65.2 us (38%)
  waiting for transfers between devices  48.4 us (28%)
  blocking collectives  31.8 us (19%)
  Pallas kernels  19.2 us (11%)
    all_to_all x1, blocking collectives, per_device(): lax.all_to_all(shares, 'col', 0, 0, tiled=True, axis_index_groups=same_core)  31.8 us
    ppermute x7, starting transfers between devices, per_device(): lax.ppermute(own, 'row', turn(n_row, k))  20.8 us
    ppermute x7, waiting for transfers between devices, per_device(): lax.ppermute(share, 'row', turn(n_row, step))  18.5 us
    ppermute x7, starting transfers between devices, per_device(): lax.ppermute(strips[k], 'row', turn(n_row, k))  13 us
    ppermute x7, starting transfers between devices, per_device(): lax.ppermute(share, 'row', turn(n_row, step))  12 us
    ppermute x7, starting transfers between devices, add_partners(): lax.ppermute(value, axis, [(i, i ^ distance) for i in range(size)])  11.1 us
    ppermute x7, waiting for transfers between devices, per_device(): lax.ppermute(own, 'row', turn(n_row, k))  9.74 us
    ppermute x7, waiting for transfers between devices, add_partners(): lax.ppermute(value, axis, [(i, i ^ distance) for i in range(size)])  8.25 us
  transfers between devices with their start and end apart: 31, of which 18 were waited for; matrix products, arithmetic and copies ran while one was open for 0% of the time, Pallas kernels for 0%

profile of v7, /device:TPU:1, one launch (start us, length us, event | category | flops | bytes accessed | tf_op | source)
XLA Modules:
  0.0 168.1 jit_solution(14879168733917151075)
XLA Ops:
  0.6 0.9 shard_map.94.refs_0_
  1.6 7.8 %collective-permute-start.6 = (bf16[2,128,256]{2,1,0:T(8,128)(2,1)S(1)}, bf16[2,128,256]{2,1,0:T(8,128)(2,1)S(1)}, u32[]{:S(2)}, u32[]{:S(2)}) collective-permute-start(bf16[2,128,256]{2,1,0:T(8,128)(2,1)S(1)} %shard_map.94.refs_0_), channel_id=1, source_target_pairs={{0,128},{32,160},{64,192},{96,224},{128,0},{160,32},{192,64},{224,... | collective-permute-start | bytes 393224 | tf_op jit(solution)/shard_map/ppermute | solution.py:225
  9.4 3.3 %collective-permute-start.4 = (bf16[2,128,256]{2,1,0:T(8,128)(2,1)S(1)}, bf16[2,128,256]{2,1,0:T(8,128)(2,1)S(1)}, u32[]{:S(2)}, u32[]{:S(2)}) collective-permute-start(bf16[2,128,256]{2,1,0:T(8,128)(2,1)S(1)} %shard_map.94.refs_0_), channel_id=1, source_target_pairs={{0,96},{32,128},{64,160},{96,192},{128,224},{160,0},{192,32},{224,... | collective-permute-start | bytes 393224 | tf_op jit(solution)/shard_map/ppermute | solution.py:225
  12.6 0.8 collective-permute-start.3
  13.4 1.6 collective-permute-start.2
  15.1 6.0 %collective-permute-start.1 = (bf16[2,128,256]{2,1,0:T(8,128)(2,1)S(1)}, bf16[2,128,256]{2,1,0:T(8,128)(2,1)S(1)}, u32[]{:S(2)}, u32[]{:S(2)}) collective-permute-start(bf16[2,128,256]{2,1,0:T(8,128)(2,1)S(1)} %shard_map.94.refs_0_), channel_id=1, source_target_pairs={{0,224},{32,0},{64,32},{96,64},{128,96},{160,128},{192,160},{224,1... | collective-permute-start | bytes 393224 | tf_op jit(solution)/shard_map/ppermute | solution.py:225
  21.0 3.8 %collective-permute-done.5.refs_6_ = bf16[2,128,256]{2,1,0:T(8,128)(2,1)S(1)} collective-permute-done((bf16[2,128,256]{2,1,0:T(8,128)(2,1)S(1)}, bf16[2,128,256]{2,1,0:T(8,128)(2,1)S(1)}, u32[]{:S(2)}, u32[]{:S(2)}) %collective-permute-start.5) | collective-permute-done | bytes 131104 | tf_op jit(solution)/shard_map/ppermute | solution.py:225
  24.8 1.3 collective-permute-start
  26.8 2.0 %collective-permute-done.4.refs_5_ = bf16[2,128,256]{2,1,0:T(8,128)(2,1)S(1)} collective-permute-done((bf16[2,128,256]{2,1,0:T(8,128)(2,1)S(1)}, bf16[2,128,256]{2,1,0:T(8,128)(2,1)S(1)}, u32[]{:S(2)}, u32[]{:S(2)}) %collective-permute-start.4) | collective-permute-done | bytes 131104 | tf_op jit(solution)/shard_map/ppermute | solution.py:225
  28.8 1.8 %collective-permute-done.3.refs_4_ = bf16[2,128,256]{2,1,0:T(8,128)(2,1)S(1)} collective-permute-done((bf16[2,128,256]{2,1,0:T(8,128)(2,1)S(1)}, bf16[2,128,256]{2,1,0:T(8,128)(2,1)S(1)}, u32[]{:S(2)}, u32[]{:S(2)}) %collective-permute-start.3) | collective-permute-done | bytes 131104 | tf_op jit(solution)/shard_map/ppermute | solution.py:225
  30.6 2.1 %collective-permute-done.1.refs_2_ = bf16[2,128,256]{2,1,0:T(8,128)(2,1)S(1)} collective-permute-done((bf16[2,128,256]{2,1,0:T(8,128)(2,1)S(1)}, bf16[2,128,256]{2,1,0:T(8,128)(2,1)S(1)}, u32[]{:S(2)}, u32[]{:S(2)}) %collective-permute-start.1) | collective-permute-done | bytes 131104 | tf_op jit(solution)/shard_map/ppermute | solution.py:225
  32.8 8.2 %shard_map.95 = (bf16[16,256,256]{2,1,0:T(8,128)(2,1)S(1)}, f32[16,256,256]{2,1,0:T(8,128)S(1)}) custom-call(s32[2]{0:T(128)S(1)} %pad_add_fusion.place, s32[1]{0:T(128)} %bitcast.8.count, s32[192]{0:T(256)} %bitcast.13, s32[192]{0:T(256)} %bitcast.15, bf16[192,128,128]{2,1,0:T(8,128)(2,1)} %bitcast.10, bf16[2,128,256]{2,1,0:T(8,128)(2,1)S(1)} %shard_map.94.refs_0_, ...), custom_call_target="tpu_custom_call" | custom-call | flops 1610612736 | bytes 14680064 | tf_op jit(solution)/shard_map/pallas_call | solution.py:227
  41.0 1.6 collective-permute-start.7
  42.6 3.8 %collective-permute-done.7 = bf16[16,256,256]{2,1,0:T(8,128)(2,1)S(1)} collective-permute-done((bf16[16,256,256]{2,1,0:T(8,128)(2,1)S(1)}, bf16[16,256,256]{2,1,0:T(8,128)(2,1)S(1)}, u32[]{:S(2)}, u32[]{:S(2)}) %collective-permute-start.7) | collective-permute-done | bytes 2097184 | tf_op jit(solution)/shard_map/ppermute | solution.py:249
  46.4 0.6 add_convert_fusion
  47.1 31.8 %all_to_all.10.parts = bf16[16,256,256]{2,1,0:T(8,128)(2,1)S(1)} all-to-all(bf16[16,256,256]{2,1,0:T(8,128)(2,1)S(1)} %add_convert_fusion), channel_id=1, replica_groups={{0,2,4,6,8,10,12,14,16,18,20,22,24,26,28,30},{1,3,5,7,9,11,13,15,17,19,..., dimensions={0} | all-to-all | bytes 4194304 | tf_op jit(solution)/shard_map/all_to_all | solution.py:251
  78.9 1.8 %shard_map.96 = (bf16[256,256]{1,0:T(8,128)(2,1)}, bf16[16,256,256]{2,1,0:T(8,128)(2,1)S(1)}, f32[32,256]{1,0:T(8,128)S(1)}, f32[32,256]{1,0:T(8,128)S(1)}, f32[...) custom-call(s32[2]{0:T(128)S(1)} %pad_add_fusion.place, ...), custom_call_target="tpu_custom_call" | custom-call | flops 100663296 | bytes 5242880 | tf_op jit(solution)/shard_map/pallas_call | solution.py:254
  80.7 1.4 copy-done
  82.1 3.7 %all-to-all-start.1 = ((bf16[16,256,256]{2,1,0:T(8,128)(2,1)}), bf16[16,256,256]{2,1,0:T(8,128)(2,1)S(1)}, u32[]{:S(2)}, u32[]{:S(2)}) async-start(bf16[16,256,256]{2,1,0:T(8,128)(2,1)} %copy-done), calls=%async_computation.1 | async-start | bytes 4194304 | tf_op jit(solution)/shard_map/all_to_all | solution.py:270
  85.8 4.7 %collective-permute-start.8 = (f32[32,256]{1,0:T(8,128)S(1)}, f32[32,256]{1,0:T(8,128)S(1)}, u32[]{:S(2)}, u32[]{:S(2)}) collective-permute-start(f32[32,256]{1,0:T(8,128)S(1)} %get-tuple-element.32), channel_id=1, source_target_pairs={{0,128},{32,160},{64,192},{96,224},{128,0},{160,32},{192,64},{224,... | collective-permute-start | bytes 98312 | tf_op jit(solution)/shard_map/ppermute | solution.py:271
  90.6 3.2 %collective-permute-start.10 = (f32[32,256]{1,0:T(8,128)S(1)}, f32[32,256]{1,0:T(8,128)S(1)}, u32[]{:S(2)}, u32[]{:S(2)}) collective-permute-start(f32[32,256]{1,0:T(8,128)S(1)} %get-tuple-element.34), channel_id=1, source_target_pairs={{0,96},{32,128},{64,160},{96,192},{128,224},{160,0},{192,32},{224,... | collective-permute-start | bytes 98312 | tf_op jit(solution)/shard_map/ppermute | solution.py:271
  93.7 1.7 collective-permute-start.11
  95.4 0.7 collective-permute-start.12
  96.1 2.7 %collective-permute-start.13 = (f32[32,256]{1,0:T(8,128)S(1)}, f32[32,256]{1,0:T(8,128)S(1)}, u32[]{:S(2)}, u32[]{:S(2)}) collective-permute-start(f32[32,256]{1,0:T(8,128)S(1)} %get-tuple-element.37), channel_id=1, source_target_pairs={{0,224},{32,0},{64,32},{96,64},{128,96},{160,128},{192,160},{224,1... | collective-permute-start | bytes 98312 | tf_op jit(solution)/shard_map/ppermute | solution.py:271
  98.8 1.8 %collective-permute-done.12 = f32[32,256]{1,0:T(8,128)S(1)} collective-permute-done((f32[32,256]{1,0:T(8,128)S(1)}, f32[32,256]{1,0:T(8,128)S(1)}, u32[]{:S(2)}, u32[]{:S(2)}) %collective-permute-start.12) | collective-permute-done | bytes 32800 | tf_op jit(solution)/shard_map/ppermute | solution.py:271
  100.6 2.5 %collective-permute-done.14 = f32[32,256]{1,0:T(8,128)S(1)} collective-permute-done((f32[32,256]{1,0:T(8,128)S(1)}, f32[32,256]{1,0:T(8,128)S(1)}, u32[]{:S(2)}, u32[]{:S(2)}) %collective-permute-start.14) | collective-permute-done | bytes 32800 | tf_op jit(solution)/shard_map/ppermute | solution.py:271
  103.1 4.4 %collective-permute-start.15 = (f32[32,256]{1,0:T(8,128)S(1)}, f32[32,256]{1,0:T(8,128)S(1)}, u32[]{:S(2)}, u32[]{:S(2)}) collective-permute-start(f32[32,256]{1,0:T(8,128)S(1)} %add_add_fusion.2), channel_id=1, source_target_pairs={{0,1},{1,0},{2,3},{3,2},{4,5},{5,4},{6,7},{7,6},{8,9},{9,8},{10,11... | collective-permute-start | bytes 98312 | tf_op jit(solution)/shard_map/ppermute | solution.py:190
  107.5 0.9 collective-permute-done.15
  108.3 2.7 %collective-permute-start.18 = (f32[32,256]{1,0:T(8,128)S(1)}, f32[32,256]{1,0:T(8,128)S(1)}, u32[]{:S(2)}, u32[]{:S(2)}) collective-permute-start(f32[32,256]{1,0:T(8,128)S(1)} %add.58), channel_id=1, source_target_pairs={{0,6},{1,7},{2,4},{3,5},{4,2},{5,3},{6,0},{7,1},{8,14},{9,15},{10,... | collective-permute-start | bytes 98312 | tf_op jit(solution)/shard_map/ppermute | solution.py:190
  111.0 0.6 collective-permute-start.17
  111.7 0.6 collective-permute-done.18
  112.3 3.6 %collective-permute-done.17 = f32[32,256]{1,0:T(8,128)S(1)} collective-permute-done((f32[32,256]{1,0:T(8,128)S(1)}, f32[32,256]{1,0:T(8,128)S(1)}, u32[]{:S(2)}, u32[]{:S(2)}) %collective-permute-start.17) | collective-permute-done | bytes 32800 | tf_op jit(solution)/shard_map/ppermute | solution.py:190
  116.0 2.2 %collective-permute-start.21 = (f32[32,256]{1,0:T(8,128)S(1)}, f32[32,256]{1,0:T(8,128)S(1)}, u32[]{:S(2)}, u32[]{:S(2)}) collective-permute-start(f32[32,256]{1,0:T(8,128)S(1)} %add_add_fusion.1), channel_id=1, source_target_pairs={{0,24},{1,25},{2,26},{3,27},{4,28},{5,29},{6,30},{7,31},{8,16},{9,... | collective-permute-start | bytes 98312 | tf_op jit(solution)/shard_map/ppermute | solution.py:190
  118.7 0.6 collective-permute-start.19
  119.3 0.7 collective-permute-done.21
  120.0 2.4 %collective-permute-done.20 = f32[32,256]{1,0:T(8,128)S(1)} collective-permute-done((f32[32,256]{1,0:T(8,128)S(1)}, f32[32,256]{1,0:T(8,128)S(1)}, u32[]{:S(2)}, u32[]{:S(2)}) %collective-permute-start.20) | collective-permute-done | bytes 32800 | tf_op jit(solution)/shard_map/ppermute | solution.py:190
  122.5 3.0 %collective-permute-start.22 = (bf16[16,256,256]{2,1,0:T(8,128)(2,1)S(1)}, bf16[16,256,256]{2,1,0:T(8,128)(2,1)S(1)}, u32[]{:S(2)}, u32[]{:S(2)}) collective-permute-start(bf16[16,256,256]{2,1,0:T(8,128)(2,1)S(1)} %all-to-all-done.1.same), channel_id=1, source_target_pairs={{0,1},{1,0},{2,3},{3,2},{4,5},{5,4},{6,7},{7,6},{8,9},{9,8},{10,11... | collective-permute-start | bytes 6291464 | tf_op jit(solution)/shard_map/ppermute | solution.py:279
  125.5 3.8 %collective-permute-done.22.other = bf16[16,256,256]{2,1,0:T(8,128)(2,1)S(1)} collective-permute-done((bf16[16,256,256]{2,1,0:T(8,128)(2,1)S(1)}, bf16[16,256,256]{2,1,0:T(8,128)(2,1)S(1)}, u32[]{:S(2)}, u32[]{:S(2)}) %collective-permute-start.22) | collective-permute-done | bytes 2097184 | tf_op jit(solution)/shard_map/ppermute | solution.py:279
  129.2 6.8 %shard_map.97 = (bf16[320,256]{1,0:T(8,128)(2,1)S(1)}, bf16[320,256]{1,0:T(8,128)(2,1)S(1)}, bf16[320,256]{1,0:T(8,128)(2,1)S(1)}, bf16[320,256]{1,0:T(8,128)(2,...) custom-call(s32[2]{0:T(128)S(1)} %pad_add_fusion.place, ...), custom_call_target="tpu_custom_call" | custom-call | flops 1610612736 | bytes 11534336 | tf_op jit(solution)/shard_map/pallas_call | solution.py:281
  136.2 2.7 %collective-permute-start.24 = (bf16[320,256]{1,0:T(8,128)(2,1)S(1)}, bf16[320,256]{1,0:T(8,128)(2,1)S(1)}, u32[]{:S(2)}, u32[]{:S(2)}) collective-permute-start(bf16[320,256]{1,0:T(8,128)(2,1)S(1)} %get-tuple-element.43), channel_id=1, source_target_pairs={{0,224},{32,0},{64,32},{96,64},{128,96},{160,128},{192,160},{224,1... | collective-permute-start | bytes 491528 | tf_op jit(solution)/shard_map/ppermute | solution.py:301
  138.8 3.6 %collective-permute-start.26 = (bf16[320,256]{1,0:T(8,128)(2,1)S(1)}, bf16[320,256]{1,0:T(8,128)(2,1)S(1)}, u32[]{:S(2)}, u32[]{:S(2)}) collective-permute-start(bf16[320,256]{1,0:T(8,128)(2,1)S(1)} %get-tuple-element.45), channel_id=1, source_target_pairs={{0,192},{32,224},{64,0},{96,32},{128,64},{160,96},{192,128},{224,1... | collective-permute-start | bytes 491528 | tf_op jit(solution)/shard_map/ppermute | solution.py:301
  142.8 4.1 %collective-permute-start.28 = (bf16[320,256]{1,0:T(8,128)(2,1)S(1)}, bf16[320,256]{1,0:T(8,128)(2,1)S(1)}, u32[]{:S(2)}, u32[]{:S(2)}) collective-permute-start(bf16[320,256]{1,0:T(8,128)(2,1)S(1)} %get-tuple-element.47), channel_id=1, source_target_pairs={{0,160},{32,192},{64,224},{96,0},{128,32},{160,64},{192,96},{224,1... | collective-permute-start | bytes 491528 | tf_op jit(solution)/shard_map/ppermute | solution.py:301
  146.9 1.6 collective-permute-start.29
  148.5 0.7 collective-permute-done.25.refs_3_
  149.2 1.1 collective-permute-done.26.refs_4_
  150.4 7.5 %collective-permute-done.27.refs_5_ = bf16[320,256]{1,0:T(8,128)(2,1)S(1)} collective-permute-done((bf16[320,256]{1,0:T(8,128)(2,1)S(1)}, bf16[320,256]{1,0:T(8,128)(2,1)S(1)}, u32[]{:S(2)}, u32[]{:S(2)}) %collective-permute-start.27) | collective-permute-done | bytes 163872 | tf_op jit(solution)/shard_map/ppermute | solution.py:301
  157.9 8.8 %collective-permute-done.28.refs_6_ = bf16[320,256]{1,0:T(8,128)(2,1)S(1)} collective-permute-done((bf16[320,256]{1,0:T(8,128)(2,1)S(1)}, bf16[320,256]{1,0:T(8,128)(2,1)S(1)}, u32[]{:S(2)}, u32[]{:S(2)}) %collective-permute-start.28) | collective-permute-done | bytes 163872 | tf_op jit(solution)/shard_map/ppermute | solution.py:301
  166.7 1.4 shard_map.98
  (32 shorter events, 1.3 us)
Async XLA Ops:
  1.6 13.5 %collective-permute-start.6 = (bf16[2,128,256]{2,1,0:T(8,128)(2,1)S(1)}, bf16[2,128,256]{2,1,0:T(8,128)(2,1)S(1)}, u32[]{:S(2)}, u32[]{:S(2)}) collective-permute-start(bf16[2,128,256]{2,1,0:T(8,128)(2,1)S(1)} %shard_map.94.refs_0_), channel_id=1, source_target_pairs={{0,128},{32,160},{64,192},{96,224},{128,0},{160,32},{192,64},{224,... | collective-permute-start | bytes 393224 | tf_op jit(solution)/shard_map/ppermute | solution.py:225
  9.4 15.4 %collective-permute-start.5 = (bf16[2,128,256]{2,1,0:T(8,128)(2,1)S(1)}, bf16[2,128,256]{2,1,0:T(8,128)(2,1)S(1)}, u32[]{:S(2)}, u32[]{:S(2)}) collective-permute-start(bf16[2,128,256]{2,1,0:T(8,128)(2,1)S(1)} %shard_map.94.refs_0_), channel_id=1, source_target_pairs={{0,160},{32,192},{64,224},{96,0},{128,32},{160,64},{192,96},{224,1... | collective-permute-start | bytes 393224 | tf_op jit(solution)/shard_map/ppermute | solution.py:225
  9.4 19.4 %collective-permute-start.4 = (bf16[2,128,256]{2,1,0:T(8,128)(2,1)S(1)}, bf16[2,128,256]{2,1,0:T(8,128)(2,1)S(1)}, u32[]{:S(2)}, u32[]{:S(2)}) collective-permute-start(bf16[2,128,256]{2,1,0:T(8,128)(2,1)S(1)} %shard_map.94.refs_0_), channel_id=1, source_target_pairs={{0,96},{32,128},{64,160},{96,192},{128,224},{160,0},{192,32},{224,... | collective-permute-start | bytes 393224 | tf_op jit(solution)/shard_map/ppermute | solution.py:225
  12.6 18.0 %collective-permute-start.3 = (bf16[2,128,256]{2,1,0:T(8,128)(2,1)S(1)}, bf16[2,128,256]{2,1,0:T(8,128)(2,1)S(1)}, u32[]{:S(2)}, u32[]{:S(2)}) collective-permute-start(bf16[2,128,256]{2,1,0:T(8,128)(2,1)S(1)} %shard_map.94.refs_0_), channel_id=1, source_target_pairs={{0,192},{32,224},{64,0},{96,32},{128,64},{160,96},{192,128},{224,1... | collective-permute-start | bytes 393224 | tf_op jit(solution)/shard_map/ppermute | solution.py:225
  13.4 17.2 %collective-permute-start.2 = (bf16[2,128,256]{2,1,0:T(8,128)(2,1)S(1)}, bf16[2,128,256]{2,1,0:T(8,128)(2,1)S(1)}, u32[]{:S(2)}, u32[]{:S(2)}) collective-permute-start(bf16[2,128,256]{2,1,0:T(8,128)(2,1)S(1)} %shard_map.94.refs_0_), channel_id=1, source_target_pairs={{0,64},{32,96},{64,128},{96,160},{128,192},{160,224},{192,0},{224,... | collective-permute-start | bytes 393224 | tf_op jit(solution)/shard_map/ppermute | solution.py:225
  15.1 17.7 %collective-permute-start.1 = (bf16[2,128,256]{2,1,0:T(8,128)(2,1)S(1)}, bf16[2,128,256]{2,1,0:T(8,128)(2,1)S(1)}, u32[]{:S(2)}, u32[]{:S(2)}) collective-permute-start(bf16[2,128,256]{2,1,0:T(8,128)(2,1)S(1)} %shard_map.94.refs_0_), channel_id=1, source_target_pairs={{0,224},{32,0},{64,32},{96,64},{128,96},{160,128},{192,160},{224,1... | collective-permute-start | bytes 393224 | tf_op jit(solution)/shard_map/ppermute | solution.py:225
  24.8 8.0 %collective-permute-start = (bf16[2,128,256]{2,1,0:T(8,128)(2,1)S(1)}, bf16[2,128,256]{2,1,0:T(8,128)(2,1)S(1)}, u32[]{:S(2)}, u32[]{:S(2)}) collective-permute-start(bf16[2,128,256]{2,1,0:T(8,128)(2,1)S(1)} %shard_map.94.refs_0_), channel_id=1, source_target_pairs={{0,32},{32,64},{64,96},{96,128},{128,160},{160,192},{192,224},{224... | collective-permute-start | bytes 393224 | tf_op jit(solution)/shard_map/ppermute | solution.py:225
  41.0 5.4 %collective-permute-start.7 = (bf16[16,256,256]{2,1,0:T(8,128)(2,1)S(1)}, bf16[16,256,256]{2,1,0:T(8,128)(2,1)S(1)}, u32[]{:S(2)}, u32[]{:S(2)}) collective-permute-start(bf16[16,256,256]{2,1,0:T(8,128)(2,1)S(1)} %get-tuple-element.28), channel_id=1, source_target_pairs={{0,1},{1,0},{2,3},{3,2},{4,5},{5,4},{6,7},{7,6},{8,9},{9,8},{10,11... | collective-permute-start | bytes 6291464 | tf_op jit(solution)/shard_map/ppermute | solution.py:249
  47.0 31.8 %copy-start.1 = (bf16[256,256]{1,0:T(8,128)(2,1)S(1)}, bf16[256,256]{1,0:T(8,128)(2,1)}, u32[]{:S(2)}) copy-start(bf16[256,256]{1,0:T(8,128)(2,1)} %weight.1) | copy-start | bytes 393220
  47.0 31.8 %copy-start.2 = (bf16[256,256]{1,0:T(8,128)(2,1)S(1)}, bf16[256,256]{1,0:T(8,128)(2,1)}, u32[]{:S(2)}) copy-start(bf16[256,256]{1,0:T(8,128)(2,1)} %cotangent.1) | copy-start | bytes 393220
  80.7 1.4 copy-start
  82.1 40.4 %all-to-all-start.1 = ((bf16[16,256,256]{2,1,0:T(8,128)(2,1)}), bf16[16,256,256]{2,1,0:T(8,128)(2,1)S(1)}, u32[]{:S(2)}, u32[]{:S(2)}) async-start(bf16[16,256,256]{2,1,0:T(8,128)(2,1)} %copy-done), calls=%async_computation.1 | async-start | bytes 4194304 | tf_op jit(solution)/shard_map/all_to_all | solution.py:270
  85.8 10.3 %collective-permute-start.8 = (f32[32,256]{1,0:T(8,128)S(1)}, f32[32,256]{1,0:T(8,128)S(1)}, u32[]{:S(2)}, u32[]{:S(2)}) collective-permute-start(f32[32,256]{1,0:T(8,128)S(1)} %get-tuple-element.32), channel_id=1, source_target_pairs={{0,128},{32,160},{64,192},{96,224},{128,0},{160,32},{192,64},{224,... | collective-permute-start | bytes 98312 | tf_op jit(solution)/shard_map/ppermute | solution.py:271
  90.5 8.3 %collective-permute-start.9 = (f32[32,256]{1,0:T(8,128)S(1)}, f32[32,256]{1,0:T(8,128)S(1)}, u32[]{:S(2)}, u32[]{:S(2)}) collective-permute-start(f32[32,256]{1,0:T(8,128)S(1)} %get-tuple-element.33), channel_id=1, source_target_pairs={{0,160},{32,192},{64,224},{96,0},{128,32},{160,64},{192,96},{224,1... | collective-permute-start | bytes 98312 | tf_op jit(solution)/shard_map/ppermute | solution.py:271
  90.6 8.2 %collective-permute-start.10 = (f32[32,256]{1,0:T(8,128)S(1)}, f32[32,256]{1,0:T(8,128)S(1)}, u32[]{:S(2)}, u32[]{:S(2)}) collective-permute-start(f32[32,256]{1,0:T(8,128)S(1)} %get-tuple-element.34), channel_id=1, source_target_pairs={{0,96},{32,128},{64,160},{96,192},{128,224},{160,0},{192,32},{224,... | collective-permute-start | bytes 98312 | tf_op jit(solution)/shard_map/ppermute | solution.py:271
  93.7 5.1 %collective-permute-start.11 = (f32[32,256]{1,0:T(8,128)S(1)}, f32[32,256]{1,0:T(8,128)S(1)}, u32[]{:S(2)}, u32[]{:S(2)}) collective-permute-start(f32[32,256]{1,0:T(8,128)S(1)} %get-tuple-element.35), channel_id=1, source_target_pairs={{0,192},{32,224},{64,0},{96,32},{128,64},{160,96},{192,128},{224,1... | collective-permute-start | bytes 98312 | tf_op jit(solution)/shard_map/ppermute | solution.py:271
  95.4 5.2 %collective-permute-start.12 = (f32[32,256]{1,0:T(8,128)S(1)}, f32[32,256]{1,0:T(8,128)S(1)}, u32[]{:S(2)}, u32[]{:S(2)}) collective-permute-start(f32[32,256]{1,0:T(8,128)S(1)} %get-tuple-element.36), channel_id=1, source_target_pairs={{0,64},{32,96},{64,128},{96,160},{128,192},{160,224},{192,0},{224,... | collective-permute-start | bytes 98312 | tf_op jit(solution)/shard_map/ppermute | solution.py:271
  96.1 4.5 %collective-permute-start.13 = (f32[32,256]{1,0:T(8,128)S(1)}, f32[32,256]{1,0:T(8,128)S(1)}, u32[]{:S(2)}, u32[]{:S(2)}) collective-permute-start(f32[32,256]{1,0:T(8,128)S(1)} %get-tuple-element.37), channel_id=1, source_target_pairs={{0,224},{32,0},{64,32},{96,64},{128,96},{160,128},{192,160},{224,1... | collective-permute-start | bytes 98312 | tf_op jit(solution)/shard_map/ppermute | solution.py:271
  98.8 4.3 %collective-permute-start.14 = (f32[32,256]{1,0:T(8,128)S(1)}, f32[32,256]{1,0:T(8,128)S(1)}, u32[]{:S(2)}, u32[]{:S(2)}) collective-permute-start(f32[32,256]{1,0:T(8,128)S(1)} %get-tuple-element.38), channel_id=1, source_target_pairs={{0,32},{32,64},{64,96},{96,128},{128,160},{160,192},{192,224},{224... | collective-permute-start | bytes 98312 | tf_op jit(solution)/shard_map/ppermute | solution.py:271
  103.1 5.3 %collective-permute-start.15 = (f32[32,256]{1,0:T(8,128)S(1)}, f32[32,256]{1,0:T(8,128)S(1)}, u32[]{:S(2)}, u32[]{:S(2)}) collective-permute-start(f32[32,256]{1,0:T(8,128)S(1)} %add_add_fusion.2), channel_id=1, source_target_pairs={{0,1},{1,0},{2,3},{3,2},{4,5},{5,4},{6,7},{7,6},{8,9},{9,8},{10,11... | collective-permute-start | bytes 98312 | tf_op jit(solution)/shard_map/ppermute | solution.py:190
  108.3 4.0 %collective-permute-start.18 = (f32[32,256]{1,0:T(8,128)S(1)}, f32[32,256]{1,0:T(8,128)S(1)}, u32[]{:S(2)}, u32[]{:S(2)}) collective-permute-start(f32[32,256]{1,0:T(8,128)S(1)} %add.58), channel_id=1, source_target_pairs={{0,6},{1,7},{2,4},{3,5},{4,2},{5,3},{6,0},{7,1},{8,14},{9,15},{10,... | collective-permute-start | bytes 98312 | tf_op jit(solution)/shard_map/ppermute | solution.py:190
  111.0 4.9 %collective-permute-start.17 = (f32[32,256]{1,0:T(8,128)S(1)}, f32[32,256]{1,0:T(8,128)S(1)}, u32[]{:S(2)}, u32[]{:S(2)}) collective-permute-start(f32[32,256]{1,0:T(8,128)S(1)} %add.58), channel_id=1, source_target_pairs={{0,4},{1,5},{2,6},{3,7},{4,0},{5,1},{6,2},{7,3},{8,12},{9,13},{10,... | collective-permute-start | bytes 98312 | tf_op jit(solution)/shard_map/ppermute | solution.py:190
  111.6 4.4 %collective-permute-start.16 = (f32[32,256]{1,0:T(8,128)S(1)}, f32[32,256]{1,0:T(8,128)S(1)}, u32[]{:S(2)}, u32[]{:S(2)}) collective-permute-start(f32[32,256]{1,0:T(8,128)S(1)} %add.58), channel_id=1, source_target_pairs={{0,2},{1,3},{2,0},{3,1},{4,6},{5,7},{6,4},{7,5},{8,10},{9,11},{10,... | collective-permute-start | bytes 98312 | tf_op jit(solution)/shard_map/ppermute | solution.py:190
  116.0 4.1 %collective-permute-start.21 = (f32[32,256]{1,0:T(8,128)S(1)}, f32[32,256]{1,0:T(8,128)S(1)}, u32[]{:S(2)}, u32[]{:S(2)}) collective-permute-start(f32[32,256]{1,0:T(8,128)S(1)} %add_add_fusion.1), channel_id=1, source_target_pairs={{0,24},{1,25},{2,26},{3,27},{4,28},{5,29},{6,30},{7,31},{8,16},{9,... | collective-permute-start | bytes 98312 | tf_op jit(solution)/shard_map/ppermute | solution.py:190
  118.2 4.3 %collective-permute-start.20 = (f32[32,256]{1,0:T(8,128)S(1)}, f32[32,256]{1,0:T(8,128)S(1)}, u32[]{:S(2)}, u32[]{:S(2)}) collective-permute-start(f32[32,256]{1,0:T(8,128)S(1)} %add_add_fusion.1), channel_id=1, source_target_pairs={{0,16},{1,17},{2,18},{3,19},{4,20},{5,21},{6,22},{7,23},{8,24},{9,... | collective-permute-start | bytes 98312 | tf_op jit(solution)/shard_map/ppermute | solution.py:190
  118.7 3.8 %collective-permute-start.19 = (f32[32,256]{1,0:T(8,128)S(1)}, f32[32,256]{1,0:T(8,128)S(1)}, u32[]{:S(2)}, u32[]{:S(2)}) collective-permute-start(f32[32,256]{1,0:T(8,128)S(1)} %add_add_fusion.1), channel_id=1, source_target_pairs={{0,8},{1,9},{2,10},{3,11},{4,12},{5,13},{6,14},{7,15},{8,0},{9,1},... | collective-permute-start | bytes 98312 | tf_op jit(solution)/shard_map/ppermute | solution.py:190
  122.5 6.8 %collective-permute-start.22 = (bf16[16,256,256]{2,1,0:T(8,128)(2,1)S(1)}, bf16[16,256,256]{2,1,0:T(8,128)(2,1)S(1)}, u32[]{:S(2)}, u32[]{:S(2)}) collective-permute-start(bf16[16,256,256]{2,1,0:T(8,128)(2,1)S(1)} %all-to-all-done.1.same), channel_id=1, source_target_pairs={{0,1},{1,0},{2,3},{3,2},{4,5},{5,4},{6,7},{7,6},{8,9},{9,8},{10,11... | collective-permute-start | bytes 6291464 | tf_op jit(solution)/shard_map/ppermute | solution.py:279
  136.1 6.7 %collective-permute-start.23 = (bf16[320,256]{1,0:T(8,128)(2,1)S(1)}, bf16[320,256]{1,0:T(8,128)(2,1)S(1)}, u32[]{:S(2)}, u32[]{:S(2)}) collective-permute-start(bf16[320,256]{1,0:T(8,128)(2,1)S(1)} %get-tuple-element.42), channel_id=1, source_target_pairs={{0,32},{32,64},{64,96},{96,128},{128,160},{160,192},{192,224},{224... | collective-permute-start | bytes 491528 | tf_op jit(solution)/shard_map/ppermute | solution.py:301
  136.2 10.7 %collective-permute-start.24 = (bf16[320,256]{1,0:T(8,128)(2,1)S(1)}, bf16[320,256]{1,0:T(8,128)(2,1)S(1)}, u32[]{:S(2)}, u32[]{:S(2)}) collective-permute-start(bf16[320,256]{1,0:T(8,128)(2,1)S(1)} %get-tuple-element.43), channel_id=1, source_target_pairs={{0,224},{32,0},{64,32},{96,64},{128,96},{160,128},{192,160},{224,1... | collective-permute-start | bytes 491528 | tf_op jit(solution)/shard_map/ppermute | solution.py:301
  138.8 10.4 %collective-permute-start.25 = (bf16[320,256]{1,0:T(8,128)(2,1)S(1)}, bf16[320,256]{1,0:T(8,128)(2,1)S(1)}, u32[]{:S(2)}, u32[]{:S(2)}) collective-permute-start(bf16[320,256]{1,0:T(8,128)(2,1)S(1)} %get-tuple-element.44), channel_id=1, source_target_pairs={{0,64},{32,96},{64,128},{96,160},{128,192},{160,224},{192,0},{224,... | collective-permute-start | bytes 491528 | tf_op jit(solution)/shard_map/ppermute | solution.py:301
  138.8 11.5 %collective-permute-start.26 = (bf16[320,256]{1,0:T(8,128)(2,1)S(1)}, bf16[320,256]{1,0:T(8,128)(2,1)S(1)}, u32[]{:S(2)}, u32[]{:S(2)}) collective-permute-start(bf16[320,256]{1,0:T(8,128)(2,1)S(1)} %get-tuple-element.45), channel_id=1, source_target_pairs={{0,192},{32,224},{64,0},{96,32},{128,64},{160,96},{192,128},{224,1... | collective-permute-start | bytes 491528 | tf_op jit(solution)/shard_map/ppermute | solution.py:301
  142.4 15.5 %collective-permute-start.27 = (bf16[320,256]{1,0:T(8,128)(2,1)S(1)}, bf16[320,256]{1,0:T(8,128)(2,1)S(1)}, u32[]{:S(2)}, u32[]{:S(2)}) collective-permute-start(bf16[320,256]{1,0:T(8,128)(2,1)S(1)} %get-tuple-element.46), channel_id=1, source_target_pairs={{0,96},{32,128},{64,160},{96,192},{128,224},{160,0},{192,32},{224,... | collective-permute-start | bytes 491528 | tf_op jit(solution)/shard_map/ppermute | solution.py:301
  142.8 23.9 %collective-permute-start.28 = (bf16[320,256]{1,0:T(8,128)(2,1)S(1)}, bf16[320,256]{1,0:T(8,128)(2,1)S(1)}, u32[]{:S(2)}, u32[]{:S(2)}) collective-permute-start(bf16[320,256]{1,0:T(8,128)(2,1)S(1)} %get-tuple-element.47), channel_id=1, source_target_pairs={{0,160},{32,192},{64,224},{96,0},{128,32},{160,64},{192,96},{224,1... | collective-permute-start | bytes 491528 | tf_op jit(solution)/shard_map/ppermute | solution.py:301
  146.9 19.8 %collective-permute-start.29 = (bf16[320,256]{1,0:T(8,128)(2,1)S(1)}, bf16[320,256]{1,0:T(8,128)(2,1)S(1)}, u32[]{:S(2)}, u32[]{:S(2)}) collective-permute-start(bf16[320,256]{1,0:T(8,128)(2,1)S(1)} %get-tuple-element.48), channel_id=1, source_target_pairs={{0,128},{32,160},{64,192},{96,224},{128,0},{160,32},{192,64},{224,... | collective-permute-start | bytes 491528 | tf_op jit(solution)/shard_map/ppermute | solution.py:301

commit v8 on v6

--- a/solution.py
+++ b/solution.py
@@ -136,7 +136,7 @@
     copy.wait()
 
 
-def dense_kernel(parts, weight, cotangent, activated, grad_agg):
+def dense_kernel(parts, weight, cotangent, activated, grad_agg, local_weight):
     total = parts[0].astype(F32)
     for chip in range(1, parts.shape[0]):
         total += parts[chip].astype(F32)
@@ -145,29 +145,38 @@
     sigma = jax.nn.sigmoid(pre)
     activated[...] = (pre * sigma).astype(BF16)
     grad_pre = (cotangent[...].astype(F32) * sigma * (1.0 + pre * (1.0 - sigma))).astype(BF16)
-    local_weight = lax.dot_general(
-        aggregated, grad_pre, (((0,), (0,)), ((), ())), preferred_element_type=F32
-    ).astype(BF16)
     grad = lax.dot_general(
         grad_pre, weight[...], (((1,), (1,)), ((), ())), preferred_element_type=F32
     ).astype(BF16)
-    nodes = grad.shape[0]
-    strip = grad_agg.shape[1] - nodes
     for chip in range(grad_agg.shape[0]):
-        grad_agg[chip, :nodes] = grad
-        grad_agg[chip, nodes:] = local_weight[chip * strip : (chip + 1) * strip]
+        grad_agg[chip] = grad
+    local_weight[...] = lax.dot_general(
+        aggregated, grad_pre, (((0,), (0,)), ((), ())), preferred_element_type=F32
+    )
 
 
 def turn(size, step):
     return [(i, (i + step) % size) for i in range(size)]
 
 
-def add_partners(value, size, distances):
+def add_partners(value, axis, size, distances):
     for other in [
-        lax.ppermute(value, "row", [(i, i ^ distance) for i in range(size)])
+        lax.ppermute(value, axis, [(i, i ^ distance) for i in range(size)])
         for distance in distances
     ]:
         value = value + other
+    return value
+
+
+def sum_halves(value, axis, size, index):
+    distance = size // 2
+    while distance:
+        half = value.shape[0] // 2
+        upper = (index // distance) % 2 == 1
+        sent = jnp.where(upper, value[:half], value[half:])
+        kept = jnp.where(upper, value[half:], value[:half])
+        value = kept + lax.ppermute(sent, axis, [(i, i ^ distance) for i in range(size)])
+        distance //= 2
     return value
 
 
@@ -227,15 +236,16 @@
     shares = (keep + arrived.astype(F32)).astype(BF16)
     parts = lax.all_to_all(shares, "col", 0, 0, tiled=True, axis_index_groups=same_core)
 
-    strip = width // chips
-    activated, grad_agg = pl.pallas_call(
+    rows_strip = width // n_row
+    activated, grad_agg, local_weight = pl.pallas_call(
         dense_kernel,
         out_shape=(
             jax.ShapeDtypeStruct((nodes, width), BF16),
-            jax.ShapeDtypeStruct((chips, nodes + strip, width), BF16),
+            jax.ShapeDtypeStruct((chips, nodes, width), BF16),
+            jax.ShapeDtypeStruct((width, width), F32),
         ),
         in_specs=[vmem] * 3,
-        out_specs=(vmem,) * 2,
+        out_specs=(vmem,) * 3,
         compiler_params=pltpu.CompilerParams(vmem_limit_bytes=24 * MIB),
         cost_estimate=pl.CostEstimate(
             flops=6 * nodes * width * width, bytes_accessed=5 * MIB, transcendentals=nodes * width
@@ -243,11 +253,15 @@
     )(parts, weight, cotangent)
 
     same = lax.all_to_all(grad_agg, "col", 0, 0, tiled=True, axis_index_groups=same_core)
+    strip = sum_halves(local_weight, "row", n_row, lax.axis_index("row"))
+    strip = add_partners(strip, "col", n_col, [1])
+    strip = add_partners(strip, "col", n_col, [2, 4, 6])
+    strip = add_partners(strip, "col", n_col, [8, 16, 24])
+    same, strip = lax.optimization_barrier((same, strip))
     other = lax.ppermute(same, "col", swap)
-    strips = jnp.sum(same[:, nodes:].astype(F32), axis=0)
-    strips = add_partners(strips, n_row, [1])
-    same, other, strips = lax.optimization_barrier((same, other, strips))
-    strips = add_partners(strips, n_row, range(2, n_row, 2))
+    copies = jnp.broadcast_to(strip[None], (n_row, rows_strip, width))
+    every = lax.all_to_all(copies, "row", 0, 0, tiled=True)
+    grad_weight = every.reshape(width, width)
 
     shares = pl.pallas_call(
         functools.partial(backward_kernel, chunk, steps),
@@ -258,7 +272,7 @@
             pltpu.SMEM((slots,), jnp.int32),
             pltpu.SMEM((slots,), jnp.int32),
             pltpu.VMEM((slots, side, side), BF16),
-            pltpu.VMEM((2, chips, nodes + strip, width), BF16),
+            pltpu.VMEM((2, chips, nodes, width), BF16),
             pltpu.VMEM((here * n_row + 1, side, width), F32),
             pltpu.SemaphoreType.DMA((2,)),
             pltpu.SemaphoreType.DMA((slots // chunk,)),
@@ -268,21 +282,11 @@
         cost_estimate=pl.CostEstimate(flops=work, bytes_accessed=11 * MIB, transcendentals=0),
     )(*scalars, values, same, other)
 
-    shares, strips = lax.optimization_barrier((shares, strips))
-    order = list(zip(steps, shares))[::-1]
-    far, close, own_share = order[: n_row // 2], order[n_row // 2 : -1], shares[0]
-    moved = [lax.ppermute(share, "row", turn(n_row, step)) for step, share in far]
-    copies = jnp.broadcast_to(strips[None], (n_col, strip, width))
-    every = lax.all_to_all(copies, "col", 0, 0, tiled=True)
-    every, held = lax.optimization_barrier((every, [share for unused, share in close]))
-    moved += [
-        lax.ppermute(share, "row", turn(n_row, step)) for (step, unused), share in zip(close, held)
-    ]
-    total = own_share.astype(F32)
-    for share in moved:
-        total += share.astype(F32)
+    *shares, grad_weight = lax.optimization_barrier((*shares, grad_weight))
+    total = shares[0].astype(F32)
+    for step, share in list(zip(steps, shares))[:0:-1]:
+        total += lax.ppermute(share, "row", turn(n_row, step)).astype(F32)
     grad_features = total.astype(BF16).reshape(1, nodes, width)
-    grad_weight = jnp.sum(every.reshape(chips, 2, strip, width), axis=1).reshape(width, width)
     return (activated, grad_weight, grad_features)
 
 

time: 167 us -> 179 us (1.072)
  the two profiles are of different devices: /device:TPU:1 before, /device:TPU:33 now
where the time goes in v8:
time: 179 us; the launch traced here: 178 us
  waiting for transfers between devices  94.2 us (53%)
  starting transfers between devices  65 us (36%)
  Pallas kernels  12 us (7%)
  other arithmetic  3.03 us (2%)
  local copies, waits for them, and re-layouts  2.79 us (2%)
    all_to_all x1, waiting for transfers between devices, per_device(): lax.all_to_all(shares, 'col', 0, 0, tiled=True, axis_index_groups=same_core)  32 us
    ppermute x7, waiting for transfers between devices, per_device(): total += lax.ppermute(share, 'row', turn(n_row, step)).astype(F32)  17 us
    ppermute x7, starting transfers between devices, per_device(): lax.ppermute(own, 'row', turn(n_row, k))  15.6 us
    ppermute x7, waiting for transfers between devices, per_device(): lax.ppermute(own, 'row', turn(n_row, k))  15.6 us
    ppermute x7, starting transfers between devices, per_device(): total += lax.ppermute(share, 'row', turn(n_row, step)).astype(F32)  13.8 us
    ppermute x3, waiting for transfers between devices, sum_halves(): lax.ppermute(sent, axis, [(i, i ^ distance) for i in range(size)])  12.7 us
    ppermute x7, starting transfers between devices, add_partners(): lax.ppermute(value, axis, [(i, i ^ distance) for i in range(size)])  9.93 us
    ppermute x7, waiting for transfers between devices, add_partners(): lax.ppermute(value, axis, [(i, i ^ distance) for i in range(size)])  8.18 us
  transfers between devices with their start and end apart: 29, of which 16 were waited for; matrix products, arithmetic and copies ran while one was open for 1% of the time, Pallas kernels for 3%

profile of v8, /device:TPU:33, one launch (start us, length us, event | category | flops | bytes accessed | tf_op | source)
XLA Modules:
  0.0 178.4 jit_solution(10303896097006921667)
XLA Ops:
  0.6 0.9 shard_map.94.refs_0_
  1.6 1.7 collective-permute-start
  3.3 4.2 %collective-permute-start.2 = (bf16[2,128,256]{2,1,0:T(8,128)(2,1)S(1)}, bf16[2,128,256]{2,1,0:T(8,128)(2,1)S(1)}, u32[]{:S(2)}, u32[]{:S(2)}) collective-permute-start(bf16[2,128,256]{2,1,0:T(8,128)(2,1)S(1)} %shard_map.94.refs_0_), channel_id=1, source_target_pairs={{0,64},{32,96},{64,128},{96,160},{128,192},{160,224},{192,0},{224,... | collective-permute-start | bytes 393224 | tf_op jit(solution)/shard_map/ppermute | solution.py:211
  7.5 0.7 collective-permute-start.3
  8.2 5.2 %collective-permute-start.4 = (bf16[2,128,256]{2,1,0:T(8,128)(2,1)S(1)}, bf16[2,128,256]{2,1,0:T(8,128)(2,1)S(1)}, u32[]{:S(2)}, u32[]{:S(2)}) collective-permute-start(bf16[2,128,256]{2,1,0:T(8,128)(2,1)S(1)} %shard_map.94.refs_0_), channel_id=1, source_target_pairs={{0,96},{32,128},{64,160},{96,192},{128,224},{160,0},{192,32},{224,... | collective-permute-start | bytes 393224 | tf_op jit(solution)/shard_map/ppermute | solution.py:211
  13.4 3.7 %collective-permute-start.6 = (bf16[2,128,256]{2,1,0:T(8,128)(2,1)S(1)}, bf16[2,128,256]{2,1,0:T(8,128)(2,1)S(1)}, u32[]{:S(2)}, u32[]{:S(2)}) collective-permute-start(bf16[2,128,256]{2,1,0:T(8,128)(2,1)S(1)} %shard_map.94.refs_0_), channel_id=1, source_target_pairs={{0,128},{32,160},{64,192},{96,224},{128,0},{160,32},{192,64},{224,... | collective-permute-start | bytes 393224 | tf_op jit(solution)/shard_map/ppermute | solution.py:211
  17.9 2.8 %collective-permute-done.4.refs_5_ = bf16[2,128,256]{2,1,0:T(8,128)(2,1)S(1)} collective-permute-done((bf16[2,128,256]{2,1,0:T(8,128)(2,1)S(1)}, bf16[2,128,256]{2,1,0:T(8,128)(2,1)S(1)}, u32[]{:S(2)}, u32[]{:S(2)}) %collective-permute-start.4) | collective-permute-done | bytes 131104 | tf_op jit(solution)/shard_map/ppermute | solution.py:211
  20.7 5.5 %collective-permute-done.5.refs_6_ = bf16[2,128,256]{2,1,0:T(8,128)(2,1)S(1)} collective-permute-done((bf16[2,128,256]{2,1,0:T(8,128)(2,1)S(1)}, bf16[2,128,256]{2,1,0:T(8,128)(2,1)S(1)}, u32[]{:S(2)}, u32[]{:S(2)}) %collective-permute-start.5) | collective-permute-done | bytes 131104 | tf_op jit(solution)/shard_map/ppermute | solution.py:211
  26.2 7.3 %collective-permute-done.6.refs_7_ = bf16[2,128,256]{2,1,0:T(8,128)(2,1)S(1)} collective-permute-done((bf16[2,128,256]{2,1,0:T(8,128)(2,1)S(1)}, bf16[2,128,256]{2,1,0:T(8,128)(2,1)S(1)}, u32[]{:S(2)}, u32[]{:S(2)}) %collective-permute-start.6) | collective-permute-done | bytes 131104 | tf_op jit(solution)/shard_map/ppermute | solution.py:211
  33.5 5.3 %shard_map.95 = (bf16[16,256,256]{2,1,0:T(8,128)(2,1)S(1)}, f32[16,256,256]{2,1,0:T(8,128)S(1)}) custom-call(s32[2]{0:T(128)S(1)} %pad_add_fusion.place, s32[1]{0:T(128)} %bitcast.10.count, s32[192]{0:T(256)} %bitcast.16, s32[192]{0:T(256)} %bitcast.18, bf16[192,128,128]{2,1,0:T(8,128)(2,1)} %bitcast.12, bf16[2,128,256]{2,1,0:T(8,128)(2,1)S(1)} %shard_map.94.refs_0_, ...), custom_call_target="tpu_custom_call" | custom-call | flops 1610612736 | bytes 14680064 | tf_op jit(solution)/shard_map/pallas_call | solution.py:213
  38.9 4.1 %collective-permute-done.7 = bf16[16,256,256]{2,1,0:T(8,128)(2,1)S(1)} collective-permute-done((bf16[16,256,256]{2,1,0:T(8,128)(2,1)S(1)}, bf16[16,256,256]{2,1,0:T(8,128)(2,1)S(1)}, u32[]{:S(2)}, u32[]{:S(2)}) %collective-permute-start.7) | collective-permute-done | bytes 2097184 | tf_op jit(solution)/shard_map/ppermute | solution.py:235
  43.1 2.0 %add_convert_fusion = bf16[16,256,256]{2,1,0:T(8,128)(2,1)} fusion(f32[16,256,256]{2,1,0:T(8,128)S(1)} %get-tuple-element.27, bf16[16,256,256]{2,1,0:T(8,128)(2,1)S(1)} %collective-permute-done.7), kind=kLoop, calls=%fused_computation | loop fusion | flops 3145728 | bytes 8388608 | tf_op jit(solution)/shard_map/convert_element_type | solution.py:236
  45.1 7.5 %all-to-all-start = ((bf16[16,256,256]{2,1,0:T(8,128)(2,1)}), bf16[16,256,256]{2,1,0:T(8,128)(2,1)S(1)}, u32[]{:S(2)}, u32[]{:S(2)}) async-start(bf16[16,256,256]{2,1,0:T(8,128)(2,1)} %add_convert_fusion), calls=%async_computation | async-start | bytes 4194304 | tf_op jit(solution)/shard_map/all_to_all | solution.py:237
  52.6 32.0 %all-to-all-done.parts = bf16[16,256,256]{2,1,0:T(8,128)(2,1)S(1)} async-done(((bf16[16,256,256]{2,1,0:T(8,128)(2,1)}), bf16[16,256,256]{2,1,0:T(8,128)(2,1)S(1)}, u32[]{:S(2)}, u32[]{:S(2)}) %all-to-all-start) | async-done | bytes 2097184 | tf_op jit(solution)/shard_map/all_to_all | solution.py:237
  84.6 1.1 shard_map.96
  85.7 1.4 copy-done
  87.0 3.7 %all-to-all-start.1 = ((bf16[16,256,256]{2,1,0:T(8,128)(2,1)}), bf16[16,256,256]{2,1,0:T(8,128)(2,1)S(1)}, u32[]{:S(2)}, u32[]{:S(2)}) async-start(bf16[16,256,256]{2,1,0:T(8,128)(2,1)} %copy-done), calls=%async_computation.1 | async-start | bytes 4194304 | tf_op jit(solution)/shard_map/all_to_all | solution.py:255
  90.8 5.0 %collective-permute-start.8 = (f32[128,256]{1,0:T(8,128)S(1)}, f32[128,256]{1,0:T(8,128)S(1)}, u32[]{:S(2)}, u32[]{:S(2)}) collective-permute-start(f32[128,256]{1,0:T(8,128)S(1)} %slice_select_fusion), channel_id=1, source_target_pairs={{0,128},{32,160},{64,192},{96,224},{128,0},{160,32},{192,64},{224,... | collective-permute-start | bytes 393224 | tf_op jit(solution)/shard_map/ppermute | solution.py:178
  95.8 5.4 %collective-permute-done.8 = f32[128,256]{1,0:T(8,128)S(1)} collective-permute-done((f32[128,256]{1,0:T(8,128)S(1)}, f32[128,256]{1,0:T(8,128)S(1)}, u32[]{:S(2)}, u32[]{:S(2)}) %collective-permute-start.8) | collective-permute-done | bytes 131104 | tf_op jit(solution)/shard_map/ppermute | solution.py:178
  101.3 4.3 %collective-permute-done.9 = f32[64,256]{1,0:T(8,128)S(1)} collective-permute-done((f32[64,256]{1,0:T(8,128)S(1)}, f32[64,256]{1,0:T(8,128)S(1)}, u32[]{:S(2)}, u32[]{:S(2)}) %collective-permute-start.9) | collective-permute-done | bytes 65568 | tf_op jit(solution)/shard_map/ppermute | solution.py:178
  105.7 3.0 %collective-permute-done.10 = f32[32,256]{1,0:T(8,128)S(1)} collective-permute-done((f32[32,256]{1,0:T(8,128)S(1)}, f32[32,256]{1,0:T(8,128)S(1)}, u32[]{:S(2)}, u32[]{:S(2)}) %collective-permute-start.10) | collective-permute-done | bytes 32800 | tf_op jit(solution)/shard_map/ppermute | solution.py:178
  108.8 3.2 %collective-permute-start.11 = (f32[32,256]{1,0:T(8,128)S(1)}, f32[32,256]{1,0:T(8,128)S(1)}, u32[]{:S(2)}, u32[]{:S(2)}) collective-permute-start(f32[32,256]{1,0:T(8,128)S(1)} %select_add_fusion.2), channel_id=1, source_target_pairs={{0,1},{1,0},{2,3},{3,2},{4,5},{5,4},{6,7},{7,6},{8,9},{9,8},{10,11... | collective-permute-start | bytes 98312 | tf_op jit(solution)/shard_map/ppermute | solution.py:164
  112.0 0.9 collective-permute-done.11
  112.9 2.1 %collective-permute-start.14 = (f32[32,256]{1,0:T(8,128)S(1)}, f32[32,256]{1,0:T(8,128)S(1)}, u32[]{:S(2)}, u32[]{:S(2)}) collective-permute-start(f32[32,256]{1,0:T(8,128)S(1)} %add.78), channel_id=1, source_target_pairs={{0,6},{1,7},{2,4},{3,5},{4,2},{5,3},{6,0},{7,1},{8,14},{9,15},{10,... | collective-permute-start | bytes 98312 | tf_op jit(solution)/shard_map/ppermute | solution.py:164
  115.0 0.6 collective-permute-start.13
  115.5 0.6 collective-permute-start.12
  116.1 1.1 collective-permute-done.14
  117.2 2.5 %collective-permute-done.13 = f32[32,256]{1,0:T(8,128)S(1)} collective-permute-done((f32[32,256]{1,0:T(8,128)S(1)}, f32[32,256]{1,0:T(8,128)S(1)}, u32[]{:S(2)}, u32[]{:S(2)}) %collective-permute-start.13) | collective-permute-done | bytes 32800 | tf_op jit(solution)/shard_map/ppermute | solution.py:164
  119.7 2.8 %collective-permute-start.17 = (f32[32,256]{1,0:T(8,128)S(1)}, f32[32,256]{1,0:T(8,128)S(1)}, u32[]{:S(2)}, u32[]{:S(2)}) collective-permute-start(f32[32,256]{1,0:T(8,128)S(1)} %add_add_fusion.1), channel_id=1, source_target_pairs={{0,24},{1,25},{2,26},{3,27},{4,28},{5,29},{6,30},{7,31},{8,16},{9,... | collective-permute-start | bytes 98312 | tf_op jit(solution)/shard_map/ppermute | solution.py:164
  122.6 0.5 collective-permute-start.16
  123.1 0.2 collective-permute-start.15
  123.2 0.6 collective-permute-done.17
  123.9 3.1 %collective-permute-done.16 = f32[32,256]{1,0:T(8,128)S(1)} collective-permute-done((f32[32,256]{1,0:T(8,128)S(1)}, f32[32,256]{1,0:T(8,128)S(1)}, u32[]{:S(2)}, u32[]{:S(2)}) %collective-permute-start.16) | collective-permute-done | bytes 32800 | tf_op jit(solution)/shard_map/ppermute | solution.py:164
  127.0 2.8 %collective-permute-start.18 = (bf16[16,256,256]{2,1,0:T(8,128)(2,1)S(1)}, bf16[16,256,256]{2,1,0:T(8,128)(2,1)}, u32[]{:S(2)}, u32[]{:S(2)}) collective-permute-start(bf16[16,256,256]{2,1,0:T(8,128)(2,1)S(1)} %all-to-all-done.1.same), channel_id=1, source_target_pairs={{0,1},{1,0},{2,3},{3,2},{4,5},{5,4},{6,7},{7,6},{8,9},{9,8},{10,11... | collective-permute-start | bytes 6291464 | tf_op jit(solution)/shard_map/ppermute | solution.py:261
  129.8 0.7 broadcast_in_dim.2
  130.5 6.4 %all-to-all-start.2 = ((f32[8,32,256]{2,1,0:T(8,128)}), f32[8,32,256]{2,1,0:T(8,128)S(1)}, u32[]{:S(2)}, u32[]{:S(2)}) async-start(f32[8,32,256]{2,1,0:T(8,128)} %broadcast_in_dim.2), calls=%async_computation.2 | async-start | bytes 524288 | tf_op jit(solution)/shard_map/all_to_all | solution.py:263
  137.0 4.7 %shard_map.97 = (bf16[256,256]{1,0:T(8,128)(2,1)S(1)}, bf16[256,256]{1,0:T(8,128)(2,1)S(1)}, bf16[256,256]{1,0:T(8,128)(2,1)S(1)}, bf16[256,256]{1,0:T(8,128)(2,...) custom-call(s32[2]{0:T(128)S(1)} %pad_add_fusion.place, ...), custom_call_target="tpu_custom_call" | custom-call | flops 1610612736 | bytes 11534336 | tf_op jit(solution)/shard_map/pallas_call | solution.py:266
  141.6 4.5 %all-to-all-done.2 = f32[8,32,256]{2,1,0:T(8,128)S(1)} async-done(((f32[8,32,256]{2,1,0:T(8,128)}), f32[8,32,256]{2,1,0:T(8,128)S(1)}, u32[]{:S(2)}, u32[]{:S(2)}) %all-to-all-start.2) | async-done | bytes 262176 | tf_op jit(solution)/shard_map/all_to_all | solution.py:263
  146.1 0.4 collective-permute-start.25
  146.5 2.8 %collective-permute-start.24 = (bf16[256,256]{1,0:T(8,128)(2,1)S(1)}, bf16[256,256]{1,0:T(8,128)(2,1)S(1)}, u32[]{:S(2)}, u32[]{:S(2)}) collective-permute-start(bf16[256,256]{1,0:T(8,128)(2,1)S(1)} %get-tuple-element.49), channel_id=1, source_target_pairs={{0,224},{32,0},{64,32},{96,64},{128,96},{160,128},{192,160},{224,1... | collective-permute-start | bytes 393224 | tf_op jit(solution)/shard_map/ppermute | solution.py:288
  149.3 3.6 %collective-permute-start.22 = (bf16[256,256]{1,0:T(8,128)(2,1)S(1)}, bf16[256,256]{1,0:T(8,128)(2,1)S(1)}, u32[]{:S(2)}, u32[]{:S(2)}) collective-permute-start(bf16[256,256]{1,0:T(8,128)(2,1)S(1)} %get-tuple-element.47), channel_id=1, source_target_pairs={{0,192},{32,224},{64,0},{96,32},{128,64},{160,96},{192,128},{224,1... | collective-permute-start | bytes 393224 | tf_op jit(solution)/shard_map/ppermute | solution.py:288
  152.9 1.1 collective-permute-start.21
  154.0 3.4 %collective-permute-start.20 = (bf16[256,256]{1,0:T(8,128)(2,1)S(1)}, bf16[256,256]{1,0:T(8,128)(2,1)S(1)}, u32[]{:S(2)}, u32[]{:S(2)}) collective-permute-start(bf16[256,256]{1,0:T(8,128)(2,1)S(1)} %get-tuple-element.45), channel_id=1, source_target_pairs={{0,160},{32,192},{64,224},{96,0},{128,32},{160,64},{192,96},{224,1... | collective-permute-start | bytes 393224 | tf_op jit(solution)/shard_map/ppermute | solution.py:288
  157.4 2.5 %collective-permute-start.19 = (bf16[256,256]{1,0:T(8,128)(2,1)S(1)}, bf16[256,256]{1,0:T(8,128)(2,1)S(1)}, u32[]{:S(2)}, u32[]{:S(2)}) collective-permute-start(bf16[256,256]{1,0:T(8,128)(2,1)S(1)} %get-tuple-element.44), channel_id=1, source_target_pairs={{0,128},{32,160},{64,192},{96,224},{128,0},{160,32},{192,64},{224,... | collective-permute-start | bytes 393224 | tf_op jit(solution)/shard_map/ppermute | solution.py:288
  159.9 12.2 %collective-permute-done.21 = bf16[256,256]{1,0:T(8,128)(2,1)S(1)} collective-permute-done((bf16[256,256]{1,0:T(8,128)(2,1)S(1)}, bf16[256,256]{1,0:T(8,128)(2,1)S(1)}, u32[]{:S(2)}, u32[]{:S(2)}) %collective-permute-start.21) | collective-permute-done | bytes 131104 | tf_op jit(solution)/shard_map/ppermute | solution.py:288
  172.0 4.8 %collective-permute-done.19 = bf16[256,256]{1,0:T(8,128)(2,1)S(1)} collective-permute-done((bf16[256,256]{1,0:T(8,128)(2,1)S(1)}, bf16[256,256]{1,0:T(8,128)(2,1)S(1)}, u32[]{:S(2)}, u32[]{:S(2)}) %collective-permute-start.19) | collective-permute-done | bytes 131104 | tf_op jit(solution)/shard_map/ppermute | solution.py:288
  176.9 0.8 fusion
  177.7 0.7 copy.12
  (34 shorter events, 0.5 us)
Async XLA Ops:
  1.6 11.9 %collective-permute-start = (bf16[2,128,256]{2,1,0:T(8,128)(2,1)S(1)}, bf16[2,128,256]{2,1,0:T(8,128)(2,1)S(1)}, u32[]{:S(2)}, u32[]{:S(2)}) collective-permute-start(bf16[2,128,256]{2,1,0:T(8,128)(2,1)S(1)} %shard_map.94.refs_0_), channel_id=1, source_target_pairs={{0,32},{32,64},{64,96},{96,128},{128,160},{160,192},{192,224},{224... | collective-permute-start | bytes 393224 | tf_op jit(solution)/shard_map/ppermute | solution.py:211
  3.3 10.2 %collective-permute-start.1 = (bf16[2,128,256]{2,1,0:T(8,128)(2,1)S(1)}, bf16[2,128,256]{2,1,0:T(8,128)(2,1)S(1)}, u32[]{:S(2)}, u32[]{:S(2)}) collective-permute-start(bf16[2,128,256]{2,1,0:T(8,128)(2,1)S(1)} %shard_map.94.refs_0_), channel_id=1, source_target_pairs={{0,224},{32,0},{64,32},{96,64},{128,96},{160,128},{192,160},{224,1... | collective-permute-start | bytes 393224 | tf_op jit(solution)/shard_map/ppermute | solution.py:211
  3.3 14.6 %collective-permute-start.2 = (bf16[2,128,256]{2,1,0:T(8,128)(2,1)S(1)}, bf16[2,128,256]{2,1,0:T(8,128)(2,1)S(1)}, u32[]{:S(2)}, u32[]{:S(2)}) collective-permute-start(bf16[2,128,256]{2,1,0:T(8,128)(2,1)S(1)} %shard_map.94.refs_0_), channel_id=1, source_target_pairs={{0,64},{32,96},{64,128},{96,160},{128,192},{160,224},{192,0},{224,... | collective-permute-start | bytes 393224 | tf_op jit(solution)/shard_map/ppermute | solution.py:211
  7.5 10.4 %collective-permute-start.3 = (bf16[2,128,256]{2,1,0:T(8,128)(2,1)S(1)}, bf16[2,128,256]{2,1,0:T(8,128)(2,1)S(1)}, u32[]{:S(2)}, u32[]{:S(2)}) collective-permute-start(bf16[2,128,256]{2,1,0:T(8,128)(2,1)S(1)} %shard_map.94.refs_0_), channel_id=1, source_target_pairs={{0,192},{32,224},{64,0},{96,32},{128,64},{160,96},{192,128},{224,1... | collective-permute-start | bytes 393224 | tf_op jit(solution)/shard_map/ppermute | solution.py:211
  8.2 12.5 %collective-permute-start.4 = (bf16[2,128,256]{2,1,0:T(8,128)(2,1)S(1)}, bf16[2,128,256]{2,1,0:T(8,128)(2,1)S(1)}, u32[]{:S(2)}, u32[]{:S(2)}) collective-permute-start(bf16[2,128,256]{2,1,0:T(8,128)(2,1)S(1)} %shard_map.94.refs_0_), channel_id=1, source_target_pairs={{0,96},{32,128},{64,160},{96,192},{128,224},{160,0},{192,32},{224,... | collective-permute-start | bytes 393224 | tf_op jit(solution)/shard_map/ppermute | solution.py:211
  13.4 12.7 %collective-permute-start.5 = (bf16[2,128,256]{2,1,0:T(8,128)(2,1)S(1)}, bf16[2,128,256]{2,1,0:T(8,128)(2,1)S(1)}, u32[]{:S(2)}, u32[]{:S(2)}) collective-permute-start(bf16[2,128,256]{2,1,0:T(8,128)(2,1)S(1)} %shard_map.94.refs_0_), channel_id=1, source_target_pairs={{0,160},{32,192},{64,224},{96,0},{128,32},{160,64},{192,96},{224,1... | collective-permute-start | bytes 393224 | tf_op jit(solution)/shard_map/ppermute | solution.py:211
  13.4 20.0 %collective-permute-start.6 = (bf16[2,128,256]{2,1,0:T(8,128)(2,1)S(1)}, bf16[2,128,256]{2,1,0:T(8,128)(2,1)S(1)}, u32[]{:S(2)}, u32[]{:S(2)}) collective-permute-start(bf16[2,128,256]{2,1,0:T(8,128)(2,1)S(1)} %shard_map.94.refs_0_), channel_id=1, source_target_pairs={{0,128},{32,160},{64,192},{96,224},{128,0},{160,32},{192,64},{224,... | collective-permute-start | bytes 393224 | tf_op jit(solution)/shard_map/ppermute | solution.py:211
  38.8 4.2 %collective-permute-start.7 = (bf16[16,256,256]{2,1,0:T(8,128)(2,1)S(1)}, bf16[16,256,256]{2,1,0:T(8,128)(2,1)S(1)}, u32[]{:S(2)}, u32[]{:S(2)}) collective-permute-start(bf16[16,256,256]{2,1,0:T(8,128)(2,1)S(1)} %get-tuple-element.28), channel_id=1, source_target_pairs={{0,1},{1,0},{2,3},{3,2},{4,5},{5,4},{6,7},{7,6},{8,9},{9,8},{10,11... | collective-permute-start | bytes 6291464 | tf_op jit(solution)/shard_map/ppermute | solution.py:235
  45.1 39.5 %copy-start.1 = (bf16[256,256]{1,0:T(8,128)(2,1)S(1)}, bf16[256,256]{1,0:T(8,128)(2,1)}, u32[]{:S(2)}) copy-start(bf16[256,256]{1,0:T(8,128)(2,1)} %weight.1) | copy-start | bytes 393220
  45.1 39.5 %copy-start.2 = (bf16[256,256]{1,0:T(8,128)(2,1)S(1)}, bf16[256,256]{1,0:T(8,128)(2,1)}, u32[]{:S(2)}) copy-start(bf16[256,256]{1,0:T(8,128)(2,1)} %cotangent.1) | copy-start | bytes 393220
  45.1 39.5 %all-to-all-start = ((bf16[16,256,256]{2,1,0:T(8,128)(2,1)}), bf16[16,256,256]{2,1,0:T(8,128)(2,1)S(1)}, u32[]{:S(2)}, u32[]{:S(2)}) async-start(bf16[16,256,256]{2,1,0:T(8,128)(2,1)} %add_convert_fusion), calls=%async_computation | async-start | bytes 4194304 | tf_op jit(solution)/shard_map/all_to_all | solution.py:237
  85.7 1.4 copy-start
  87.0 39.9 %all-to-all-start.1 = ((bf16[16,256,256]{2,1,0:T(8,128)(2,1)}), bf16[16,256,256]{2,1,0:T(8,128)(2,1)S(1)}, u32[]{:S(2)}, u32[]{:S(2)}) async-start(bf16[16,256,256]{2,1,0:T(8,128)(2,1)} %copy-done), calls=%async_computation.1 | async-start | bytes 4194304 | tf_op jit(solution)/shard_map/all_to_all | solution.py:255
  90.8 10.4 %collective-permute-start.8 = (f32[128,256]{1,0:T(8,128)S(1)}, f32[128,256]{1,0:T(8,128)S(1)}, u32[]{:S(2)}, u32[]{:S(2)}) collective-permute-start(f32[128,256]{1,0:T(8,128)S(1)} %slice_select_fusion), channel_id=1, source_target_pairs={{0,128},{32,160},{64,192},{96,224},{128,0},{160,32},{192,64},{224,... | collective-permute-start | bytes 393224 | tf_op jit(solution)/shard_map/ppermute | solution.py:178
  101.2 4.4 %collective-permute-start.9 = (f32[64,256]{1,0:T(8,128)S(1)}, f32[64,256]{1,0:T(8,128)S(1)}, u32[]{:S(2)}, u32[]{:S(2)}) collective-permute-start(f32[64,256]{1,0:T(8,128)S(1)} %slice_select_fusion.1), channel_id=1, source_target_pairs={{0,64},{32,96},{64,0},{96,32},{128,192},{160,224},{192,128},{224,1... | collective-permute-start | bytes 196616 | tf_op jit(solution)/shard_map/ppermute | solution.py:178
  105.6 3.1 %collective-permute-start.10 = (f32[32,256]{1,0:T(8,128)S(1)}, f32[32,256]{1,0:T(8,128)S(1)}, u32[]{:S(2)}, u32[]{:S(2)}) collective-permute-start(f32[32,256]{1,0:T(8,128)S(1)} %slice_select_fusion.2), channel_id=1, source_target_pairs={{0,32},{32,0},{64,96},{96,64},{128,160},{160,128},{192,224},{224,1... | collective-permute-start | bytes 98312 | tf_op jit(solution)/shard_map/ppermute | solution.py:178
  108.8 4.1 %collective-permute-start.11 = (f32[32,256]{1,0:T(8,128)S(1)}, f32[32,256]{1,0:T(8,128)S(1)}, u32[]{:S(2)}, u32[]{:S(2)}) collective-permute-start(f32[32,256]{1,0:T(8,128)S(1)} %select_add_fusion.2), channel_id=1, source_target_pairs={{0,1},{1,0},{2,3},{3,2},{4,5},{5,4},{6,7},{7,6},{8,9},{9,8},{10,11... | collective-permute-start | bytes 98312 | tf_op jit(solution)/shard_map/ppermute | solution.py:164
  112.9 4.3 %collective-permute-start.14 = (f32[32,256]{1,0:T(8,128)S(1)}, f32[32,256]{1,0:T(8,128)S(1)}, u32[]{:S(2)}, u32[]{:S(2)}) collective-permute-start(f32[32,256]{1,0:T(8,128)S(1)} %add.78), channel_id=1, source_target_pairs={{0,6},{1,7},{2,4},{3,5},{4,2},{5,3},{6,0},{7,1},{8,14},{9,15},{10,... | collective-permute-start | bytes 98312 | tf_op jit(solution)/shard_map/ppermute | solution.py:164
  115.0 4.7 %collective-permute-start.13 = (f32[32,256]{1,0:T(8,128)S(1)}, f32[32,256]{1,0:T(8,128)S(1)}, u32[]{:S(2)}, u32[]{:S(2)}) collective-permute-start(f32[32,256]{1,0:T(8,128)S(1)} %add.78), channel_id=1, source_target_pairs={{0,4},{1,5},{2,6},{3,7},{4,0},{5,1},{6,2},{7,3},{8,12},{9,13},{10,... | collective-permute-start | bytes 98312 | tf_op jit(solution)/shard_map/ppermute | solution.py:164
  115.5 4.2 %collective-permute-start.12 = (f32[32,256]{1,0:T(8,128)S(1)}, f32[32,256]{1,0:T(8,128)S(1)}, u32[]{:S(2)}, u32[]{:S(2)}) collective-permute-start(f32[32,256]{1,0:T(8,128)S(1)} %add.78), channel_id=1, source_target_pairs={{0,2},{1,3},{2,0},{3,1},{4,6},{5,7},{6,4},{7,5},{8,10},{9,11},{10,... | collective-permute-start | bytes 98312 | tf_op jit(solution)/shard_map/ppermute | solution.py:164
  119.7 4.1 %collective-permute-start.17 = (f32[32,256]{1,0:T(8,128)S(1)}, f32[32,256]{1,0:T(8,128)S(1)}, u32[]{:S(2)}, u32[]{:S(2)}) collective-permute-start(f32[32,256]{1,0:T(8,128)S(1)} %add_add_fusion.1), channel_id=1, source_target_pairs={{0,24},{1,25},{2,26},{3,27},{4,28},{5,29},{6,30},{7,31},{8,16},{9,... | collective-permute-start | bytes 98312 | tf_op jit(solution)/shard_map/ppermute | solution.py:164
  122.6 4.4 %collective-permute-start.16 = (f32[32,256]{1,0:T(8,128)S(1)}, f32[32,256]{1,0:T(8,128)S(1)}, u32[]{:S(2)}, u32[]{:S(2)}) collective-permute-start(f32[32,256]{1,0:T(8,128)S(1)} %add_add_fusion.1), channel_id=1, source_target_pairs={{0,16},{1,17},{2,18},{3,19},{4,20},{5,21},{6,22},{7,23},{8,24},{9,... | collective-permute-start | bytes 98312 | tf_op jit(solution)/shard_map/ppermute | solution.py:164
  123.1 3.9 %collective-permute-start.15 = (f32[32,256]{1,0:T(8,128)S(1)}, f32[32,256]{1,0:T(8,128)S(1)}, u32[]{:S(2)}, u32[]{:S(2)}) collective-permute-start(f32[32,256]{1,0:T(8,128)S(1)} %add_add_fusion.1), channel_id=1, source_target_pairs={{0,8},{1,9},{2,10},{3,11},{4,12},{5,13},{6,14},{7,15},{8,0},{9,1},... | collective-permute-start | bytes 98312 | tf_op jit(solution)/shard_map/ppermute | solution.py:164
  127.0 10.0 %collective-permute-start.18 = (bf16[16,256,256]{2,1,0:T(8,128)(2,1)S(1)}, bf16[16,256,256]{2,1,0:T(8,128)(2,1)}, u32[]{:S(2)}, u32[]{:S(2)}) collective-permute-start(bf16[16,256,256]{2,1,0:T(8,128)(2,1)S(1)} %all-to-all-done.1.same), channel_id=1, source_target_pairs={{0,1},{1,0},{2,3},{3,2},{4,5},{5,4},{6,7},{7,6},{8,9},{9,8},{10,11... | collective-permute-start | bytes 6291464 | tf_op jit(solution)/shard_map/ppermute | solution.py:261
  130.5 15.6 %all-to-all-start.2 = ((f32[8,32,256]{2,1,0:T(8,128)}), f32[8,32,256]{2,1,0:T(8,128)S(1)}, u32[]{:S(2)}, u32[]{:S(2)}) async-start(f32[8,32,256]{2,1,0:T(8,128)} %broadcast_in_dim.2), calls=%async_computation.2 | async-start | bytes 524288 | tf_op jit(solution)/shard_map/all_to_all | solution.py:263
  146.1 7.9 %collective-permute-start.25 = (bf16[256,256]{1,0:T(8,128)(2,1)S(1)}, bf16[256,256]{1,0:T(8,128)(2,1)S(1)}, u32[]{:S(2)}, u32[]{:S(2)}) collective-permute-start(bf16[256,256]{1,0:T(8,128)(2,1)S(1)} %get-tuple-element.50), channel_id=1, source_target_pairs={{0,32},{32,64},{64,96},{96,128},{128,160},{160,192},{192,224},{224... | collective-permute-start | bytes 393224 | tf_op jit(solution)/shard_map/ppermute | solution.py:288
  146.5 10.9 %collective-permute-start.24 = (bf16[256,256]{1,0:T(8,128)(2,1)S(1)}, bf16[256,256]{1,0:T(8,128)(2,1)S(1)}, u32[]{:S(2)}, u32[]{:S(2)}) collective-permute-start(bf16[256,256]{1,0:T(8,128)(2,1)S(1)} %get-tuple-element.49), channel_id=1, source_target_pairs={{0,224},{32,0},{64,32},{96,64},{128,96},{160,128},{192,160},{224,1... | collective-permute-start | bytes 393224 | tf_op jit(solution)/shard_map/ppermute | solution.py:288
  149.3 10.5 %collective-permute-start.23 = (bf16[256,256]{1,0:T(8,128)(2,1)S(1)}, bf16[256,256]{1,0:T(8,128)(2,1)S(1)}, u32[]{:S(2)}, u32[]{:S(2)}) collective-permute-start(bf16[256,256]{1,0:T(8,128)(2,1)S(1)} %get-tuple-element.48), channel_id=1, source_target_pairs={{0,64},{32,96},{64,128},{96,160},{128,192},{160,224},{192,0},{224,... | collective-permute-start | bytes 393224 | tf_op jit(solution)/shard_map/ppermute | solution.py:288
  149.3 10.5 %collective-permute-start.22 = (bf16[256,256]{1,0:T(8,128)(2,1)S(1)}, bf16[256,256]{1,0:T(8,128)(2,1)S(1)}, u32[]{:S(2)}, u32[]{:S(2)}) collective-permute-start(bf16[256,256]{1,0:T(8,128)(2,1)S(1)} %get-tuple-element.47), channel_id=1, source_target_pairs={{0,192},{32,224},{64,0},{96,32},{128,64},{160,96},{192,128},{224,1... | collective-permute-start | bytes 393224 | tf_op jit(solution)/shard_map/ppermute | solution.py:288
  152.9 19.1 %collective-permute-start.21 = (bf16[256,256]{1,0:T(8,128)(2,1)S(1)}, bf16[256,256]{1,0:T(8,128)(2,1)S(1)}, u32[]{:S(2)}, u32[]{:S(2)}) collective-permute-start(bf16[256,256]{1,0:T(8,128)(2,1)S(1)} %get-tuple-element.46), channel_id=1, source_target_pairs={{0,96},{32,128},{64,160},{96,192},{128,224},{160,0},{192,32},{224,... | collective-permute-start | bytes 393224 | tf_op jit(solution)/shard_map/ppermute | solution.py:288
  154.0 18.0 %collective-permute-start.20 = (bf16[256,256]{1,0:T(8,128)(2,1)S(1)}, bf16[256,256]{1,0:T(8,128)(2,1)S(1)}, u32[]{:S(2)}, u32[]{:S(2)}) collective-permute-start(bf16[256,256]{1,0:T(8,128)(2,1)S(1)} %get-tuple-element.45), channel_id=1, source_target_pairs={{0,160},{32,192},{64,224},{96,0},{128,32},{160,64},{192,96},{224,1... | collective-permute-start | bytes 393224 | tf_op jit(solution)/shard_map/ppermute | solution.py:288
  157.4 19.5 %collective-permute-start.19 = (bf16[256,256]{1,0:T(8,128)(2,1)S(1)}, bf16[256,256]{1,0:T(8,128)(2,1)S(1)}, u32[]{:S(2)}, u32[]{:S(2)}) collective-permute-start(bf16[256,256]{1,0:T(8,128)(2,1)S(1)} %get-tuple-element.44), channel_id=1, source_target_pairs={{0,128},{32,160},{64,192},{96,224},{128,0},{160,32},{192,64},{224,... | collective-permute-start | bytes 393224 | tf_op jit(solution)/shard_map/ppermute | solution.py:288

commit v9 on v6

--- a/solution.py
+++ b/solution.py
@@ -128,12 +128,6 @@
         owner = lax.rem(row + step, n_row)
         mine = total[pl.ds(owner * blocks_here, blocks_here)]
         out[...] = mine.reshape(out.shape).astype(BF16)
-
-
-def copy_kernel(source, target, sem):
-    copy = pltpu.make_async_copy(source, target, sem)
-    copy.start()
-    copy.wait()
 
 
 def dense_kernel(parts, weight, cotangent, activated, grad_agg):
@@ -190,24 +184,18 @@
     same_core = [list(range(core, n_col, 2)) for core in range(2)]
     work = 2 * slots * side * side * width
 
-    own = pl.pallas_call(
-        copy_kernel,
-        out_shape=jax.ShapeDtypeStruct((here, side, width), BF16),
-        in_specs=[hbm],
-        out_specs=vmem,
-        scratch_shapes=[pltpu.SemaphoreType.DMA],
-        compiler_params=pltpu.CompilerParams(vmem_limit_bytes=4 * MIB),
-    )(in_hbm(features.reshape(here, side, width)))
+    own = features.reshape(here, side, width)
     steps = [0] + sorted(range(1, n_row), key=lambda k: (min(k, n_row - k), k))
-    pieces = [own] + [lax.ppermute(own, "row", turn(n_row, k)) for k in steps[1:]]
+    arrival = [0] + steps[:0:-1]
+    pieces = [in_hbm(own)] + [lax.ppermute(own, "row", turn(n_row, k)) for k in arrival[1:]]
 
     send, keep = pl.pallas_call(
-        functools.partial(forward_kernel, chunk, steps),
+        functools.partial(forward_kernel, chunk, arrival),
         out_shape=(
             jax.ShapeDtypeStruct((chips, nodes, width), BF16),
             jax.ShapeDtypeStruct((chips, nodes, width), F32),
         ),
-        in_specs=[smem] * 2 + [hbm] * 3 + [near] * n_row,
+        in_specs=[smem] * 2 + [hbm] * 4 + [near] * (n_row - 1),
         out_specs=(vmem, vmem),
         scratch_shapes=[
             pltpu.SMEM((slots,), jnp.int32),
@@ -245,9 +233,9 @@
     same = lax.all_to_all(grad_agg, "col", 0, 0, tiled=True, axis_index_groups=same_core)
     other = lax.ppermute(same, "col", swap)
     strips = jnp.sum(same[:, nodes:].astype(F32), axis=0)
-    strips = add_partners(strips, n_row, [1])
+    strips = add_partners(strips, n_row, range(1, n_row // 2))
     same, other, strips = lax.optimization_barrier((same, other, strips))
-    strips = add_partners(strips, n_row, range(2, n_row, 2))
+    strips = add_partners(strips, n_row, [n_row // 2])
 
     shares = pl.pallas_call(
         functools.partial(backward_kernel, chunk, steps),

time: 167 us -> 166 us (level)
  waiting for transfers between devices: 27.2 us -> 25.4 us
    ppermute x4, starting transfers between devices: 6.43 us -> 11.4 us  [add_partners(): lax.ppermute(value, 'row', [(i, i ^ distance) for i in range(size)])]
    all_to_all x1, waiting for transfers between devices: 1.87 us -> 5.05 us  [per_device(): every = lax.all_to_all(copies, 'col', 0, 0, tiled=True)]
    ppermute x7, waiting for transfers between devices: 8.64 us -> 5.48 us  [per_device(): lax.ppermute(share, 'row', turn(n_row, step))]
    ppermute x7, starting transfers between devices: 18 us -> 15 us  [per_device(): lax.ppermute(share, 'row', turn(n_row, step))]
    ppermute x7, starting transfers between devices: 20.8 us -> 18.5 us  [per_device(): lax.ppermute(own, 'row', turn(n_row, k))]
    pallas_call x2 -> x1, Pallas kernels: 9.13 us -> 8.05 us  [per_device(): pl.pallas_call(functools.partial(forward_kernel, chunk, arrival), out_sha...]
  transfers between devices with their start and end apart: 21 -> 21, of which waited for: 11 -> 9; matrix products, arithmetic and copies ran while one was open for 1% -> 1% of each run, Pallas kernels for 5% -> 5%
where the time goes in v9:
time: 166 us; the launch traced here: 165 us
  blocking collectives  63.7 us (38%)
  starting transfers between devices  55 us (33%)
  waiting for transfers between devices  25.4 us (15%)
  Pallas kernels  16.7 us (10%)
  other arithmetic  2.42 us (1%)
    all_to_all x1, blocking collectives, per_device(): lax.all_to_all(shares, 'col', 0, 0, tiled=True, axis_index_groups=same_core)  32.1 us
    all_to_all x1, blocking collectives, per_device(): lax.all_to_all(grad_agg, 'col', 0, 0, tiled=True, axis_index_groups=same_...  31.6 us
    ppermute x7, starting transfers between devices, per_device(): lax.ppermute(own, 'row', turn(n_row, k))  18.5 us
    ppermute x7, starting transfers between devices, per_device(): lax.ppermute(share, 'row', turn(n_row, step))  15 us
    ppermute x4, starting transfers between devices, add_partners(): lax.ppermute(value, 'row', [(i, i ^ distance) for i in range(size)])  11.4 us
    ppermute x7, waiting for transfers between devices, per_device(): lax.ppermute(own, 'row', turn(n_row, k))  8.49 us
    pallas_call x1, Pallas kernels, per_device(): pl.pallas_call(functools.partial(forward_kernel, chunk, arrival), out_sha...  8.05 us
    pallas_call x1, Pallas kernels, per_device(): pl.pallas_call(functools.partial(backward_kernel, chunk, steps), out_shap...  7.54 us
  transfers between devices with their start and end apart: 21, of which 9 were waited for; matrix products, arithmetic and copies ran while one was open for 1% of the time, Pallas kernels for 5%

profile of v9, /device:TPU:1, one launch (start us, length us, event | category | flops | bytes accessed | tf_op | source)
XLA Modules:
  0.0 165.4 jit_solution(4648630856644319604)
XLA Ops:
  0.6 2.5 %collective-permute-start.6 = (bf16[2,128,256]{2,1,0:T(8,128)(2,1)}, bf16[2,128,256]{2,1,0:T(8,128)(2,1)S(1)}, u32[]{:S(2)}, u32[]{:S(2)}) collective-permute-start(bf16[2,128,256]{2,1,0:T(8,128)(2,1)} %bitcast.17), channel_id=1, source_target_pairs={{0,32},{32,64},{64,96},{96,128},{128,160},{160,192},{192,224},{224... | collective-permute-start | bytes 393224 | tf_op jit(solution)/shard_map/ppermute | solution.py:190
  3.2 4.0 %collective-permute-start.5 = (bf16[2,128,256]{2,1,0:T(8,128)(2,1)}, bf16[2,128,256]{2,1,0:T(8,128)(2,1)S(1)}, u32[]{:S(2)}, u32[]{:S(2)}) collective-permute-start(bf16[2,128,256]{2,1,0:T(8,128)(2,1)} %bitcast.18), channel_id=1, source_target_pairs={{0,224},{32,0},{64,32},{96,64},{128,96},{160,128},{192,160},{224,1... | collective-permute-start | bytes 393224 | tf_op jit(solution)/shard_map/ppermute | solution.py:190
  7.2 0.0 collective-permute-start.4
  7.2 3.6 %collective-permute-start.3 = (bf16[2,128,256]{2,1,0:T(8,128)(2,1)}, bf16[2,128,256]{2,1,0:T(8,128)(2,1)S(1)}, u32[]{:S(2)}, u32[]{:S(2)}) collective-permute-start(bf16[2,128,256]{2,1,0:T(8,128)(2,1)} %bitcast.20), channel_id=1, source_target_pairs={{0,192},{32,224},{64,0},{96,32},{128,64},{160,96},{192,128},{224,1... | collective-permute-start | bytes 393224 | tf_op jit(solution)/shard_map/ppermute | solution.py:190
  10.8 0.3 collective-permute-start.2
  11.1 0.0 collective-permute-done.6.refs_7_
  11.1 4.2 %collective-permute-start.1 = (bf16[2,128,256]{2,1,0:T(8,128)(2,1)}, bf16[2,128,256]{2,1,0:T(8,128)(2,1)S(1)}, u32[]{:S(2)}, u32[]{:S(2)}) collective-permute-start(bf16[2,128,256]{2,1,0:T(8,128)(2,1)} %bitcast.22), channel_id=1, source_target_pairs={{0,160},{32,192},{64,224},{96,0},{128,32},{160,64},{192,96},{224,1... | collective-permute-start | bytes 393224 | tf_op jit(solution)/shard_map/ppermute | solution.py:190
  15.3 0.0 collective-permute-done.5.refs_6_
  15.3 3.9 %collective-permute-start = (bf16[2,128,256]{2,1,0:T(8,128)(2,1)}, bf16[2,128,256]{2,1,0:T(8,128)(2,1)S(1)}, u32[]{:S(2)}, u32[]{:S(2)}) collective-permute-start(bf16[2,128,256]{2,1,0:T(8,128)(2,1)} %bitcast.23), channel_id=1, source_target_pairs={{0,128},{32,160},{64,192},{96,224},{128,0},{160,32},{192,64},{224,... | collective-permute-start | bytes 393224 | tf_op jit(solution)/shard_map/ppermute | solution.py:190
  19.8 0.1 pad_add_fusion.place
  19.9 0.0 collective-permute-done.4.refs_5_
  19.9 0.1 collective-permute-done.3.refs_4_
  20.0 8.4 %collective-permute-done.2.refs_3_ = bf16[2,128,256]{2,1,0:T(8,128)(2,1)S(1)} collective-permute-done((bf16[2,128,256]{2,1,0:T(8,128)(2,1)}, bf16[2,128,256]{2,1,0:T(8,128)(2,1)S(1)}, u32[]{:S(2)}, u32[]{:S(2)}) %collective-permute-start.2) | collective-permute-done | bytes 131104 | tf_op jit(solution)/shard_map/ppermute | solution.py:190
  28.4 0.0 collective-permute-done.1.refs_2_
  28.4 0.0 collective-permute-done.refs_1_
  28.4 8.1 %shard_map.94 = (bf16[16,256,256]{2,1,0:T(8,128)(2,1)S(1)}, f32[16,256,256]{2,1,0:T(8,128)S(1)}) custom-call(s32[2]{0:T(128)S(1)} %pad_add_fusion.place, s32[1]{0:T(128)} %bitcast.12.count, s32[192]{0:T(256)} %bitcast.25, s32[192]{0:T(256)} %bitcast.27, bf16[192,128,128]{2,1,0:T(8,128)(2,1)} %bitcast.14, bf16[2,128,256]{2,1,0:T(8,128)(2,1)} %bitcast.24, ...), custom_call_target="tpu_custom_call" | custom-call | flops 1610612736 | bytes 14680064 | tf_op jit(solution)/shard_map/pallas_call | solution.py:192
  36.5 1.9 %collective-permute-start.7 = (bf16[16,256,256]{2,1,0:T(8,128)(2,1)S(1)}, bf16[16,256,256]{2,1,0:T(8,128)(2,1)S(1)}, u32[]{:S(2)}, u32[]{:S(2)}) collective-permute-start(bf16[16,256,256]{2,1,0:T(8,128)(2,1)S(1)} %get-tuple-element.32), channel_id=1, source_target_pairs={{0,1},{1,0},{2,3},{3,2},{4,5},{5,4},{6,7},{7,6},{8,9},{9,8},{10,11... | collective-permute-start | bytes 6291464 | tf_op jit(solution)/shard_map/ppermute | solution.py:214
  38.4 3.8 %collective-permute-done.7 = bf16[16,256,256]{2,1,0:T(8,128)(2,1)S(1)} collective-permute-done((bf16[16,256,256]{2,1,0:T(8,128)(2,1)S(1)}, bf16[16,256,256]{2,1,0:T(8,128)(2,1)S(1)}, u32[]{:S(2)}, u32[]{:S(2)}) %collective-permute-start.7) | collective-permute-done | bytes 2097184 | tf_op jit(solution)/shard_map/ppermute | solution.py:214
  42.2 0.8 add_convert_fusion
  43.0 0.0 copy-start
  43.0 0.0 copy-start.1
  43.0 32.1 %all_to_all.15.parts = bf16[16,256,256]{2,1,0:T(8,128)(2,1)S(1)} all-to-all(bf16[16,256,256]{2,1,0:T(8,128)(2,1)S(1)} %add_convert_fusion), channel_id=1, replica_groups={{0,2,4,6,8,10,12,14,16,18,20,22,24,26,28,30},{1,3,5,7,9,11,13,15,17,19,..., dimensions={0} | all-to-all | bytes 4194304 | tf_op jit(solution)/shard_map/all_to_all | solution.py:216
  75.1 1.1 shard_map.95
  76.1 31.6 %all_to_all.16.same = bf16[16,272,256]{2,1,0:T(8,128)(2,1)S(1)} all-to-all(bf16[16,272,256]{2,1,0:T(8,128)(2,1)S(1)} %get-tuple-element.34), channel_id=1, replica_groups={{0,2,4,6,8,10,12,14,16,18,20,22,24,26,28,30},{1,3,5,7,9,11,13,15,17,19,..., dimensions={0} | all-to-all | bytes 4456448 | tf_op jit(solution)/shard_map/all_to_all | solution.py:233
  107.7 2.5 %collective-permute-start.8 = (bf16[16,272,256]{2,1,0:T(8,128)(2,1)S(1)}, bf16[16,272,256]{2,1,0:T(8,128)(2,1)S(1)}, u32[]{:S(2)}, u32[]{:S(2)}) collective-permute-start(bf16[16,272,256]{2,1,0:T(8,128)(2,1)S(1)} %all_to_all.16.same), channel_id=1, source_target_pairs={{0,1},{1,0},{2,3},{3,2},{4,5},{5,4},{6,7},{7,6},{8,9},{9,8},{10,11... | collective-permute-start | bytes 6684680 | tf_op jit(solution)/shard_map/ppermute | solution.py:234
  110.3 4.0 %collective-permute-start.11 = (f32[16,256]{1,0:T(8,128)S(1)}, f32[16,256]{1,0:T(8,128)S(1)}, u32[]{:S(2)}, u32[]{:S(2)}) collective-permute-start(f32[16,256]{1,0:T(8,128)S(1)} %convert_reduce_fusion), channel_id=1, source_target_pairs={{0,96},{32,64},{64,32},{96,0},{128,224},{160,192},{192,160},{224,1... | collective-permute-start | bytes 49160 | tf_op jit(solution)/shard_map/ppermute | solution.py:161
  114.3 2.7 %collective-permute-start.10 = (f32[16,256]{1,0:T(8,128)S(1)}, f32[16,256]{1,0:T(8,128)S(1)}, u32[]{:S(2)}, u32[]{:S(2)}) collective-permute-start(f32[16,256]{1,0:T(8,128)S(1)} %convert_reduce_fusion), channel_id=1, source_target_pairs={{0,64},{32,96},{64,0},{96,32},{128,192},{160,224},{192,128},{224,1... | collective-permute-start | bytes 49160 | tf_op jit(solution)/shard_map/ppermute | solution.py:161
  117.0 1.3 collective-permute-done.10
  118.2 1.3 collective-permute-done.9
  119.5 0.0 collective-permute-done.8.other
  119.5 4.8 %collective-permute-start.12 = (f32[16,256]{1,0:T(8,128)S(1)}, f32[16,256]{1,0:T(8,128)S(1)}, u32[]{:S(2)}, u32[]{:S(2)}) collective-permute-start(f32[16,256]{1,0:T(8,128)S(1)} %add_add_fusion), channel_id=1, source_target_pairs={{0,128},{32,160},{64,192},{96,224},{128,0},{160,32},{192,64},{224,... | collective-permute-start | bytes 49160 | tf_op jit(solution)/shard_map/ppermute | solution.py:161
  124.3 7.5 %shard_map.96 = (bf16[256,256]{1,0:T(8,128)(2,1)S(1)}, bf16[256,256]{1,0:T(8,128)(2,1)S(1)}, bf16[256,256]{1,0:T(8,128)(2,1)S(1)}, bf16[256,256]{1,0:T(8,128)(2,...) custom-call(s32[2]{0:T(128)S(1)} %pad_add_fusion.place, ...), custom_call_target="tpu_custom_call" | custom-call | flops 1610612736 | bytes 11534336 | tf_op jit(solution)/shard_map/pallas_call | solution.py:240
  131.9 0.0 collective-permute-done.12
  131.9 0.9 broadcast_in_dim.2
  132.8 5.6 %all-to-all-start.2 = ((f32[32,16,256]{2,1,0:T(8,128)}), f32[32,16,256]{2,1,0:T(8,128)S(1)}, u32[]{:S(2)}, u32[]{:S(2)}) async-start(f32[32,16,256]{2,1,0:T(8,128)} %broadcast_in_dim.2), calls=%async_computation.2 | async-start | bytes 1048576 | tf_op jit(solution)/shard_map/all_to_all | solution.py:264
  138.4 0.1 collective-permute-start.13
  138.5 3.2 %collective-permute-start.14 = (bf16[256,256]{1,0:T(8,128)(2,1)S(1)}, bf16[256,256]{1,0:T(8,128)(2,1)S(1)}, u32[]{:S(2)}, u32[]{:S(2)}) collective-permute-start(bf16[256,256]{1,0:T(8,128)(2,1)S(1)} %get-tuple-element.53), channel_id=1, source_target_pairs={{0,160},{32,192},{64,224},{96,0},{128,32},{160,64},{192,96},{224,1... | collective-permute-start | bytes 393224 | tf_op jit(solution)/shard_map/ppermute | solution.py:262
  141.6 0.2 collective-permute-start.15
  141.8 3.2 %collective-permute-start.16 = (bf16[256,256]{1,0:T(8,128)(2,1)S(1)}, bf16[256,256]{1,0:T(8,128)(2,1)S(1)}, u32[]{:S(2)}, u32[]{:S(2)}) collective-permute-start(bf16[256,256]{1,0:T(8,128)(2,1)S(1)} %get-tuple-element.55), channel_id=1, source_target_pairs={{0,192},{32,224},{64,0},{96,32},{128,64},{160,96},{192,128},{224,1... | collective-permute-start | bytes 393224 | tf_op jit(solution)/shard_map/ppermute | solution.py:262
  145.0 5.1 %all-to-all-done.2 = f32[32,16,256]{2,1,0:T(8,128)S(1)} async-done(((f32[32,16,256]{2,1,0:T(8,128)}), f32[32,16,256]{2,1,0:T(8,128)S(1)}, u32[]{:S(2)}, u32[]{:S(2)}) %all-to-all-start.2) | async-done | bytes 524320 | tf_op jit(solution)/shard_map/all_to_all | solution.py:264
  150.1 1.3 collective-permute-start.18
  151.3 7.1 %collective-permute-start.19 = (bf16[256,256]{1,0:T(8,128)(2,1)S(1)}, bf16[256,256]{1,0:T(8,128)(2,1)S(1)}, u32[]{:S(2)}, u32[]{:S(2)}) collective-permute-start(bf16[256,256]{1,0:T(8,128)(2,1)S(1)} %get-tuple-element.58), channel_id=1, source_target_pairs={{0,32},{32,64},{64,96},{96,128},{128,160},{160,192},{192,224},{224... | collective-permute-start | bytes 393224 | tf_op jit(solution)/shard_map/ppermute | solution.py:267
  158.4 0.7 bitcast_reduce_fusion
  159.1 1.2 collective-permute-done.16
  160.4 2.3 %collective-permute-done.17 = bf16[256,256]{1,0:T(8,128)(2,1)S(1)} collective-permute-done((bf16[256,256]{1,0:T(8,128)(2,1)S(1)}, bf16[256,256]{1,0:T(8,128)(2,1)S(1)}, u32[]{:S(2)}, u32[]{:S(2)}) %collective-permute-start.17) | collective-permute-done | bytes 131104 | tf_op jit(solution)/shard_map/ppermute | solution.py:267
  162.6 0.0 collective-permute-done.18
  162.6 2.0 %collective-permute-done.19 = bf16[256,256]{1,0:T(8,128)(2,1)S(1)} collective-permute-done((bf16[256,256]{1,0:T(8,128)(2,1)S(1)}, bf16[256,256]{1,0:T(8,128)(2,1)S(1)}, u32[]{:S(2)}, u32[]{:S(2)}) %collective-permute-start.19) | collective-permute-done | bytes 131104 | tf_op jit(solution)/shard_map/ppermute | solution.py:267
  164.6 0.8 fusion
  (11 shorter events, 0.1 us)
Async XLA Ops:
  0.6 10.5 %collective-permute-start.6 = (bf16[2,128,256]{2,1,0:T(8,128)(2,1)}, bf16[2,128,256]{2,1,0:T(8,128)(2,1)S(1)}, u32[]{:S(2)}, u32[]{:S(2)}) collective-permute-start(bf16[2,128,256]{2,1,0:T(8,128)(2,1)} %bitcast.17), channel_id=1, source_target_pairs={{0,32},{32,64},{64,96},{96,128},{128,160},{160,192},{192,224},{224... | collective-permute-start | bytes 393224 | tf_op jit(solution)/shard_map/ppermute | solution.py:190
  3.2 12.1 %collective-permute-start.5 = (bf16[2,128,256]{2,1,0:T(8,128)(2,1)}, bf16[2,128,256]{2,1,0:T(8,128)(2,1)S(1)}, u32[]{:S(2)}, u32[]{:S(2)}) collective-permute-start(bf16[2,128,256]{2,1,0:T(8,128)(2,1)} %bitcast.18), channel_id=1, source_target_pairs={{0,224},{32,0},{64,32},{96,64},{128,96},{160,128},{192,160},{224,1... | collective-permute-start | bytes 393224 | tf_op jit(solution)/shard_map/ppermute | solution.py:190
  7.2 12.7 %collective-permute-start.4 = (bf16[2,128,256]{2,1,0:T(8,128)(2,1)}, bf16[2,128,256]{2,1,0:T(8,128)(2,1)S(1)}, u32[]{:S(2)}, u32[]{:S(2)}) collective-permute-start(bf16[2,128,256]{2,1,0:T(8,128)(2,1)} %bitcast.19), channel_id=1, source_target_pairs={{0,64},{32,96},{64,128},{96,160},{128,192},{160,224},{192,0},{224,... | collective-permute-start | bytes 393224 | tf_op jit(solution)/shard_map/ppermute | solution.py:190
  7.2 12.8 %collective-permute-start.3 = (bf16[2,128,256]{2,1,0:T(8,128)(2,1)}, bf16[2,128,256]{2,1,0:T(8,128)(2,1)S(1)}, u32[]{:S(2)}, u32[]{:S(2)}) collective-permute-start(bf16[2,128,256]{2,1,0:T(8,128)(2,1)} %bitcast.20), channel_id=1, source_target_pairs={{0,192},{32,224},{64,0},{96,32},{128,64},{160,96},{192,128},{224,1... | collective-permute-start | bytes 393224 | tf_op jit(solution)/shard_map/ppermute | solution.py:190
  10.8 17.6 %collective-permute-start.2 = (bf16[2,128,256]{2,1,0:T(8,128)(2,1)}, bf16[2,128,256]{2,1,0:T(8,128)(2,1)S(1)}, u32[]{:S(2)}, u32[]{:S(2)}) collective-permute-start(bf16[2,128,256]{2,1,0:T(8,128)(2,1)} %bitcast.21), channel_id=1, source_target_pairs={{0,96},{32,128},{64,160},{96,192},{128,224},{160,0},{192,32},{224,... | collective-permute-start | bytes 393224 | tf_op jit(solution)/shard_map/ppermute | solution.py:190
  11.1 17.3 %collective-permute-start.1 = (bf16[2,128,256]{2,1,0:T(8,128)(2,1)}, bf16[2,128,256]{2,1,0:T(8,128)(2,1)S(1)}, u32[]{:S(2)}, u32[]{:S(2)}) collective-permute-start(bf16[2,128,256]{2,1,0:T(8,128)(2,1)} %bitcast.22), channel_id=1, source_target_pairs={{0,160},{32,192},{64,224},{96,0},{128,32},{160,64},{192,96},{224,1... | collective-permute-start | bytes 393224 | tf_op jit(solution)/shard_map/ppermute | solution.py:190
  15.3 13.1 %collective-permute-start = (bf16[2,128,256]{2,1,0:T(8,128)(2,1)}, bf16[2,128,256]{2,1,0:T(8,128)(2,1)S(1)}, u32[]{:S(2)}, u32[]{:S(2)}) collective-permute-start(bf16[2,128,256]{2,1,0:T(8,128)(2,1)} %bitcast.23), channel_id=1, source_target_pairs={{0,128},{32,160},{64,192},{96,224},{128,0},{160,32},{192,64},{224,... | collective-permute-start | bytes 393224 | tf_op jit(solution)/shard_map/ppermute | solution.py:190
  36.5 5.7 %collective-permute-start.7 = (bf16[16,256,256]{2,1,0:T(8,128)(2,1)S(1)}, bf16[16,256,256]{2,1,0:T(8,128)(2,1)S(1)}, u32[]{:S(2)}, u32[]{:S(2)}) collective-permute-start(bf16[16,256,256]{2,1,0:T(8,128)(2,1)S(1)} %get-tuple-element.32), channel_id=1, source_target_pairs={{0,1},{1,0},{2,3},{3,2},{4,5},{5,4},{6,7},{7,6},{8,9},{9,8},{10,11... | collective-permute-start | bytes 6291464 | tf_op jit(solution)/shard_map/ppermute | solution.py:214
  43.0 32.1 %copy-start = (bf16[256,256]{1,0:T(8,128)(2,1)S(1)}, bf16[256,256]{1,0:T(8,128)(2,1)}, u32[]{:S(2)}) copy-start(bf16[256,256]{1,0:T(8,128)(2,1)} %weight.1) | copy-start | bytes 393220
  43.0 32.1 %copy-start.1 = (bf16[256,256]{1,0:T(8,128)(2,1)S(1)}, bf16[256,256]{1,0:T(8,128)(2,1)}, u32[]{:S(2)}) copy-start(bf16[256,256]{1,0:T(8,128)(2,1)} %cotangent.1) | copy-start | bytes 393220
  107.7 11.8 %collective-permute-start.8 = (bf16[16,272,256]{2,1,0:T(8,128)(2,1)S(1)}, bf16[16,272,256]{2,1,0:T(8,128)(2,1)S(1)}, u32[]{:S(2)}, u32[]{:S(2)}) collective-permute-start(bf16[16,272,256]{2,1,0:T(8,128)(2,1)S(1)} %all_to_all.16.same), channel_id=1, source_target_pairs={{0,1},{1,0},{2,3},{3,2},{4,5},{5,4},{6,7},{7,6},{8,9},{9,8},{10,11... | collective-permute-start | bytes 6684680 | tf_op jit(solution)/shard_map/ppermute | solution.py:234
  110.3 6.7 %collective-permute-start.11 = (f32[16,256]{1,0:T(8,128)S(1)}, f32[16,256]{1,0:T(8,128)S(1)}, u32[]{:S(2)}, u32[]{:S(2)}) collective-permute-start(f32[16,256]{1,0:T(8,128)S(1)} %convert_reduce_fusion), channel_id=1, source_target_pairs={{0,96},{32,64},{64,32},{96,0},{128,224},{160,192},{192,160},{224,1... | collective-permute-start | bytes 49160 | tf_op jit(solution)/shard_map/ppermute | solution.py:161
  114.3 4.0 %collective-permute-start.10 = (f32[16,256]{1,0:T(8,128)S(1)}, f32[16,256]{1,0:T(8,128)S(1)}, u32[]{:S(2)}, u32[]{:S(2)}) collective-permute-start(f32[16,256]{1,0:T(8,128)S(1)} %convert_reduce_fusion), channel_id=1, source_target_pairs={{0,64},{32,96},{64,0},{96,32},{128,192},{160,224},{192,128},{224,1... | collective-permute-start | bytes 49160 | tf_op jit(solution)/shard_map/ppermute | solution.py:161
  116.9 2.6 %collective-permute-start.9 = (f32[16,256]{1,0:T(8,128)S(1)}, f32[16,256]{1,0:T(8,128)S(1)}, u32[]{:S(2)}, u32[]{:S(2)}) collective-permute-start(f32[16,256]{1,0:T(8,128)S(1)} %convert_reduce_fusion), channel_id=1, source_target_pairs={{0,32},{32,0},{64,96},{96,64},{128,160},{160,128},{192,224},{224,1... | collective-permute-start | bytes 49160 | tf_op jit(solution)/shard_map/ppermute | solution.py:161
  119.5 12.4 %collective-permute-start.12 = (f32[16,256]{1,0:T(8,128)S(1)}, f32[16,256]{1,0:T(8,128)S(1)}, u32[]{:S(2)}, u32[]{:S(2)}) collective-permute-start(f32[16,256]{1,0:T(8,128)S(1)} %add_add_fusion), channel_id=1, source_target_pairs={{0,128},{32,160},{64,192},{96,224},{128,0},{160,32},{192,64},{224,... | collective-permute-start | bytes 49160 | tf_op jit(solution)/shard_map/ppermute | solution.py:161
  132.8 17.3 %all-to-all-start.2 = ((f32[32,16,256]{2,1,0:T(8,128)}), f32[32,16,256]{2,1,0:T(8,128)S(1)}, u32[]{:S(2)}, u32[]{:S(2)}) async-start(f32[32,16,256]{2,1,0:T(8,128)} %broadcast_in_dim.2), calls=%async_computation.2 | async-start | bytes 1048576 | tf_op jit(solution)/shard_map/all_to_all | solution.py:264
  138.4 11.7 %collective-permute-start.13 = (bf16[256,256]{1,0:T(8,128)(2,1)S(1)}, bf16[256,256]{1,0:T(8,128)(2,1)S(1)}, u32[]{:S(2)}, u32[]{:S(2)}) collective-permute-start(bf16[256,256]{1,0:T(8,128)(2,1)S(1)} %get-tuple-element.52), channel_id=1, source_target_pairs={{0,128},{32,160},{64,192},{96,224},{128,0},{160,32},{192,64},{224,... | collective-permute-start | bytes 393224 | tf_op jit(solution)/shard_map/ppermute | solution.py:262
  138.5 12.9 %collective-permute-start.14 = (bf16[256,256]{1,0:T(8,128)(2,1)S(1)}, bf16[256,256]{1,0:T(8,128)(2,1)S(1)}, u32[]{:S(2)}, u32[]{:S(2)}) collective-permute-start(bf16[256,256]{1,0:T(8,128)(2,1)S(1)} %get-tuple-element.53), channel_id=1, source_target_pairs={{0,160},{32,192},{64,224},{96,0},{128,32},{160,64},{192,96},{224,1... | collective-permute-start | bytes 393224 | tf_op jit(solution)/shard_map/ppermute | solution.py:262
  141.6 17.5 %collective-permute-start.15 = (bf16[256,256]{1,0:T(8,128)(2,1)S(1)}, bf16[256,256]{1,0:T(8,128)(2,1)S(1)}, u32[]{:S(2)}, u32[]{:S(2)}) collective-permute-start(bf16[256,256]{1,0:T(8,128)(2,1)S(1)} %get-tuple-element.54), channel_id=1, source_target_pairs={{0,96},{32,128},{64,160},{96,192},{128,224},{160,0},{192,32},{224,... | collective-permute-start | bytes 393224 | tf_op jit(solution)/shard_map/ppermute | solution.py:262
  141.8 18.6 %collective-permute-start.16 = (bf16[256,256]{1,0:T(8,128)(2,1)S(1)}, bf16[256,256]{1,0:T(8,128)(2,1)S(1)}, u32[]{:S(2)}, u32[]{:S(2)}) collective-permute-start(bf16[256,256]{1,0:T(8,128)(2,1)S(1)} %get-tuple-element.55), channel_id=1, source_target_pairs={{0,192},{32,224},{64,0},{96,32},{128,64},{160,96},{192,128},{224,1... | collective-permute-start | bytes 393224 | tf_op jit(solution)/shard_map/ppermute | solution.py:262
  150.0 12.6 %collective-permute-start.17 = (bf16[256,256]{1,0:T(8,128)(2,1)S(1)}, bf16[256,256]{1,0:T(8,128)(2,1)S(1)}, u32[]{:S(2)}, u32[]{:S(2)}) collective-permute-start(bf16[256,256]{1,0:T(8,128)(2,1)S(1)} %get-tuple-element.56), channel_id=1, source_target_pairs={{0,64},{32,96},{64,128},{96,160},{128,192},{160,224},{192,0},{224,... | collective-permute-start | bytes 393224 | tf_op jit(solution)/shard_map/ppermute | solution.py:267
  150.1 12.6 %collective-permute-start.18 = (bf16[256,256]{1,0:T(8,128)(2,1)S(1)}, bf16[256,256]{1,0:T(8,128)(2,1)S(1)}, u32[]{:S(2)}, u32[]{:S(2)}) collective-permute-start(bf16[256,256]{1,0:T(8,128)(2,1)S(1)} %get-tuple-element.57), channel_id=1, source_target_pairs={{0,224},{32,0},{64,32},{96,64},{128,96},{160,128},{192,160},{224,1... | collective-permute-start | bytes 393224 | tf_op jit(solution)/shard_map/ppermute | solution.py:267
  151.3 13.3 %collective-permute-start.19 = (bf16[256,256]{1,0:T(8,128)(2,1)S(1)}, bf16[256,256]{1,0:T(8,128)(2,1)S(1)}, u32[]{:S(2)}, u32[]{:S(2)}) collective-permute-start(bf16[256,256]{1,0:T(8,128)(2,1)S(1)} %get-tuple-element.58), channel_id=1, source_target_pairs={{0,32},{32,64},{64,96},{96,128},{128,160},{160,192},{192,224},{224... | collective-permute-start | bytes 393224 | tf_op jit(solution)/shard_map/ppermute | solution.py:267

commit v10 on v9

--- a/solution.py
+++ b/solution.py
@@ -233,9 +233,9 @@
     same = lax.all_to_all(grad_agg, "col", 0, 0, tiled=True, axis_index_groups=same_core)
     other = lax.ppermute(same, "col", swap)
     strips = jnp.sum(same[:, nodes:].astype(F32), axis=0)
-    strips = add_partners(strips, n_row, range(1, n_row // 2))
+    strips = add_partners(strips, n_row, [1])
     same, other, strips = lax.optimization_barrier((same, other, strips))
-    strips = add_partners(strips, n_row, [n_row // 2])
+    strips = add_partners(strips, n_row, range(2, n_row, 2))
 
     shares = pl.pallas_call(
         functools.partial(backward_kernel, chunk, steps),

time: 166 us -> 167 us (level)
  starting transfers between devices: 55 us -> 57.4 us
    ppermute x7, waiting for transfers between devices: 5.48 us -> 9.14 us  [per_device(): lax.ppermute(share, 'row', turn(n_row, step))]
    all_to_all x1, waiting for transfers between devices: 5.05 us -> 1.72 us  [per_device(): every = lax.all_to_all(copies, 'col', 0, 0, tiled=True)]
    ppermute x7, starting transfers between devices: 15 us -> 17.6 us  [per_device(): lax.ppermute(share, 'row', turn(n_row, step))]
  transfers between devices with their start and end apart: 21 -> 21, of which waited for: 9 -> 8; matrix products, arithmetic and copies ran while one was open for 1% -> 1% of each run, Pallas kernels for 5% -> 5%
where the time goes in v10:
time: 167 us; the launch traced here: 166 us
  blocking collectives  63.5 us (38%)
  starting transfers between devices  57.4 us (34%)
  waiting for transfers between devices  24.3 us (15%)
  Pallas kernels  16.7 us (10%)
  other arithmetic  2.42 us (1%)
    all_to_all x1, blocking collectives, per_device(): lax.all_to_all(shares, 'col', 0, 0, tiled=True, axis_index_groups=same_core)  31.9 us
    all_to_all x1, blocking collectives, per_device(): lax.all_to_all(grad_agg, 'col', 0, 0, tiled=True, axis_index_groups=same_...  31.6 us
    ppermute x7, starting transfers between devices, per_device(): lax.ppermute(own, 'row', turn(n_row, k))  18.5 us
    ppermute x7, starting transfers between devices, per_device(): lax.ppermute(share, 'row', turn(n_row, step))  17.6 us
    ppermute x4, starting transfers between devices, add_partners(): lax.ppermute(value, 'row', [(i, i ^ distance) for i in range(size)])  11.5 us
    ppermute x7, waiting for transfers between devices, per_device(): lax.ppermute(share, 'row', turn(n_row, step))  9.14 us
    ppermute x7, waiting for transfers between devices, per_device(): lax.ppermute(own, 'row', turn(n_row, k))  8.49 us
    pallas_call x1, Pallas kernels, per_device(): pl.pallas_call(functools.partial(forward_kernel, chunk, arrival), out_sha...  8.05 us
  transfers between devices with their start and end apart: 21, of which 8 were waited for; matrix products, arithmetic and copies ran while one was open for 1% of the time, Pallas kernels for 5%

profile of v10, /device:TPU:1, one launch (start us, length us, event | category | flops | bytes accessed | tf_op | source)
XLA Modules:
  0.0 166.5 jit_solution(18017813009849579760)
XLA Ops:
  0.6 2.5 %collective-permute-start.6 = (bf16[2,128,256]{2,1,0:T(8,128)(2,1)}, bf16[2,128,256]{2,1,0:T(8,128)(2,1)S(1)}, u32[]{:S(2)}, u32[]{:S(2)}) collective-permute-start(bf16[2,128,256]{2,1,0:T(8,128)(2,1)} %bitcast.17), channel_id=1, source_target_pairs={{0,32},{32,64},{64,96},{96,128},{128,160},{160,192},{192,224},{224... | collective-permute-start | bytes 393224 | tf_op jit(solution)/shard_map/ppermute | solution.py:190
  3.2 4.0 %collective-permute-start.5 = (bf16[2,128,256]{2,1,0:T(8,128)(2,1)}, bf16[2,128,256]{2,1,0:T(8,128)(2,1)S(1)}, u32[]{:S(2)}, u32[]{:S(2)}) collective-permute-start(bf16[2,128,256]{2,1,0:T(8,128)(2,1)} %bitcast.18), channel_id=1, source_target_pairs={{0,224},{32,0},{64,32},{96,64},{128,96},{160,128},{192,160},{224,1... | collective-permute-start | bytes 393224 | tf_op jit(solution)/shard_map/ppermute | solution.py:190
  7.2 3.6 %collective-permute-start.3 = (bf16[2,128,256]{2,1,0:T(8,128)(2,1)}, bf16[2,128,256]{2,1,0:T(8,128)(2,1)S(1)}, u32[]{:S(2)}, u32[]{:S(2)}) collective-permute-start(bf16[2,128,256]{2,1,0:T(8,128)(2,1)} %bitcast.20), channel_id=1, source_target_pairs={{0,192},{32,224},{64,0},{96,32},{128,64},{160,96},{192,128},{224,1... | collective-permute-start | bytes 393224 | tf_op jit(solution)/shard_map/ppermute | solution.py:190
  10.8 0.3 collective-permute-start.2
  11.1 0.0 collective-permute-done.6.refs_7_
  11.1 4.2 %collective-permute-start.1 = (bf16[2,128,256]{2,1,0:T(8,128)(2,1)}, bf16[2,128,256]{2,1,0:T(8,128)(2,1)S(1)}, u32[]{:S(2)}, u32[]{:S(2)}) collective-permute-start(bf16[2,128,256]{2,1,0:T(8,128)(2,1)} %bitcast.22), channel_id=1, source_target_pairs={{0,160},{32,192},{64,224},{96,0},{128,32},{160,64},{192,96},{224,1... | collective-permute-start | bytes 393224 | tf_op jit(solution)/shard_map/ppermute | solution.py:190
  15.3 0.0 collective-permute-done.5.refs_6_
  15.3 3.9 %collective-permute-start = (bf16[2,128,256]{2,1,0:T(8,128)(2,1)}, bf16[2,128,256]{2,1,0:T(8,128)(2,1)S(1)}, u32[]{:S(2)}, u32[]{:S(2)}) collective-permute-start(bf16[2,128,256]{2,1,0:T(8,128)(2,1)} %bitcast.23), channel_id=1, source_target_pairs={{0,128},{32,160},{64,192},{96,224},{128,0},{160,32},{192,64},{224,... | collective-permute-start | bytes 393224 | tf_op jit(solution)/shard_map/ppermute | solution.py:190
  19.8 0.1 pad_add_fusion.place
  19.9 0.0 collective-permute-done.4.refs_5_
  19.9 0.1 collective-permute-done.3.refs_4_
  20.0 8.4 %collective-permute-done.2.refs_3_ = bf16[2,128,256]{2,1,0:T(8,128)(2,1)S(1)} collective-permute-done((bf16[2,128,256]{2,1,0:T(8,128)(2,1)}, bf16[2,128,256]{2,1,0:T(8,128)(2,1)S(1)}, u32[]{:S(2)}, u32[]{:S(2)}) %collective-permute-start.2) | collective-permute-done | bytes 131104 | tf_op jit(solution)/shard_map/ppermute | solution.py:190
  28.4 0.0 collective-permute-done.1.refs_2_
  28.4 0.0 collective-permute-done.refs_1_
  28.4 8.1 %shard_map.94 = (bf16[16,256,256]{2,1,0:T(8,128)(2,1)S(1)}, f32[16,256,256]{2,1,0:T(8,128)S(1)}) custom-call(s32[2]{0:T(128)S(1)} %pad_add_fusion.place, s32[1]{0:T(128)} %bitcast.12.count, s32[192]{0:T(256)} %bitcast.25, s32[192]{0:T(256)} %bitcast.27, bf16[192,128,128]{2,1,0:T(8,128)(2,1)} %bitcast.14, bf16[2,128,256]{2,1,0:T(8,128)(2,1)} %bitcast.24, ...), custom_call_target="tpu_custom_call" | custom-call | flops 1610612736 | bytes 14680064 | tf_op jit(solution)/shard_map/pallas_call | solution.py:192
  36.5 1.9 %collective-permute-start.7 = (bf16[16,256,256]{2,1,0:T(8,128)(2,1)S(1)}, bf16[16,256,256]{2,1,0:T(8,128)(2,1)S(1)}, u32[]{:S(2)}, u32[]{:S(2)}) collective-permute-start(bf16[16,256,256]{2,1,0:T(8,128)(2,1)S(1)} %get-tuple-element.32), channel_id=1, source_target_pairs={{0,1},{1,0},{2,3},{3,2},{4,5},{5,4},{6,7},{7,6},{8,9},{9,8},{10,11... | collective-permute-start | bytes 6291464 | tf_op jit(solution)/shard_map/ppermute | solution.py:214
  38.4 3.8 %collective-permute-done.7 = bf16[16,256,256]{2,1,0:T(8,128)(2,1)S(1)} collective-permute-done((bf16[16,256,256]{2,1,0:T(8,128)(2,1)S(1)}, bf16[16,256,256]{2,1,0:T(8,128)(2,1)S(1)}, u32[]{:S(2)}, u32[]{:S(2)}) %collective-permute-start.7) | collective-permute-done | bytes 2097184 | tf_op jit(solution)/shard_map/ppermute | solution.py:214
  42.2 0.8 add_convert_fusion
  43.0 0.0 copy-start
  43.0 0.0 copy-start.1
  43.0 31.9 %all_to_all.15.parts = bf16[16,256,256]{2,1,0:T(8,128)(2,1)S(1)} all-to-all(bf16[16,256,256]{2,1,0:T(8,128)(2,1)S(1)} %add_convert_fusion), channel_id=1, replica_groups={{0,2,4,6,8,10,12,14,16,18,20,22,24,26,28,30},{1,3,5,7,9,11,13,15,17,19,..., dimensions={0} | all-to-all | bytes 4194304 | tf_op jit(solution)/shard_map/all_to_all | solution.py:216
  74.9 1.1 shard_map.95
  76.0 31.6 %all_to_all.16.same = bf16[16,272,256]{2,1,0:T(8,128)(2,1)S(1)} all-to-all(bf16[16,272,256]{2,1,0:T(8,128)(2,1)S(1)} %get-tuple-element.34), channel_id=1, replica_groups={{0,2,4,6,8,10,12,14,16,18,20,22,24,26,28,30},{1,3,5,7,9,11,13,15,17,19,..., dimensions={0} | all-to-all | bytes 4456448 | tf_op jit(solution)/shard_map/all_to_all | solution.py:233
  107.6 2.5 %collective-permute-start.8 = (bf16[16,272,256]{2,1,0:T(8,128)(2,1)S(1)}, bf16[16,272,256]{2,1,0:T(8,128)(2,1)S(1)}, u32[]{:S(2)}, u32[]{:S(2)}) collective-permute-start(bf16[16,272,256]{2,1,0:T(8,128)(2,1)S(1)} %all_to_all.16.same), channel_id=1, source_target_pairs={{0,1},{1,0},{2,3},{3,2},{4,5},{5,4},{6,7},{7,6},{8,9},{9,8},{10,11... | collective-permute-start | bytes 6684680 | tf_op jit(solution)/shard_map/ppermute | solution.py:234
  110.1 5.7 %collective-permute-start.9 = (f32[16,256]{1,0:T(8,128)S(1)}, f32[16,256]{1,0:T(8,128)S(1)}, u32[]{:S(2)}, u32[]{:S(2)}) collective-permute-start(f32[16,256]{1,0:T(8,128)S(1)} %convert_reduce_fusion), channel_id=1, source_target_pairs={{0,32},{32,0},{64,96},{96,64},{128,160},{160,128},{192,224},{224,1... | collective-permute-start | bytes 49160 | tf_op jit(solution)/shard_map/ppermute | solution.py:161
  115.8 1.1 collective-permute-done.9
  117.0 3.4 %collective-permute-start.12 = (f32[16,256]{1,0:T(8,128)S(1)}, f32[16,256]{1,0:T(8,128)S(1)}, u32[]{:S(2)}, u32[]{:S(2)}) collective-permute-start(f32[16,256]{1,0:T(8,128)S(1)} %add.42), channel_id=1, source_target_pairs={{0,192},{32,224},{64,128},{96,160},{128,64},{160,96},{192,0},{224,... | collective-permute-start | bytes 49160 | tf_op jit(solution)/shard_map/ppermute | solution.py:161
  120.4 1.4 collective-permute-start.11
  121.8 0.9 collective-permute-start.10
  122.7 7.5 %shard_map.96 = (bf16[256,256]{1,0:T(8,128)(2,1)S(1)}, bf16[256,256]{1,0:T(8,128)(2,1)S(1)}, bf16[256,256]{1,0:T(8,128)(2,1)S(1)}, bf16[256,256]{1,0:T(8,128)(2,...) custom-call(s32[2]{0:T(128)S(1)} %pad_add_fusion.place, ...), custom_call_target="tpu_custom_call" | custom-call | flops 1610612736 | bytes 11534336 | tf_op jit(solution)/shard_map/pallas_call | solution.py:240
  130.3 0.0 collective-permute-done.12
  130.3 0.0 collective-permute-done.10
  130.3 0.9 broadcast_in_dim.2
  131.2 5.2 %all-to-all-start.2 = ((f32[32,16,256]{2,1,0:T(8,128)}), f32[32,16,256]{2,1,0:T(8,128)S(1)}, u32[]{:S(2)}, u32[]{:S(2)}) async-start(f32[32,16,256]{2,1,0:T(8,128)} %broadcast_in_dim.2), calls=%async_computation.2 | async-start | bytes 1048576 | tf_op jit(solution)/shard_map/all_to_all | solution.py:264
  136.4 3.6 %collective-permute-start.13 = (bf16[256,256]{1,0:T(8,128)(2,1)S(1)}, bf16[256,256]{1,0:T(8,128)(2,1)S(1)}, u32[]{:S(2)}, u32[]{:S(2)}) collective-permute-start(bf16[256,256]{1,0:T(8,128)(2,1)S(1)} %get-tuple-element.52), channel_id=1, source_target_pairs={{0,128},{32,160},{64,192},{96,224},{128,0},{160,32},{192,64},{224,... | collective-permute-start | bytes 393224 | tf_op jit(solution)/shard_map/ppermute | solution.py:262
  140.1 1.9 %collective-permute-start.14 = (bf16[256,256]{1,0:T(8,128)(2,1)S(1)}, bf16[256,256]{1,0:T(8,128)(2,1)S(1)}, u32[]{:S(2)}, u32[]{:S(2)}) collective-permute-start(bf16[256,256]{1,0:T(8,128)(2,1)S(1)} %get-tuple-element.53), channel_id=1, source_target_pairs={{0,160},{32,192},{64,224},{96,0},{128,32},{160,64},{192,96},{224,1... | collective-permute-start | bytes 393224 | tf_op jit(solution)/shard_map/ppermute | solution.py:262
  142.0 1.3 collective-permute-start.15
  143.3 3.1 %collective-permute-start.16 = (bf16[256,256]{1,0:T(8,128)(2,1)S(1)}, bf16[256,256]{1,0:T(8,128)(2,1)S(1)}, u32[]{:S(2)}, u32[]{:S(2)}) collective-permute-start(bf16[256,256]{1,0:T(8,128)(2,1)S(1)} %get-tuple-element.55), channel_id=1, source_target_pairs={{0,192},{32,224},{64,0},{96,32},{128,64},{160,96},{192,128},{224,1... | collective-permute-start | bytes 393224 | tf_op jit(solution)/shard_map/ppermute | solution.py:262
  146.4 1.7 %all-to-all-done.2 = f32[32,16,256]{2,1,0:T(8,128)S(1)} async-done(((f32[32,16,256]{2,1,0:T(8,128)}), f32[32,16,256]{2,1,0:T(8,128)S(1)}, u32[]{:S(2)}, u32[]{:S(2)}) %all-to-all-start.2) | async-done | bytes 524320 | tf_op jit(solution)/shard_map/all_to_all | solution.py:264
  148.1 0.0 collective-permute-start.17
  148.1 0.0 collective-permute-done.13
  148.1 3.6 %collective-permute-start.18 = (bf16[256,256]{1,0:T(8,128)(2,1)S(1)}, bf16[256,256]{1,0:T(8,128)(2,1)S(1)}, u32[]{:S(2)}, u32[]{:S(2)}) collective-permute-start(bf16[256,256]{1,0:T(8,128)(2,1)S(1)} %get-tuple-element.57), channel_id=1, source_target_pairs={{0,224},{32,0},{64,32},{96,64},{128,96},{160,128},{192,160},{224,1... | collective-permute-start | bytes 393224 | tf_op jit(solution)/shard_map/ppermute | solution.py:267
  151.7 4.8 %collective-permute-done.14 = bf16[256,256]{1,0:T(8,128)(2,1)S(1)} collective-permute-done((bf16[256,256]{1,0:T(8,128)(2,1)S(1)}, bf16[256,256]{1,0:T(8,128)(2,1)S(1)}, u32[]{:S(2)}, u32[]{:S(2)}) %collective-permute-start.14) | collective-permute-done | bytes 131104 | tf_op jit(solution)/shard_map/ppermute | solution.py:262
  156.5 4.1 %collective-permute-start.19 = (bf16[256,256]{1,0:T(8,128)(2,1)S(1)}, bf16[256,256]{1,0:T(8,128)(2,1)S(1)}, u32[]{:S(2)}, u32[]{:S(2)}) collective-permute-start(bf16[256,256]{1,0:T(8,128)(2,1)S(1)} %get-tuple-element.58), channel_id=1, source_target_pairs={{0,32},{32,64},{64,96},{96,128},{128,160},{160,192},{192,224},{224... | collective-permute-start | bytes 393224 | tf_op jit(solution)/shard_map/ppermute | solution.py:267
  160.6 0.7 bitcast_reduce_fusion
  161.3 2.0 %collective-permute-done.16 = bf16[256,256]{1,0:T(8,128)(2,1)S(1)} collective-permute-done((bf16[256,256]{1,0:T(8,128)(2,1)S(1)}, bf16[256,256]{1,0:T(8,128)(2,1)S(1)}, u32[]{:S(2)}, u32[]{:S(2)}) %collective-permute-start.16) | collective-permute-done | bytes 131104 | tf_op jit(solution)/shard_map/ppermute | solution.py:262
  163.3 2.3 %collective-permute-done.18 = bf16[256,256]{1,0:T(8,128)(2,1)S(1)} collective-permute-done((bf16[256,256]{1,0:T(8,128)(2,1)S(1)}, bf16[256,256]{1,0:T(8,128)(2,1)S(1)}, u32[]{:S(2)}, u32[]{:S(2)}) %collective-permute-start.18) | collective-permute-done | bytes 131104 | tf_op jit(solution)/shard_map/ppermute | solution.py:267
  165.7 0.8 fusion
  (11 shorter events, 0.1 us)
Async XLA Ops:
  0.6 10.5 %collective-permute-start.6 = (bf16[2,128,256]{2,1,0:T(8,128)(2,1)}, bf16[2,128,256]{2,1,0:T(8,128)(2,1)S(1)}, u32[]{:S(2)}, u32[]{:S(2)}) collective-permute-start(bf16[2,128,256]{2,1,0:T(8,128)(2,1)} %bitcast.17), channel_id=1, source_target_pairs={{0,32},{32,64},{64,96},{96,128},{128,160},{160,192},{192,224},{224... | collective-permute-start | bytes 393224 | tf_op jit(solution)/shard_map/ppermute | solution.py:190
  3.2 12.1 %collective-permute-start.5 = (bf16[2,128,256]{2,1,0:T(8,128)(2,1)}, bf16[2,128,256]{2,1,0:T(8,128)(2,1)S(1)}, u32[]{:S(2)}, u32[]{:S(2)}) collective-permute-start(bf16[2,128,256]{2,1,0:T(8,128)(2,1)} %bitcast.18), channel_id=1, source_target_pairs={{0,224},{32,0},{64,32},{96,64},{128,96},{160,128},{192,160},{224,1... | collective-permute-start | bytes 393224 | tf_op jit(solution)/shard_map/ppermute | solution.py:190
  7.2 12.7 %collective-permute-start.4 = (bf16[2,128,256]{2,1,0:T(8,128)(2,1)}, bf16[2,128,256]{2,1,0:T(8,128)(2,1)S(1)}, u32[]{:S(2)}, u32[]{:S(2)}) collective-permute-start(bf16[2,128,256]{2,1,0:T(8,128)(2,1)} %bitcast.19), channel_id=1, source_target_pairs={{0,64},{32,96},{64,128},{96,160},{128,192},{160,224},{192,0},{224,... | collective-permute-start | bytes 393224 | tf_op jit(solution)/shard_map/ppermute | solution.py:190
  7.2 12.8 %collective-permute-start.3 = (bf16[2,128,256]{2,1,0:T(8,128)(2,1)}, bf16[2,128,256]{2,1,0:T(8,128)(2,1)S(1)}, u32[]{:S(2)}, u32[]{:S(2)}) collective-permute-start(bf16[2,128,256]{2,1,0:T(8,128)(2,1)} %bitcast.20), channel_id=1, source_target_pairs={{0,192},{32,224},{64,0},{96,32},{128,64},{160,96},{192,128},{224,1... | collective-permute-start | bytes 393224 | tf_op jit(solution)/shard_map/ppermute | solution.py:190
  10.8 17.6 %collective-permute-start.2 = (bf16[2,128,256]{2,1,0:T(8,128)(2,1)}, bf16[2,128,256]{2,1,0:T(8,128)(2,1)S(1)}, u32[]{:S(2)}, u32[]{:S(2)}) collective-permute-start(bf16[2,128,256]{2,1,0:T(8,128)(2,1)} %bitcast.21), channel_id=1, source_target_pairs={{0,96},{32,128},{64,160},{96,192},{128,224},{160,0},{192,32},{224,... | collective-permute-start | bytes 393224 | tf_op jit(solution)/shard_map/ppermute | solution.py:190
  11.1 17.3 %collective-permute-start.1 = (bf16[2,128,256]{2,1,0:T(8,128)(2,1)}, bf16[2,128,256]{2,1,0:T(8,128)(2,1)S(1)}, u32[]{:S(2)}, u32[]{:S(2)}) collective-permute-start(bf16[2,128,256]{2,1,0:T(8,128)(2,1)} %bitcast.22), channel_id=1, source_target_pairs={{0,160},{32,192},{64,224},{96,0},{128,32},{160,64},{192,96},{224,1... | collective-permute-start | bytes 393224 | tf_op jit(solution)/shard_map/ppermute | solution.py:190
  15.3 13.1 %collective-permute-start = (bf16[2,128,256]{2,1,0:T(8,128)(2,1)}, bf16[2,128,256]{2,1,0:T(8,128)(2,1)S(1)}, u32[]{:S(2)}, u32[]{:S(2)}) collective-permute-start(bf16[2,128,256]{2,1,0:T(8,128)(2,1)} %bitcast.23), channel_id=1, source_target_pairs={{0,128},{32,160},{64,192},{96,224},{128,0},{160,32},{192,64},{224,... | collective-permute-start | bytes 393224 | tf_op jit(solution)/shard_map/ppermute | solution.py:190
  36.5 5.7 %collective-permute-start.7 = (bf16[16,256,256]{2,1,0:T(8,128)(2,1)S(1)}, bf16[16,256,256]{2,1,0:T(8,128)(2,1)S(1)}, u32[]{:S(2)}, u32[]{:S(2)}) collective-permute-start(bf16[16,256,256]{2,1,0:T(8,128)(2,1)S(1)} %get-tuple-element.32), channel_id=1, source_target_pairs={{0,1},{1,0},{2,3},{3,2},{4,5},{5,4},{6,7},{7,6},{8,9},{9,8},{10,11... | collective-permute-start | bytes 6291464 | tf_op jit(solution)/shard_map/ppermute | solution.py:214
  43.0 31.9 %copy-start = (bf16[256,256]{1,0:T(8,128)(2,1)S(1)}, bf16[256,256]{1,0:T(8,128)(2,1)}, u32[]{:S(2)}) copy-start(bf16[256,256]{1,0:T(8,128)(2,1)} %weight.1) | copy-start | bytes 393220
  43.0 31.9 %copy-start.1 = (bf16[256,256]{1,0:T(8,128)(2,1)S(1)}, bf16[256,256]{1,0:T(8,128)(2,1)}, u32[]{:S(2)}) copy-start(bf16[256,256]{1,0:T(8,128)(2,1)} %cotangent.1) | copy-start | bytes 393220
  107.6 9.4 %collective-permute-start.8 = (bf16[16,272,256]{2,1,0:T(8,128)(2,1)S(1)}, bf16[16,272,256]{2,1,0:T(8,128)(2,1)S(1)}, u32[]{:S(2)}, u32[]{:S(2)}) collective-permute-start(bf16[16,272,256]{2,1,0:T(8,128)(2,1)S(1)} %all_to_all.16.same), channel_id=1, source_target_pairs={{0,1},{1,0},{2,3},{3,2},{4,5},{5,4},{6,7},{7,6},{8,9},{9,8},{10,11... | collective-permute-start | bytes 6684680 | tf_op jit(solution)/shard_map/ppermute | solution.py:234
  110.1 6.9 %collective-permute-start.9 = (f32[16,256]{1,0:T(8,128)S(1)}, f32[16,256]{1,0:T(8,128)S(1)}, u32[]{:S(2)}, u32[]{:S(2)}) collective-permute-start(f32[16,256]{1,0:T(8,128)S(1)} %convert_reduce_fusion), channel_id=1, source_target_pairs={{0,32},{32,0},{64,96},{96,64},{128,160},{160,128},{192,224},{224,1... | collective-permute-start | bytes 49160 | tf_op jit(solution)/shard_map/ppermute | solution.py:161
  117.0 13.3 %collective-permute-start.12 = (f32[16,256]{1,0:T(8,128)S(1)}, f32[16,256]{1,0:T(8,128)S(1)}, u32[]{:S(2)}, u32[]{:S(2)}) collective-permute-start(f32[16,256]{1,0:T(8,128)S(1)} %add.42), channel_id=1, source_target_pairs={{0,192},{32,224},{64,128},{96,160},{128,64},{160,96},{192,0},{224,... | collective-permute-start | bytes 49160 | tf_op jit(solution)/shard_map/ppermute | solution.py:161
  120.4 9.9 %collective-permute-start.11 = (f32[16,256]{1,0:T(8,128)S(1)}, f32[16,256]{1,0:T(8,128)S(1)}, u32[]{:S(2)}, u32[]{:S(2)}) collective-permute-start(f32[16,256]{1,0:T(8,128)S(1)} %add.42), channel_id=1, source_target_pairs={{0,128},{32,160},{64,192},{96,224},{128,0},{160,32},{192,64},{224,... | collective-permute-start | bytes 49160 | tf_op jit(solution)/shard_map/ppermute | solution.py:161
  121.8 8.5 %collective-permute-start.10 = (f32[16,256]{1,0:T(8,128)S(1)}, f32[16,256]{1,0:T(8,128)S(1)}, u32[]{:S(2)}, u32[]{:S(2)}) collective-permute-start(f32[16,256]{1,0:T(8,128)S(1)} %add.42), channel_id=1, source_target_pairs={{0,64},{32,96},{64,0},{96,32},{128,192},{160,224},{192,128},{224,1... | collective-permute-start | bytes 49160 | tf_op jit(solution)/shard_map/ppermute | solution.py:161
  131.2 16.9 %all-to-all-start.2 = ((f32[32,16,256]{2,1,0:T(8,128)}), f32[32,16,256]{2,1,0:T(8,128)S(1)}, u32[]{:S(2)}, u32[]{:S(2)}) async-start(f32[32,16,256]{2,1,0:T(8,128)} %broadcast_in_dim.2), calls=%async_computation.2 | async-start | bytes 1048576 | tf_op jit(solution)/shard_map/all_to_all | solution.py:264
  136.4 11.7 %collective-permute-start.13 = (bf16[256,256]{1,0:T(8,128)(2,1)S(1)}, bf16[256,256]{1,0:T(8,128)(2,1)S(1)}, u32[]{:S(2)}, u32[]{:S(2)}) collective-permute-start(bf16[256,256]{1,0:T(8,128)(2,1)S(1)} %get-tuple-element.52), channel_id=1, source_target_pairs={{0,128},{32,160},{64,192},{96,224},{128,0},{160,32},{192,64},{224,... | collective-permute-start | bytes 393224 | tf_op jit(solution)/shard_map/ppermute | solution.py:262
  140.1 16.4 %collective-permute-start.14 = (bf16[256,256]{1,0:T(8,128)(2,1)S(1)}, bf16[256,256]{1,0:T(8,128)(2,1)S(1)}, u32[]{:S(2)}, u32[]{:S(2)}) collective-permute-start(bf16[256,256]{1,0:T(8,128)(2,1)S(1)} %get-tuple-element.53), channel_id=1, source_target_pairs={{0,160},{32,192},{64,224},{96,0},{128,32},{160,64},{192,96},{224,1... | collective-permute-start | bytes 393224 | tf_op jit(solution)/shard_map/ppermute | solution.py:262
  142.0 19.3 %collective-permute-start.15 = (bf16[256,256]{1,0:T(8,128)(2,1)S(1)}, bf16[256,256]{1,0:T(8,128)(2,1)S(1)}, u32[]{:S(2)}, u32[]{:S(2)}) collective-permute-start(bf16[256,256]{1,0:T(8,128)(2,1)S(1)} %get-tuple-element.54), channel_id=1, source_target_pairs={{0,96},{32,128},{64,160},{96,192},{128,224},{160,0},{192,32},{224,... | collective-permute-start | bytes 393224 | tf_op jit(solution)/shard_map/ppermute | solution.py:262
  143.3 20.0 %collective-permute-start.16 = (bf16[256,256]{1,0:T(8,128)(2,1)S(1)}, bf16[256,256]{1,0:T(8,128)(2,1)S(1)}, u32[]{:S(2)}, u32[]{:S(2)}) collective-permute-start(bf16[256,256]{1,0:T(8,128)(2,1)S(1)} %get-tuple-element.55), channel_id=1, source_target_pairs={{0,192},{32,224},{64,0},{96,32},{128,64},{160,96},{192,128},{224,1... | collective-permute-start | bytes 393224 | tf_op jit(solution)/shard_map/ppermute | solution.py:262
  148.1 15.2 %collective-permute-start.17 = (bf16[256,256]{1,0:T(8,128)(2,1)S(1)}, bf16[256,256]{1,0:T(8,128)(2,1)S(1)}, u32[]{:S(2)}, u32[]{:S(2)}) collective-permute-start(bf16[256,256]{1,0:T(8,128)(2,1)S(1)} %get-tuple-element.56), channel_id=1, source_target_pairs={{0,64},{32,96},{64,128},{96,160},{128,192},{160,224},{192,0},{224,... | collective-permute-start | bytes 393224 | tf_op jit(solution)/shard_map/ppermute | solution.py:267
  148.1 17.6 %collective-permute-start.18 = (bf16[256,256]{1,0:T(8,128)(2,1)S(1)}, bf16[256,256]{1,0:T(8,128)(2,1)S(1)}, u32[]{:S(2)}, u32[]{:S(2)}) collective-permute-start(bf16[256,256]{1,0:T(8,128)(2,1)S(1)} %get-tuple-element.57), channel_id=1, source_target_pairs={{0,224},{32,0},{64,32},{96,64},{128,96},{160,128},{192,160},{224,1... | collective-permute-start | bytes 393224 | tf_op jit(solution)/shard_map/ppermute | solution.py:267
  156.5 9.2 %collective-permute-start.19 = (bf16[256,256]{1,0:T(8,128)(2,1)S(1)}, bf16[256,256]{1,0:T(8,128)(2,1)S(1)}, u32[]{:S(2)}, u32[]{:S(2)}) collective-permute-start(bf16[256,256]{1,0:T(8,128)(2,1)S(1)} %get-tuple-element.58), channel_id=1, source_target_pairs={{0,32},{32,64},{64,96},{96,128},{128,160},{160,192},{192,224},{224... | collective-permute-start | bytes 393224 | tf_op jit(solution)/shard_map/ppermute | solution.py:267

commit v11 on v10

--- a/solution.py
+++ b/solution.py
@@ -156,15 +156,6 @@
     return [(i, (i + step) % size) for i in range(size)]
 
 
-def add_partners(value, size, distances):
-    for other in [
-        lax.ppermute(value, "row", [(i, i ^ distance) for i in range(size)])
-        for distance in distances
-    ]:
-        value = value + other
-    return value
-
-
 def per_device(features, weight, cotangent, blk_vals, blk_rows, blk_cols, blk_count):
     n_row, n_col = lax.axis_size("row"), lax.axis_size("col")
     nodes, width = cotangent.shape
@@ -233,9 +224,8 @@
     same = lax.all_to_all(grad_agg, "col", 0, 0, tiled=True, axis_index_groups=same_core)
     other = lax.ppermute(same, "col", swap)
     strips = jnp.sum(same[:, nodes:].astype(F32), axis=0)
-    strips = add_partners(strips, n_row, [1])
-    same, other, strips = lax.optimization_barrier((same, other, strips))
-    strips = add_partners(strips, n_row, range(2, n_row, 2))
+    copies = jnp.broadcast_to(strips[None], (n_row, strip, width))
+    strips = lax.all_to_all(copies, "row", 0, 0, tiled=True)
 
     shares = pl.pallas_call(
         functools.partial(backward_kernel, chunk, steps),
@@ -260,7 +250,7 @@
     order = list(zip(steps, shares))[::-1]
     far, close, own_share = order[: n_row // 2], order[n_row // 2 : -1], shares[0]
     moved = [lax.ppermute(share, "row", turn(n_row, step)) for step, share in far]
-    copies = jnp.broadcast_to(strips[None], (n_col, strip, width))
+    copies = jnp.broadcast_to(jnp.sum(strips, axis=0)[None], (n_col, strip, width))
     every = lax.all_to_all(copies, "col", 0, 0, tiled=True)
     every, held = lax.optimization_barrier((every, [share for unused, share in close]))
     moved += [

time: 167 us -> 165 us (0.988)
  starting transfers between devices: 57.4 us -> 49 us
  waiting for transfers between devices: 24.3 us -> 29 us
    ppermute x4 -> x0, starting transfers between devices: 11.5 us -> none  [add_partners(): lax.ppermute(value, 'row', [(i, i ^ distance) for i in range(size)])]
    all_to_all x0 -> x1, starting transfers between devices: none -> 10.4 us  [per_device(): strips = lax.all_to_all(copies, 'row', 0, 0, tiled=True)]
    ppermute x7, starting transfers between devices: 17.6 us -> 11.1 us  [per_device(): lax.ppermute(share, 'row', turn(n_row, step))]
    ppermute x7, waiting for transfers between devices: 9.14 us -> 13.5 us  [per_device(): lax.ppermute(share, 'row', turn(n_row, step))]
  transfers between devices with their start and end apart: 21 -> 18, of which waited for: 8 -> 7; matrix products, arithmetic and copies ran while one was open for 1% -> 1% of each run, Pallas kernels for 5% -> 6%
where the time goes in v11:
time: 165 us
  blocking collectives  63.4 us (38%)
  starting transfers between devices  49 us (30%)
  waiting for transfers between devices  29 us (18%)
  Pallas kernels  18.2 us (11%)
  other arithmetic  2.42 us (1%)
    all_to_all x1, blocking collectives, per_device(): lax.all_to_all(shares, 'col', 0, 0, tiled=True, axis_index_groups=same_core)  31.8 us
    all_to_all x1, blocking collectives, per_device(): lax.all_to_all(grad_agg, 'col', 0, 0, tiled=True, axis_index_groups=same_...  31.6 us
    ppermute x7, starting transfers between devices, per_device(): lax.ppermute(own, 'row', turn(n_row, k))  18.5 us
    ppermute x7, waiting for transfers between devices, per_device(): lax.ppermute(share, 'row', turn(n_row, step))  13.5 us
    ppermute x7, starting transfers between devices, per_device(): lax.ppermute(share, 'row', turn(n_row, step))  11.1 us
    all_to_all x1, starting transfers between devices, per_device(): strips = lax.all_to_all(copies, 'row', 0, 0, tiled=True)  10.4 us
    pallas_call x1, Pallas kernels, per_device(): pl.pallas_call(functools.partial(backward_kernel, chunk, steps), out_shap...  9.1 us
    ppermute x7, waiting for transfers between devices, per_device(): lax.ppermute(own, 'row', turn(n_row, k))  8.49 us
  transfers between devices with their start and end apart: 18, of which 7 were waited for; matrix products, arithmetic and copies ran while one was open for 1% of the time, Pallas kernels for 6%

profile of v11, /device:TPU:1, one launch (start us, length us, event | category | flops | bytes accessed | tf_op | source)
XLA Modules:
  0.0 164.9 jit_solution(5341235738851507082)
XLA Ops:
  0.6 2.5 %collective-permute-start.6 = (bf16[2,128,256]{2,1,0:T(8,128)(2,1)}, bf16[2,128,256]{2,1,0:T(8,128)(2,1)S(1)}, u32[]{:S(2)}, u32[]{:S(2)}) collective-permute-start(bf16[2,128,256]{2,1,0:T(8,128)(2,1)} %bitcast.17), channel_id=1, source_target_pairs={{0,32},{32,64},{64,96},{96,128},{128,160},{160,192},{192,224},{224... | collective-permute-start | bytes 393224 | tf_op jit(solution)/shard_map/ppermute | solution.py:181
  3.2 4.0 %collective-permute-start.5 = (bf16[2,128,256]{2,1,0:T(8,128)(2,1)}, bf16[2,128,256]{2,1,0:T(8,128)(2,1)S(1)}, u32[]{:S(2)}, u32[]{:S(2)}) collective-permute-start(bf16[2,128,256]{2,1,0:T(8,128)(2,1)} %bitcast.18), channel_id=1, source_target_pairs={{0,224},{32,0},{64,32},{96,64},{128,96},{160,128},{192,160},{224,1... | collective-permute-start | bytes 393224 | tf_op jit(solution)/shard_map/ppermute | solution.py:181
  7.2 0.0 collective-permute-start.4
  7.2 3.6 %collective-permute-start.3 = (bf16[2,128,256]{2,1,0:T(8,128)(2,1)}, bf16[2,128,256]{2,1,0:T(8,128)(2,1)S(1)}, u32[]{:S(2)}, u32[]{:S(2)}) collective-permute-start(bf16[2,128,256]{2,1,0:T(8,128)(2,1)} %bitcast.20), channel_id=1, source_target_pairs={{0,192},{32,224},{64,0},{96,32},{128,64},{160,96},{192,128},{224,1... | collective-permute-start | bytes 393224 | tf_op jit(solution)/shard_map/ppermute | solution.py:181
  10.8 0.3 collective-permute-start.2
  11.1 0.0 collective-permute-done.6.refs_7_
  11.1 4.2 %collective-permute-start.1 = (bf16[2,128,256]{2,1,0:T(8,128)(2,1)}, bf16[2,128,256]{2,1,0:T(8,128)(2,1)S(1)}, u32[]{:S(2)}, u32[]{:S(2)}) collective-permute-start(bf16[2,128,256]{2,1,0:T(8,128)(2,1)} %bitcast.22), channel_id=1, source_target_pairs={{0,160},{32,192},{64,224},{96,0},{128,32},{160,64},{192,96},{224,1... | collective-permute-start | bytes 393224 | tf_op jit(solution)/shard_map/ppermute | solution.py:181
  15.3 0.0 collective-permute-done.5.refs_6_
  15.3 3.9 %collective-permute-start = (bf16[2,128,256]{2,1,0:T(8,128)(2,1)}, bf16[2,128,256]{2,1,0:T(8,128)(2,1)S(1)}, u32[]{:S(2)}, u32[]{:S(2)}) collective-permute-start(bf16[2,128,256]{2,1,0:T(8,128)(2,1)} %bitcast.23), channel_id=1, source_target_pairs={{0,128},{32,160},{64,192},{96,224},{128,0},{160,32},{192,64},{224,... | collective-permute-start | bytes 393224 | tf_op jit(solution)/shard_map/ppermute | solution.py:181
  19.8 0.1 pad_add_fusion.place
  19.9 0.0 collective-permute-done.4.refs_5_
  19.9 0.1 collective-permute-done.3.refs_4_
  20.0 8.4 %collective-permute-done.2.refs_3_ = bf16[2,128,256]{2,1,0:T(8,128)(2,1)S(1)} collective-permute-done((bf16[2,128,256]{2,1,0:T(8,128)(2,1)}, bf16[2,128,256]{2,1,0:T(8,128)(2,1)S(1)}, u32[]{:S(2)}, u32[]{:S(2)}) %collective-permute-start.2) | collective-permute-done | bytes 131104 | tf_op jit(solution)/shard_map/ppermute | solution.py:181
  28.4 0.0 collective-permute-done.1.refs_2_
  28.4 0.0 collective-permute-done.refs_1_
  28.4 8.1 %shard_map.94 = (bf16[16,256,256]{2,1,0:T(8,128)(2,1)S(1)}, f32[16,256,256]{2,1,0:T(8,128)S(1)}) custom-call(s32[2]{0:T(128)S(1)} %pad_add_fusion.place, s32[1]{0:T(128)} %bitcast.12.count, s32[192]{0:T(256)} %bitcast.25, s32[192]{0:T(256)} %bitcast.27, bf16[192,128,128]{2,1,0:T(8,128)(2,1)} %bitcast.14, bf16[2,128,256]{2,1,0:T(8,128)(2,1)} %bitcast.24, ...), custom_call_target="tpu_custom_call" | custom-call | flops 1610612736 | bytes 14680064 | tf_op jit(solution)/shard_map/pallas_call | solution.py:183
  36.5 1.9 %collective-permute-start.7 = (bf16[16,256,256]{2,1,0:T(8,128)(2,1)S(1)}, bf16[16,256,256]{2,1,0:T(8,128)(2,1)S(1)}, u32[]{:S(2)}, u32[]{:S(2)}) collective-permute-start(bf16[16,256,256]{2,1,0:T(8,128)(2,1)S(1)} %get-tuple-element.29), channel_id=1, source_target_pairs={{0,1},{1,0},{2,3},{3,2},{4,5},{5,4},{6,7},{7,6},{8,9},{9,8},{10,11... | collective-permute-start | bytes 6291464 | tf_op jit(solution)/shard_map/ppermute | solution.py:205
  38.4 3.8 %collective-permute-done.7 = bf16[16,256,256]{2,1,0:T(8,128)(2,1)S(1)} collective-permute-done((bf16[16,256,256]{2,1,0:T(8,128)(2,1)S(1)}, bf16[16,256,256]{2,1,0:T(8,128)(2,1)S(1)}, u32[]{:S(2)}, u32[]{:S(2)}) %collective-permute-start.7) | collective-permute-done | bytes 2097184 | tf_op jit(solution)/shard_map/ppermute | solution.py:205
  42.2 0.8 add_convert_fusion
  43.0 0.0 copy-start
  43.0 0.0 copy-start.1
  43.0 31.8 %all_to_all.20.parts = bf16[16,256,256]{2,1,0:T(8,128)(2,1)S(1)} all-to-all(bf16[16,256,256]{2,1,0:T(8,128)(2,1)S(1)} %add_convert_fusion), channel_id=1, replica_groups={{0,2,4,6,8,10,12,14,16,18,20,22,24,26,28,30},{1,3,5,7,9,11,13,15,17,19,..., dimensions={0} | all-to-all | bytes 4194304 | tf_op jit(solution)/shard_map/all_to_all | solution.py:207
  74.8 1.1 shard_map.95
  75.9 31.6 %all_to_all.21.same = bf16[16,272,256]{2,1,0:T(8,128)(2,1)S(1)} all-to-all(bf16[16,272,256]{2,1,0:T(8,128)(2,1)S(1)} %get-tuple-element.31), channel_id=1, replica_groups={{0,2,4,6,8,10,12,14,16,18,20,22,24,26,28,30},{1,3,5,7,9,11,13,15,17,19,..., dimensions={0} | all-to-all | bytes 4456448 | tf_op jit(solution)/shard_map/all_to_all | solution.py:224
  107.5 2.5 %collective-permute-start.8 = (bf16[16,272,256]{2,1,0:T(8,128)(2,1)S(1)}, bf16[16,272,256]{2,1,0:T(8,128)(2,1)}, u32[]{:S(2)}, u32[]{:S(2)}) collective-permute-start(bf16[16,272,256]{2,1,0:T(8,128)(2,1)S(1)} %all_to_all.21.same), channel_id=1, source_target_pairs={{0,1},{1,0},{2,3},{3,2},{4,5},{5,4},{6,7},{7,6},{8,9},{9,8},{10,11... | collective-permute-start | bytes 6684680 | tf_op jit(solution)/shard_map/ppermute | solution.py:225
  110.0 0.7 broadcast_in_dim.4
  110.7 10.4 %all-to-all-start.2 = ((f32[8,16,256]{2,1,0:T(8,128)}), f32[8,16,256]{2,1,0:T(8,128)S(1)}, u32[]{:S(2)}, u32[]{:S(2)}) async-start(f32[8,16,256]{2,1,0:T(8,128)} %broadcast_in_dim.4), calls=%async_computation.2 | async-start | bytes 262144 | tf_op jit(solution)/shard_map/all_to_all | solution.py:228
  121.1 0.0 collective-permute-done.8.other
  121.2 9.1 %shard_map.96 = (bf16[256,256]{1,0:T(8,128)(2,1)S(1)}, bf16[256,256]{1,0:T(8,128)(2,1)S(1)}, bf16[256,256]{1,0:T(8,128)(2,1)S(1)}, bf16[256,256]{1,0:T(8,128)(2,...) custom-call(s32[2]{0:T(128)S(1)} %pad_add_fusion.place, ...), custom_call_target="tpu_custom_call" | custom-call | flops 1610612736 | bytes 11534336 | tf_op jit(solution)/shard_map/pallas_call | solution.py:230
  130.3 0.0 all-to-all-done.2
  130.3 0.9 broadcast_in_dim.5
  131.2 4.4 %all-to-all-start.3 = ((f32[32,16,256]{2,1,0:T(8,128)}), f32[32,16,256]{2,1,0:T(8,128)S(1)}, u32[]{:S(2)}, u32[]{:S(2)}) async-start(f32[32,16,256]{2,1,0:T(8,128)} %broadcast_in_dim.5), calls=%async_computation.3 | async-start | bytes 1048576 | tf_op jit(solution)/shard_map/all_to_all | solution.py:254
  135.6 4.0 %collective-permute-start.9 = (bf16[256,256]{1,0:T(8,128)(2,1)S(1)}, bf16[256,256]{1,0:T(8,128)(2,1)S(1)}, u32[]{:S(2)}, u32[]{:S(2)}) collective-permute-start(bf16[256,256]{1,0:T(8,128)(2,1)S(1)} %get-tuple-element.46), channel_id=1, source_target_pairs={{0,128},{32,160},{64,192},{96,224},{128,0},{160,32},{192,64},{224,... | collective-permute-start | bytes 393224 | tf_op jit(solution)/shard_map/ppermute | solution.py:252
  139.5 0.6 collective-permute-start.10
  140.1 2.7 %collective-permute-start.11 = (bf16[256,256]{1,0:T(8,128)(2,1)S(1)}, bf16[256,256]{1,0:T(8,128)(2,1)S(1)}, u32[]{:S(2)}, u32[]{:S(2)}) collective-permute-start(bf16[256,256]{1,0:T(8,128)(2,1)S(1)} %get-tuple-element.48), channel_id=1, source_target_pairs={{0,96},{32,128},{64,160},{96,192},{128,224},{160,0},{192,32},{224,... | collective-permute-start | bytes 393224 | tf_op jit(solution)/shard_map/ppermute | solution.py:252
  142.8 1.3 collective-permute-start.12
  144.1 3.2 %all-to-all-done.3 = f32[32,16,256]{2,1,0:T(8,128)S(1)} async-done(((f32[32,16,256]{2,1,0:T(8,128)}), f32[32,16,256]{2,1,0:T(8,128)S(1)}, u32[]{:S(2)}, u32[]{:S(2)}) %all-to-all-start.3) | async-done | bytes 524320 | tf_op jit(solution)/shard_map/all_to_all | solution.py:254
  147.3 0.1 collective-permute-start.13
  147.3 0.0 collective-permute-done.9
  147.3 2.5 %collective-permute-start.14 = (bf16[256,256]{1,0:T(8,128)(2,1)S(1)}, bf16[256,256]{1,0:T(8,128)(2,1)S(1)}, u32[]{:S(2)}, u32[]{:S(2)}) collective-permute-start(bf16[256,256]{1,0:T(8,128)(2,1)S(1)} %get-tuple-element.51), channel_id=1, source_target_pairs={{0,224},{32,0},{64,32},{96,64},{128,96},{160,128},{192,160},{224,1... | collective-permute-start | bytes 393224 | tf_op jit(solution)/shard_map/ppermute | solution.py:257
  149.8 5.8 %collective-permute-done.10 = bf16[256,256]{1,0:T(8,128)(2,1)S(1)} collective-permute-done((bf16[256,256]{1,0:T(8,128)(2,1)S(1)}, bf16[256,256]{1,0:T(8,128)(2,1)S(1)}, u32[]{:S(2)}, u32[]{:S(2)}) %collective-permute-start.10) | collective-permute-done | bytes 131104 | tf_op jit(solution)/shard_map/ppermute | solution.py:252
  155.6 0.0 collective-permute-start.15
  155.6 0.7 bitcast_reduce_fusion
  156.4 0.0 collective-permute-done.11
  156.4 5.1 %collective-permute-done.12 = bf16[256,256]{1,0:T(8,128)(2,1)S(1)} collective-permute-done((bf16[256,256]{1,0:T(8,128)(2,1)S(1)}, bf16[256,256]{1,0:T(8,128)(2,1)S(1)}, u32[]{:S(2)}, u32[]{:S(2)}) %collective-permute-start.12) | collective-permute-done | bytes 131104 | tf_op jit(solution)/shard_map/ppermute | solution.py:252
  161.5 0.0 collective-permute-done.13
  161.5 2.6 %collective-permute-done.14 = bf16[256,256]{1,0:T(8,128)(2,1)S(1)} collective-permute-done((bf16[256,256]{1,0:T(8,128)(2,1)S(1)}, bf16[256,256]{1,0:T(8,128)(2,1)S(1)}, u32[]{:S(2)}, u32[]{:S(2)}) %collective-permute-start.14) | collective-permute-done | bytes 131104 | tf_op jit(solution)/shard_map/ppermute | solution.py:257
  164.1 0.8 fusion
  (5 shorter events, 0.0 us)
Async XLA Ops:
  0.6 10.5 %collective-permute-start.6 = (bf16[2,128,256]{2,1,0:T(8,128)(2,1)}, bf16[2,128,256]{2,1,0:T(8,128)(2,1)S(1)}, u32[]{:S(2)}, u32[]{:S(2)}) collective-permute-start(bf16[2,128,256]{2,1,0:T(8,128)(2,1)} %bitcast.17), channel_id=1, source_target_pairs={{0,32},{32,64},{64,96},{96,128},{128,160},{160,192},{192,224},{224... | collective-permute-start | bytes 393224 | tf_op jit(solution)/shard_map/ppermute | solution.py:181
  3.2 12.1 %collective-permute-start.5 = (bf16[2,128,256]{2,1,0:T(8,128)(2,1)}, bf16[2,128,256]{2,1,0:T(8,128)(2,1)S(1)}, u32[]{:S(2)}, u32[]{:S(2)}) collective-permute-start(bf16[2,128,256]{2,1,0:T(8,128)(2,1)} %bitcast.18), channel_id=1, source_target_pairs={{0,224},{32,0},{64,32},{96,64},{128,96},{160,128},{192,160},{224,1... | collective-permute-start | bytes 393224 | tf_op jit(solution)/shard_map/ppermute | solution.py:181
  7.2 12.7 %collective-permute-start.4 = (bf16[2,128,256]{2,1,0:T(8,128)(2,1)}, bf16[2,128,256]{2,1,0:T(8,128)(2,1)S(1)}, u32[]{:S(2)}, u32[]{:S(2)}) collective-permute-start(bf16[2,128,256]{2,1,0:T(8,128)(2,1)} %bitcast.19), channel_id=1, source_target_pairs={{0,64},{32,96},{64,128},{96,160},{128,192},{160,224},{192,0},{224,... | collective-permute-start | bytes 393224 | tf_op jit(solution)/shard_map/ppermute | solution.py:181
  7.2 12.8 %collective-permute-start.3 = (bf16[2,128,256]{2,1,0:T(8,128)(2,1)}, bf16[2,128,256]{2,1,0:T(8,128)(2,1)S(1)}, u32[]{:S(2)}, u32[]{:S(2)}) collective-permute-start(bf16[2,128,256]{2,1,0:T(8,128)(2,1)} %bitcast.20), channel_id=1, source_target_pairs={{0,192},{32,224},{64,0},{96,32},{128,64},{160,96},{192,128},{224,1... | collective-permute-start | bytes 393224 | tf_op jit(solution)/shard_map/ppermute | solution.py:181
  10.8 17.6 %collective-permute-start.2 = (bf16[2,128,256]{2,1,0:T(8,128)(2,1)}, bf16[2,128,256]{2,1,0:T(8,128)(2,1)S(1)}, u32[]{:S(2)}, u32[]{:S(2)}) collective-permute-start(bf16[2,128,256]{2,1,0:T(8,128)(2,1)} %bitcast.21), channel_id=1, source_target_pairs={{0,96},{32,128},{64,160},{96,192},{128,224},{160,0},{192,32},{224,... | collective-permute-start | bytes 393224 | tf_op jit(solution)/shard_map/ppermute | solution.py:181
  11.1 17.3 %collective-permute-start.1 = (bf16[2,128,256]{2,1,0:T(8,128)(2,1)}, bf16[2,128,256]{2,1,0:T(8,128)(2,1)S(1)}, u32[]{:S(2)}, u32[]{:S(2)}) collective-permute-start(bf16[2,128,256]{2,1,0:T(8,128)(2,1)} %bitcast.22), channel_id=1, source_target_pairs={{0,160},{32,192},{64,224},{96,0},{128,32},{160,64},{192,96},{224,1... | collective-permute-start | bytes 393224 | tf_op jit(solution)/shard_map/ppermute | solution.py:181
  15.3 13.1 %collective-permute-start = (bf16[2,128,256]{2,1,0:T(8,128)(2,1)}, bf16[2,128,256]{2,1,0:T(8,128)(2,1)S(1)}, u32[]{:S(2)}, u32[]{:S(2)}) collective-permute-start(bf16[2,128,256]{2,1,0:T(8,128)(2,1)} %bitcast.23), channel_id=1, source_target_pairs={{0,128},{32,160},{64,192},{96,224},{128,0},{160,32},{192,64},{224,... | collective-permute-start | bytes 393224 | tf_op jit(solution)/shard_map/ppermute | solution.py:181
  36.5 5.7 %collective-permute-start.7 = (bf16[16,256,256]{2,1,0:T(8,128)(2,1)S(1)}, bf16[16,256,256]{2,1,0:T(8,128)(2,1)S(1)}, u32[]{:S(2)}, u32[]{:S(2)}) collective-permute-start(bf16[16,256,256]{2,1,0:T(8,128)(2,1)S(1)} %get-tuple-element.29), channel_id=1, source_target_pairs={{0,1},{1,0},{2,3},{3,2},{4,5},{5,4},{6,7},{7,6},{8,9},{9,8},{10,11... | collective-permute-start | bytes 6291464 | tf_op jit(solution)/shard_map/ppermute | solution.py:205
  43.0 31.8 %copy-start = (bf16[256,256]{1,0:T(8,128)(2,1)S(1)}, bf16[256,256]{1,0:T(8,128)(2,1)}, u32[]{:S(2)}) copy-start(bf16[256,256]{1,0:T(8,128)(2,1)} %weight.1) | copy-start | bytes 393220
  43.0 31.8 %copy-start.1 = (bf16[256,256]{1,0:T(8,128)(2,1)S(1)}, bf16[256,256]{1,0:T(8,128)(2,1)}, u32[]{:S(2)}) copy-start(bf16[256,256]{1,0:T(8,128)(2,1)} %cotangent.1) | copy-start | bytes 393220
  107.5 13.7 %collective-permute-start.8 = (bf16[16,272,256]{2,1,0:T(8,128)(2,1)S(1)}, bf16[16,272,256]{2,1,0:T(8,128)(2,1)}, u32[]{:S(2)}, u32[]{:S(2)}) collective-permute-start(bf16[16,272,256]{2,1,0:T(8,128)(2,1)S(1)} %all_to_all.21.same), channel_id=1, source_target_pairs={{0,1},{1,0},{2,3},{3,2},{4,5},{5,4},{6,7},{7,6},{8,9},{9,8},{10,11... | collective-permute-start | bytes 6684680 | tf_op jit(solution)/shard_map/ppermute | solution.py:225
  110.7 19.6 %all-to-all-start.2 = ((f32[8,16,256]{2,1,0:T(8,128)}), f32[8,16,256]{2,1,0:T(8,128)S(1)}, u32[]{:S(2)}, u32[]{:S(2)}) async-start(f32[8,16,256]{2,1,0:T(8,128)} %broadcast_in_dim.4), calls=%async_computation.2 | async-start | bytes 262144 | tf_op jit(solution)/shard_map/all_to_all | solution.py:228
  131.2 16.1 %all-to-all-start.3 = ((f32[32,16,256]{2,1,0:T(8,128)}), f32[32,16,256]{2,1,0:T(8,128)S(1)}, u32[]{:S(2)}, u32[]{:S(2)}) async-start(f32[32,16,256]{2,1,0:T(8,128)} %broadcast_in_dim.5), calls=%async_computation.3 | async-start | bytes 1048576 | tf_op jit(solution)/shard_map/all_to_all | solution.py:254
  135.6 11.7 %collective-permute-start.9 = (bf16[256,256]{1,0:T(8,128)(2,1)S(1)}, bf16[256,256]{1,0:T(8,128)(2,1)S(1)}, u32[]{:S(2)}, u32[]{:S(2)}) collective-permute-start(bf16[256,256]{1,0:T(8,128)(2,1)S(1)} %get-tuple-element.46), channel_id=1, source_target_pairs={{0,128},{32,160},{64,192},{96,224},{128,0},{160,32},{192,64},{224,... | collective-permute-start | bytes 393224 | tf_op jit(solution)/shard_map/ppermute | solution.py:252
  139.5 16.1 %collective-permute-start.10 = (bf16[256,256]{1,0:T(8,128)(2,1)S(1)}, bf16[256,256]{1,0:T(8,128)(2,1)S(1)}, u32[]{:S(2)}, u32[]{:S(2)}) collective-permute-start(bf16[256,256]{1,0:T(8,128)(2,1)S(1)} %get-tuple-element.47), channel_id=1, source_target_pairs={{0,160},{32,192},{64,224},{96,0},{128,32},{160,64},{192,96},{224,1... | collective-permute-start | bytes 393224 | tf_op jit(solution)/shard_map/ppermute | solution.py:252
  140.1 16.3 %collective-permute-start.11 = (bf16[256,256]{1,0:T(8,128)(2,1)S(1)}, bf16[256,256]{1,0:T(8,128)(2,1)S(1)}, u32[]{:S(2)}, u32[]{:S(2)}) collective-permute-start(bf16[256,256]{1,0:T(8,128)(2,1)S(1)} %get-tuple-element.48), channel_id=1, source_target_pairs={{0,96},{32,128},{64,160},{96,192},{128,224},{160,0},{192,32},{224,... | collective-permute-start | bytes 393224 | tf_op jit(solution)/shard_map/ppermute | solution.py:252
  142.8 18.7 %collective-permute-start.12 = (bf16[256,256]{1,0:T(8,128)(2,1)S(1)}, bf16[256,256]{1,0:T(8,128)(2,1)S(1)}, u32[]{:S(2)}, u32[]{:S(2)}) collective-permute-start(bf16[256,256]{1,0:T(8,128)(2,1)S(1)} %get-tuple-element.49), channel_id=1, source_target_pairs={{0,192},{32,224},{64,0},{96,32},{128,64},{160,96},{192,128},{224,1... | collective-permute-start | bytes 393224 | tf_op jit(solution)/shard_map/ppermute | solution.py:252
  147.3 14.2 %collective-permute-start.13 = (bf16[256,256]{1,0:T(8,128)(2,1)S(1)}, bf16[256,256]{1,0:T(8,128)(2,1)S(1)}, u32[]{:S(2)}, u32[]{:S(2)}) collective-permute-start(bf16[256,256]{1,0:T(8,128)(2,1)S(1)} %get-tuple-element.50), channel_id=1, source_target_pairs={{0,64},{32,96},{64,128},{96,160},{128,192},{160,224},{192,0},{224,... | collective-permute-start | bytes 393224 | tf_op jit(solution)/shard_map/ppermute | solution.py:257
  147.3 16.8 %collective-permute-start.14 = (bf16[256,256]{1,0:T(8,128)(2,1)S(1)}, bf16[256,256]{1,0:T(8,128)(2,1)S(1)}, u32[]{:S(2)}, u32[]{:S(2)}) collective-permute-start(bf16[256,256]{1,0:T(8,128)(2,1)S(1)} %get-tuple-element.51), channel_id=1, source_target_pairs={{0,224},{32,0},{64,32},{96,64},{128,96},{160,128},{192,160},{224,1... | collective-permute-start | bytes 393224 | tf_op jit(solution)/shard_map/ppermute | solution.py:257
  155.6 8.5 %collective-permute-start.15 = (bf16[256,256]{1,0:T(8,128)(2,1)S(1)}, bf16[256,256]{1,0:T(8,128)(2,1)S(1)}, u32[]{:S(2)}, u32[]{:S(2)}) collective-permute-start(bf16[256,256]{1,0:T(8,128)(2,1)S(1)} %get-tuple-element.52), channel_id=1, source_target_pairs={{0,32},{32,64},{64,96},{96,128},{128,160},{160,192},{192,224},{224... | collective-permute-start | bytes 393224 | tf_op jit(solution)/shard_map/ppermute | solution.py:257
